TPU v7x, 256 devices: a whole 4x4x8 slice. The times are simulated.
256 devices in a mesh: seq: 64 (over z, y, core), tp: 4 (over x).
Axes of the slice: x: 4, y: 4, z: 8, core: 2. Of those that a mesh axis runs over, the one named last changes fastest.
Arguments:
- text_query_matrix: bfloat16 [16384, 8192], P('seq', 'tp'), may hold values from -12 to 12
- vision: bfloat16 [16384, 8192], P(('seq', 'tp')), may hold values from -12 to 12
- key_matrix: bfloat16 [8192, 1024], P(None, 'tp'), may hold values from -0.0625 to 0.0625
- value_matrix: bfloat16 [8192, 1024], P(None, 'tp'), may hold values from -0.0625 to 0.0625
- query_norm_gain: float32 [128], replicated, may hold values from 0.5 to 1.5
- key_gain: float32 [128], replicated, may hold values from 0.5 to 1.5
- block_mask: int32 [256, 64], P('seq'), may hold values from 0 to 1, as said below
Outputs:
- attended: bfloat16 [16384, 8192], P('seq', 'tp')
Inputs may be any that keep to these rules, and one draw needn't show every extreme that they name: block_mask[b, i] is 1 on exactly one run of consecutive blocks b; the run starts in the blocks of text shard i (blocks i * 4 to (i + 1) * 4 - 1) and ends at or before the last block of text shard i + 3; in every draw some image's run ends exactly at that last block.
All inputs are finite; a program needn't handle non-finite values.
Results may differ from a plain program's by a relative error of at most 0.0076.
Values may be sent and summed in bfloat16 or wider, within the bound.
No kernel may reach another device: no remote copies, remote signals or barrier semaphores. Data moves between devices by JAX's collectives and lax.ppermute only.
A program may use at most 128 MiB of HBM per device.

v0:
```python
import jax
import jax.numpy as jnp
from jax import lax
from jax.sharding import PartitionSpec as P

HEAD_SIZE = 128
REACH = 4
BLOCK = 64


def shifted(value, axis, by):
    length = lax.axis_size(axis)
    pairs = [(i, i + by) for i in range(length) if 0 <= i + by < length]
    return lax.ppermute(value, axis, pairs)


def heads_normalized(tensor, scale_gain):
    return (
        tensor * lax.rsqrt(jnp.mean(tensor * tensor, axis=-1, keepdims=True) + 1e-05) * scale_gain
    )


def project(vision_rows, key_matrix, value_matrix, key_gain):
    kv_heads = key_matrix.shape[1] // HEAD_SIZE
    count = vision_rows.shape[0]
    key_projected = jnp.dot(vision_rows, key_matrix, preferred_element_type=jnp.float32).reshape(
        count, kv_heads, HEAD_SIZE
    )
    key_matrix_rows = (
        heads_normalized(key_projected, key_gain)
        .astype(jnp.bfloat16)
        .reshape(count, kv_heads * HEAD_SIZE)
    )
    value_matrix_rows = jnp.dot(
        vision_rows, value_matrix, preferred_element_type=jnp.float32
    ).astype(jnp.bfloat16)
    return jnp.stack([key_matrix_rows, value_matrix_rows])


def attend(carried, kv_block, weight_col, queries):
    totals, accumulated = carried
    kv_heads = queries.shape[1]
    score_scale = HEAD_SIZE ** (-0.5)
    split_block = kv_block.reshape(2, kv_block.shape[1], kv_heads, HEAD_SIZE)
    new_totals = []
    new_sums = []
    for kv_index in range(kv_heads):
        scores = (
            jnp.einsum(
                "tgd,kd->gtk",
                queries[:, kv_index],
                split_block[0, :, kv_index],
                preferred_element_type=jnp.float32,
            )
            * score_scale
        )
        weights = jnp.exp(scores) * weight_col[None, :, None]
        new_totals.append(totals[kv_index] + jnp.sum(weights, axis=2))
        new_sums.append(
            accumulated[:, kv_index]
            + jnp.einsum(
                "gtk,kd->tgd",
                weights.astype(jnp.bfloat16),
                split_block[1, :, kv_index],
                preferred_element_type=jnp.float32,
            )
        )
    return (jnp.stack(new_totals), jnp.stack(new_sums, axis=1))


def body(
    text_query_matrix, vision, key_matrix, value_matrix, query_norm_gain, key_gain, block_mask
):
    vision_rows = lax.all_gather(vision, "tp", axis=0, tiled=True)
    kv_heads = key_matrix.shape[1] // HEAD_SIZE
    query_group_width = text_query_matrix.shape[1] // HEAD_SIZE // kv_heads
    text_rows = text_query_matrix.shape[0]
    queries = heads_normalized(
        text_query_matrix.astype(jnp.float32).reshape(
            text_rows, kv_heads, query_group_width, HEAD_SIZE
        ),
        query_norm_gain,
    ).astype(jnp.bfloat16)
    arrivals = [vision_rows] + [
        shifted(vision_rows, "seq", distance) for distance in range(1, REACH)
    ]
    kv_blocks = [project(arrived, key_matrix, value_matrix, key_gain) for arrived in arrivals]
    carried = (
        jnp.zeros((kv_heads, query_group_width, text_rows), jnp.float32),
        jnp.zeros((text_rows, kv_heads, query_group_width, HEAD_SIZE), jnp.float32),
    )
    position = lax.axis_index("seq")
    for distance in range(REACH):
        image_index = position - distance
        column = lax.dynamic_slice_in_dim(block_mask, jnp.maximum(image_index, 0), 1, 1)[:, 0]
        column = jnp.where(image_index >= 0, column, jnp.zeros_like(column))
        weight_col = jnp.repeat(column.astype(jnp.float32), BLOCK)
        carried = attend(carried, kv_blocks[distance], weight_col, queries)
    totals, accumulated = carried
    totals_t = jnp.transpose(totals, (2, 0, 1))[..., None]
    has_image = totals_t > 0
    averaged = accumulated / jnp.where(has_image, totals_t, jnp.ones_like(totals_t))
    result_rows = jnp.where(has_image, averaged, jnp.zeros_like(averaged))
    return result_rows.astype(jnp.bfloat16).reshape(
        text_rows, kv_heads * query_group_width * HEAD_SIZE
    )


def solution(mesh):
    placed = (
        P("seq", "tp"),
        P(("seq", "tp"), None),
        P(None, "tp"),
        P(None, "tp"),
        P(),
        P(),
        P("seq", None),
    )
    return jax.shard_map(
        body, mesh=mesh, in_specs=placed, out_specs=P("seq", "tp"), check_vma=False
    )
```

profile of v0, /device:TPU:32, one launch (start us, length us, event | category | flops | bytes accessed | tf_op | source)
XLA Modules:
  0.0 340.6 jit_solution(10686656299928051354)
XLA Ops:
  7.3 55.3 %all-gather.2.cloned.1.call-done = bf16[256,8192]{1,0:T(8,128)(2,1)} async-done(((bf16[64,8192]{1,0:T(8,128)(2,1)}), bf16[256,8192]{1,0:T(8,128)(2,1)}) %all-gather.2.cloned.1.call-update) | async-done | bytes 4194320 | tf_op jit(solution)/shard_map/all_gather | solution.py:74
  62.6 2.8 collective-permute-start.2
  65.4 3.4 collective-permute-start.1
  68.8 2.9 collective-permute-start
  71.8 1.1 convert_reduce_fusion
  73.5 1.5 copy.19
  76.5 1.2 copy-done
  77.7 4.0 %bitcast_reduce_fusion.11 = (f32[256,2]{0,1:T(2,128)S(1)}, f32[256,256]{0,1:T(8,128)S(1)}) fusion(bf16[256,8192]{1,0:T(8,128)(2,1)} %all-gather.2.cloned.1.call-done, bf16[8192,256]{1,0:T(8,128)(2,1)S(1)} %copy-done), kind=kOutput, calls=%fused_computation.72 | convolution fusion | flops 1073872384 | bytes 8652800 | tf_op jit(solution)/shard_map/dot_general | solution.py:26
  81.9 5.3 %convolution_convert_fusion.3 = bf16[256,256]{0,1:T(8,128)(2,1)S(1)} fusion(bf16[256,8192]{1,0:T(8,128)(2,1)} %all-gather.2.cloned.1.call-done, bf16[8192,256]{1,0:T(8,128)(2,1)} %param.10), kind=kOutput, calls=%fused_computation.40 | convolution fusion | flops 1073807360 | bytes 8519680 | tf_op jit(solution)/shard_map/dot_general | solution.py:34
  87.2 67.9 %collective-permute-done.2 = bf16[256,8192]{1,0:T(8,128)(2,1)} collective-permute-done((bf16[256,8192]{1,0:T(8,128)(2,1)}, bf16[256,8192]{1,0:T(8,128)(2,1)}, u32[]{:S(2)}, u32[]{:S(2)}) %collective-permute-start.2) | collective-permute-done | bytes 4194336 | tf_op jit(solution)/shard_map/ppermute | solution.py:14
  155.1 4.0 %bitcast_reduce_fusion.8 = (f32[256,2]{0,1:T(2,128)S(1)}, f32[256,256]{0,1:T(8,128)S(1)}) fusion(bf16[256,8192]{1,0:T(8,128)(2,1)} %collective-permute-done.2, bf16[8192,256]{1,0:T(8,128)(2,1)S(1)} %copy-done.1), kind=kOutput, calls=%fused_computation.69 | convolution fusion | flops 1073872384 | bytes 8652800 | tf_op jit(solution)/shard_map/dot_general | solution.py:26
  159.3 97.8 %collective-permute-done.1 = bf16[256,8192]{1,0:T(8,128)(2,1)} collective-permute-done((bf16[256,8192]{1,0:T(8,128)(2,1)}, bf16[256,8192]{1,0:T(8,128)(2,1)}, u32[]{:S(2)}, u32[]{:S(2)}) %collective-permute-start.1) | collective-permute-done | bytes 4194336 | tf_op jit(solution)/shard_map/ppermute | solution.py:14
  257.1 5.2 %bitcast_reduce_fusion.9 = (f32[256,2]{0,1:T(2,128)S(1)}, f32[256,256]{0,1:T(8,128)S(1)}) fusion(bf16[256,8192]{1,0:T(8,128)(2,1)} %collective-permute-done.1, bf16[8192,256]{1,0:T(8,128)(2,1)} %param.9), kind=kOutput, calls=%fused_computation.70 | convolution fusion | flops 1073872384 | bytes 8652800 | tf_op jit(solution)/shard_map/dot_general | solution.py:26
  262.5 40.5 %collective-permute-done = bf16[256,8192]{1,0:T(8,128)(2,1)} collective-permute-done((bf16[256,8192]{1,0:T(8,128)(2,1)}, bf16[256,8192]{1,0:T(8,128)(2,1)}, u32[]{:S(2)}, u32[]{:S(2)}) %collective-permute-start) | collective-permute-done | bytes 4194336 | tf_op jit(solution)/shard_map/ppermute | solution.py:14
  302.9 5.2 %bitcast_reduce_fusion.10 = (f32[256,2]{0,1:T(2,128)S(1)}, f32[256,256]{0,1:T(8,128)S(1)}) fusion(bf16[256,8192]{1,0:T(8,128)(2,1)} %collective-permute-done, bf16[8192,256]{1,0:T(8,128)(2,1)} %param.9), kind=kOutput, calls=%fused_computation.71 | convolution fusion | flops 1073872384 | bytes 8652800 | tf_op jit(solution)/shard_map/dot_general | solution.py:26
  310.4 0.9 bitcast_reduce_fusion.4
  311.3 1.1 bitcast_reduce_fusion.6
  312.4 0.9 bitcast_reduce_fusion.5
  313.4 0.9 bitcast_reduce_fusion.7
  315.4 1.1 copy-done.2
  316.5 4.0 %convolution_convert_fusion.2 = bf16[256,256]{0,1:T(8,128)(2,1)S(1)} fusion(bf16[256,8192]{1,0:T(8,128)(2,1)} %collective-permute-done, bf16[8192,256]{1,0:T(8,128)(2,1)S(1)} %copy-done.2), kind=kOutput, calls=%fused_computation.39 | convolution fusion | flops 1073807360 | bytes 8519680 | tf_op jit(solution)/shard_map/dot_general | solution.py:34
  321.1 4.0 %convolution_convert_fusion.1 = bf16[256,256]{0,1:T(8,128)(2,1)S(1)} fusion(bf16[256,8192]{1,0:T(8,128)(2,1)} %collective-permute-done.1, bf16[8192,256]{1,0:T(8,128)(2,1)S(1)} %copy-done.2), kind=kOutput, calls=%fused_computation.38 | convolution fusion | flops 1073807360 | bytes 8519680 | tf_op jit(solution)/shard_map/dot_general | solution.py:34
  325.7 4.0 %convolution_convert_fusion = bf16[256,256]{0,1:T(8,128)(2,1)S(1)} fusion(bf16[256,8192]{1,0:T(8,128)(2,1)} %collective-permute-done.2, bf16[8192,256]{1,0:T(8,128)(2,1)S(1)} %copy-done.2), kind=kOutput, calls=%fused_computation.37 | convolution fusion | flops 1073807360 | bytes 8519680 | tf_op jit(solution)/shard_map/dot_general | solution.py:34
  332.4 1.4 copy.32
  (46 shorter events, 10.2 us)
Async XLA Ops:
  6.5 56.1 %all-gather.2.cloned.1.call-start = ((), (), s32[]{:S(2)}) async-start(), calls=%async_computation | async-start | bytes 5242880 | tf_op jit(solution)/shard_map/all_gather | solution.py:74
  62.6 92.5 %collective-permute-start.2 = (bf16[256,8192]{1,0:T(8,128)(2,1)}, bf16[256,8192]{1,0:T(8,128)(2,1)}, u32[]{:S(2)}, u32[]{:S(2)}) collective-permute-start(bf16[256,8192]{1,0:T(8,128)(2,1)} %all-gather.2.cloned.1.call-done), channel_id=1, source_target_pairs={{0,12},{4,16},{8,20},{12,24},{16,28},{20,32},{24,36},{28,40},{32,4... | collective-permute-start | bytes 12582920 | tf_op jit(solution)/shard_map/ppermute | solution.py:14
  65.4 191.7 %collective-permute-start.1 = (bf16[256,8192]{1,0:T(8,128)(2,1)}, bf16[256,8192]{1,0:T(8,128)(2,1)}, u32[]{:S(2)}, u32[]{:S(2)}) collective-permute-start(bf16[256,8192]{1,0:T(8,128)(2,1)} %all-gather.2.cloned.1.call-done), channel_id=1, source_target_pairs={{0,8},{4,12},{8,16},{12,20},{16,24},{20,28},{24,32},{28,36},{32,40... | collective-permute-start | bytes 12582920 | tf_op jit(solution)/shard_map/ppermute | solution.py:14
  68.8 234.1 %collective-permute-start = (bf16[256,8192]{1,0:T(8,128)(2,1)}, bf16[256,8192]{1,0:T(8,128)(2,1)}, u32[]{:S(2)}, u32[]{:S(2)}) collective-permute-start(bf16[256,8192]{1,0:T(8,128)(2,1)} %all-gather.2.cloned.1.call-done), channel_id=1, source_target_pairs={{0,4},{4,8},{8,12},{12,16},{16,20},{20,24},{24,28},{28,32},{32,36}... | collective-permute-start | bytes 12582920 | tf_op jit(solution)/shard_map/ppermute | solution.py:14
  75.0 0.8 copy-start.4
  75.5 2.2 copy-start
  81.9 73.2 %copy-start.1 = (bf16[8192,256]{1,0:T(8,128)(2,1)S(1)}, bf16[8192,256]{1,0:T(8,128)(2,1)}, u32[]{:S(2)}) copy-start(bf16[8192,256]{1,0:T(8,128)(2,1)} %param.9) | copy-start | bytes 12582916
  262.4 45.9 %copy-start.3 = (f32[128]{0:T(128)S(1)}, f32[128]{0:T(128)}, u32[]{:S(2)}) copy-start(f32[128]{0:T(128)} %param.12) | copy-start | bytes 1540
  314.3 2.2 copy-start.2
Sparse Core Ops, SparseCore 0:
  9.2 53.3 all-gather.1
where the time goes:
time: 341 us
  waiting for transfers between devices  262 us (77%)
  matrix products  46 us (13%)
  between operations  13.7 us (4%)
  starting transfers between devices  9.15 us (3%)
  local copies, waits for them, and re-layouts  6.85 us (2%)
    ppermute x3, waiting for transfers between devices, shifted(): return lax.ppermute(value, axis, pairs)  206 us
    all_gather x1, waiting for transfers between devices, body(): vision_rows = lax.all_gather(vision, 'tp', axis=0, tiled=True)  55.3 us
    dot_general x4, matrix products, project(): jnp.dot(vision_rows, key_matrix, preferred_element_type=jnp.float32)  18.5 us
    dot_general x4, matrix products, project(): jnp.dot(vision_rows, value_matrix, preferred_element_type=jnp.float32)  17.4 us
    ppermute x3, starting transfers between devices, shifted(): return lax.ppermute(value, axis, pairs)  9.15 us
  transfers between devices with their start and end apart: 4, of which 4 were waited for; matrix products, arithmetic and copies ran while one was open for 7% of the time, Pallas kernels for 0%

commit v1 on v0

v1 whole, which is shorter than its diff:
```python
import functools
import math

import jax
import jax.numpy as jnp
from jax import lax
from jax.experimental import pallas as pl
from jax.experimental.pallas import tpu as pltpu
from jax.sharding import PartitionSpec as P

HEAD_SIZE = 128
REACH = 4
BLOCK = 64
EPS = 1e-05
SCORE_SCALE = HEAD_SIZE ** (-0.5) * math.log2(math.e)
VMEM_LIMIT = 48 * 1024 * 1024


def shifted(value, axis, by):
    length = lax.axis_size(axis)
    pairs = [(i, i + by) for i in range(length) if 0 <= i + by < length]
    return lax.ppermute(value, axis, pairs)


def turned(value, axis, by):
    length = lax.axis_size(axis)
    return lax.ppermute(value, axis, [(i, (i + by) % length) for i in range(length)])


def project_kernel(count, *refs):
    row_refs = refs[:count]
    key_ref, value_ref, gain_ref, out_ref, total = refs[count:]
    step = pl.program_id(0)
    width = key_ref.shape[1]
    rows = [ref[...] for ref in row_refs]
    rows = rows[0] if count == 1 else jnp.concatenate(rows, axis=0)

    @pl.when(step == 0)
    def _():
        total[...] = jnp.zeros_like(total)

    total[:, :width] += jnp.dot(rows, key_ref[...], preferred_element_type=jnp.float32)
    total[:, width:] += jnp.dot(rows, value_ref[...], preferred_element_type=jnp.float32)

    @pl.when(step == pl.num_programs(0) - 1)
    def _():
        for head in range(width // HEAD_SIZE):
            at = slice(head * HEAD_SIZE, (head + 1) * HEAD_SIZE)
            keys = total[:, at]
            mean = jnp.mean(keys * keys, axis=-1, keepdims=True)
            out_ref[:, at] = (keys * lax.rsqrt(mean + EPS) * gain_ref[...]).astype(out_ref.dtype)
        out_ref[:, width:] = total[:, width:].astype(out_ref.dtype)


def project(row_parts, key_matrix, value_matrix, key_gain, name):
    depth, width = key_matrix.shape
    part = depth // 8
    rows = sum(each.shape[0] for each in row_parts)
    return pl.pallas_call(
        functools.partial(project_kernel, len(row_parts)),
        out_shape=jax.ShapeDtypeStruct((rows, 2 * width), jnp.bfloat16),
        grid=(depth // part,),
        in_specs=[pl.BlockSpec((each.shape[0], part), lambda i: (0, i)) for each in row_parts]
        + [pl.BlockSpec((part, width), lambda i: (i, 0))] * 2
        + [pl.BlockSpec((1, HEAD_SIZE), lambda i: (0, 0))],
        out_specs=pl.BlockSpec((rows, 2 * width), lambda i: (0, 0)),
        scratch_shapes=[pltpu.VMEM((rows, 2 * width), jnp.float32)],
        compiler_params=pltpu.CompilerParams(vmem_limit_bytes=VMEM_LIMIT),
        name=name,
    )(*row_parts, key_matrix, value_matrix, key_gain)


def attend_kernel(first, last, group, *refs):
    refs = list(refs)
    query_ref = refs.pop(0)
    key_refs = [refs.pop(0) for _ in range(REACH)]
    value_refs = [refs.pop(0) for _ in range(REACH)]
    open_ref = refs.pop(0)
    if first:
        gain_ref, normed_ref = refs.pop(0), refs.pop(0)
    else:
        sums_in, totals_in = refs.pop(0), refs.pop(0)
    rows = query_ref.shape[0]
    count = key_refs[0].shape[0]
    keys = jnp.concatenate([ref[...] for ref in key_refs], axis=0)
    values = jnp.concatenate([ref[...] for ref in value_refs], axis=0)
    values = jnp.concatenate([values, jnp.ones_like(values)], axis=1)
    image = lax.broadcasted_iota(jnp.int32, (rows, REACH * count), 1) // count
    is_open = jnp.zeros((rows, REACH * count), jnp.float32)
    for at in range(REACH):
        is_open = jnp.where(image == at, open_ref[:, at : at + 1], is_open)
    lane = lax.broadcasted_iota(jnp.int32, (rows, HEAD_SIZE), 1)
    totals = jnp.zeros((rows, HEAD_SIZE), jnp.float32)
    for head in range(group):
        at = slice(head * HEAD_SIZE, (head + 1) * HEAD_SIZE)
        if first:
            raw = query_ref[:, at].astype(jnp.float32)
            mean = jnp.mean(raw * raw, axis=-1, keepdims=True)
            query = (raw * lax.rsqrt(mean + EPS) * gain_ref[...]).astype(jnp.bfloat16)
            normed_ref[:, at] = query
        else:
            query = query_ref[:, at]
        scores = lax.dot_general(
            query, keys, (((1,), (1,)), ((), ())), preferred_element_type=jnp.float32
        )
        weights = (jnp.exp2(scores) * is_open).astype(jnp.bfloat16)
        both = jnp.dot(weights, values, preferred_element_type=jnp.float32)
        sums, total = both[:, :HEAD_SIZE], both[:, HEAD_SIZE:]
        if not first:
            sums = sums + sums_in[:, at]
            total = total + totals_in[:, head : head + 1]
        if last:
            has_image = total > 0
            safe = jnp.where(has_image, total, jnp.ones_like(total))
            result = jnp.where(has_image, sums / safe, jnp.zeros_like(sums))
            refs[0][:, at] = result.astype(jnp.bfloat16)
        else:
            refs[0][:, at] = sums
            totals = jnp.where(lane == head, total, totals)
    if not last:
        refs[1][...] = totals


def attend(query, blocks, is_open, gain, carried, last, name):
    first = carried is None
    rows, width = query.shape
    count = blocks[0].shape[0]
    kv_heads = blocks[0].shape[1] // (2 * HEAD_SIZE)
    wide = width // kv_heads
    query_spec = pl.BlockSpec((rows, wide), lambda i: (0, i))
    totals_spec = pl.BlockSpec((rows, HEAD_SIZE), lambda i: (0, i))
    in_specs = [query_spec]
    in_specs += [pl.BlockSpec((count, HEAD_SIZE), lambda i: (0, i))] * REACH
    in_specs += [pl.BlockSpec((count, HEAD_SIZE), lambda i: (0, kv_heads + i))] * REACH
    in_specs += [pl.BlockSpec((rows, REACH), lambda i: (0, 0))]
    operands = [query, *blocks, *blocks, is_open]
    if first:
        in_specs += [pl.BlockSpec((1, HEAD_SIZE), lambda i: (0, 0))]
        operands += [gain]
    else:
        in_specs += [query_spec, totals_spec]
        operands += list(carried)
    if last:
        out_shape = [jax.ShapeDtypeStruct((rows, width), jnp.bfloat16)]
        out_specs = [query_spec]
    else:
        out_shape = [
            jax.ShapeDtypeStruct((rows, width), jnp.float32),
            jax.ShapeDtypeStruct((rows, kv_heads * HEAD_SIZE), jnp.float32),
        ]
        out_specs = [query_spec, totals_spec]
    if first:
        out_shape.insert(0, jax.ShapeDtypeStruct((rows, width), jnp.bfloat16))
        out_specs.insert(0, query_spec)
    return pl.pallas_call(
        functools.partial(attend_kernel, first, last, wide // HEAD_SIZE),
        out_shape=out_shape,
        grid=(kv_heads,),
        in_specs=in_specs,
        out_specs=out_specs,
        compiler_params=pltpu.CompilerParams(vmem_limit_bytes=VMEM_LIMIT),
        name=name,
    )(*operands)


def body(
    text_query_matrix, vision, key_matrix, value_matrix, query_norm_gain, key_gain, block_mask
):
    position = lax.axis_index("seq")
    rows = text_query_matrix.shape[0]
    images = lax.broadcasted_iota(jnp.int32, (1, block_mask.shape[1], REACH), 1)
    wanted = position - lax.broadcasted_iota(jnp.int32, (1, block_mask.shape[1], REACH), 2)
    is_open = jnp.sum(jnp.where(images == wanted, block_mask[:, :, None], 0), axis=1)
    is_open = jnp.repeat(is_open.astype(jnp.float32), BLOCK, axis=0)
    query_gain = (query_norm_gain * SCORE_SCALE).reshape(1, HEAD_SIZE)
    key_gain = key_gain.reshape(1, HEAD_SIZE)

    half = vision.shape[0] // 2
    upper, lower = vision[:half], vision[half:]
    upper_left = turned(upper, "tp", 1)
    lower_right = turned(lower, "tp", -1)
    lower_left = turned(lower, "tp", 1)
    upper_right = turned(upper, "tp", -1)
    upper_across = turned(upper_left, "tp", 1)
    lower_across = turned(lower_right, "tp", -1)

    def reached(row_parts, name):
        own = project(row_parts, key_matrix, value_matrix, key_gain, "project_" + name)
        return [own] + [shifted(own, "seq", by) for by in range(1, REACH)]

    own = reached([vision], "own")
    normed, *carried = attend(
        text_query_matrix, own, is_open, query_gain, None, False, "attend_own"
    )
    sides = reached([upper_left, lower_left, upper_right, lower_right], "sides")
    carried = attend(normed, sides, is_open, None, carried, False, "attend_sides")
    across = reached([upper_across, lower_across], "across")
    (result,) = attend(normed, across, is_open, None, carried, True, "attend_across")
    return result


def solution(mesh):
    placed = (
        P("seq", "tp"),
        P(("seq", "tp"), None),
        P(None, "tp"),
        P(None, "tp"),
        P(),
        P(),
        P("seq", None),
    )
    return jax.shard_map(
        body, mesh=mesh, in_specs=placed, out_specs=P("seq", "tp"), check_vma=False
    )
```

time: 341 us -> 89.5 us (0.26)
  the two profiles are of different devices: /device:TPU:32 before, /device:TPU:79 now
where the time goes in v1:
time: 89.5 us; the launch traced here: 88.8 us
  starting transfers between devices  41.2 us (46%)
  Pallas kernels  29.3 us (33%)
  waiting for transfers between devices  10.1 us (11%)
  local copies, waits for them, and re-layouts  7.68 us (9%)
    ppermute x9, starting transfers between devices, shifted(): return lax.ppermute(value, axis, pairs)  34.4 us
    pallas_call x3, Pallas kernels, project(): pl.pallas_call(functools.partial(project_kernel, len(row_parts)), out_sha...  19.2 us
    pallas_call x3, Pallas kernels, attend(): pl.pallas_call(functools.partial(attend_kernel, first, last, wide // HEAD...  10.1 us
    ppermute x6, waiting for transfers between devices, turned(): lax.ppermute(value, axis, [(i, (i + by) % length) for i in range(length)])  10.1 us
    ppermute x6, starting transfers between devices, turned(): lax.ppermute(value, axis, [(i, (i + by) % length) for i in range(length)])  6.82 us
    unnamed x18, local copies, waits for them, and re-layouts  5.42 us
    slice x1, local copies, waits for them, and re-layouts, body(): upper, lower = (vision[:half], vision[half:])  2.25 us
  transfers between devices with their start and end apart: 15, of which 1 were waited for; matrix products, arithmetic and copies ran while one was open for 0% of the time, Pallas kernels for 30%

profile of v1, /device:TPU:79, one launch (start us, length us, event | category | flops | bytes accessed | tf_op | source)
XLA Modules:
  0.0 88.8 jit_solution(15604129569950940698)
XLA Ops:
  0.0 2.2 %fusion = (bf16[32,8192]{1,0:T(8,128)(2,1)}, bf16[32,8192]{1,0:T(8,128)(2,1)}) fusion(bf16[64,8192]{1,0:T(8,128)(2,1)} %refs_0_.2), kind=kLoop, calls=%fused_computation.4 | loop fusion | bytes 2097152 | tf_op jit(solution)/shard_map/slice | solution.py:179
  2.8 2.1 %collective-permute-start.3 = (bf16[32,8192]{1,0:T(8,128)(2,1)}, bf16[32,8192]{1,0:T(8,128)(2,1)S(1)}, u32[]{:S(2)}, u32[]{:S(2)}) collective-permute-start(bf16[32,8192]{1,0:T(8,128)(2,1)} %get-tuple-element.16), channel_id=1, source_target_pairs={{0,1},{1,2},{2,3},{3,0},{4,5},{5,6},{6,7},{7,4},{8,9},{9,10},{10,1... | collective-permute-start | bytes 1572872 | tf_op jit(solution)/shard_map/ppermute | solution.py:27
  5.0 1.4 %collective-permute-start.11 = (bf16[32,8192]{1,0:T(8,128)(2,1)}, bf16[32,8192]{1,0:T(8,128)(2,1)S(1)}, u32[]{:S(2)}, u32[]{:S(2)}) collective-permute-start(bf16[32,8192]{1,0:T(8,128)(2,1)} %get-tuple-element.16), channel_id=1, source_target_pairs={{0,3},{1,0},{2,1},{3,2},{4,7},{5,4},{6,5},{7,6},{8,11},{9,8},{10,9... | collective-permute-start | bytes 1572872 | tf_op jit(solution)/shard_map/ppermute | solution.py:27
  6.4 10.1 %collective-permute-done.5.refs_3_ = bf16[32,8192]{1,0:T(8,128)(2,1)S(1)} collective-permute-done((bf16[32,8192]{1,0:T(8,128)(2,1)}, bf16[32,8192]{1,0:T(8,128)(2,1)S(1)}, u32[]{:S(2)}, u32[]{:S(2)}) %collective-permute-start.5) | collective-permute-done | bytes 524320 | tf_op jit(solution)/shard_map/ppermute | solution.py:27
  16.5 2.7 %collective-permute-start.4 = (bf16[32,8192]{1,0:T(8,128)(2,1)S(1)}, bf16[32,8192]{1,0:T(8,128)(2,1)S(1)}, u32[]{:S(2)}, u32[]{:S(2)}) collective-permute-start(bf16[32,8192]{1,0:T(8,128)(2,1)S(1)} %collective-permute-done.3.refs_0_), channel_id=1, source_target_pairs={{0,1},{1,2},{2,3},{3,0},{4,5},{5,6},{6,7},{7,4},{8,9},{9,10},{10,1... | collective-permute-start | bytes 1572872 | tf_op jit(solution)/shard_map/ppermute | solution.py:27
  19.1 2.2 %copy-done = bf16[8192,256]{1,0:T(8,128)(2,1)S(1)} copy-done((bf16[8192,256]{1,0:T(8,128)(2,1)S(1)}, bf16[8192,256]{1,0:T(8,128)(2,1)}, u32[]{:S(2)}) %copy-start) | copy-done | bytes 4194328
  21.3 1.2 %copy-done.2 = bf16[64,8192]{1,0:T(8,128)(2,1)S(1)} copy-done((bf16[64,8192]{1,0:T(8,128)(2,1)S(1)}, bf16[64,8192]{1,0:T(8,128)(2,1)}, u32[]{:S(2)}) %copy-start.2) | copy-done | bytes 1048600
  22.6 0.7 copy-done.5
  23.2 6.0 %project_own.1.refs_1_.refs_5_ = bf16[64,512]{1,0:T(8,128)(2,1)S(1)} custom-call(bf16[64,8192]{1,0:T(8,128)(2,1)S(1)} %copy-done.2, bf16[8192,256]{1,0:T(8,128)(2,1)S(1)} %copy-done, bf16[8192,256]{1,0:T(8,128)(2,1)} %refs_5_.1, f32[1,128]{1,0:T(1,128)S(1)} %bitcast.7), custom_call_target="tpu_custom_call" | custom-call | tf_op jit(solution)/shard_map/project_own/pallas_call | solution.py:59
  29.2 7.1 %collective-permute-start.2 = (bf16[64,512]{1,0:T(8,128)(2,1)S(1)}, bf16[64,512]{1,0:T(8,128)(2,1)S(1)}, u32[]{:S(2)}, u32[]{:S(2)}) collective-permute-start(bf16[64,512]{1,0:T(8,128)(2,1)S(1)} %project_own.1.refs_1_.refs_5_), channel_id=1, source_target_pairs={{0,12},{4,16},{8,20},{12,24},{16,28},{20,32},{24,36},{28,40},{32,4... | collective-permute-start | bytes 196616 | tf_op jit(solution)/shard_map/ppermute | solution.py:22
  36.5 2.9 %collective-permute-start.1 = (bf16[64,512]{1,0:T(8,128)(2,1)S(1)}, bf16[64,512]{1,0:T(8,128)(2,1)S(1)}, u32[]{:S(2)}, u32[]{:S(2)}) collective-permute-start(bf16[64,512]{1,0:T(8,128)(2,1)S(1)} %project_own.1.refs_1_.refs_5_), channel_id=1, source_target_pairs={{0,8},{4,12},{8,16},{12,20},{16,24},{20,28},{24,32},{28,36},{32,40... | collective-permute-start | bytes 196616 | tf_op jit(solution)/shard_map/ppermute | solution.py:22
  39.3 1.9 %collective-permute-start = (bf16[64,512]{1,0:T(8,128)(2,1)S(1)}, bf16[64,512]{1,0:T(8,128)(2,1)S(1)}, u32[]{:S(2)}, u32[]{:S(2)}) collective-permute-start(bf16[64,512]{1,0:T(8,128)(2,1)S(1)} %project_own.1.refs_1_.refs_5_), channel_id=1, source_target_pairs={{0,4},{4,8},{8,12},{12,16},{16,20},{20,24},{24,28},{28,32},{32,36}... | collective-permute-start | bytes 196616 | tf_op jit(solution)/shard_map/ppermute | solution.py:22
  41.3 7.0 %project_sides.1.refs_1_.refs_5_ = bf16[128,512]{1,0:T(8,128)(2,1)S(1)} custom-call(bf16[32,8192]{1,0:T(8,128)(2,1)S(1)} %collective-permute-done.3.refs_0_, bf16[32,8192]{1,0:T(8,128)(2,1)S(1)} %collective-permute-done.10.refs_1_, bf16[32,8192]{1,0:T(8,128)(2,1)S(1)} %collective-permute-done.11.refs_2_, ...), custom_call_target="tpu_custom_call" | custom-call | tf_op jit(solution)/shard_map/project_sides/pallas_call | solution.py:59
  48.3 5.8 %collective-permute-start.14 = (bf16[128,512]{1,0:T(8,128)(2,1)S(1)}, bf16[128,512]{1,0:T(8,128)(2,1)S(1)}, u32[]{:S(2)}, u32[]{:S(2)}) collective-permute-start(bf16[128,512]{1,0:T(8,128)(2,1)S(1)} %project_sides.1.refs_1_.refs_5_), channel_id=1, source_target_pairs={{0,12},{4,16},{8,20},{12,24},{16,28},{20,32},{24,36},{28,40},{32,4... | collective-permute-start | bytes 393224 | tf_op jit(solution)/shard_map/ppermute | solution.py:22
  54.1 1.9 %collective-permute-start.13 = (bf16[128,512]{1,0:T(8,128)(2,1)S(1)}, bf16[128,512]{1,0:T(8,128)(2,1)S(1)}, u32[]{:S(2)}, u32[]{:S(2)}) collective-permute-start(bf16[128,512]{1,0:T(8,128)(2,1)S(1)} %project_sides.1.refs_1_.refs_5_), channel_id=1, source_target_pairs={{0,8},{4,12},{8,16},{12,20},{16,24},{20,28},{24,32},{28,36},{32,40... | collective-permute-start | bytes 393224 | tf_op jit(solution)/shard_map/ppermute | solution.py:22
  56.1 2.7 %collective-permute-start.12 = (bf16[128,512]{1,0:T(8,128)(2,1)S(1)}, bf16[128,512]{1,0:T(8,128)(2,1)S(1)}, u32[]{:S(2)}, u32[]{:S(2)}) collective-permute-start(bf16[128,512]{1,0:T(8,128)(2,1)S(1)} %project_sides.1.refs_1_.refs_5_), channel_id=1, source_target_pairs={{0,4},{4,8},{8,12},{12,16},{16,20},{20,24},{24,28},{28,32},{32,36}... | collective-permute-start | bytes 393224 | tf_op jit(solution)/shard_map/ppermute | solution.py:22
  58.9 6.1 %project_across.1.refs_1_.refs_5_ = bf16[64,512]{1,0:T(8,128)(2,1)S(1)} custom-call(bf16[32,8192]{1,0:T(8,128)(2,1)S(1)} %collective-permute-done.4.refs_0_, bf16[32,8192]{1,0:T(8,128)(2,1)S(1)} %collective-permute-done.6.refs_1_, bf16[8192,256]{1,0:T(8,128)(2,1)S(1)} %copy-done.1, bf16[8192,256]{1,0:T(8,128)(2,1)} %refs_5_.1, f32[1,128]{1,0:T(1,128)S(1)} %bitcast.9), custom_call_target="tpu_custom_call" | custom-call | tf_op jit(solution)/shard_map/project_across/pallas_call | solution.py:59
  65.0 6.0 %collective-permute-start.9 = (bf16[64,512]{1,0:T(8,128)(2,1)S(1)}, bf16[64,512]{1,0:T(8,128)(2,1)S(1)}, u32[]{:S(2)}, u32[]{:S(2)}) collective-permute-start(bf16[64,512]{1,0:T(8,128)(2,1)S(1)} %project_across.1.refs_1_.refs_5_), channel_id=1, source_target_pairs={{0,12},{4,16},{8,20},{12,24},{16,28},{20,32},{24,36},{28,40},{32,4... | collective-permute-start | bytes 196616 | tf_op jit(solution)/shard_map/ppermute | solution.py:22
  71.0 2.6 %collective-permute-start.8 = (bf16[64,512]{1,0:T(8,128)(2,1)S(1)}, bf16[64,512]{1,0:T(8,128)(2,1)S(1)}, u32[]{:S(2)}, u32[]{:S(2)}) collective-permute-start(bf16[64,512]{1,0:T(8,128)(2,1)S(1)} %project_across.1.refs_1_.refs_5_), channel_id=1, source_target_pairs={{0,8},{4,12},{8,16},{12,20},{16,24},{20,28},{24,32},{28,36},{32,40... | collective-permute-start | bytes 196616 | tf_op jit(solution)/shard_map/ppermute | solution.py:22
  73.6 3.4 %collective-permute-start.7 = (bf16[64,512]{1,0:T(8,128)(2,1)S(1)}, bf16[64,512]{1,0:T(8,128)(2,1)S(1)}, u32[]{:S(2)}, u32[]{:S(2)}) collective-permute-start(bf16[64,512]{1,0:T(8,128)(2,1)S(1)} %project_across.1.refs_1_.refs_5_), channel_id=1, source_target_pairs={{0,4},{4,8},{8,12},{12,16},{16,20},{20,24},{24,28},{28,32},{32,36}... | collective-permute-start | bytes 196616 | tf_op jit(solution)/shard_map/ppermute | solution.py:22
  77.3 2.8 %attend_own.1 = (bf16[256,2048]{1,0:T(8,128)(2,1)S(1)}, f32[256,2048]{1,0:T(8,128)S(1)}, f32[256,256]{1,0:T(8,128)S(1)}) custom-call(bf16[256,2048]{1,0:T(8,128)(2,1)S(1)} %copy-done.4, bf16[64,512]{1,0:T(8,128)(2,1)S(1)} %project_own.1.refs_1_.refs_5_, bf16[64,512]{1,0:T(8,128)(2,1)S(1)} %collective-permute-done.refs_2_.refs_6_, ...), custom_call_target="tpu_custom_call" | custom-call | tf_op jit(solution)/shard_map/attend_own/pallas_call | solution.py:155
  80.1 1.3 %copy-done.3 = f32[256,2048]{1,0:T(8,128)} copy-done((f32[256,2048]{1,0:T(8,128)}, f32[256,2048]{1,0:T(8,128)S(1)}, u32[]{:S(2)}) %copy-start.3) | copy-done | bytes 2097176
  81.4 4.4 %attend_sides.1 = (f32[256,2048]{1,0:T(8,128)S(1)}, f32[256,256]{1,0:T(8,128)S(1)}) custom-call(bf16[256,2048]{1,0:T(8,128)(2,1)S(1)} %get-tuple-element.10.refs_0_, bf16[128,512]{1,0:T(8,128)(2,1)S(1)} %project_sides.1.refs_1_.refs_5_, bf16[128,512]{1,0:T(8,128)(2,1)S(1)} %collective-permute-done.12.refs_2_.refs_6_, ...), custom_call_target="tpu_custom_call" | custom-call | tf_op jit(solution)/shard_map/attend_sides/pallas_call | solution.py:155
  85.8 2.9 %attend_across.1 = bf16[256,2048]{1,0:T(8,128)(2,1)} custom-call(bf16[256,2048]{1,0:T(8,128)(2,1)S(1)} %get-tuple-element.10.refs_0_, bf16[64,512]{1,0:T(8,128)(2,1)S(1)} %project_across.1.refs_1_.refs_5_, bf16[64,512]{1,0:T(8,128)(2,1)S(1)} %collective-permute-done.7.refs_2_.refs_6_, bf16[64,512]{1,0:T(8,128)(2,1)S(1)} %collective-permute-done.8.refs_3_.refs_7_, ...), custom_call_target="tpu_custom_call" | custom-call | tf_op jit(solution)/shard_map/attend_across/pallas_call | solution.py:155
  (37 shorter events, 0.9 us)
Async XLA Ops:
  2.2 14.2 %collective-permute-start.5 = (bf16[32,8192]{1,0:T(8,128)(2,1)}, bf16[32,8192]{1,0:T(8,128)(2,1)S(1)}, u32[]{:S(2)}, u32[]{:S(2)}) collective-permute-start(bf16[32,8192]{1,0:T(8,128)(2,1)} %get-tuple-element.15), channel_id=1, source_target_pairs={{0,3},{1,0},{2,1},{3,2},{4,7},{5,4},{6,5},{7,6},{8,11},{9,8},{10,9... | collective-permute-start | bytes 1572872 | tf_op jit(solution)/shard_map/ppermute | solution.py:27
  2.8 13.7 %collective-permute-start.3 = (bf16[32,8192]{1,0:T(8,128)(2,1)}, bf16[32,8192]{1,0:T(8,128)(2,1)S(1)}, u32[]{:S(2)}, u32[]{:S(2)}) collective-permute-start(bf16[32,8192]{1,0:T(8,128)(2,1)} %get-tuple-element.16), channel_id=1, source_target_pairs={{0,1},{1,2},{2,3},{3,0},{4,5},{5,6},{6,7},{7,4},{8,9},{9,10},{10,1... | collective-permute-start | bytes 1572872 | tf_op jit(solution)/shard_map/ppermute | solution.py:27
  4.9 31.5 %collective-permute-start.10 = (bf16[32,8192]{1,0:T(8,128)(2,1)}, bf16[32,8192]{1,0:T(8,128)(2,1)S(1)}, u32[]{:S(2)}, u32[]{:S(2)}) collective-permute-start(bf16[32,8192]{1,0:T(8,128)(2,1)} %get-tuple-element.15), channel_id=1, source_target_pairs={{0,1},{1,2},{2,3},{3,0},{4,5},{5,6},{6,7},{7,4},{8,9},{9,10},{10,1... | collective-permute-start | bytes 1572872 | tf_op jit(solution)/shard_map/ppermute | solution.py:27
  5.0 34.4 %collective-permute-start.11 = (bf16[32,8192]{1,0:T(8,128)(2,1)}, bf16[32,8192]{1,0:T(8,128)(2,1)S(1)}, u32[]{:S(2)}, u32[]{:S(2)}) collective-permute-start(bf16[32,8192]{1,0:T(8,128)(2,1)} %get-tuple-element.16), channel_id=1, source_target_pairs={{0,3},{1,0},{2,1},{3,2},{4,7},{5,4},{6,5},{7,6},{8,11},{9,8},{10,9... | collective-permute-start | bytes 1572872 | tf_op jit(solution)/shard_map/ppermute | solution.py:27
  16.5 37.7 %collective-permute-start.6 = (bf16[32,8192]{1,0:T(8,128)(2,1)S(1)}, bf16[32,8192]{1,0:T(8,128)(2,1)S(1)}, u32[]{:S(2)}, u32[]{:S(2)}) collective-permute-start(bf16[32,8192]{1,0:T(8,128)(2,1)S(1)} %collective-permute-done.5.refs_3_), channel_id=1, source_target_pairs={{0,3},{1,0},{2,1},{3,2},{4,7},{5,4},{6,5},{7,6},{8,11},{9,8},{10,9... | collective-permute-start | bytes 1572872 | tf_op jit(solution)/shard_map/ppermute | solution.py:27
  16.5 39.6 %collective-permute-start.4 = (bf16[32,8192]{1,0:T(8,128)(2,1)S(1)}, bf16[32,8192]{1,0:T(8,128)(2,1)S(1)}, u32[]{:S(2)}, u32[]{:S(2)}) collective-permute-start(bf16[32,8192]{1,0:T(8,128)(2,1)S(1)} %collective-permute-done.3.refs_0_), channel_id=1, source_target_pairs={{0,1},{1,2},{2,3},{3,0},{4,5},{5,6},{6,7},{7,4},{8,9},{9,10},{10,1... | collective-permute-start | bytes 1572872 | tf_op jit(solution)/shard_map/ppermute | solution.py:27
  19.1 2.2 %copy-start = (bf16[8192,256]{1,0:T(8,128)(2,1)S(1)}, bf16[8192,256]{1,0:T(8,128)(2,1)}, u32[]{:S(2)}) copy-start(bf16[8192,256]{1,0:T(8,128)(2,1)} %refs_4_.1) | copy-start | bytes 12582916
  21.3 1.2 %copy-start.2 = (bf16[64,8192]{1,0:T(8,128)(2,1)S(1)}, bf16[64,8192]{1,0:T(8,128)(2,1)}, u32[]{:S(2)}) copy-start(bf16[64,8192]{1,0:T(8,128)(2,1)} %refs_0_.2) | copy-start | bytes 3145732
  22.6 0.7 copy-start.5
  23.2 18.0 %copy-start.6 = (f32[128]{0:T(128)S(1)}, f32[128]{0:T(128)}, u32[]{:S(2)}) copy-start(f32[128]{0:T(128)} %param.12) | copy-start | bytes 1540
  29.2 19.1 %collective-permute-start.2 = (bf16[64,512]{1,0:T(8,128)(2,1)S(1)}, bf16[64,512]{1,0:T(8,128)(2,1)S(1)}, u32[]{:S(2)}, u32[]{:S(2)}) collective-permute-start(bf16[64,512]{1,0:T(8,128)(2,1)S(1)} %project_own.1.refs_1_.refs_5_), channel_id=1, source_target_pairs={{0,12},{4,16},{8,20},{12,24},{16,28},{20,32},{24,36},{28,40},{32,4... | collective-permute-start | bytes 196616 | tf_op jit(solution)/shard_map/ppermute | solution.py:22
  36.4 22.4 %copy-start.8 = (f32[128]{0:T(128)S(1)}, f32[128]{0:T(128)}, u32[]{:S(2)}) copy-start(f32[128]{0:T(128)} %param.11) | copy-start | bytes 1540
  36.4 22.4 %copy-start.1 = (bf16[8192,256]{1,0:T(8,128)(2,1)S(1)}, bf16[8192,256]{1,0:T(8,128)(2,1)}, u32[]{:S(2)}) copy-start(bf16[8192,256]{1,0:T(8,128)(2,1)} %refs_4_.1) | copy-start | bytes 12582916
  36.5 28.6 %collective-permute-start.1 = (bf16[64,512]{1,0:T(8,128)(2,1)S(1)}, bf16[64,512]{1,0:T(8,128)(2,1)S(1)}, u32[]{:S(2)}, u32[]{:S(2)}) collective-permute-start(bf16[64,512]{1,0:T(8,128)(2,1)S(1)} %project_own.1.refs_1_.refs_5_), channel_id=1, source_target_pairs={{0,8},{4,12},{8,16},{12,20},{16,24},{20,28},{24,32},{28,36},{32,40... | collective-permute-start | bytes 196616 | tf_op jit(solution)/shard_map/ppermute | solution.py:22
  39.3 31.7 %collective-permute-start = (bf16[64,512]{1,0:T(8,128)(2,1)S(1)}, bf16[64,512]{1,0:T(8,128)(2,1)S(1)}, u32[]{:S(2)}, u32[]{:S(2)}) collective-permute-start(bf16[64,512]{1,0:T(8,128)(2,1)S(1)} %project_own.1.refs_1_.refs_5_), channel_id=1, source_target_pairs={{0,4},{4,8},{8,12},{12,16},{16,20},{20,24},{24,28},{28,32},{32,36}... | collective-permute-start | bytes 196616 | tf_op jit(solution)/shard_map/ppermute | solution.py:22
  48.3 25.3 %collective-permute-start.14 = (bf16[128,512]{1,0:T(8,128)(2,1)S(1)}, bf16[128,512]{1,0:T(8,128)(2,1)S(1)}, u32[]{:S(2)}, u32[]{:S(2)}) collective-permute-start(bf16[128,512]{1,0:T(8,128)(2,1)S(1)} %project_sides.1.refs_1_.refs_5_), channel_id=1, source_target_pairs={{0,12},{4,16},{8,20},{12,24},{16,28},{20,32},{24,36},{28,40},{32,4... | collective-permute-start | bytes 393224 | tf_op jit(solution)/shard_map/ppermute | solution.py:22
  54.1 27.3 %collective-permute-start.13 = (bf16[128,512]{1,0:T(8,128)(2,1)S(1)}, bf16[128,512]{1,0:T(8,128)(2,1)S(1)}, u32[]{:S(2)}, u32[]{:S(2)}) collective-permute-start(bf16[128,512]{1,0:T(8,128)(2,1)S(1)} %project_sides.1.refs_1_.refs_5_), channel_id=1, source_target_pairs={{0,8},{4,12},{8,16},{12,20},{16,24},{20,28},{24,32},{28,36},{32,40... | collective-permute-start | bytes 393224 | tf_op jit(solution)/shard_map/ppermute | solution.py:22
  56.1 25.3 %collective-permute-start.12 = (bf16[128,512]{1,0:T(8,128)(2,1)S(1)}, bf16[128,512]{1,0:T(8,128)(2,1)S(1)}, u32[]{:S(2)}, u32[]{:S(2)}) collective-permute-start(bf16[128,512]{1,0:T(8,128)(2,1)S(1)} %project_sides.1.refs_1_.refs_5_), channel_id=1, source_target_pairs={{0,4},{4,8},{8,12},{12,16},{16,20},{20,24},{24,28},{28,32},{32,36}... | collective-permute-start | bytes 393224 | tf_op jit(solution)/shard_map/ppermute | solution.py:22
  58.9 18.2 %copy-start.7 = (s32[4,64]{1,0:T(4,128)S(1)}, s32[4,64]{1,0:T(4,128)}, u32[]{:S(2)}) copy-start(s32[4,64]{1,0:T(4,128)} %param.13) | copy-start | bytes 3076
  58.9 18.4 %copy-start.4 = (bf16[256,2048]{1,0:T(8,128)(2,1)S(1)}, bf16[256,2048]{1,0:T(8,128)(2,1)}, u32[]{:S(2)}) copy-start(bf16[256,2048]{1,0:T(8,128)(2,1)} %refs_0_.3) | copy-start | bytes 3145732
  65.0 20.8 %collective-permute-start.9 = (bf16[64,512]{1,0:T(8,128)(2,1)S(1)}, bf16[64,512]{1,0:T(8,128)(2,1)S(1)}, u32[]{:S(2)}, u32[]{:S(2)}) collective-permute-start(bf16[64,512]{1,0:T(8,128)(2,1)S(1)} %project_across.1.refs_1_.refs_5_), channel_id=1, source_target_pairs={{0,12},{4,16},{8,20},{12,24},{16,28},{20,32},{24,36},{28,40},{32,4... | collective-permute-start | bytes 196616 | tf_op jit(solution)/shard_map/ppermute | solution.py:22
  71.0 14.8 %collective-permute-start.8 = (bf16[64,512]{1,0:T(8,128)(2,1)S(1)}, bf16[64,512]{1,0:T(8,128)(2,1)S(1)}, u32[]{:S(2)}, u32[]{:S(2)}) collective-permute-start(bf16[64,512]{1,0:T(8,128)(2,1)S(1)} %project_across.1.refs_1_.refs_5_), channel_id=1, source_target_pairs={{0,8},{4,12},{8,16},{12,20},{16,24},{20,28},{24,32},{28,36},{32,40... | collective-permute-start | bytes 196616 | tf_op jit(solution)/shard_map/ppermute | solution.py:22
  73.6 12.2 %collective-permute-start.7 = (bf16[64,512]{1,0:T(8,128)(2,1)S(1)}, bf16[64,512]{1,0:T(8,128)(2,1)S(1)}, u32[]{:S(2)}, u32[]{:S(2)}) collective-permute-start(bf16[64,512]{1,0:T(8,128)(2,1)S(1)} %project_across.1.refs_1_.refs_5_), channel_id=1, source_target_pairs={{0,4},{4,8},{8,12},{12,16},{16,20},{20,24},{24,28},{28,32},{32,36}... | collective-permute-start | bytes 196616 | tf_op jit(solution)/shard_map/ppermute | solution.py:22
  80.0 1.3 %copy-start.3 = (f32[256,2048]{1,0:T(8,128)}, f32[256,2048]{1,0:T(8,128)S(1)}, u32[]{:S(2)}) copy-start(f32[256,2048]{1,0:T(8,128)S(1)} %get-tuple-element.11.refs_10_) | copy-start | bytes 6291460

commit v2 on v1

v2 whole, which is shorter than its diff:
```python
import functools
import math

import jax
import jax.numpy as jnp
from jax import lax
from jax.experimental import pallas as pl
from jax.experimental.pallas import tpu as pltpu
from jax.sharding import PartitionSpec as P

HEAD_SIZE = 128
REACH = 4
BLOCK = 64
EPS = 1e-05
SCORE_SCALE = HEAD_SIZE ** (-0.5) * math.log2(math.e)
PROJECT_VMEM = 8 * 1024 * 1024
ATTEND_VMEM = 20 * 1024 * 1024
WHOLE = pl.BlockSpec(memory_space=pltpu.VMEM)


def shifted(value, axis, by):
    length = lax.axis_size(axis)
    pairs = [(i, i + by) for i in range(length) if 0 <= i + by < length]
    return lax.ppermute(value, axis, pairs)


def turned(value, axis, by):
    length = lax.axis_size(axis)
    return lax.ppermute(value, axis, [(i, (i + by) % length) for i in range(length)])


def project_rows(row_refs, key_ref, value_ref, gain_ref, out_ref):
    width = key_ref.shape[1]
    rows = [ref[...] for ref in row_refs]
    rows = rows[0] if len(rows) == 1 else jnp.concatenate(rows, axis=0)
    keys = jnp.dot(rows, key_ref[...], preferred_element_type=jnp.float32)
    values = jnp.dot(rows, value_ref[...], preferred_element_type=jnp.float32)
    for head in range(width // HEAD_SIZE):
        at = slice(head * HEAD_SIZE, (head + 1) * HEAD_SIZE)
        own = keys[:, at]
        mean = jnp.mean(own * own, axis=-1, keepdims=True)
        out_ref[:, at] = (own * lax.rsqrt(mean + EPS) * gain_ref[...]).astype(out_ref.dtype)
    out_ref[:, width:] = values.astype(out_ref.dtype)


def project_cost(rows, key_matrix):
    size = math.prod(key_matrix.shape)
    return pl.CostEstimate(flops=4 * rows * size, transcendentals=0, bytes_accessed=4 * size)


def project_kernel(*refs):
    *row_refs, key_ref, value_ref, gain_ref, out_ref = refs
    project_rows(row_refs, key_ref, value_ref, gain_ref, out_ref)


def project(row_parts, key_matrix, value_matrix, key_gain, name):
    width = key_matrix.shape[1]
    rows = sum(each.shape[0] for each in row_parts)
    return pl.pallas_call(
        project_kernel,
        out_shape=jax.ShapeDtypeStruct((rows, 2 * width), jnp.bfloat16),
        in_specs=[WHOLE] * (len(row_parts) + 3),
        out_specs=WHOLE,
        cost_estimate=project_cost(rows, key_matrix),
        compiler_params=pltpu.CompilerParams(vmem_limit_bytes=PROJECT_VMEM),
        name=name,
    )(*row_parts, key_matrix, value_matrix, key_gain)


def attend_kernel(first, last, kv_heads, *refs):
    refs = list(refs)
    query_ref = refs.pop(0)
    block_refs = [refs.pop(0) for _ in range(REACH)]
    open_ref = refs.pop(0)
    if first:
        gain_ref, normed_ref = refs.pop(0), refs.pop(0)
    else:
        sums_in, totals_in = refs.pop(0), refs.pop(0)
    rows = query_ref.shape[0]
    count = block_refs[0].shape[0]
    group = query_ref.shape[1] // HEAD_SIZE // kv_heads
    image = lax.broadcasted_iota(jnp.int32, (rows, REACH * count), 1) // count
    is_open = jnp.zeros((rows, REACH * count), jnp.float32)
    for at in range(REACH):
        is_open = jnp.where(image == at, open_ref[:, at : at + 1], is_open)
    is_open = jnp.concatenate([is_open] * group, axis=0)
    lane = lax.broadcasted_iota(jnp.int32, (rows, HEAD_SIZE), 1)
    totals = jnp.zeros((rows, HEAD_SIZE), jnp.float32)

    def columns(head):
        return slice(head * HEAD_SIZE, (head + 1) * HEAD_SIZE)

    for kv_head in range(kv_heads):
        heads = range(kv_head * group, (kv_head + 1) * group)
        keys = jnp.concatenate([ref[:, columns(kv_head)] for ref in block_refs], axis=0)
        values = jnp.concatenate(
            [ref[:, columns(kv_heads + kv_head)] for ref in block_refs], axis=0
        )
        values = jnp.concatenate([values, jnp.ones_like(values)], axis=1)
        queries = []
        for head in heads:
            query = query_ref[:, columns(head)]
            if first:
                raw = query.astype(jnp.float32)
                mean = jnp.mean(raw * raw, axis=-1, keepdims=True)
                query = (raw * lax.rsqrt(mean + EPS) * gain_ref[...]).astype(jnp.bfloat16)
                normed_ref[:, columns(head)] = query
            queries.append(query)
        scores = lax.dot_general(
            jnp.concatenate(queries, axis=0),
            keys,
            (((1,), (1,)), ((), ())),
            preferred_element_type=jnp.float32,
        )
        weights = (jnp.exp2(scores) * is_open).astype(jnp.bfloat16)
        both = jnp.dot(weights, values, preferred_element_type=jnp.float32)
        for at, head in enumerate(heads):
            sums = both[at * rows : (at + 1) * rows, :HEAD_SIZE]
            total = both[at * rows : (at + 1) * rows, HEAD_SIZE:]
            if not first:
                sums = sums + sums_in[:, columns(head)]
                total = total + totals_in[:, head : head + 1]
            if last:
                safe = jnp.where(total > 0, total, jnp.ones_like(total))
                inverse = pl.reciprocal(safe, approx=True)
                inverse = inverse * (2.0 - safe * inverse)
                refs[0][:, columns(head)] = (sums * inverse).astype(jnp.bfloat16)
            else:
                refs[0][:, columns(head)] = sums
                totals = jnp.where(lane == head, total, totals)
    if not last:
        refs[1][...] = totals


def attend_cost(rows, width, keys):
    return pl.CostEstimate(
        flops=16 * rows * width * keys,
        transcendentals=rows * width // HEAD_SIZE * keys,
        bytes_accessed=2 * rows * width,
    )


def attend(query, blocks, is_open, gain, carried, last, name):
    first = carried is None
    rows, width = query.shape
    kv_heads = blocks[0].shape[1] // (2 * HEAD_SIZE)
    operands = [query, *blocks, is_open] + ([gain] if first else list(carried))
    if last:
        out_shape = [jax.ShapeDtypeStruct((rows, width), jnp.bfloat16)]
    else:
        out_shape = [
            jax.ShapeDtypeStruct((rows, width), jnp.float32),
            jax.ShapeDtypeStruct((rows, HEAD_SIZE), jnp.float32),
        ]
    if first:
        out_shape.insert(0, jax.ShapeDtypeStruct((rows, width), jnp.bfloat16))
    return pl.pallas_call(
        functools.partial(attend_kernel, first, last, kv_heads),
        out_shape=out_shape,
        in_specs=[WHOLE] * len(operands),
        out_specs=[WHOLE] * len(out_shape),
        cost_estimate=attend_cost(rows, width, REACH * blocks[0].shape[0]),
        compiler_params=pltpu.CompilerParams(vmem_limit_bytes=ATTEND_VMEM),
        name=name,
    )(*operands)


def after(values, *others):
    return lax.optimization_barrier((values, others))[0]


def body(
    text_query_matrix, vision, key_matrix, value_matrix, query_norm_gain, key_gain, block_mask
):
    position = lax.axis_index("seq")
    images = lax.broadcasted_iota(jnp.int32, (1, block_mask.shape[1], REACH), 1)
    wanted = position - lax.broadcasted_iota(jnp.int32, (1, block_mask.shape[1], REACH), 2)
    is_open = jnp.sum(jnp.where(images == wanted, block_mask[:, :, None], 0), axis=1)
    is_open = jnp.repeat(is_open.astype(jnp.float32), BLOCK, axis=0)
    query_gain = (query_norm_gain * SCORE_SCALE).reshape(1, HEAD_SIZE)
    key_gain = key_gain.reshape(1, HEAD_SIZE)

    def projected(row_parts, name):
        return project(row_parts, key_matrix, value_matrix, key_gain, "project_" + name)

    def reached(block):
        return [block] + [shifted(block, "seq", by) for by in range(1, REACH)]

    left = turned(vision, "tp", 1)
    right = turned(vision, "tp", -1)
    own = projected([vision], "own")
    own_blocks = reached(own)
    normed, *carried = attend(
        text_query_matrix, own_blocks, is_open, query_gain, None, False, "attend_own"
    )

    half = vision.shape[0] // 2
    left, right = after((left, right), carried)
    upper_across = turned(left[:half], "tp", 1)
    lower_across = turned(right[half:], "tp", -1)
    sides = projected([left, right], "sides")
    side_blocks = reached(sides)
    upper_across, lower_across = after((upper_across, lower_across), sides)
    across = projected([upper_across, lower_across], "across")
    across_blocks = reached(across)
    side_blocks = after(side_blocks, across)
    carried = attend(normed, side_blocks, is_open, None, carried, False, "attend_sides")
    across_blocks = after(across_blocks, carried)
    (result,) = attend(normed, across_blocks, is_open, None, carried, True, "attend_across")
    return result


def solution(mesh):
    placed = (
        P("seq", "tp"),
        P(("seq", "tp"), None),
        P(None, "tp"),
        P(None, "tp"),
        P(),
        P(),
        P("seq", None),
    )
    return jax.shard_map(
        body, mesh=mesh, in_specs=placed, out_specs=P("seq", "tp"), check_vma=False
    )
```

time: 89.5 us -> 63.3 us (0.71)
  the two profiles are of different devices: /device:TPU:79 before, /device:TPU:96 now
where the time goes in v2:
time: 63.3 us; the launch traced here: 62.9 us
  starting transfers between devices  36.7 us (58%)
  Pallas kernels  11.5 us (18%)
  waiting for transfers between devices  7.84 us (12%)
  local copies, waits for them, and re-layouts  6.36 us (10%)
    ppermute x9, starting transfers between devices, shifted(): return lax.ppermute(value, axis, pairs)  30.6 us
    pallas_call x3, Pallas kernels, attend(): pl.pallas_call(functools.partial(attend_kernel, first, last, kv_heads), o...  6.83 us
    unnamed x20, local copies, waits for them, and re-layouts  6.28 us
    ppermute x4, starting transfers between devices, turned(): lax.ppermute(value, axis, [(i, (i + by) % length) for i in range(length)])  6.07 us
    ppermute x9, waiting for transfers between devices, shifted(): return lax.ppermute(value, axis, pairs)  5.98 us
    pallas_call x3, Pallas kernels, project(): pl.pallas_call(project_kernel, out_shape=jax.ShapeDtypeStruct((rows, 2 *...  4.69 us
    ppermute x4, waiting for transfers between devices, turned(): lax.ppermute(value, axis, [(i, (i + by) % length) for i in range(length)])  1.86 us
  transfers between devices with their start and end apart: 13, of which 4 were waited for; matrix products, arithmetic and copies ran while one was open for 0% of the time, Pallas kernels for 14%

profile of v2, /device:TPU:96, one launch (start us, length us, event | category | flops | bytes accessed | tf_op | source)
XLA Modules:
  0.0 62.9 jit_solution(6258988116427245056)
XLA Ops:
  0.0 2.8 %collective-permute-start.4 = (bf16[64,8192]{1,0:T(8,128)(2,1)}, bf16[64,8192]{1,0:T(8,128)(2,1)S(1)}, u32[]{:S(2)}, u32[]{:S(2)}) collective-permute-start(bf16[64,8192]{1,0:T(8,128)(2,1)} %refs_0_.2), channel_id=1, source_target_pairs={{0,3},{1,0},{2,1},{3,2},{4,7},{5,4},{6,5},{7,6},{8,11},{9,8},{10,9... | collective-permute-start | bytes 3145736 | tf_op jit(solution)/shard_map/ppermute | solution.py:29
  2.8 2.2 %copy-done = bf16[8192,256]{1,0:T(8,128)(2,1)S(1)} copy-done((bf16[8192,256]{1,0:T(8,128)(2,1)S(1)}, bf16[8192,256]{1,0:T(8,128)(2,1)}, u32[]{:S(2)}) %copy-start) | copy-done | bytes 4194328
  5.0 2.2 %copy-done.2 = bf16[8192,256]{1,0:T(8,128)(2,1)S(1)} copy-done((bf16[8192,256]{1,0:T(8,128)(2,1)S(1)}, bf16[8192,256]{1,0:T(8,128)(2,1)}, u32[]{:S(2)}) %copy-start.2) | copy-done | bytes 4194328
  7.1 1.2 %copy-done.4 = bf16[64,8192]{1,0:T(8,128)(2,1)S(1)} copy-done((bf16[64,8192]{1,0:T(8,128)(2,1)S(1)}, bf16[64,8192]{1,0:T(8,128)(2,1)}, u32[]{:S(2)}) %copy-start.4) | copy-done | bytes 1048600
  9.0 1.6 %project_own.1.refs_1_ = bf16[64,512]{1,0:T(8,128)(2,1)S(1)} custom-call(bf16[64,8192]{1,0:T(8,128)(2,1)S(1)} %copy-done.4, bf16[8192,256]{1,0:T(8,128)(2,1)S(1)} %copy-done, bf16[8192,256]{1,0:T(8,128)(2,1)S(1)} %copy-done.2, f32[1,128]{1,0:T(1,128)S(1)} %bitcast.7), custom_call_target="tpu_custom_call" | custom-call | flops 536870912 | bytes 8388608 | tf_op jit(solution)/shard_map/project_own/pallas_call | solution.py:59
  10.7 2.6 %collective-permute-start.2 = (bf16[64,512]{1,0:T(8,128)(2,1)S(1)}, bf16[64,512]{1,0:T(8,128)(2,1)S(1)}, u32[]{:S(2)}, u32[]{:S(2)}) collective-permute-start(bf16[64,512]{1,0:T(8,128)(2,1)S(1)} %project_own.1.refs_1_), channel_id=1, source_target_pairs={{0,12},{4,16},{8,20},{12,24},{16,28},{20,32},{24,36},{28,40},{32,4... | collective-permute-start | bytes 196616 | tf_op jit(solution)/shard_map/ppermute | solution.py:24
  13.3 3.5 %collective-permute-start.1 = (bf16[64,512]{1,0:T(8,128)(2,1)S(1)}, bf16[64,512]{1,0:T(8,128)(2,1)S(1)}, u32[]{:S(2)}, u32[]{:S(2)}) collective-permute-start(bf16[64,512]{1,0:T(8,128)(2,1)S(1)} %project_own.1.refs_1_), channel_id=1, source_target_pairs={{0,8},{4,12},{8,16},{12,20},{16,24},{20,28},{24,32},{28,36},{32,40... | collective-permute-start | bytes 196616 | tf_op jit(solution)/shard_map/ppermute | solution.py:24
  16.8 3.3 %collective-permute-start = (bf16[64,512]{1,0:T(8,128)(2,1)S(1)}, bf16[64,512]{1,0:T(8,128)(2,1)S(1)}, u32[]{:S(2)}, u32[]{:S(2)}) collective-permute-start(bf16[64,512]{1,0:T(8,128)(2,1)S(1)} %project_own.1.refs_1_), channel_id=1, source_target_pairs={{0,4},{4,8},{8,12},{12,16},{16,20},{20,24},{24,28},{28,32},{32,36}... | collective-permute-start | bytes 196616 | tf_op jit(solution)/shard_map/ppermute | solution.py:24
  20.4 1.2 %collective-permute-done.1.refs_3_ = bf16[64,512]{1,0:T(8,128)(2,1)S(1)} collective-permute-done((bf16[64,512]{1,0:T(8,128)(2,1)S(1)}, bf16[64,512]{1,0:T(8,128)(2,1)S(1)}, u32[]{:S(2)}, u32[]{:S(2)}) %collective-permute-start.1) | collective-permute-done | bytes 65568 | tf_op jit(solution)/shard_map/ppermute | solution.py:24
  21.6 3.5 %collective-permute-done.refs_2_ = bf16[64,512]{1,0:T(8,128)(2,1)S(1)} collective-permute-done((bf16[64,512]{1,0:T(8,128)(2,1)S(1)}, bf16[64,512]{1,0:T(8,128)(2,1)S(1)}, u32[]{:S(2)}, u32[]{:S(2)}) %collective-permute-start) | collective-permute-done | bytes 65568 | tf_op jit(solution)/shard_map/ppermute | solution.py:24
  25.2 1.7 %attend_own.1 = (bf16[256,2048]{1,0:T(8,128)(2,1)S(1)}, f32[256,2048]{1,0:T(8,128)S(1)}, f32[256,128]{1,0:T(8,128)S(1)}) custom-call(bf16[256,2048]{1,0:T(8,128)(2,1)S(1)} %copy-done.7, bf16[64,512]{1,0:T(8,128)(2,1)S(1)} %project_own.1.refs_1_, bf16[64,512]{1,0:T(8,128)(2,1)S(1)} %collective-permute-done.refs_2_, ...), custom_call_target="tpu_custom_call" | custom-call | flops 2147483648 | bytes 1048576 | tf_op jit(solution)/shard_map/attend_own/pallas_call | solution.py:157
  26.9 1.9 %collective-permute-done.3.refs_0_ = bf16[64,8192]{1,0:T(8,128)(2,1)S(1)} collective-permute-done((bf16[64,8192]{1,0:T(8,128)(2,1)}, bf16[64,8192]{1,0:T(8,128)(2,1)S(1)}, u32[]{:S(2)}, u32[]{:S(2)}) %collective-permute-start.3) | collective-permute-done | bytes 1048608 | tf_op jit(solution)/shard_map/ppermute | solution.py:29
  29.0 3.2 %collective-permute-start.6 = (bf16[32,8192]{1,0:T(8,128)(2,1)S(1)}, bf16[32,8192]{1,0:T(8,128)(2,1)S(1)}, u32[]{:S(2)}, u32[]{:S(2)}) collective-permute-start(bf16[32,8192]{1,0:T(8,128)(2,1)S(1)} %slice.7), channel_id=1, source_target_pairs={{0,3},{1,0},{2,1},{3,2},{4,7},{5,4},{6,5},{7,6},{8,11},{9,8},{10,9... | collective-permute-start | bytes 1572872 | tf_op jit(solution)/shard_map/ppermute | solution.py:29
  32.2 1.4 %project_sides.1.refs_1_ = bf16[128,512]{1,0:T(8,128)(2,1)S(1)} custom-call(bf16[64,8192]{1,0:T(8,128)(2,1)S(1)} %collective-permute-done.3.refs_0_, bf16[64,8192]{1,0:T(8,128)(2,1)S(1)} %collective-permute-done.4.refs_1_, bf16[8192,256]{1,0:T(8,128)(2,1)S(1)} %copy-done.1, bf16[8192,256]{1,0:T(8,128)(2,1)S(1)} %copy-done.3, f32[1,128]{1,0:T(1,128)S(1)} %bitcast.8), custom_call_target="tpu_custom_call" | custom-call | flops 1073741824 | bytes 8388608 | tf_op jit(solution)/shard_map/project_sides/pallas_call | solution.py:59
  33.6 1.9 %collective-permute-start.12 = (bf16[128,512]{1,0:T(8,128)(2,1)S(1)}, bf16[128,512]{1,0:T(8,128)(2,1)S(1)}, u32[]{:S(2)}, u32[]{:S(2)}) collective-permute-start(bf16[128,512]{1,0:T(8,128)(2,1)S(1)} %project_sides.1.refs_1_), channel_id=1, source_target_pairs={{0,12},{4,16},{8,20},{12,24},{16,28},{20,32},{24,36},{28,40},{32,4... | collective-permute-start | bytes 393224 | tf_op jit(solution)/shard_map/ppermute | solution.py:24
  35.5 3.5 %collective-permute-start.11 = (bf16[128,512]{1,0:T(8,128)(2,1)S(1)}, bf16[128,512]{1,0:T(8,128)(2,1)S(1)}, u32[]{:S(2)}, u32[]{:S(2)}) collective-permute-start(bf16[128,512]{1,0:T(8,128)(2,1)S(1)} %project_sides.1.refs_1_), channel_id=1, source_target_pairs={{0,8},{4,12},{8,16},{12,20},{16,24},{20,28},{24,32},{28,36},{32,40... | collective-permute-start | bytes 393224 | tf_op jit(solution)/shard_map/ppermute | solution.py:24
  39.0 4.0 %collective-permute-start.10 = (bf16[128,512]{1,0:T(8,128)(2,1)S(1)}, bf16[128,512]{1,0:T(8,128)(2,1)S(1)}, u32[]{:S(2)}, u32[]{:S(2)}) collective-permute-start(bf16[128,512]{1,0:T(8,128)(2,1)S(1)} %project_sides.1.refs_1_), channel_id=1, source_target_pairs={{0,4},{4,8},{8,12},{12,16},{16,20},{20,24},{24,28},{28,32},{32,36}... | collective-permute-start | bytes 393224 | tf_op jit(solution)/shard_map/ppermute | solution.py:24
  43.1 1.6 %project_across.1.refs_1_ = bf16[64,512]{1,0:T(8,128)(2,1)S(1)} custom-call(bf16[32,8192]{1,0:T(8,128)(2,1)S(1)} %collective-permute-done.5.refs_0_, bf16[32,8192]{1,0:T(8,128)(2,1)S(1)} %collective-permute-done.6.refs_1_, bf16[8192,256]{1,0:T(8,128)(2,1)S(1)} %copy-done.1, bf16[8192,256]{1,0:T(8,128)(2,1)S(1)} %copy-done.3, f32[1,128]{1,0:T(1,128)S(1)} %bitcast.9), custom_call_target="tpu_custom_call" | custom-call | flops 536870912 | bytes 8388608 | tf_op jit(solution)/shard_map/project_across/pallas_call | solution.py:59
  44.7 3.7 %collective-permute-start.9 = (bf16[64,512]{1,0:T(8,128)(2,1)S(1)}, bf16[64,512]{1,0:T(8,128)(2,1)S(1)}, u32[]{:S(2)}, u32[]{:S(2)}) collective-permute-start(bf16[64,512]{1,0:T(8,128)(2,1)S(1)} %project_across.1.refs_1_), channel_id=1, source_target_pairs={{0,12},{4,16},{8,20},{12,24},{16,28},{20,32},{24,36},{28,40},{32,4... | collective-permute-start | bytes 196616 | tf_op jit(solution)/shard_map/ppermute | solution.py:24
  48.5 4.1 %collective-permute-start.8 = (bf16[64,512]{1,0:T(8,128)(2,1)S(1)}, bf16[64,512]{1,0:T(8,128)(2,1)S(1)}, u32[]{:S(2)}, u32[]{:S(2)}) collective-permute-start(bf16[64,512]{1,0:T(8,128)(2,1)S(1)} %project_across.1.refs_1_), channel_id=1, source_target_pairs={{0,8},{4,12},{8,16},{12,20},{16,24},{20,28},{24,32},{28,36},{32,40... | collective-permute-start | bytes 196616 | tf_op jit(solution)/shard_map/ppermute | solution.py:24
  52.6 3.9 %collective-permute-start.7 = (bf16[64,512]{1,0:T(8,128)(2,1)S(1)}, bf16[64,512]{1,0:T(8,128)(2,1)S(1)}, u32[]{:S(2)}, u32[]{:S(2)}) collective-permute-start(bf16[64,512]{1,0:T(8,128)(2,1)S(1)} %project_across.1.refs_1_), channel_id=1, source_target_pairs={{0,4},{4,8},{8,12},{12,16},{16,20},{20,24},{24,28},{28,32},{32,36}... | collective-permute-start | bytes 196616 | tf_op jit(solution)/shard_map/ppermute | solution.py:24
  56.5 2.6 %attend_sides.1 = (f32[256,2048]{1,0:T(8,128)S(1)}, f32[256,128]{1,0:T(8,128)S(1)}) custom-call(bf16[256,2048]{1,0:T(8,128)(2,1)S(1)} %get-tuple-element.22.refs_0_, bf16[128,512]{1,0:T(8,128)(2,1)S(1)} %project_sides.1.refs_1_, bf16[128,512]{1,0:T(8,128)(2,1)S(1)} %collective-permute-done.10.refs_2_, bf16[128,512]{1,0:T(8,128)(2,1)S(1)} %collective-permute-done.11.refs_3_, ...), custom_call_target="tpu_custom_call" | custom-call | flops 4294967296 | bytes 1048576 | tf_op jit(solution)/shard_map/attend_sides/pallas_call | solution.py:157
  59.2 1.2 %collective-permute-done.7.refs_2_ = bf16[64,512]{1,0:T(8,128)(2,1)S(1)} collective-permute-done((bf16[64,512]{1,0:T(8,128)(2,1)S(1)}, bf16[64,512]{1,0:T(8,128)(2,1)S(1)}, u32[]{:S(2)}, u32[]{:S(2)}) %collective-permute-start.7) | collective-permute-done | bytes 65568 | tf_op jit(solution)/shard_map/ppermute | solution.py:24
  60.4 2.5 %attend_across.1 = bf16[256,2048]{1,0:T(8,128)(2,1)} custom-call(bf16[256,2048]{1,0:T(8,128)(2,1)S(1)} %get-tuple-element.22.refs_0_, bf16[64,512]{1,0:T(8,128)(2,1)S(1)} %project_across.1.refs_1_, bf16[64,512]{1,0:T(8,128)(2,1)S(1)} %collective-permute-done.7.refs_2_, bf16[64,512]{1,0:T(8,128)(2,1)S(1)} %collective-permute-done.8.refs_3_, ...), custom_call_target="tpu_custom_call" | custom-call | flops 2147483648 | bytes 1048576 | tf_op jit(solution)/shard_map/attend_across/pallas_call | solution.py:157
  (36 shorter events, 1.1 us)
Async XLA Ops:
  0.0 26.9 %collective-permute-start.4 = (bf16[64,8192]{1,0:T(8,128)(2,1)}, bf16[64,8192]{1,0:T(8,128)(2,1)S(1)}, u32[]{:S(2)}, u32[]{:S(2)}) collective-permute-start(bf16[64,8192]{1,0:T(8,128)(2,1)} %refs_0_.2), channel_id=1, source_target_pairs={{0,3},{1,0},{2,1},{3,2},{4,7},{5,4},{6,5},{7,6},{8,11},{9,8},{10,9... | collective-permute-start | bytes 3145736 | tf_op jit(solution)/shard_map/ppermute | solution.py:29
  2.8 26.0 %collective-permute-start.3 = (bf16[64,8192]{1,0:T(8,128)(2,1)}, bf16[64,8192]{1,0:T(8,128)(2,1)S(1)}, u32[]{:S(2)}, u32[]{:S(2)}) collective-permute-start(bf16[64,8192]{1,0:T(8,128)(2,1)} %refs_0_.2), channel_id=1, source_target_pairs={{0,1},{1,2},{2,3},{3,0},{4,5},{5,6},{6,7},{7,4},{8,9},{9,10},{10,1... | collective-permute-start | bytes 3145736 | tf_op jit(solution)/shard_map/ppermute | solution.py:29
  2.8 2.2 %copy-start = (bf16[8192,256]{1,0:T(8,128)(2,1)S(1)}, bf16[8192,256]{1,0:T(8,128)(2,1)}, u32[]{:S(2)}) copy-start(bf16[8192,256]{1,0:T(8,128)(2,1)} %refs_2_.5) | copy-start | bytes 12582916
  5.0 2.2 %copy-start.2 = (bf16[8192,256]{1,0:T(8,128)(2,1)S(1)}, bf16[8192,256]{1,0:T(8,128)(2,1)}, u32[]{:S(2)}) copy-start(bf16[8192,256]{1,0:T(8,128)(2,1)} %refs_3_.3) | copy-start | bytes 12582916
  7.1 1.2 %copy-start.4 = (bf16[64,8192]{1,0:T(8,128)(2,1)S(1)}, bf16[64,8192]{1,0:T(8,128)(2,1)}, u32[]{:S(2)}) copy-start(bf16[64,8192]{1,0:T(8,128)(2,1)} %refs_0_.2) | copy-start | bytes 3145732
  8.4 0.7 %copy-start.5 = (f32[128]{0:T(128)S(1)}, f32[128]{0:T(128)}, u32[]{:S(2)}) copy-start(f32[128]{0:T(128)} %param.12) | copy-start | bytes 1540
  9.0 11.2 %copy-start.9 = (f32[128]{0:T(128)S(1)}, f32[128]{0:T(128)}, u32[]{:S(2)}) copy-start(f32[128]{0:T(128)} %param.11) | copy-start | bytes 1540
  9.0 11.2 %copy-start.8 = (s32[4,64]{1,0:T(4,128)S(1)}, s32[4,64]{1,0:T(4,128)}, u32[]{:S(2)}) copy-start(s32[4,64]{1,0:T(4,128)} %param.13) | copy-start | bytes 3076
  9.0 16.1 %copy-start.7 = (bf16[256,2048]{1,0:T(8,128)(2,1)S(1)}, bf16[256,2048]{1,0:T(8,128)(2,1)}, u32[]{:S(2)}) copy-start(bf16[256,2048]{1,0:T(8,128)(2,1)} %refs_0_.3) | copy-start | bytes 3145732
  10.7 9.7 %collective-permute-start.2 = (bf16[64,512]{1,0:T(8,128)(2,1)S(1)}, bf16[64,512]{1,0:T(8,128)(2,1)S(1)}, u32[]{:S(2)}, u32[]{:S(2)}) collective-permute-start(bf16[64,512]{1,0:T(8,128)(2,1)S(1)} %project_own.1.refs_1_), channel_id=1, source_target_pairs={{0,12},{4,16},{8,20},{12,24},{16,28},{20,32},{24,36},{28,40},{32,4... | collective-permute-start | bytes 196616 | tf_op jit(solution)/shard_map/ppermute | solution.py:24
  13.3 8.3 %collective-permute-start.1 = (bf16[64,512]{1,0:T(8,128)(2,1)S(1)}, bf16[64,512]{1,0:T(8,128)(2,1)S(1)}, u32[]{:S(2)}, u32[]{:S(2)}) collective-permute-start(bf16[64,512]{1,0:T(8,128)(2,1)S(1)} %project_own.1.refs_1_), channel_id=1, source_target_pairs={{0,8},{4,12},{8,16},{12,20},{16,24},{20,28},{24,32},{28,36},{32,40... | collective-permute-start | bytes 196616 | tf_op jit(solution)/shard_map/ppermute | solution.py:24
  16.8 8.3 %collective-permute-start = (bf16[64,512]{1,0:T(8,128)(2,1)S(1)}, bf16[64,512]{1,0:T(8,128)(2,1)S(1)}, u32[]{:S(2)}, u32[]{:S(2)}) collective-permute-start(bf16[64,512]{1,0:T(8,128)(2,1)S(1)} %project_own.1.refs_1_), channel_id=1, source_target_pairs={{0,4},{4,8},{8,12},{12,16},{16,20},{20,24},{24,28},{28,32},{32,36}... | collective-permute-start | bytes 196616 | tf_op jit(solution)/shard_map/ppermute | solution.py:24
  25.2 7.0 %copy-start.1 = (bf16[8192,256]{1,0:T(8,128)(2,1)S(1)}, bf16[8192,256]{1,0:T(8,128)(2,1)}, u32[]{:S(2)}) copy-start(bf16[8192,256]{1,0:T(8,128)(2,1)} %refs_2_.5) | copy-start | bytes 12582916
  25.2 7.0 %copy-start.3 = (bf16[8192,256]{1,0:T(8,128)(2,1)S(1)}, bf16[8192,256]{1,0:T(8,128)(2,1)}, u32[]{:S(2)}) copy-start(bf16[8192,256]{1,0:T(8,128)(2,1)} %refs_3_.3) | copy-start | bytes 12582916
  25.2 7.0 %copy-start.6 = (f32[128]{0:T(128)S(1)}, f32[128]{0:T(128)}, u32[]{:S(2)}) copy-start(f32[128]{0:T(128)} %param.12) | copy-start | bytes 1540
  28.9 14.2 %collective-permute-start.5 = (bf16[32,8192]{1,0:T(8,128)(2,1)S(1)}, bf16[32,8192]{1,0:T(8,128)(2,1)S(1)}, u32[]{:S(2)}, u32[]{:S(2)}) collective-permute-start(bf16[32,8192]{1,0:T(8,128)(2,1)S(1)} %slice.6), channel_id=1, source_target_pairs={{0,1},{1,2},{2,3},{3,0},{4,5},{5,6},{6,7},{7,4},{8,9},{9,10},{10,1... | collective-permute-start | bytes 1572872 | tf_op jit(solution)/shard_map/ppermute | solution.py:29
  29.0 14.1 %collective-permute-start.6 = (bf16[32,8192]{1,0:T(8,128)(2,1)S(1)}, bf16[32,8192]{1,0:T(8,128)(2,1)S(1)}, u32[]{:S(2)}, u32[]{:S(2)}) collective-permute-start(bf16[32,8192]{1,0:T(8,128)(2,1)S(1)} %slice.7), channel_id=1, source_target_pairs={{0,3},{1,0},{2,1},{3,2},{4,7},{5,4},{6,5},{7,6},{8,11},{9,8},{10,9... | collective-permute-start | bytes 1572872 | tf_op jit(solution)/shard_map/ppermute | solution.py:29
  33.6 18.9 %collective-permute-start.12 = (bf16[128,512]{1,0:T(8,128)(2,1)S(1)}, bf16[128,512]{1,0:T(8,128)(2,1)S(1)}, u32[]{:S(2)}, u32[]{:S(2)}) collective-permute-start(bf16[128,512]{1,0:T(8,128)(2,1)S(1)} %project_sides.1.refs_1_), channel_id=1, source_target_pairs={{0,12},{4,16},{8,20},{12,24},{16,28},{20,32},{24,36},{28,40},{32,4... | collective-permute-start | bytes 393224 | tf_op jit(solution)/shard_map/ppermute | solution.py:24
  35.5 21.0 %collective-permute-start.11 = (bf16[128,512]{1,0:T(8,128)(2,1)S(1)}, bf16[128,512]{1,0:T(8,128)(2,1)S(1)}, u32[]{:S(2)}, u32[]{:S(2)}) collective-permute-start(bf16[128,512]{1,0:T(8,128)(2,1)S(1)} %project_sides.1.refs_1_), channel_id=1, source_target_pairs={{0,8},{4,12},{8,16},{12,20},{16,24},{20,28},{24,32},{28,36},{32,40... | collective-permute-start | bytes 393224 | tf_op jit(solution)/shard_map/ppermute | solution.py:24
  39.0 17.5 %collective-permute-start.10 = (bf16[128,512]{1,0:T(8,128)(2,1)S(1)}, bf16[128,512]{1,0:T(8,128)(2,1)S(1)}, u32[]{:S(2)}, u32[]{:S(2)}) collective-permute-start(bf16[128,512]{1,0:T(8,128)(2,1)S(1)} %project_sides.1.refs_1_), channel_id=1, source_target_pairs={{0,4},{4,8},{8,12},{12,16},{16,20},{20,24},{24,28},{28,32},{32,36}... | collective-permute-start | bytes 393224 | tf_op jit(solution)/shard_map/ppermute | solution.py:24
  44.7 14.4 %collective-permute-start.9 = (bf16[64,512]{1,0:T(8,128)(2,1)S(1)}, bf16[64,512]{1,0:T(8,128)(2,1)S(1)}, u32[]{:S(2)}, u32[]{:S(2)}) collective-permute-start(bf16[64,512]{1,0:T(8,128)(2,1)S(1)} %project_across.1.refs_1_), channel_id=1, source_target_pairs={{0,12},{4,16},{8,20},{12,24},{16,28},{20,32},{24,36},{28,40},{32,4... | collective-permute-start | bytes 196616 | tf_op jit(solution)/shard_map/ppermute | solution.py:24
  48.5 10.7 %collective-permute-start.8 = (bf16[64,512]{1,0:T(8,128)(2,1)S(1)}, bf16[64,512]{1,0:T(8,128)(2,1)S(1)}, u32[]{:S(2)}, u32[]{:S(2)}) collective-permute-start(bf16[64,512]{1,0:T(8,128)(2,1)S(1)} %project_across.1.refs_1_), channel_id=1, source_target_pairs={{0,8},{4,12},{8,16},{12,20},{16,24},{20,28},{24,32},{28,36},{32,40... | collective-permute-start | bytes 196616 | tf_op jit(solution)/shard_map/ppermute | solution.py:24
  52.6 7.9 %collective-permute-start.7 = (bf16[64,512]{1,0:T(8,128)(2,1)S(1)}, bf16[64,512]{1,0:T(8,128)(2,1)S(1)}, u32[]{:S(2)}, u32[]{:S(2)}) collective-permute-start(bf16[64,512]{1,0:T(8,128)(2,1)S(1)} %project_across.1.refs_1_), channel_id=1, source_target_pairs={{0,4},{4,8},{8,12},{12,16},{16,20},{20,24},{24,28},{28,32},{32,36}... | collective-permute-start | bytes 196616 | tf_op jit(solution)/shard_map/ppermute | solution.py:24

commit v3 on v2

--- a/solution.py
+++ b/solution.py
@@ -16,12 +16,6 @@
 PROJECT_VMEM = 8 * 1024 * 1024
 ATTEND_VMEM = 20 * 1024 * 1024
 WHOLE = pl.BlockSpec(memory_space=pltpu.VMEM)
-
-
-def shifted(value, axis, by):
-    length = lax.axis_size(axis)
-    pairs = [(i, i + by) for i in range(length) if 0 <= i + by < length]
-    return lax.ppermute(value, axis, pairs)
 
 
 def turned(value, axis, by):
@@ -184,7 +178,7 @@
         return project(row_parts, key_matrix, value_matrix, key_gain, "project_" + name)
 
     def reached(block):
-        return [block] + [shifted(block, "seq", by) for by in range(1, REACH)]
+        return [block] + [turned(block, "seq", by) for by in range(1, REACH)]
 
     left = turned(vision, "tp", 1)
     right = turned(vision, "tp", -1)

time: 63.3 us -> 59.3 us (0.937)
  the two profiles are of different devices: /device:TPU:96 before, /device:TPU:1 now
where the time goes in v3:
time: 59.3 us; the launch traced here: 59.1 us
  starting transfers between devices  22.1 us (37%)
  waiting for transfers between devices  18.8 us (32%)
  Pallas kernels  11.5 us (19%)
  local copies, waits for them, and re-layouts  6.36 us (11%)
    ppermute x13, starting transfers between devices, turned(): lax.ppermute(value, axis, [(i, (i + by) % length) for i in range(length)])  22.1 us
    ppermute x13, waiting for transfers between devices, turned(): lax.ppermute(value, axis, [(i, (i + by) % length) for i in range(length)])  18.8 us
    pallas_call x3, Pallas kernels, attend(): pl.pallas_call(functools.partial(attend_kernel, first, last, kv_heads), o...  6.83 us
    unnamed x20, local copies, waits for them, and re-layouts  6.28 us
    pallas_call x3, Pallas kernels, project(): pl.pallas_call(project_kernel, out_shape=jax.ShapeDtypeStruct((rows, 2 *...  4.69 us
  transfers between devices with their start and end apart: 13, of which 5 were waited for; matrix products, arithmetic and copies ran while one was open for 0% of the time, Pallas kernels for 15%

profile of v3, /device:TPU:1, one launch (start us, length us, event | category | flops | bytes accessed | tf_op | source)
XLA Modules:
  0.0 59.1 jit_solution(15866613593584863618)
XLA Ops:
  0.0 3.3 %collective-permute-start.4 = (bf16[64,8192]{1,0:T(8,128)(2,1)}, bf16[64,8192]{1,0:T(8,128)(2,1)S(1)}, u32[]{:S(2)}, u32[]{:S(2)}) collective-permute-start(bf16[64,8192]{1,0:T(8,128)(2,1)} %refs_0_.2), channel_id=1, source_target_pairs={{0,3},{1,0},{2,1},{3,2},{4,7},{5,4},{6,5},{7,6},{8,11},{9,8},{10,9... | collective-permute-start | bytes 3145736 | tf_op jit(solution)/shard_map/ppermute | solution.py:23
  3.3 2.2 %copy-done = bf16[8192,256]{1,0:T(8,128)(2,1)S(1)} copy-done((bf16[8192,256]{1,0:T(8,128)(2,1)S(1)}, bf16[8192,256]{1,0:T(8,128)(2,1)}, u32[]{:S(2)}) %copy-start) | copy-done | bytes 4194328
  5.5 2.2 %copy-done.2 = bf16[8192,256]{1,0:T(8,128)(2,1)S(1)} copy-done((bf16[8192,256]{1,0:T(8,128)(2,1)S(1)}, bf16[8192,256]{1,0:T(8,128)(2,1)}, u32[]{:S(2)}) %copy-start.2) | copy-done | bytes 4194328
  7.7 1.2 %copy-done.4 = bf16[64,8192]{1,0:T(8,128)(2,1)S(1)} copy-done((bf16[64,8192]{1,0:T(8,128)(2,1)S(1)}, bf16[64,8192]{1,0:T(8,128)(2,1)}, u32[]{:S(2)}) %copy-start.4) | copy-done | bytes 1048600
  8.9 0.7 %copy-done.5 = f32[128]{0:T(128)S(1)} copy-done((f32[128]{0:T(128)S(1)}, f32[128]{0:T(128)}, u32[]{:S(2)}) %copy-start.5) | copy-done | bytes 536
  9.6 1.6 %project_own.1.refs_1_ = bf16[64,512]{1,0:T(8,128)(2,1)S(1)} custom-call(bf16[64,8192]{1,0:T(8,128)(2,1)S(1)} %copy-done.4, bf16[8192,256]{1,0:T(8,128)(2,1)S(1)} %copy-done, bf16[8192,256]{1,0:T(8,128)(2,1)S(1)} %copy-done.2, f32[1,128]{1,0:T(1,128)S(1)} %bitcast.7), custom_call_target="tpu_custom_call" | custom-call | flops 536870912 | bytes 8388608 | tf_op jit(solution)/shard_map/project_own/pallas_call | solution.py:53
  11.2 3.8 %collective-permute-start.2 = (bf16[64,512]{1,0:T(8,128)(2,1)S(1)}, bf16[64,512]{1,0:T(8,128)(2,1)S(1)}, u32[]{:S(2)}, u32[]{:S(2)}) collective-permute-start(bf16[64,512]{1,0:T(8,128)(2,1)S(1)} %project_own.1.refs_1_), channel_id=1, source_target_pairs={{0,12},{4,16},{8,20},{12,24},{16,28},{20,32},{24,36},{28,40},{32,4... | collective-permute-start | bytes 196616 | tf_op jit(solution)/shard_map/ppermute | solution.py:23
  15.1 0.4 collective-permute-start.1
  15.6 0.1 select_reduce_fusion
  15.7 7.4 %collective-permute-done.2.refs_4_ = bf16[64,512]{1,0:T(8,128)(2,1)S(1)} collective-permute-done((bf16[64,512]{1,0:T(8,128)(2,1)S(1)}, bf16[64,512]{1,0:T(8,128)(2,1)S(1)}, u32[]{:S(2)}, u32[]{:S(2)}) %collective-permute-start.2) | collective-permute-done | bytes 65568 | tf_op jit(solution)/shard_map/ppermute | solution.py:23
  23.2 1.7 %attend_own.1 = (bf16[256,2048]{1,0:T(8,128)(2,1)S(1)}, f32[256,2048]{1,0:T(8,128)S(1)}, f32[256,128]{1,0:T(8,128)S(1)}) custom-call(bf16[256,2048]{1,0:T(8,128)(2,1)S(1)} %copy-done.7, bf16[64,512]{1,0:T(8,128)(2,1)S(1)} %project_own.1.refs_1_, bf16[64,512]{1,0:T(8,128)(2,1)S(1)} %collective-permute-done.refs_2_, ...), custom_call_target="tpu_custom_call" | custom-call | flops 2147483648 | bytes 1048576 | tf_op jit(solution)/shard_map/attend_own/pallas_call | solution.py:151
  24.9 0.5 collective-permute-done.4.refs_1_
  25.5 3.0 %collective-permute-done.3.refs_0_ = bf16[64,8192]{1,0:T(8,128)(2,1)S(1)} collective-permute-done((bf16[64,8192]{1,0:T(8,128)(2,1)}, bf16[64,8192]{1,0:T(8,128)(2,1)S(1)}, u32[]{:S(2)}, u32[]{:S(2)}) %collective-permute-start.3) | collective-permute-done | bytes 1048608 | tf_op jit(solution)/shard_map/ppermute | solution.py:23
  28.6 2.7 %collective-permute-start.6 = (bf16[32,8192]{1,0:T(8,128)(2,1)S(1)}, bf16[32,8192]{1,0:T(8,128)(2,1)S(1)}, u32[]{:S(2)}, u32[]{:S(2)}) collective-permute-start(bf16[32,8192]{1,0:T(8,128)(2,1)S(1)} %slice.7), channel_id=1, source_target_pairs={{0,3},{1,0},{2,1},{3,2},{4,7},{5,4},{6,5},{7,6},{8,11},{9,8},{10,9... | collective-permute-start | bytes 1572872 | tf_op jit(solution)/shard_map/ppermute | solution.py:23
  31.3 1.4 %project_sides.1.refs_1_ = bf16[128,512]{1,0:T(8,128)(2,1)S(1)} custom-call(bf16[64,8192]{1,0:T(8,128)(2,1)S(1)} %collective-permute-done.3.refs_0_, bf16[64,8192]{1,0:T(8,128)(2,1)S(1)} %collective-permute-done.4.refs_1_, bf16[8192,256]{1,0:T(8,128)(2,1)S(1)} %copy-done.1, bf16[8192,256]{1,0:T(8,128)(2,1)S(1)} %copy-done.3, f32[1,128]{1,0:T(1,128)S(1)} %bitcast.8), custom_call_target="tpu_custom_call" | custom-call | flops 1073741824 | bytes 8388608 | tf_op jit(solution)/shard_map/project_sides/pallas_call | solution.py:53
  32.7 5.3 %collective-permute-start.12 = (bf16[128,512]{1,0:T(8,128)(2,1)S(1)}, bf16[128,512]{1,0:T(8,128)(2,1)S(1)}, u32[]{:S(2)}, u32[]{:S(2)}) collective-permute-start(bf16[128,512]{1,0:T(8,128)(2,1)S(1)} %project_sides.1.refs_1_), channel_id=1, source_target_pairs={{0,12},{4,16},{8,20},{12,24},{16,28},{20,32},{24,36},{28,40},{32,4... | collective-permute-start | bytes 393224 | tf_op jit(solution)/shard_map/ppermute | solution.py:23
  38.0 0.4 collective-permute-start.11
  38.4 3.0 %collective-permute-done.5.refs_0_ = bf16[32,8192]{1,0:T(8,128)(2,1)S(1)} collective-permute-done((bf16[32,8192]{1,0:T(8,128)(2,1)S(1)}, bf16[32,8192]{1,0:T(8,128)(2,1)S(1)}, u32[]{:S(2)}, u32[]{:S(2)}) %collective-permute-start.5) | collective-permute-done | bytes 524320 | tf_op jit(solution)/shard_map/ppermute | solution.py:23
  41.4 1.6 %project_across.1.refs_1_ = bf16[64,512]{1,0:T(8,128)(2,1)S(1)} custom-call(bf16[32,8192]{1,0:T(8,128)(2,1)S(1)} %collective-permute-done.5.refs_0_, bf16[32,8192]{1,0:T(8,128)(2,1)S(1)} %collective-permute-done.6.refs_1_, bf16[8192,256]{1,0:T(8,128)(2,1)S(1)} %copy-done.1, bf16[8192,256]{1,0:T(8,128)(2,1)S(1)} %copy-done.3, f32[1,128]{1,0:T(1,128)S(1)} %bitcast.9), custom_call_target="tpu_custom_call" | custom-call | flops 536870912 | bytes 8388608 | tf_op jit(solution)/shard_map/project_across/pallas_call | solution.py:53
  43.0 5.7 %collective-permute-start.9 = (bf16[64,512]{1,0:T(8,128)(2,1)S(1)}, bf16[64,512]{1,0:T(8,128)(2,1)S(1)}, u32[]{:S(2)}, u32[]{:S(2)}) collective-permute-start(bf16[64,512]{1,0:T(8,128)(2,1)S(1)} %project_across.1.refs_1_), channel_id=1, source_target_pairs={{0,12},{4,16},{8,20},{12,24},{16,28},{20,32},{24,36},{28,40},{32,4... | collective-permute-start | bytes 196616 | tf_op jit(solution)/shard_map/ppermute | solution.py:23
  48.7 0.4 collective-permute-start.8
  49.1 2.6 %attend_sides.1 = (f32[256,2048]{1,0:T(8,128)S(1)}, f32[256,128]{1,0:T(8,128)S(1)}) custom-call(bf16[256,2048]{1,0:T(8,128)(2,1)S(1)} %get-tuple-element.22.refs_0_, bf16[128,512]{1,0:T(8,128)(2,1)S(1)} %project_sides.1.refs_1_, bf16[128,512]{1,0:T(8,128)(2,1)S(1)} %collective-permute-done.10.refs_2_, bf16[128,512]{1,0:T(8,128)(2,1)S(1)} %collective-permute-done.11.refs_3_, ...), custom_call_target="tpu_custom_call" | custom-call | flops 4294967296 | bytes 1048576 | tf_op jit(solution)/shard_map/attend_sides/pallas_call | solution.py:151
  51.8 4.9 %collective-permute-done.9.refs_4_ = bf16[64,512]{1,0:T(8,128)(2,1)S(1)} collective-permute-done((bf16[64,512]{1,0:T(8,128)(2,1)S(1)}, bf16[64,512]{1,0:T(8,128)(2,1)S(1)}, u32[]{:S(2)}, u32[]{:S(2)}) %collective-permute-start.9) | collective-permute-done | bytes 65568 | tf_op jit(solution)/shard_map/ppermute | solution.py:23
  56.7 2.5 %attend_across.1 = bf16[256,2048]{1,0:T(8,128)(2,1)} custom-call(bf16[256,2048]{1,0:T(8,128)(2,1)S(1)} %get-tuple-element.22.refs_0_, bf16[64,512]{1,0:T(8,128)(2,1)S(1)} %project_across.1.refs_1_, bf16[64,512]{1,0:T(8,128)(2,1)S(1)} %collective-permute-done.7.refs_2_, bf16[64,512]{1,0:T(8,128)(2,1)S(1)} %collective-permute-done.8.refs_3_, ...), custom_call_target="tpu_custom_call" | custom-call | flops 2147483648 | bytes 1048576 | tf_op jit(solution)/shard_map/attend_across/pallas_call | solution.py:151
  (36 shorter events, 0.3 us)
Async XLA Ops:
  0.0 25.5 %collective-permute-start.4 = (bf16[64,8192]{1,0:T(8,128)(2,1)}, bf16[64,8192]{1,0:T(8,128)(2,1)S(1)}, u32[]{:S(2)}, u32[]{:S(2)}) collective-permute-start(bf16[64,8192]{1,0:T(8,128)(2,1)} %refs_0_.2), channel_id=1, source_target_pairs={{0,3},{1,0},{2,1},{3,2},{4,7},{5,4},{6,5},{7,6},{8,11},{9,8},{10,9... | collective-permute-start | bytes 3145736 | tf_op jit(solution)/shard_map/ppermute | solution.py:23
  3.3 25.1 %collective-permute-start.3 = (bf16[64,8192]{1,0:T(8,128)(2,1)}, bf16[64,8192]{1,0:T(8,128)(2,1)S(1)}, u32[]{:S(2)}, u32[]{:S(2)}) collective-permute-start(bf16[64,8192]{1,0:T(8,128)(2,1)} %refs_0_.2), channel_id=1, source_target_pairs={{0,1},{1,2},{2,3},{3,0},{4,5},{5,6},{6,7},{7,4},{8,9},{9,10},{10,1... | collective-permute-start | bytes 3145736 | tf_op jit(solution)/shard_map/ppermute | solution.py:23
  3.3 2.2 %copy-start = (bf16[8192,256]{1,0:T(8,128)(2,1)S(1)}, bf16[8192,256]{1,0:T(8,128)(2,1)}, u32[]{:S(2)}) copy-start(bf16[8192,256]{1,0:T(8,128)(2,1)} %refs_2_.5) | copy-start | bytes 12582916
  5.5 2.2 %copy-start.2 = (bf16[8192,256]{1,0:T(8,128)(2,1)S(1)}, bf16[8192,256]{1,0:T(8,128)(2,1)}, u32[]{:S(2)}) copy-start(bf16[8192,256]{1,0:T(8,128)(2,1)} %refs_3_.3) | copy-start | bytes 12582916
  7.7 1.2 %copy-start.4 = (bf16[64,8192]{1,0:T(8,128)(2,1)S(1)}, bf16[64,8192]{1,0:T(8,128)(2,1)}, u32[]{:S(2)}) copy-start(bf16[64,8192]{1,0:T(8,128)(2,1)} %refs_0_.2) | copy-start | bytes 3145732
  8.9 0.7 %copy-start.5 = (f32[128]{0:T(128)S(1)}, f32[128]{0:T(128)}, u32[]{:S(2)}) copy-start(f32[128]{0:T(128)} %param.12) | copy-start | bytes 1540
  9.6 6.0 %copy-start.9 = (f32[128]{0:T(128)S(1)}, f32[128]{0:T(128)}, u32[]{:S(2)}) copy-start(f32[128]{0:T(128)} %param.11) | copy-start | bytes 1540
  9.6 6.0 %copy-start.8 = (s32[4,64]{1,0:T(4,128)S(1)}, s32[4,64]{1,0:T(4,128)}, u32[]{:S(2)}) copy-start(s32[4,64]{1,0:T(4,128)} %param.13) | copy-start | bytes 3076
  9.6 13.6 %copy-start.7 = (bf16[256,2048]{1,0:T(8,128)(2,1)S(1)}, bf16[256,2048]{1,0:T(8,128)(2,1)}, u32[]{:S(2)}) copy-start(bf16[256,2048]{1,0:T(8,128)(2,1)} %refs_0_.3) | copy-start | bytes 3145732
  11.2 11.9 %collective-permute-start.2 = (bf16[64,512]{1,0:T(8,128)(2,1)S(1)}, bf16[64,512]{1,0:T(8,128)(2,1)S(1)}, u32[]{:S(2)}, u32[]{:S(2)}) collective-permute-start(bf16[64,512]{1,0:T(8,128)(2,1)S(1)} %project_own.1.refs_1_), channel_id=1, source_target_pairs={{0,12},{4,16},{8,20},{12,24},{16,28},{20,32},{24,36},{28,40},{32,4... | collective-permute-start | bytes 196616 | tf_op jit(solution)/shard_map/ppermute | solution.py:23
  15.1 8.1 %collective-permute-start.1 = (bf16[64,512]{1,0:T(8,128)(2,1)S(1)}, bf16[64,512]{1,0:T(8,128)(2,1)S(1)}, u32[]{:S(2)}, u32[]{:S(2)}) collective-permute-start(bf16[64,512]{1,0:T(8,128)(2,1)S(1)} %project_own.1.refs_1_), channel_id=1, source_target_pairs={{0,8},{4,12},{8,16},{12,20},{16,24},{20,28},{24,32},{28,36},{32,40... | collective-permute-start | bytes 196616 | tf_op jit(solution)/shard_map/ppermute | solution.py:23
  15.5 7.7 %collective-permute-start = (bf16[64,512]{1,0:T(8,128)(2,1)S(1)}, bf16[64,512]{1,0:T(8,128)(2,1)S(1)}, u32[]{:S(2)}, u32[]{:S(2)}) collective-permute-start(bf16[64,512]{1,0:T(8,128)(2,1)S(1)} %project_own.1.refs_1_), channel_id=1, source_target_pairs={{0,4},{4,8},{8,12},{12,16},{16,20},{20,24},{24,28},{28,32},{32,36}... | collective-permute-start | bytes 196616 | tf_op jit(solution)/shard_map/ppermute | solution.py:23
  23.2 8.1 %copy-start.1 = (bf16[8192,256]{1,0:T(8,128)(2,1)S(1)}, bf16[8192,256]{1,0:T(8,128)(2,1)}, u32[]{:S(2)}) copy-start(bf16[8192,256]{1,0:T(8,128)(2,1)} %refs_2_.5) | copy-start | bytes 12582916
  23.2 8.1 %copy-start.3 = (bf16[8192,256]{1,0:T(8,128)(2,1)S(1)}, bf16[8192,256]{1,0:T(8,128)(2,1)}, u32[]{:S(2)}) copy-start(bf16[8192,256]{1,0:T(8,128)(2,1)} %refs_3_.3) | copy-start | bytes 12582916
  23.2 8.1 %copy-start.6 = (f32[128]{0:T(128)S(1)}, f32[128]{0:T(128)}, u32[]{:S(2)}) copy-start(f32[128]{0:T(128)} %param.12) | copy-start | bytes 1540
  28.5 12.8 %collective-permute-start.5 = (bf16[32,8192]{1,0:T(8,128)(2,1)S(1)}, bf16[32,8192]{1,0:T(8,128)(2,1)S(1)}, u32[]{:S(2)}, u32[]{:S(2)}) collective-permute-start(bf16[32,8192]{1,0:T(8,128)(2,1)S(1)} %slice.6), channel_id=1, source_target_pairs={{0,1},{1,2},{2,3},{3,0},{4,5},{5,6},{6,7},{7,4},{8,9},{9,10},{10,1... | collective-permute-start | bytes 1572872 | tf_op jit(solution)/shard_map/ppermute | solution.py:23
  28.6 12.8 %collective-permute-start.6 = (bf16[32,8192]{1,0:T(8,128)(2,1)S(1)}, bf16[32,8192]{1,0:T(8,128)(2,1)S(1)}, u32[]{:S(2)}, u32[]{:S(2)}) collective-permute-start(bf16[32,8192]{1,0:T(8,128)(2,1)S(1)} %slice.7), channel_id=1, source_target_pairs={{0,3},{1,0},{2,1},{3,2},{4,7},{5,4},{6,5},{7,6},{8,11},{9,8},{10,9... | collective-permute-start | bytes 1572872 | tf_op jit(solution)/shard_map/ppermute | solution.py:23
  32.7 16.4 %collective-permute-start.12 = (bf16[128,512]{1,0:T(8,128)(2,1)S(1)}, bf16[128,512]{1,0:T(8,128)(2,1)S(1)}, u32[]{:S(2)}, u32[]{:S(2)}) collective-permute-start(bf16[128,512]{1,0:T(8,128)(2,1)S(1)} %project_sides.1.refs_1_), channel_id=1, source_target_pairs={{0,12},{4,16},{8,20},{12,24},{16,28},{20,32},{24,36},{28,40},{32,4... | collective-permute-start | bytes 393224 | tf_op jit(solution)/shard_map/ppermute | solution.py:23
  38.0 11.1 %collective-permute-start.11 = (bf16[128,512]{1,0:T(8,128)(2,1)S(1)}, bf16[128,512]{1,0:T(8,128)(2,1)S(1)}, u32[]{:S(2)}, u32[]{:S(2)}) collective-permute-start(bf16[128,512]{1,0:T(8,128)(2,1)S(1)} %project_sides.1.refs_1_), channel_id=1, source_target_pairs={{0,8},{4,12},{8,16},{12,20},{16,24},{20,28},{24,32},{28,36},{32,40... | collective-permute-start | bytes 393224 | tf_op jit(solution)/shard_map/ppermute | solution.py:23
  38.4 10.7 %collective-permute-start.10 = (bf16[128,512]{1,0:T(8,128)(2,1)S(1)}, bf16[128,512]{1,0:T(8,128)(2,1)S(1)}, u32[]{:S(2)}, u32[]{:S(2)}) collective-permute-start(bf16[128,512]{1,0:T(8,128)(2,1)S(1)} %project_sides.1.refs_1_), channel_id=1, source_target_pairs={{0,4},{4,8},{8,12},{12,16},{16,20},{20,24},{24,28},{28,32},{32,36}... | collective-permute-start | bytes 393224 | tf_op jit(solution)/shard_map/ppermute | solution.py:23
  43.0 13.7 %collective-permute-start.9 = (bf16[64,512]{1,0:T(8,128)(2,1)S(1)}, bf16[64,512]{1,0:T(8,128)(2,1)S(1)}, u32[]{:S(2)}, u32[]{:S(2)}) collective-permute-start(bf16[64,512]{1,0:T(8,128)(2,1)S(1)} %project_across.1.refs_1_), channel_id=1, source_target_pairs={{0,12},{4,16},{8,20},{12,24},{16,28},{20,32},{24,36},{28,40},{32,4... | collective-permute-start | bytes 196616 | tf_op jit(solution)/shard_map/ppermute | solution.py:23
  48.7 8.0 %collective-permute-start.8 = (bf16[64,512]{1,0:T(8,128)(2,1)S(1)}, bf16[64,512]{1,0:T(8,128)(2,1)S(1)}, u32[]{:S(2)}, u32[]{:S(2)}) collective-permute-start(bf16[64,512]{1,0:T(8,128)(2,1)S(1)} %project_across.1.refs_1_), channel_id=1, source_target_pairs={{0,8},{4,12},{8,16},{12,20},{16,24},{20,28},{24,32},{28,36},{32,40... | collective-permute-start | bytes 196616 | tf_op jit(solution)/shard_map/ppermute | solution.py:23
  49.1 7.6 %collective-permute-start.7 = (bf16[64,512]{1,0:T(8,128)(2,1)S(1)}, bf16[64,512]{1,0:T(8,128)(2,1)S(1)}, u32[]{:S(2)}, u32[]{:S(2)}) collective-permute-start(bf16[64,512]{1,0:T(8,128)(2,1)S(1)} %project_across.1.refs_1_), channel_id=1, source_target_pairs={{0,4},{4,8},{8,12},{12,16},{16,20},{20,24},{24,28},{28,32},{32,36}... | collective-permute-start | bytes 196616 | tf_op jit(solution)/shard_map/ppermute | solution.py:23

commit v4 on v3

--- a/solution.py
+++ b/solution.py
@@ -128,7 +128,7 @@
 
 def attend_cost(rows, width, keys):
     return pl.CostEstimate(
-        flops=16 * rows * width * keys,
+        flops=12 * rows * width * keys,
         transcendentals=rows * width // HEAD_SIZE * keys,
         bytes_accessed=2 * rows * width,
     )
@@ -180,19 +180,25 @@
     def reached(block):
         return [block] + [turned(block, "seq", by) for by in range(1, REACH)]
 
-    left = turned(vision, "tp", 1)
-    right = turned(vision, "tp", -1)
+    half = vision.shape[0] // 2
+    upper = vision[:half]
+    lower = after(vision, upper)[half:]
+    upper_left = turned(upper, "tp", 1)
+    lower_right = turned(lower, "tp", -1)
+    lower_left = turned(lower, "tp", 1)
+    upper_right = turned(upper, "tp", -1)
+
     own = projected([vision], "own")
     own_blocks = reached(own)
+    upper_left, lower_right = after((upper_left, lower_right), own)
+    upper_across = turned(upper_left, "tp", 1)
+    lower_across = turned(lower_right, "tp", -1)
     normed, *carried = attend(
         text_query_matrix, own_blocks, is_open, query_gain, None, False, "attend_own"
     )
 
-    half = vision.shape[0] // 2
-    left, right = after((left, right), carried)
-    upper_across = turned(left[:half], "tp", 1)
-    lower_across = turned(right[half:], "tp", -1)
-    sides = projected([left, right], "sides")
+    lower_left, upper_right = after((lower_left, upper_right), carried)
+    sides = projected([upper_left, lower_left, upper_right, lower_right], "sides")
     side_blocks = reached(sides)
     upper_across, lower_across = after((upper_across, lower_across), sides)
     across = projected([upper_across, lower_across], "across")

time: 59.3 us -> 64.2 us (1.083); the launches traced: 59.1 us -> 62.9 us
  local copies, waits for them, and re-layouts: 6.36 us -> 12.2 us
  waiting for transfers between devices: 18.8 us -> 17.5 us
  starting transfers between devices: 22.1 us -> 21.2 us
    slice x2, local copies, waits for them, and re-layouts: 0.07 us -> 3.75 us  [the longest x1 1.88 us: body(): lower = after(vision, upper)[half:]]
    unnamed x20, local copies, waits for them, and re-layouts: 6.28 us -> 8.46 us
    ppermute x13 -> x15, waiting for transfers between devices: 18.8 us -> 17.5 us  [turned(): lax.ppermute(value, axis, [(i, (i + by) % length) for i in range(length)])]
    ppermute x13 -> x15, starting transfers between devices: 22.1 us -> 21.2 us  [turned(): lax.ppermute(value, axis, [(i, (i + by) % length) for i in range(length)])]
  transfers between devices with their start and end apart: 13 -> 15, of which waited for: 5 -> 5; matrix products, arithmetic and copies ran while one was open for 0% -> 0% of each run, Pallas kernels for 15% -> 15%
where the time goes in v4:
time: 64.2 us; the launch traced here: 62.9 us
  starting transfers between devices  21.2 us (33%)
  waiting for transfers between devices  17.5 us (27%)
  local copies, waits for them, and re-layouts  12.2 us (19%)
  Pallas kernels  11.6 us (18%)
    ppermute x15, starting transfers between devices, turned(): lax.ppermute(value, axis, [(i, (i + by) % length) for i in range(length)])  21.2 us
    ppermute x15, waiting for transfers between devices, turned(): lax.ppermute(value, axis, [(i, (i + by) % length) for i in range(length)])  17.5 us
    unnamed x20, local copies, waits for them, and re-layouts  8.46 us
    pallas_call x3, Pallas kernels, attend(): pl.pallas_call(functools.partial(attend_kernel, first, last, kv_heads), o...  6.92 us
    pallas_call x3, Pallas kernels, project(): pl.pallas_call(project_kernel, out_shape=jax.ShapeDtypeStruct((rows, 2 *...  4.69 us
    slice x1, local copies, waits for them, and re-layouts, body(): lower = after(vision, upper)[half:]  1.88 us
    slice x1, local copies, waits for them, and re-layouts, body(): upper = vision[:half]  1.87 us
  transfers between devices with their start and end apart: 15, of which 5 were waited for; matrix products, arithmetic and copies ran while one was open for 0% of the time, Pallas kernels for 15%

profile of v4, /device:TPU:1, one launch (start us, length us, event | category | flops | bytes accessed | tf_op | source)
XLA Modules:
  0.0 62.9 jit_solution(17341706341518129820)
XLA Ops:
  0.0 1.9 %slice.6 = bf16[32,8192]{1,0:T(8,128)(2,1)} slice(bf16[64,8192]{1,0:T(8,128)(2,1)} %refs_0_.2), slice={[0:32], [0:8192]} | slice | bytes 1048576 | tf_op jit(solution)/shard_map/slice | solution.py:184
  1.9 1.9 %slice.7 = bf16[32,8192]{1,0:T(8,128)(2,1)} slice(bf16[64,8192]{1,0:T(8,128)(2,1)} %refs_0_.2), slice={[32:64], [0:8192]} | slice | bytes 1048576 | tf_op jit(solution)/shard_map/slice | solution.py:185
  3.8 3.3 %collective-permute-start.4 = (bf16[32,8192]{1,0:T(8,128)(2,1)}, bf16[32,8192]{1,0:T(8,128)(2,1)S(1)}, u32[]{:S(2)}, u32[]{:S(2)}) collective-permute-start(bf16[32,8192]{1,0:T(8,128)(2,1)} %slice.7), channel_id=1, source_target_pairs={{0,3},{1,0},{2,1},{3,2},{4,7},{5,4},{6,5},{7,6},{8,11},{9,8},{10,9... | collective-permute-start | bytes 1572872 | tf_op jit(solution)/shard_map/ppermute | solution.py:23
  7.3 2.5 %collective-permute-start.8 = (bf16[32,8192]{1,0:T(8,128)(2,1)}, bf16[32,8192]{1,0:T(8,128)(2,1)S(1)}, u32[]{:S(2)}, u32[]{:S(2)}) collective-permute-start(bf16[32,8192]{1,0:T(8,128)(2,1)} %slice.6), channel_id=1, source_target_pairs={{0,3},{1,0},{2,1},{3,2},{4,7},{5,4},{6,5},{7,6},{8,11},{9,8},{10,9... | collective-permute-start | bytes 1572872 | tf_op jit(solution)/shard_map/ppermute | solution.py:23
  9.8 2.2 %copy-done = bf16[8192,256]{1,0:T(8,128)(2,1)S(1)} copy-done((bf16[8192,256]{1,0:T(8,128)(2,1)S(1)}, bf16[8192,256]{1,0:T(8,128)(2,1)}, u32[]{:S(2)}) %copy-start) | copy-done | bytes 4194328
  12.0 2.2 %copy-done.2 = bf16[8192,256]{1,0:T(8,128)(2,1)S(1)} copy-done((bf16[8192,256]{1,0:T(8,128)(2,1)S(1)}, bf16[8192,256]{1,0:T(8,128)(2,1)}, u32[]{:S(2)}) %copy-start.2) | copy-done | bytes 4194328
  14.2 1.2 %copy-done.4 = bf16[64,8192]{1,0:T(8,128)(2,1)S(1)} copy-done((bf16[64,8192]{1,0:T(8,128)(2,1)S(1)}, bf16[64,8192]{1,0:T(8,128)(2,1)}, u32[]{:S(2)}) %copy-start.4) | copy-done | bytes 1048600
  16.0 1.6 %project_own.1.refs_1_ = bf16[64,512]{1,0:T(8,128)(2,1)S(1)} custom-call(bf16[64,8192]{1,0:T(8,128)(2,1)S(1)} %copy-done.4, bf16[8192,256]{1,0:T(8,128)(2,1)S(1)} %copy-done, bf16[8192,256]{1,0:T(8,128)(2,1)S(1)} %copy-done.2, f32[1,128]{1,0:T(1,128)S(1)} %bitcast.7), custom_call_target="tpu_custom_call" | custom-call | flops 536870912 | bytes 8388608 | tf_op jit(solution)/shard_map/project_own/pallas_call | solution.py:53
  17.7 2.8 %collective-permute-start = (bf16[64,512]{1,0:T(8,128)(2,1)S(1)}, bf16[64,512]{1,0:T(8,128)(2,1)S(1)}, u32[]{:S(2)}, u32[]{:S(2)}) collective-permute-start(bf16[64,512]{1,0:T(8,128)(2,1)S(1)} %project_own.1.refs_1_), channel_id=1, source_target_pairs={{0,4},{4,8},{8,12},{12,16},{16,20},{20,24},{24,28},{28,32},{32,36}... | collective-permute-start | bytes 196616 | tf_op jit(solution)/shard_map/ppermute | solution.py:23
  20.6 1.3 %collective-permute-start.1 = (bf16[64,512]{1,0:T(8,128)(2,1)S(1)}, bf16[64,512]{1,0:T(8,128)(2,1)S(1)}, u32[]{:S(2)}, u32[]{:S(2)}) collective-permute-start(bf16[64,512]{1,0:T(8,128)(2,1)S(1)} %project_own.1.refs_1_), channel_id=1, source_target_pairs={{0,8},{4,12},{8,16},{12,20},{16,24},{20,28},{24,32},{28,36},{32,40... | collective-permute-start | bytes 196616 | tf_op jit(solution)/shard_map/ppermute | solution.py:23
  21.9 2.7 %collective-permute-start.6 = (bf16[32,8192]{1,0:T(8,128)(2,1)S(1)}, bf16[32,8192]{1,0:T(8,128)(2,1)S(1)}, u32[]{:S(2)}, u32[]{:S(2)}) collective-permute-start(bf16[32,8192]{1,0:T(8,128)(2,1)S(1)} %collective-permute-done.4.refs_3_), channel_id=1, source_target_pairs={{0,3},{1,0},{2,1},{3,2},{4,7},{5,4},{6,5},{7,6},{8,11},{9,8},{10,9... | collective-permute-start | bytes 1572872 | tf_op jit(solution)/shard_map/ppermute | solution.py:23
  24.6 3.6 %collective-permute-done.1.refs_3_ = bf16[64,512]{1,0:T(8,128)(2,1)S(1)} collective-permute-done((bf16[64,512]{1,0:T(8,128)(2,1)S(1)}, bf16[64,512]{1,0:T(8,128)(2,1)S(1)}, u32[]{:S(2)}, u32[]{:S(2)}) %collective-permute-start.1) | collective-permute-done | bytes 65568 | tf_op jit(solution)/shard_map/ppermute | solution.py:23
  28.2 2.3 %collective-permute-start.2 = (bf16[64,512]{1,0:T(8,128)(2,1)S(1)}, bf16[64,512]{1,0:T(8,128)(2,1)S(1)}, u32[]{:S(2)}, u32[]{:S(2)}) collective-permute-start(bf16[64,512]{1,0:T(8,128)(2,1)S(1)} %project_own.1.refs_1_), channel_id=1, source_target_pairs={{0,12},{4,16},{8,20},{12,24},{16,28},{20,32},{24,36},{28,40},{32,4... | collective-permute-start | bytes 196616 | tf_op jit(solution)/shard_map/ppermute | solution.py:23
  30.6 7.3 %collective-permute-done.2.refs_4_ = bf16[64,512]{1,0:T(8,128)(2,1)S(1)} collective-permute-done((bf16[64,512]{1,0:T(8,128)(2,1)S(1)}, bf16[64,512]{1,0:T(8,128)(2,1)S(1)}, u32[]{:S(2)}, u32[]{:S(2)}) %collective-permute-start.2) | collective-permute-done | bytes 65568 | tf_op jit(solution)/shard_map/ppermute | solution.py:23
  37.9 1.8 %attend_own.1 = (bf16[256,2048]{1,0:T(8,128)(2,1)S(1)}, f32[256,2048]{1,0:T(8,128)S(1)}, f32[256,128]{1,0:T(8,128)S(1)}) custom-call(bf16[256,2048]{1,0:T(8,128)(2,1)S(1)} %copy-done.7, bf16[64,512]{1,0:T(8,128)(2,1)S(1)} %project_own.1.refs_1_, bf16[64,512]{1,0:T(8,128)(2,1)S(1)} %collective-permute-done.refs_2_, ...), custom_call_target="tpu_custom_call" | custom-call | flops 1610612736 | bytes 1048576 | tf_op jit(solution)/shard_map/attend_own/pallas_call | solution.py:151
  39.7 2.2 %copy-done.3 = bf16[8192,256]{1,0:T(8,128)(2,1)S(1)} copy-done((bf16[8192,256]{1,0:T(8,128)(2,1)S(1)}, bf16[8192,256]{1,0:T(8,128)(2,1)}, u32[]{:S(2)}) %copy-start.3) | copy-done | bytes 4194328
  41.9 1.4 %project_sides.1.refs_1_ = bf16[128,512]{1,0:T(8,128)(2,1)S(1)} custom-call(bf16[32,8192]{1,0:T(8,128)(2,1)S(1)} %collective-permute-done.3.refs_0_, bf16[32,8192]{1,0:T(8,128)(2,1)S(1)} %collective-permute-done.7.refs_1_, bf16[32,8192]{1,0:T(8,128)(2,1)S(1)} %collective-permute-done.8.refs_2_, bf16[32,8192]{1,0:T(8,128)(2,1)S(1)} %collective-permute-done.4.refs_3_, ...), custom_call_target="tpu_custom_call" | custom-call | flops 1073741824 | bytes 8388608 | tf_op jit(solution)/shard_map/project_sides/pallas_call | solution.py:53
  43.7 1.6 %project_across.1.refs_1_ = bf16[64,512]{1,0:T(8,128)(2,1)S(1)} custom-call(bf16[32,8192]{1,0:T(8,128)(2,1)S(1)} %collective-permute-done.5.refs_0_, bf16[32,8192]{1,0:T(8,128)(2,1)S(1)} %collective-permute-done.6.refs_1_, bf16[8192,256]{1,0:T(8,128)(2,1)S(1)} %copy-done.1, bf16[8192,256]{1,0:T(8,128)(2,1)S(1)} %copy-done.3, f32[1,128]{1,0:T(1,128)S(1)} %bitcast.9), custom_call_target="tpu_custom_call" | custom-call | flops 536870912 | bytes 8388608 | tf_op jit(solution)/shard_map/project_across/pallas_call | solution.py:53
  45.4 1.1 %collective-permute-start.10 = (bf16[64,512]{1,0:T(8,128)(2,1)S(1)}, bf16[64,512]{1,0:T(8,128)(2,1)S(1)}, u32[]{:S(2)}, u32[]{:S(2)}) collective-permute-start(bf16[64,512]{1,0:T(8,128)(2,1)S(1)} %project_across.1.refs_1_), channel_id=1, source_target_pairs={{0,8},{4,12},{8,16},{12,20},{16,24},{20,28},{24,32},{28,36},{32,40... | collective-permute-start | bytes 196616 | tf_op jit(solution)/shard_map/ppermute | solution.py:23
  46.5 4.7 %collective-permute-start.11 = (bf16[64,512]{1,0:T(8,128)(2,1)S(1)}, bf16[64,512]{1,0:T(8,128)(2,1)S(1)}, u32[]{:S(2)}, u32[]{:S(2)}) collective-permute-start(bf16[64,512]{1,0:T(8,128)(2,1)S(1)} %project_across.1.refs_1_), channel_id=1, source_target_pairs={{0,12},{4,16},{8,20},{12,24},{16,28},{20,32},{24,36},{28,40},{32,4... | collective-permute-start | bytes 196616 | tf_op jit(solution)/shard_map/ppermute | solution.py:23
  51.1 5.8 %collective-permute-done.13.refs_3_ = bf16[128,512]{1,0:T(8,128)(2,1)S(1)} collective-permute-done((bf16[128,512]{1,0:T(8,128)(2,1)S(1)}, bf16[128,512]{1,0:T(8,128)(2,1)S(1)}, u32[]{:S(2)}, u32[]{:S(2)}) %collective-permute-start.13) | collective-permute-done | bytes 131104 | tf_op jit(solution)/shard_map/ppermute | solution.py:23
  56.9 0.8 %collective-permute-done.14.refs_4_ = bf16[128,512]{1,0:T(8,128)(2,1)S(1)} collective-permute-done((bf16[128,512]{1,0:T(8,128)(2,1)S(1)}, bf16[128,512]{1,0:T(8,128)(2,1)S(1)}, u32[]{:S(2)}, u32[]{:S(2)}) %collective-permute-start.14) | collective-permute-done | bytes 131104 | tf_op jit(solution)/shard_map/ppermute | solution.py:23
  57.7 2.7 %attend_sides.1 = (f32[256,2048]{1,0:T(8,128)S(1)}, f32[256,128]{1,0:T(8,128)S(1)}) custom-call(bf16[256,2048]{1,0:T(8,128)(2,1)S(1)} %get-tuple-element.25.refs_0_, bf16[128,512]{1,0:T(8,128)(2,1)S(1)} %project_sides.1.refs_1_, bf16[128,512]{1,0:T(8,128)(2,1)S(1)} %collective-permute-done.12.refs_2_, bf16[128,512]{1,0:T(8,128)(2,1)S(1)} %collective-permute-done.13.refs_3_, ...), custom_call_target="tpu_custom_call" | custom-call | flops 3221225472 | bytes 1048576 | tf_op jit(solution)/shard_map/attend_sides/pallas_call | solution.py:151
  60.5 2.5 %attend_across.1 = bf16[256,2048]{1,0:T(8,128)(2,1)} custom-call(bf16[256,2048]{1,0:T(8,128)(2,1)S(1)} %get-tuple-element.25.refs_0_, bf16[64,512]{1,0:T(8,128)(2,1)S(1)} %project_across.1.refs_1_, bf16[64,512]{1,0:T(8,128)(2,1)S(1)} %collective-permute-done.9.refs_2_, bf16[64,512]{1,0:T(8,128)(2,1)S(1)} %collective-permute-done.10.refs_3_, ...), custom_call_target="tpu_custom_call" | custom-call | flops 1610612736 | bytes 1048576 | tf_op jit(solution)/shard_map/attend_across/pallas_call | solution.py:151
  (40 shorter events, 1.6 us)
Async XLA Ops:
  3.8 16.8 %collective-permute-start.4 = (bf16[32,8192]{1,0:T(8,128)(2,1)}, bf16[32,8192]{1,0:T(8,128)(2,1)S(1)}, u32[]{:S(2)}, u32[]{:S(2)}) collective-permute-start(bf16[32,8192]{1,0:T(8,128)(2,1)} %slice.7), channel_id=1, source_target_pairs={{0,3},{1,0},{2,1},{3,2},{4,7},{5,4},{6,5},{7,6},{8,11},{9,8},{10,9... | collective-permute-start | bytes 1572872 | tf_op jit(solution)/shard_map/ppermute | solution.py:23
  7.1 14.8 %collective-permute-start.3 = (bf16[32,8192]{1,0:T(8,128)(2,1)}, bf16[32,8192]{1,0:T(8,128)(2,1)S(1)}, u32[]{:S(2)}, u32[]{:S(2)}) collective-permute-start(bf16[32,8192]{1,0:T(8,128)(2,1)} %slice.6), channel_id=1, source_target_pairs={{0,1},{1,2},{2,3},{3,0},{4,5},{5,6},{6,7},{7,4},{8,9},{9,10},{10,1... | collective-permute-start | bytes 1572872 | tf_op jit(solution)/shard_map/ppermute | solution.py:23
  7.1 32.6 %collective-permute-start.7 = (bf16[32,8192]{1,0:T(8,128)(2,1)}, bf16[32,8192]{1,0:T(8,128)(2,1)S(1)}, u32[]{:S(2)}, u32[]{:S(2)}) collective-permute-start(bf16[32,8192]{1,0:T(8,128)(2,1)} %slice.7), channel_id=1, source_target_pairs={{0,1},{1,2},{2,3},{3,0},{4,5},{5,6},{6,7},{7,4},{8,9},{9,10},{10,1... | collective-permute-start | bytes 1572872 | tf_op jit(solution)/shard_map/ppermute | solution.py:23
  7.3 32.4 %collective-permute-start.8 = (bf16[32,8192]{1,0:T(8,128)(2,1)}, bf16[32,8192]{1,0:T(8,128)(2,1)S(1)}, u32[]{:S(2)}, u32[]{:S(2)}) collective-permute-start(bf16[32,8192]{1,0:T(8,128)(2,1)} %slice.6), channel_id=1, source_target_pairs={{0,3},{1,0},{2,1},{3,2},{4,7},{5,4},{6,5},{7,6},{8,11},{9,8},{10,9... | collective-permute-start | bytes 1572872 | tf_op jit(solution)/shard_map/ppermute | solution.py:23
  9.8 2.2 %copy-start = (bf16[8192,256]{1,0:T(8,128)(2,1)S(1)}, bf16[8192,256]{1,0:T(8,128)(2,1)}, u32[]{:S(2)}) copy-start(bf16[8192,256]{1,0:T(8,128)(2,1)} %refs_2_.3) | copy-start | bytes 12582916
  12.0 2.2 %copy-start.2 = (bf16[8192,256]{1,0:T(8,128)(2,1)S(1)}, bf16[8192,256]{1,0:T(8,128)(2,1)}, u32[]{:S(2)}) copy-start(bf16[8192,256]{1,0:T(8,128)(2,1)} %refs_3_.1) | copy-start | bytes 12582916
  14.1 1.2 %copy-start.4 = (bf16[64,8192]{1,0:T(8,128)(2,1)S(1)}, bf16[64,8192]{1,0:T(8,128)(2,1)}, u32[]{:S(2)}) copy-start(bf16[64,8192]{1,0:T(8,128)(2,1)} %refs_0_.2) | copy-start | bytes 3145732
  16.0 8.5 %copy-start.9 = (f32[128]{0:T(128)S(1)}, f32[128]{0:T(128)}, u32[]{:S(2)}) copy-start(f32[128]{0:T(128)} %param.11) | copy-start | bytes 1540
  16.0 14.4 %copy-start.8 = (s32[4,64]{1,0:T(4,128)S(1)}, s32[4,64]{1,0:T(4,128)}, u32[]{:S(2)}) copy-start(s32[4,64]{1,0:T(4,128)} %param.13) | copy-start | bytes 3076
  16.0 21.8 %copy-start.7 = (bf16[256,2048]{1,0:T(8,128)(2,1)S(1)}, bf16[256,2048]{1,0:T(8,128)(2,1)}, u32[]{:S(2)}) copy-start(bf16[256,2048]{1,0:T(8,128)(2,1)} %refs_0_.3) | copy-start | bytes 3145732
  17.7 22.0 %copy-start.6 = (f32[128]{0:T(128)S(1)}, f32[128]{0:T(128)}, u32[]{:S(2)}) copy-start(f32[128]{0:T(128)} %param.12) | copy-start | bytes 1540
  17.7 4.2 %collective-permute-start = (bf16[64,512]{1,0:T(8,128)(2,1)S(1)}, bf16[64,512]{1,0:T(8,128)(2,1)S(1)}, u32[]{:S(2)}, u32[]{:S(2)}) collective-permute-start(bf16[64,512]{1,0:T(8,128)(2,1)S(1)} %project_own.1.refs_1_), channel_id=1, source_target_pairs={{0,4},{4,8},{8,12},{12,16},{16,20},{20,24},{24,28},{28,32},{32,36}... | collective-permute-start | bytes 196616 | tf_op jit(solution)/shard_map/ppermute | solution.py:23
  20.5 19.2 %copy-start.1 = (bf16[8192,256]{1,0:T(8,128)(2,1)S(1)}, bf16[8192,256]{1,0:T(8,128)(2,1)}, u32[]{:S(2)}) copy-start(bf16[8192,256]{1,0:T(8,128)(2,1)} %refs_2_.3) | copy-start | bytes 12582916
  20.6 7.6 %collective-permute-start.1 = (bf16[64,512]{1,0:T(8,128)(2,1)S(1)}, bf16[64,512]{1,0:T(8,128)(2,1)S(1)}, u32[]{:S(2)}, u32[]{:S(2)}) collective-permute-start(bf16[64,512]{1,0:T(8,128)(2,1)S(1)} %project_own.1.refs_1_), channel_id=1, source_target_pairs={{0,8},{4,12},{8,16},{12,20},{16,24},{20,28},{24,32},{28,36},{32,40... | collective-permute-start | bytes 196616 | tf_op jit(solution)/shard_map/ppermute | solution.py:23
  21.9 21.8 %collective-permute-start.5 = (bf16[32,8192]{1,0:T(8,128)(2,1)S(1)}, bf16[32,8192]{1,0:T(8,128)(2,1)S(1)}, u32[]{:S(2)}, u32[]{:S(2)}) collective-permute-start(bf16[32,8192]{1,0:T(8,128)(2,1)S(1)} %collective-permute-done.3.refs_0_), channel_id=1, source_target_pairs={{0,1},{1,2},{2,3},{3,0},{4,5},{5,6},{6,7},{7,4},{8,9},{9,10},{10,1... | collective-permute-start | bytes 1572872 | tf_op jit(solution)/shard_map/ppermute | solution.py:23
  21.9 21.8 %collective-permute-start.6 = (bf16[32,8192]{1,0:T(8,128)(2,1)S(1)}, bf16[32,8192]{1,0:T(8,128)(2,1)S(1)}, u32[]{:S(2)}, u32[]{:S(2)}) collective-permute-start(bf16[32,8192]{1,0:T(8,128)(2,1)S(1)} %collective-permute-done.4.refs_3_), channel_id=1, source_target_pairs={{0,3},{1,0},{2,1},{3,2},{4,7},{5,4},{6,5},{7,6},{8,11},{9,8},{10,9... | collective-permute-start | bytes 1572872 | tf_op jit(solution)/shard_map/ppermute | solution.py:23
  28.2 9.7 %collective-permute-start.2 = (bf16[64,512]{1,0:T(8,128)(2,1)S(1)}, bf16[64,512]{1,0:T(8,128)(2,1)S(1)}, u32[]{:S(2)}, u32[]{:S(2)}) collective-permute-start(bf16[64,512]{1,0:T(8,128)(2,1)S(1)} %project_own.1.refs_1_), channel_id=1, source_target_pairs={{0,12},{4,16},{8,20},{12,24},{16,28},{20,32},{24,36},{28,40},{32,4... | collective-permute-start | bytes 196616 | tf_op jit(solution)/shard_map/ppermute | solution.py:23
  39.7 2.2 %copy-start.3 = (bf16[8192,256]{1,0:T(8,128)(2,1)S(1)}, bf16[8192,256]{1,0:T(8,128)(2,1)}, u32[]{:S(2)}) copy-start(bf16[8192,256]{1,0:T(8,128)(2,1)} %refs_3_.1) | copy-start | bytes 12582916
  43.3 7.8 %collective-permute-start.12 = (bf16[128,512]{1,0:T(8,128)(2,1)S(1)}, bf16[128,512]{1,0:T(8,128)(2,1)S(1)}, u32[]{:S(2)}, u32[]{:S(2)}) collective-permute-start(bf16[128,512]{1,0:T(8,128)(2,1)S(1)} %project_sides.1.refs_1_), channel_id=1, source_target_pairs={{0,4},{4,8},{8,12},{12,16},{16,20},{20,24},{24,28},{28,32},{32,36}... | collective-permute-start | bytes 393224 | tf_op jit(solution)/shard_map/ppermute | solution.py:23
  43.4 13.5 %collective-permute-start.13 = (bf16[128,512]{1,0:T(8,128)(2,1)S(1)}, bf16[128,512]{1,0:T(8,128)(2,1)S(1)}, u32[]{:S(2)}, u32[]{:S(2)}) collective-permute-start(bf16[128,512]{1,0:T(8,128)(2,1)S(1)} %project_sides.1.refs_1_), channel_id=1, source_target_pairs={{0,8},{4,12},{8,16},{12,20},{16,24},{20,28},{24,32},{28,36},{32,40... | collective-permute-start | bytes 393224 | tf_op jit(solution)/shard_map/ppermute | solution.py:23
  43.6 14.1 %collective-permute-start.14 = (bf16[128,512]{1,0:T(8,128)(2,1)S(1)}, bf16[128,512]{1,0:T(8,128)(2,1)S(1)}, u32[]{:S(2)}, u32[]{:S(2)}) collective-permute-start(bf16[128,512]{1,0:T(8,128)(2,1)S(1)} %project_sides.1.refs_1_), channel_id=1, source_target_pairs={{0,12},{4,16},{8,20},{12,24},{16,28},{20,32},{24,36},{28,40},{32,4... | collective-permute-start | bytes 393224 | tf_op jit(solution)/shard_map/ppermute | solution.py:23
  45.4 15.0 %collective-permute-start.10 = (bf16[64,512]{1,0:T(8,128)(2,1)S(1)}, bf16[64,512]{1,0:T(8,128)(2,1)S(1)}, u32[]{:S(2)}, u32[]{:S(2)}) collective-permute-start(bf16[64,512]{1,0:T(8,128)(2,1)S(1)} %project_across.1.refs_1_), channel_id=1, source_target_pairs={{0,8},{4,12},{8,16},{12,20},{16,24},{20,28},{24,32},{28,36},{32,40... | collective-permute-start | bytes 196616 | tf_op jit(solution)/shard_map/ppermute | solution.py:23
  46.5 14.0 %collective-permute-start.11 = (bf16[64,512]{1,0:T(8,128)(2,1)S(1)}, bf16[64,512]{1,0:T(8,128)(2,1)S(1)}, u32[]{:S(2)}, u32[]{:S(2)}) collective-permute-start(bf16[64,512]{1,0:T(8,128)(2,1)S(1)} %project_across.1.refs_1_), channel_id=1, source_target_pairs={{0,12},{4,16},{8,20},{12,24},{16,28},{20,32},{24,36},{28,40},{32,4... | collective-permute-start | bytes 196616 | tf_op jit(solution)/shard_map/ppermute | solution.py:23
  51.1 9.4 %collective-permute-start.9 = (bf16[64,512]{1,0:T(8,128)(2,1)S(1)}, bf16[64,512]{1,0:T(8,128)(2,1)S(1)}, u32[]{:S(2)}, u32[]{:S(2)}) collective-permute-start(bf16[64,512]{1,0:T(8,128)(2,1)S(1)} %project_across.1.refs_1_), channel_id=1, source_target_pairs={{0,4},{4,8},{8,12},{12,16},{16,20},{20,24},{24,28},{28,32},{32,36}... | collective-permute-start | bytes 196616 | tf_op jit(solution)/shard_map/ppermute | solution.py:23
  (1 other events, 0.7 us)

commit v5 on v3

--- a/solution.py
+++ b/solution.py
@@ -14,13 +14,30 @@
 EPS = 1e-05
 SCORE_SCALE = HEAD_SIZE ** (-0.5) * math.log2(math.e)
 PROJECT_VMEM = 8 * 1024 * 1024
+FETCH_PASSES = 4
 ATTEND_VMEM = 20 * 1024 * 1024
 WHOLE = pl.BlockSpec(memory_space=pltpu.VMEM)
 
 
+def sent(value, axis, target):
+    length = lax.axis_size(axis)
+    return lax.ppermute(value, axis, [(i, target(i) % length) for i in range(length)])
+
+
 def turned(value, axis, by):
-    length = lax.axis_size(axis)
-    return lax.ppermute(value, axis, [(i, (i + by) % length) for i in range(length)])
+    return sent(value, axis, lambda i: i + by)
+
+
+def from_reach(block):
+    across = sent(block, "seq", lambda s: s + 2)
+    other = sent(block, "seq", lambda s: s + 1 + 2 * (s % 2))
+    swapped = sent(across, "seq", lambda s: s + 1 - 2 * (s % 2))
+    return [block, other, across, swapped]
+
+
+def from_distances(position, at):
+    near_far = jnp.where(position % 2 == 0, 3, 1)
+    return jnp.where(at == 1, near_far, jnp.where(at == 3, 4 - near_far, at))
 
 
 def project_rows(row_refs, key_ref, value_ref, gain_ref, out_ref):
@@ -126,9 +143,9 @@
         refs[1][...] = totals
 
 
-def attend_cost(rows, width, keys):
+def attend_cost(rows, width, keys, passes):
     return pl.CostEstimate(
-        flops=16 * rows * width * keys,
+        flops=4 * passes * rows * width * keys,
         transcendentals=rows * width // HEAD_SIZE * keys,
         bytes_accessed=2 * rows * width,
     )
@@ -153,7 +170,7 @@
         out_shape=out_shape,
         in_specs=[WHOLE] * len(operands),
         out_specs=[WHOLE] * len(out_shape),
-        cost_estimate=attend_cost(rows, width, REACH * blocks[0].shape[0]),
+        cost_estimate=attend_cost(rows, width, REACH * blocks[0].shape[0], FETCH_PASSES if first else 1),
         compiler_params=pltpu.CompilerParams(vmem_limit_bytes=ATTEND_VMEM),
         name=name,
     )(*operands)
@@ -168,7 +185,8 @@
 ):
     position = lax.axis_index("seq")
     images = lax.broadcasted_iota(jnp.int32, (1, block_mask.shape[1], REACH), 1)
-    wanted = position - lax.broadcasted_iota(jnp.int32, (1, block_mask.shape[1], REACH), 2)
+    at = lax.broadcasted_iota(jnp.int32, (1, block_mask.shape[1], REACH), 2)
+    wanted = position - from_distances(position, at)
     is_open = jnp.sum(jnp.where(images == wanted, block_mask[:, :, None], 0), axis=1)
     is_open = jnp.repeat(is_open.astype(jnp.float32), BLOCK, axis=0)
     query_gain = (query_norm_gain * SCORE_SCALE).reshape(1, HEAD_SIZE)
@@ -177,13 +195,10 @@
     def projected(row_parts, name):
         return project(row_parts, key_matrix, value_matrix, key_gain, "project_" + name)
 
-    def reached(block):
-        return [block] + [turned(block, "seq", by) for by in range(1, REACH)]
-
     left = turned(vision, "tp", 1)
     right = turned(vision, "tp", -1)
     own = projected([vision], "own")
-    own_blocks = reached(own)
+    own_blocks = from_reach(own)
     normed, *carried = attend(
         text_query_matrix, own_blocks, is_open, query_gain, None, False, "attend_own"
     )
@@ -193,13 +208,11 @@
     upper_across = turned(left[:half], "tp", 1)
     lower_across = turned(right[half:], "tp", -1)
     sides = projected([left, right], "sides")
-    side_blocks = reached(sides)
-    upper_across, lower_across = after((upper_across, lower_across), sides)
+    side_blocks = from_reach(sides)
+    carried = attend(normed, side_blocks, is_open, None, carried, False, "attend_sides")
+    upper_across, lower_across = after((upper_across, lower_across), carried)
     across = projected([upper_across, lower_across], "across")
-    across_blocks = reached(across)
-    side_blocks = after(side_blocks, across)
-    carried = attend(normed, side_blocks, is_open, None, carried, False, "attend_sides")
-    across_blocks = after(across_blocks, carried)
+    across_blocks = from_reach(across)
     (result,) = attend(normed, across_blocks, is_open, None, carried, True, "attend_across")
     return result
 

time: 59.3 us -> 64.2 us (1.083)
  starting transfers between devices: 22.1 us -> 25.7 us
  waiting for transfers between devices: 18.8 us -> 20.2 us
    ppermute x13, starting transfers between devices: 22.1 us -> 25.7 us  [sent(): lax.ppermute(value, axis, [(i, target(i) % length) for i in range(length)])]
    ppermute x13, waiting for transfers between devices: 18.8 us -> 20.2 us  [sent(): lax.ppermute(value, axis, [(i, target(i) % length) for i in range(length)])]
  transfers between devices with their start and end apart: 13 -> 13, of which waited for: 5 -> 7; matrix products, arithmetic and copies ran while one was open for 0% -> 0% of each run, Pallas kernels for 15% -> 11%
where the time goes in v5:
time: 64.2 us; the launch traced here: 64 us
  starting transfers between devices  25.7 us (40%)
  waiting for transfers between devices  20.2 us (31%)
  Pallas kernels  11.4 us (18%)
  local copies, waits for them, and re-layouts  6.36 us (10%)
    ppermute x13, starting transfers between devices, sent(): lax.ppermute(value, axis, [(i, target(i) % length) for i in range(length)])  25.7 us
    ppermute x13, waiting for transfers between devices, sent(): lax.ppermute(value, axis, [(i, target(i) % length) for i in range(length)])  20.2 us
    pallas_call x3, Pallas kernels, attend(): pl.pallas_call(functools.partial(attend_kernel, first, last, kv_heads), o...  6.73 us
    unnamed x20, local copies, waits for them, and re-layouts  6.28 us
    pallas_call x3, Pallas kernels, project(): pl.pallas_call(project_kernel, out_shape=jax.ShapeDtypeStruct((rows, 2 *...  4.63 us
  transfers between devices with their start and end apart: 13, of which 7 were waited for; matrix products, arithmetic and copies ran while one was open for 0% of the time, Pallas kernels for 11%

profile of v5, /device:TPU:1, one launch (start us, length us, event | category | flops | bytes accessed | tf_op | source)
XLA Modules:
  0.0 64.0 jit_solution(8133301478097181583)
XLA Ops:
  0.0 3.3 %collective-permute-start.4 = (bf16[64,8192]{1,0:T(8,128)(2,1)}, bf16[64,8192]{1,0:T(8,128)(2,1)S(1)}, u32[]{:S(2)}, u32[]{:S(2)}) collective-permute-start(bf16[64,8192]{1,0:T(8,128)(2,1)} %refs_0_.2), channel_id=1, source_target_pairs={{0,3},{1,0},{2,1},{3,2},{4,7},{5,4},{6,5},{7,6},{8,11},{9,8},{10,9... | collective-permute-start | bytes 3145736 | tf_op jit(solution)/shard_map/ppermute | solution.py:24
  3.3 2.2 %copy-done = bf16[8192,256]{1,0:T(8,128)(2,1)S(1)} copy-done((bf16[8192,256]{1,0:T(8,128)(2,1)S(1)}, bf16[8192,256]{1,0:T(8,128)(2,1)}, u32[]{:S(2)}) %copy-start) | copy-done | bytes 4194328
  5.5 2.2 %copy-done.2 = bf16[8192,256]{1,0:T(8,128)(2,1)S(1)} copy-done((bf16[8192,256]{1,0:T(8,128)(2,1)S(1)}, bf16[8192,256]{1,0:T(8,128)(2,1)}, u32[]{:S(2)}) %copy-start.2) | copy-done | bytes 4194328
  7.7 1.2 %copy-done.4 = bf16[64,8192]{1,0:T(8,128)(2,1)S(1)} copy-done((bf16[64,8192]{1,0:T(8,128)(2,1)S(1)}, bf16[64,8192]{1,0:T(8,128)(2,1)}, u32[]{:S(2)}) %copy-start.4) | copy-done | bytes 1048600
  9.6 1.6 %project_own.1.refs_1_ = bf16[64,512]{1,0:T(8,128)(2,1)S(1)} custom-call(bf16[64,8192]{1,0:T(8,128)(2,1)S(1)} %copy-done.4, bf16[8192,256]{1,0:T(8,128)(2,1)S(1)} %copy-done, bf16[8192,256]{1,0:T(8,128)(2,1)S(1)} %copy-done.2, f32[1,128]{1,0:T(1,128)S(1)} %bitcast.7), custom_call_target="tpu_custom_call" | custom-call | flops 536870912 | bytes 8388608 | tf_op jit(solution)/shard_map/project_own/pallas_call | solution.py:70
  11.2 1.4 %collective-permute-start.1 = (bf16[64,512]{1,0:T(8,128)(2,1)S(1)}, bf16[64,512]{1,0:T(8,128)(2,1)S(1)}, u32[]{:S(2)}, u32[]{:S(2)}) collective-permute-start(bf16[64,512]{1,0:T(8,128)(2,1)S(1)} %project_own.1.refs_1_), channel_id=1, source_target_pairs={{0,8},{4,12},{8,16},{12,20},{16,24},{20,28},{24,32},{28,36},{32,40... | collective-permute-start | bytes 196616 | tf_op jit(solution)/shard_map/ppermute | solution.py:24
  12.6 3.7 %collective-permute-start = (bf16[64,512]{1,0:T(8,128)(2,1)S(1)}, bf16[64,512]{1,0:T(8,128)(2,1)S(1)}, u32[]{:S(2)}, u32[]{:S(2)}) collective-permute-start(bf16[64,512]{1,0:T(8,128)(2,1)S(1)} %project_own.1.refs_1_), channel_id=1, source_target_pairs={{0,4},{4,16},{8,12},{12,24},{16,20},{20,32},{24,28},{28,40},{32,36... | collective-permute-start | bytes 196616 | tf_op jit(solution)/shard_map/ppermute | solution.py:24
  16.4 4.5 %collective-permute-done.1.refs_3_ = bf16[64,512]{1,0:T(8,128)(2,1)S(1)} collective-permute-done((bf16[64,512]{1,0:T(8,128)(2,1)S(1)}, bf16[64,512]{1,0:T(8,128)(2,1)S(1)}, u32[]{:S(2)}, u32[]{:S(2)}) %collective-permute-start.1) | collective-permute-done | bytes 65568 | tf_op jit(solution)/shard_map/ppermute | solution.py:24
  21.0 2.6 %collective-permute-start.2 = (bf16[64,512]{1,0:T(8,128)(2,1)S(1)}, bf16[64,512]{1,0:T(8,128)(2,1)S(1)}, u32[]{:S(2)}, u32[]{:S(2)}) collective-permute-start(bf16[64,512]{1,0:T(8,128)(2,1)S(1)} %collective-permute-done.1.refs_3_), channel_id=1, source_target_pairs={{0,4},{4,0},{8,12},{12,8},{16,20},{20,16},{24,28},{28,24},{32,36},... | collective-permute-start | bytes 196616 | tf_op jit(solution)/shard_map/ppermute | solution.py:24
  24.5 1.7 %attend_own.1 = (bf16[256,2048]{1,0:T(8,128)(2,1)S(1)}, f32[256,2048]{1,0:T(8,128)S(1)}, f32[256,128]{1,0:T(8,128)S(1)}) custom-call(bf16[256,2048]{1,0:T(8,128)(2,1)S(1)} %copy-done.7, bf16[64,512]{1,0:T(8,128)(2,1)S(1)} %project_own.1.refs_1_, bf16[64,512]{1,0:T(8,128)(2,1)S(1)} %collective-permute-done.refs_2_, ...), custom_call_target="tpu_custom_call" | custom-call | flops 2147483648 | bytes 1048576 | tf_op jit(solution)/shard_map/attend_own/pallas_call | solution.py:168
  26.3 2.2 %collective-permute-done.3.refs_0_ = bf16[64,8192]{1,0:T(8,128)(2,1)S(1)} collective-permute-done((bf16[64,8192]{1,0:T(8,128)(2,1)}, bf16[64,8192]{1,0:T(8,128)(2,1)S(1)}, u32[]{:S(2)}, u32[]{:S(2)}) %collective-permute-start.3) | collective-permute-done | bytes 1048608 | tf_op jit(solution)/shard_map/ppermute | solution.py:24
  28.6 2.7 %collective-permute-start.6 = (bf16[32,8192]{1,0:T(8,128)(2,1)S(1)}, bf16[32,8192]{1,0:T(8,128)(2,1)S(1)}, u32[]{:S(2)}, u32[]{:S(2)}) collective-permute-start(bf16[32,8192]{1,0:T(8,128)(2,1)S(1)} %slice.7), channel_id=1, source_target_pairs={{0,3},{1,0},{2,1},{3,2},{4,7},{5,4},{6,5},{7,6},{8,11},{9,8},{10,9... | collective-permute-start | bytes 1572872 | tf_op jit(solution)/shard_map/ppermute | solution.py:24
  31.3 1.3 %project_sides.1.refs_1_ = bf16[128,512]{1,0:T(8,128)(2,1)S(1)} custom-call(bf16[64,8192]{1,0:T(8,128)(2,1)S(1)} %collective-permute-done.3.refs_0_, bf16[64,8192]{1,0:T(8,128)(2,1)S(1)} %collective-permute-done.4.refs_1_, bf16[8192,256]{1,0:T(8,128)(2,1)S(1)} %copy-done.1, bf16[8192,256]{1,0:T(8,128)(2,1)S(1)} %copy-done.3, f32[1,128]{1,0:T(1,128)S(1)} %bitcast.8), custom_call_target="tpu_custom_call" | custom-call | flops 1073741824 | bytes 8388608 | tf_op jit(solution)/shard_map/project_sides/pallas_call | solution.py:70
  32.6 1.4 %collective-permute-start.8 = (bf16[128,512]{1,0:T(8,128)(2,1)S(1)}, bf16[128,512]{1,0:T(8,128)(2,1)S(1)}, u32[]{:S(2)}, u32[]{:S(2)}) collective-permute-start(bf16[128,512]{1,0:T(8,128)(2,1)S(1)} %project_sides.1.refs_1_), channel_id=1, source_target_pairs={{0,8},{4,12},{8,16},{12,20},{16,24},{20,28},{24,32},{28,36},{32,40... | collective-permute-start | bytes 393224 | tf_op jit(solution)/shard_map/ppermute | solution.py:24
  34.0 5.2 %collective-permute-start.7 = (bf16[128,512]{1,0:T(8,128)(2,1)S(1)}, bf16[128,512]{1,0:T(8,128)(2,1)S(1)}, u32[]{:S(2)}, u32[]{:S(2)}) collective-permute-start(bf16[128,512]{1,0:T(8,128)(2,1)S(1)} %project_sides.1.refs_1_), channel_id=1, source_target_pairs={{0,4},{4,16},{8,12},{12,24},{16,20},{20,32},{24,28},{28,40},{32,36... | collective-permute-start | bytes 393224 | tf_op jit(solution)/shard_map/ppermute | solution.py:24
  39.2 4.2 %collective-permute-done.8.refs_3_ = bf16[128,512]{1,0:T(8,128)(2,1)S(1)} collective-permute-done((bf16[128,512]{1,0:T(8,128)(2,1)S(1)}, bf16[128,512]{1,0:T(8,128)(2,1)S(1)}, u32[]{:S(2)}, u32[]{:S(2)}) %collective-permute-start.8) | collective-permute-done | bytes 131104 | tf_op jit(solution)/shard_map/ppermute | solution.py:24
  43.4 3.5 %collective-permute-start.9 = (bf16[128,512]{1,0:T(8,128)(2,1)S(1)}, bf16[128,512]{1,0:T(8,128)(2,1)S(1)}, u32[]{:S(2)}, u32[]{:S(2)}) collective-permute-start(bf16[128,512]{1,0:T(8,128)(2,1)S(1)} %collective-permute-done.8.refs_3_), channel_id=1, source_target_pairs={{0,4},{4,0},{8,12},{12,8},{16,20},{20,16},{24,28},{28,24},{32,36},... | collective-permute-start | bytes 393224 | tf_op jit(solution)/shard_map/ppermute | solution.py:24
  46.8 1.0 %collective-permute-done.9.refs_4_ = bf16[128,512]{1,0:T(8,128)(2,1)S(1)} collective-permute-done((bf16[128,512]{1,0:T(8,128)(2,1)S(1)}, bf16[128,512]{1,0:T(8,128)(2,1)S(1)}, u32[]{:S(2)}, u32[]{:S(2)}) %collective-permute-start.9) | collective-permute-done | bytes 131104 | tf_op jit(solution)/shard_map/ppermute | solution.py:24
  47.8 2.6 %attend_sides.1 = (f32[256,2048]{1,0:T(8,128)S(1)}, f32[256,128]{1,0:T(8,128)S(1)}) custom-call(bf16[256,2048]{1,0:T(8,128)(2,1)S(1)} %get-tuple-element.14.refs_0_, bf16[128,512]{1,0:T(8,128)(2,1)S(1)} %project_sides.1.refs_1_, bf16[128,512]{1,0:T(8,128)(2,1)S(1)} %collective-permute-done.7.refs_2_, bf16[128,512]{1,0:T(8,128)(2,1)S(1)} %collective-permute-done.8.refs_3_, ...), custom_call_target="tpu_custom_call" | custom-call | flops 1073741824 | bytes 1048576 | tf_op jit(solution)/shard_map/attend_sides/pallas_call | solution.py:168
  50.5 1.6 %project_across.1.refs_1_ = bf16[64,512]{1,0:T(8,128)(2,1)S(1)} custom-call(bf16[32,8192]{1,0:T(8,128)(2,1)S(1)} %collective-permute-done.5.refs_0_, bf16[32,8192]{1,0:T(8,128)(2,1)S(1)} %collective-permute-done.6.refs_1_, bf16[8192,256]{1,0:T(8,128)(2,1)S(1)} %copy-done.1, bf16[8192,256]{1,0:T(8,128)(2,1)S(1)} %copy-done.3, f32[1,128]{1,0:T(1,128)S(1)} %bitcast.9), custom_call_target="tpu_custom_call" | custom-call | flops 536870912 | bytes 8388608 | tf_op jit(solution)/shard_map/project_across/pallas_call | solution.py:70
  52.3 6.6 %collective-permute-done.11.refs_3_ = bf16[64,512]{1,0:T(8,128)(2,1)S(1)} collective-permute-done((bf16[64,512]{1,0:T(8,128)(2,1)S(1)}, bf16[64,512]{1,0:T(8,128)(2,1)S(1)}, u32[]{:S(2)}, u32[]{:S(2)}) %collective-permute-start.11) | collective-permute-done | bytes 65568 | tf_op jit(solution)/shard_map/ppermute | solution.py:24
  58.9 1.8 %collective-permute-start.12 = (bf16[64,512]{1,0:T(8,128)(2,1)S(1)}, bf16[64,512]{1,0:T(8,128)(2,1)S(1)}, u32[]{:S(2)}, u32[]{:S(2)}) collective-permute-start(bf16[64,512]{1,0:T(8,128)(2,1)S(1)} %collective-permute-done.11.refs_3_), channel_id=1, source_target_pairs={{0,4},{4,0},{8,12},{12,8},{16,20},{20,16},{24,28},{28,24},{32,36},... | collective-permute-start | bytes 196616 | tf_op jit(solution)/shard_map/ppermute | solution.py:24
  60.7 0.9 %collective-permute-done.12.refs_4_ = bf16[64,512]{1,0:T(8,128)(2,1)S(1)} collective-permute-done((bf16[64,512]{1,0:T(8,128)(2,1)S(1)}, bf16[64,512]{1,0:T(8,128)(2,1)S(1)}, u32[]{:S(2)}, u32[]{:S(2)}) %collective-permute-start.12) | collective-permute-done | bytes 65568 | tf_op jit(solution)/shard_map/ppermute | solution.py:24
  61.6 2.4 %attend_across.1 = bf16[256,2048]{1,0:T(8,128)(2,1)} custom-call(bf16[256,2048]{1,0:T(8,128)(2,1)S(1)} %get-tuple-element.14.refs_0_, bf16[64,512]{1,0:T(8,128)(2,1)S(1)} %project_across.1.refs_1_, bf16[64,512]{1,0:T(8,128)(2,1)S(1)} %collective-permute-done.10.refs_2_, bf16[64,512]{1,0:T(8,128)(2,1)S(1)} %collective-permute-done.11.refs_3_, ...), custom_call_target="tpu_custom_call" | custom-call | flops 536870912 | bytes 1048576 | tf_op jit(solution)/shard_map/attend_across/pallas_call | solution.py:168
  (36 shorter events, 2.0 us)
Async XLA Ops:
  0.0 26.2 %collective-permute-start.4 = (bf16[64,8192]{1,0:T(8,128)(2,1)}, bf16[64,8192]{1,0:T(8,128)(2,1)S(1)}, u32[]{:S(2)}, u32[]{:S(2)}) collective-permute-start(bf16[64,8192]{1,0:T(8,128)(2,1)} %refs_0_.2), channel_id=1, source_target_pairs={{0,3},{1,0},{2,1},{3,2},{4,7},{5,4},{6,5},{7,6},{8,11},{9,8},{10,9... | collective-permute-start | bytes 3145736 | tf_op jit(solution)/shard_map/ppermute | solution.py:24
  3.3 25.1 %collective-permute-start.3 = (bf16[64,8192]{1,0:T(8,128)(2,1)}, bf16[64,8192]{1,0:T(8,128)(2,1)S(1)}, u32[]{:S(2)}, u32[]{:S(2)}) collective-permute-start(bf16[64,8192]{1,0:T(8,128)(2,1)} %refs_0_.2), channel_id=1, source_target_pairs={{0,1},{1,2},{2,3},{3,0},{4,5},{5,6},{6,7},{7,4},{8,9},{9,10},{10,1... | collective-permute-start | bytes 3145736 | tf_op jit(solution)/shard_map/ppermute | solution.py:24
  3.3 2.2 %copy-start = (bf16[8192,256]{1,0:T(8,128)(2,1)S(1)}, bf16[8192,256]{1,0:T(8,128)(2,1)}, u32[]{:S(2)}) copy-start(bf16[8192,256]{1,0:T(8,128)(2,1)} %refs_2_.5) | copy-start | bytes 12582916
  5.5 2.2 %copy-start.2 = (bf16[8192,256]{1,0:T(8,128)(2,1)S(1)}, bf16[8192,256]{1,0:T(8,128)(2,1)}, u32[]{:S(2)}) copy-start(bf16[8192,256]{1,0:T(8,128)(2,1)} %refs_3_.3) | copy-start | bytes 12582916
  7.7 1.2 %copy-start.4 = (bf16[64,8192]{1,0:T(8,128)(2,1)S(1)}, bf16[64,8192]{1,0:T(8,128)(2,1)}, u32[]{:S(2)}) copy-start(bf16[64,8192]{1,0:T(8,128)(2,1)} %refs_0_.2) | copy-start | bytes 3145732
  8.9 0.7 %copy-start.5 = (f32[128]{0:T(128)S(1)}, f32[128]{0:T(128)}, u32[]{:S(2)}) copy-start(f32[128]{0:T(128)} %param.12) | copy-start | bytes 1540
  9.6 6.9 %copy-start.9 = (f32[128]{0:T(128)S(1)}, f32[128]{0:T(128)}, u32[]{:S(2)}) copy-start(f32[128]{0:T(128)} %param.11) | copy-start | bytes 1540
  9.6 14.0 %copy-start.8 = (s32[4,64]{1,0:T(4,128)S(1)}, s32[4,64]{1,0:T(4,128)}, u32[]{:S(2)}) copy-start(s32[4,64]{1,0:T(4,128)} %param.13) | copy-start | bytes 3076
  9.6 14.9 %copy-start.7 = (bf16[256,2048]{1,0:T(8,128)(2,1)S(1)}, bf16[256,2048]{1,0:T(8,128)(2,1)}, u32[]{:S(2)}) copy-start(bf16[256,2048]{1,0:T(8,128)(2,1)} %refs_0_.3) | copy-start | bytes 3145732
  11.2 9.8 %collective-permute-start.1 = (bf16[64,512]{1,0:T(8,128)(2,1)S(1)}, bf16[64,512]{1,0:T(8,128)(2,1)S(1)}, u32[]{:S(2)}, u32[]{:S(2)}) collective-permute-start(bf16[64,512]{1,0:T(8,128)(2,1)S(1)} %project_own.1.refs_1_), channel_id=1, source_target_pairs={{0,8},{4,12},{8,16},{12,20},{16,24},{20,28},{24,32},{28,36},{32,40... | collective-permute-start | bytes 196616 | tf_op jit(solution)/shard_map/ppermute | solution.py:24
  12.6 11.1 %collective-permute-start = (bf16[64,512]{1,0:T(8,128)(2,1)S(1)}, bf16[64,512]{1,0:T(8,128)(2,1)S(1)}, u32[]{:S(2)}, u32[]{:S(2)}) collective-permute-start(bf16[64,512]{1,0:T(8,128)(2,1)S(1)} %project_own.1.refs_1_), channel_id=1, source_target_pairs={{0,4},{4,16},{8,12},{12,24},{16,20},{20,32},{24,28},{28,40},{32,36... | collective-permute-start | bytes 196616 | tf_op jit(solution)/shard_map/ppermute | solution.py:24
  21.0 3.5 %collective-permute-start.2 = (bf16[64,512]{1,0:T(8,128)(2,1)S(1)}, bf16[64,512]{1,0:T(8,128)(2,1)S(1)}, u32[]{:S(2)}, u32[]{:S(2)}) collective-permute-start(bf16[64,512]{1,0:T(8,128)(2,1)S(1)} %collective-permute-done.1.refs_3_), channel_id=1, source_target_pairs={{0,4},{4,0},{8,12},{12,8},{16,20},{20,16},{24,28},{28,24},{32,36},... | collective-permute-start | bytes 196616 | tf_op jit(solution)/shard_map/ppermute | solution.py:24
  24.5 6.8 %copy-start.1 = (bf16[8192,256]{1,0:T(8,128)(2,1)S(1)}, bf16[8192,256]{1,0:T(8,128)(2,1)}, u32[]{:S(2)}) copy-start(bf16[8192,256]{1,0:T(8,128)(2,1)} %refs_2_.5) | copy-start | bytes 12582916
  24.5 6.8 %copy-start.3 = (bf16[8192,256]{1,0:T(8,128)(2,1)S(1)}, bf16[8192,256]{1,0:T(8,128)(2,1)}, u32[]{:S(2)}) copy-start(bf16[8192,256]{1,0:T(8,128)(2,1)} %refs_3_.3) | copy-start | bytes 12582916
  24.5 6.8 %copy-start.6 = (f32[128]{0:T(128)S(1)}, f32[128]{0:T(128)}, u32[]{:S(2)}) copy-start(f32[128]{0:T(128)} %param.12) | copy-start | bytes 1540
  28.5 21.9 %collective-permute-start.5 = (bf16[32,8192]{1,0:T(8,128)(2,1)S(1)}, bf16[32,8192]{1,0:T(8,128)(2,1)S(1)}, u32[]{:S(2)}, u32[]{:S(2)}) collective-permute-start(bf16[32,8192]{1,0:T(8,128)(2,1)S(1)} %slice.6), channel_id=1, source_target_pairs={{0,1},{1,2},{2,3},{3,0},{4,5},{5,6},{6,7},{7,4},{8,9},{9,10},{10,1... | collective-permute-start | bytes 1572872 | tf_op jit(solution)/shard_map/ppermute | solution.py:24
  28.6 21.8 %collective-permute-start.6 = (bf16[32,8192]{1,0:T(8,128)(2,1)S(1)}, bf16[32,8192]{1,0:T(8,128)(2,1)S(1)}, u32[]{:S(2)}, u32[]{:S(2)}) collective-permute-start(bf16[32,8192]{1,0:T(8,128)(2,1)S(1)} %slice.7), channel_id=1, source_target_pairs={{0,3},{1,0},{2,1},{3,2},{4,7},{5,4},{6,5},{7,6},{8,11},{9,8},{10,9... | collective-permute-start | bytes 1572872 | tf_op jit(solution)/shard_map/ppermute | solution.py:24
  32.6 10.8 %collective-permute-start.8 = (bf16[128,512]{1,0:T(8,128)(2,1)S(1)}, bf16[128,512]{1,0:T(8,128)(2,1)S(1)}, u32[]{:S(2)}, u32[]{:S(2)}) collective-permute-start(bf16[128,512]{1,0:T(8,128)(2,1)S(1)} %project_sides.1.refs_1_), channel_id=1, source_target_pairs={{0,8},{4,12},{8,16},{12,20},{16,24},{20,28},{24,32},{28,36},{32,40... | collective-permute-start | bytes 393224 | tf_op jit(solution)/shard_map/ppermute | solution.py:24
  34.0 12.8 %collective-permute-start.7 = (bf16[128,512]{1,0:T(8,128)(2,1)S(1)}, bf16[128,512]{1,0:T(8,128)(2,1)S(1)}, u32[]{:S(2)}, u32[]{:S(2)}) collective-permute-start(bf16[128,512]{1,0:T(8,128)(2,1)S(1)} %project_sides.1.refs_1_), channel_id=1, source_target_pairs={{0,4},{4,16},{8,12},{12,24},{16,20},{20,32},{24,28},{28,40},{32,36... | collective-permute-start | bytes 393224 | tf_op jit(solution)/shard_map/ppermute | solution.py:24
  43.4 4.4 %collective-permute-start.9 = (bf16[128,512]{1,0:T(8,128)(2,1)S(1)}, bf16[128,512]{1,0:T(8,128)(2,1)S(1)}, u32[]{:S(2)}, u32[]{:S(2)}) collective-permute-start(bf16[128,512]{1,0:T(8,128)(2,1)S(1)} %collective-permute-done.8.refs_3_), channel_id=1, source_target_pairs={{0,4},{4,0},{8,12},{12,8},{16,20},{20,16},{24,28},{28,24},{32,36},... | collective-permute-start | bytes 393224 | tf_op jit(solution)/shard_map/ppermute | solution.py:24
  52.1 6.8 %collective-permute-start.11 = (bf16[64,512]{1,0:T(8,128)(2,1)S(1)}, bf16[64,512]{1,0:T(8,128)(2,1)S(1)}, u32[]{:S(2)}, u32[]{:S(2)}) collective-permute-start(bf16[64,512]{1,0:T(8,128)(2,1)S(1)} %project_across.1.refs_1_), channel_id=1, source_target_pairs={{0,8},{4,12},{8,16},{12,20},{16,24},{20,28},{24,32},{28,36},{32,40... | collective-permute-start | bytes 196616 | tf_op jit(solution)/shard_map/ppermute | solution.py:24
  52.2 8.5 %collective-permute-start.10 = (bf16[64,512]{1,0:T(8,128)(2,1)S(1)}, bf16[64,512]{1,0:T(8,128)(2,1)S(1)}, u32[]{:S(2)}, u32[]{:S(2)}) collective-permute-start(bf16[64,512]{1,0:T(8,128)(2,1)S(1)} %project_across.1.refs_1_), channel_id=1, source_target_pairs={{0,4},{4,16},{8,12},{12,24},{16,20},{20,32},{24,28},{28,40},{32,36... | collective-permute-start | bytes 196616 | tf_op jit(solution)/shard_map/ppermute | solution.py:24
  58.9 2.7 %collective-permute-start.12 = (bf16[64,512]{1,0:T(8,128)(2,1)S(1)}, bf16[64,512]{1,0:T(8,128)(2,1)S(1)}, u32[]{:S(2)}, u32[]{:S(2)}) collective-permute-start(bf16[64,512]{1,0:T(8,128)(2,1)S(1)} %collective-permute-done.11.refs_3_), channel_id=1, source_target_pairs={{0,4},{4,0},{8,12},{12,8},{16,20},{20,16},{24,28},{28,24},{32,36},... | collective-permute-start | bytes 196616 | tf_op jit(solution)/shard_map/ppermute | solution.py:24

commit v6 on v5

--- a/solution.py
+++ b/solution.py
@@ -19,19 +19,21 @@
 WHOLE = pl.BlockSpec(memory_space=pltpu.VMEM)
 
 
-def sent(value, axis, target):
+def turned(value, axis, by):
     length = lax.axis_size(axis)
-    return lax.ppermute(value, axis, [(i, target(i) % length) for i in range(length)])
-
-
-def turned(value, axis, by):
-    return sent(value, axis, lambda i: i + by)
-
-
-def from_reach(block):
-    across = sent(block, "seq", lambda s: s + 2)
-    other = sent(block, "seq", lambda s: s + 1 + 2 * (s % 2))
-    swapped = sent(across, "seq", lambda s: s + 1 - 2 * (s % 2))
+    return lax.ppermute(value, axis, [(i, (i + by) % length) for i in range(length)])
+
+
+def moved(value, axis, target):
+    length = lax.axis_size(axis)
+    pairs = [(i, target(i)) for i in range(length) if target(i) < length]
+    return lax.ppermute(value, axis, pairs)
+
+
+def from_reach(block, between=lambda across: across):
+    across = moved(block, "seq", lambda s: s + 2)
+    other = moved(block, "seq", lambda s: s + 1 + 2 * (s % 2))
+    swapped = moved(between(across), "seq", lambda s: s + 1 - 2 * (s % 2))
     return [block, other, across, swapped]
 
 
@@ -209,10 +211,11 @@
     lower_across = turned(right[half:], "tp", -1)
     sides = projected([left, right], "sides")
     side_blocks = from_reach(sides)
+    upper_across, lower_across = after((upper_across, lower_across), sides)
+    across = projected([upper_across, lower_across], "across")
+    side_blocks = after(side_blocks, across)
     carried = attend(normed, side_blocks, is_open, None, carried, False, "attend_sides")
-    upper_across, lower_across = after((upper_across, lower_across), carried)
-    across = projected([upper_across, lower_across], "across")
-    across_blocks = from_reach(across)
+    across_blocks = from_reach(across, lambda block: after(block, carried))
     (result,) = attend(normed, across_blocks, is_open, None, carried, True, "attend_across")
     return result
 

time: 64.2 us -> 61.7 us (0.961)
  the two profiles are of different devices: /device:TPU:1 before, /device:TPU:105 now
where the time goes in v6:
time: 61.7 us; the launch traced here: 61.3 us
  starting transfers between devices  36.1 us (59%)
  Pallas kernels  11.5 us (19%)
  waiting for transfers between devices  6.8 us (11%)
  local copies, waits for them, and re-layouts  6.36 us (10%)
    ppermute x9, starting transfers between devices, moved(): return lax.ppermute(value, axis, pairs)  30.9 us
    pallas_call x3, Pallas kernels, attend(): pl.pallas_call(functools.partial(attend_kernel, first, last, kv_heads), o...  6.82 us
    unnamed x20, local copies, waits for them, and re-layouts  6.28 us
    ppermute x4, starting transfers between devices, turned(): lax.ppermute(value, axis, [(i, (i + by) % length) for i in range(length)])  5.23 us
    pallas_call x3, Pallas kernels, project(): pl.pallas_call(project_kernel, out_shape=jax.ShapeDtypeStruct((rows, 2 *...  4.69 us
    ppermute x4, waiting for transfers between devices, turned(): lax.ppermute(value, axis, [(i, (i + by) % length) for i in range(length)])  4.47 us
    ppermute x9, waiting for transfers between devices, moved(): return lax.ppermute(value, axis, pairs)  2.32 us
  transfers between devices with their start and end apart: 13, of which 5 were waited for; matrix products, arithmetic and copies ran while one was open for 0% of the time, Pallas kernels for 15%

profile of v6, /device:TPU:105, one launch (start us, length us, event | category | flops | bytes accessed | tf_op | source)
XLA Modules:
  0.0 61.3 jit_solution(11765359446956615049)
XLA Ops:
  0.0 2.5 %collective-permute-start.4 = (bf16[64,8192]{1,0:T(8,128)(2,1)}, bf16[64,8192]{1,0:T(8,128)(2,1)S(1)}, u32[]{:S(2)}, u32[]{:S(2)}) collective-permute-start(bf16[64,8192]{1,0:T(8,128)(2,1)} %refs_0_.2), channel_id=1, source_target_pairs={{0,3},{1,0},{2,1},{3,2},{4,7},{5,4},{6,5},{7,6},{8,11},{9,8},{10,9... | collective-permute-start | bytes 3145736 | tf_op jit(solution)/shard_map/ppermute | solution.py:24
  2.5 2.2 %copy-done = bf16[8192,256]{1,0:T(8,128)(2,1)S(1)} copy-done((bf16[8192,256]{1,0:T(8,128)(2,1)S(1)}, bf16[8192,256]{1,0:T(8,128)(2,1)}, u32[]{:S(2)}) %copy-start) | copy-done | bytes 4194328
  4.7 2.2 %copy-done.2 = bf16[8192,256]{1,0:T(8,128)(2,1)S(1)} copy-done((bf16[8192,256]{1,0:T(8,128)(2,1)S(1)}, bf16[8192,256]{1,0:T(8,128)(2,1)}, u32[]{:S(2)}) %copy-start.2) | copy-done | bytes 4194328
  6.9 1.2 %copy-done.4 = bf16[64,8192]{1,0:T(8,128)(2,1)S(1)} copy-done((bf16[64,8192]{1,0:T(8,128)(2,1)S(1)}, bf16[64,8192]{1,0:T(8,128)(2,1)}, u32[]{:S(2)}) %copy-start.4) | copy-done | bytes 1048600
  8.1 0.7 %copy-done.5 = f32[128]{0:T(128)S(1)} copy-done((f32[128]{0:T(128)S(1)}, f32[128]{0:T(128)}, u32[]{:S(2)}) %copy-start.5) | copy-done | bytes 536
  8.7 1.6 %project_own.1.refs_1_ = bf16[64,512]{1,0:T(8,128)(2,1)S(1)} custom-call(bf16[64,8192]{1,0:T(8,128)(2,1)S(1)} %copy-done.4, bf16[8192,256]{1,0:T(8,128)(2,1)S(1)} %copy-done, bf16[8192,256]{1,0:T(8,128)(2,1)S(1)} %copy-done.2, f32[1,128]{1,0:T(1,128)S(1)} %bitcast.7), custom_call_target="tpu_custom_call" | custom-call | flops 536870912 | bytes 8388608 | tf_op jit(solution)/shard_map/project_own/pallas_call | solution.py:72
  10.4 3.2 %collective-permute-start.1 = (bf16[64,512]{1,0:T(8,128)(2,1)S(1)}, bf16[64,512]{1,0:T(8,128)(2,1)S(1)}, u32[]{:S(2)}, u32[]{:S(2)}) collective-permute-start(bf16[64,512]{1,0:T(8,128)(2,1)S(1)} %project_own.1.refs_1_), channel_id=1, source_target_pairs={{0,8},{4,12},{8,16},{12,20},{16,24},{20,28},{24,32},{28,36},{32,40... | collective-permute-start | bytes 196616 | tf_op jit(solution)/shard_map/ppermute | solution.py:30
  13.6 6.3 %collective-permute-start = (bf16[64,512]{1,0:T(8,128)(2,1)S(1)}, bf16[64,512]{1,0:T(8,128)(2,1)S(1)}, u32[]{:S(2)}, u32[]{:S(2)}) collective-permute-start(bf16[64,512]{1,0:T(8,128)(2,1)S(1)} %project_own.1.refs_1_), channel_id=1, source_target_pairs={{0,4},{4,16},{8,12},{12,24},{16,20},{20,32},{24,28},{28,40},{32,36... | collective-permute-start | bytes 196616 | tf_op jit(solution)/shard_map/ppermute | solution.py:30
  20.1 0.1 select_reduce_fusion
  20.3 0.9 %collective-permute-done.refs_2_ = bf16[64,512]{1,0:T(8,128)(2,1)S(1)} collective-permute-done((bf16[64,512]{1,0:T(8,128)(2,1)S(1)}, bf16[64,512]{1,0:T(8,128)(2,1)S(1)}, u32[]{:S(2)}, u32[]{:S(2)}) %collective-permute-start) | collective-permute-done | bytes 65568 | tf_op jit(solution)/shard_map/ppermute | solution.py:30
  21.2 0.2 collective-permute-done.2.refs_4_
  21.4 1.7 %attend_own.1 = (bf16[256,2048]{1,0:T(8,128)(2,1)S(1)}, f32[256,2048]{1,0:T(8,128)S(1)}, f32[256,128]{1,0:T(8,128)S(1)}) custom-call(bf16[256,2048]{1,0:T(8,128)(2,1)S(1)} %copy-done.7, bf16[64,512]{1,0:T(8,128)(2,1)S(1)} %project_own.1.refs_1_, bf16[64,512]{1,0:T(8,128)(2,1)S(1)} %collective-permute-done.refs_2_, ...), custom_call_target="tpu_custom_call" | custom-call | flops 2147483648 | bytes 1048576 | tf_op jit(solution)/shard_map/attend_own/pallas_call | solution.py:170
  23.1 1.5 %collective-permute-done.4.refs_1_ = bf16[64,8192]{1,0:T(8,128)(2,1)S(1)} collective-permute-done((bf16[64,8192]{1,0:T(8,128)(2,1)}, bf16[64,8192]{1,0:T(8,128)(2,1)S(1)}, u32[]{:S(2)}, u32[]{:S(2)}) %collective-permute-start.4) | collective-permute-done | bytes 1048608 | tf_op jit(solution)/shard_map/ppermute | solution.py:24
  24.6 3.0 %collective-permute-done.3.refs_0_ = bf16[64,8192]{1,0:T(8,128)(2,1)S(1)} collective-permute-done((bf16[64,8192]{1,0:T(8,128)(2,1)}, bf16[64,8192]{1,0:T(8,128)(2,1)S(1)}, u32[]{:S(2)}, u32[]{:S(2)}) %collective-permute-start.3) | collective-permute-done | bytes 1048608 | tf_op jit(solution)/shard_map/ppermute | solution.py:24
  27.8 2.7 %collective-permute-start.6 = (bf16[32,8192]{1,0:T(8,128)(2,1)S(1)}, bf16[32,8192]{1,0:T(8,128)(2,1)S(1)}, u32[]{:S(2)}, u32[]{:S(2)}) collective-permute-start(bf16[32,8192]{1,0:T(8,128)(2,1)S(1)} %slice.7), channel_id=1, source_target_pairs={{0,3},{1,0},{2,1},{3,2},{4,7},{5,4},{6,5},{7,6},{8,11},{9,8},{10,9... | collective-permute-start | bytes 1572872 | tf_op jit(solution)/shard_map/ppermute | solution.py:24
  30.5 1.4 %project_sides.1.refs_1_ = bf16[128,512]{1,0:T(8,128)(2,1)S(1)} custom-call(bf16[64,8192]{1,0:T(8,128)(2,1)S(1)} %collective-permute-done.3.refs_0_, bf16[64,8192]{1,0:T(8,128)(2,1)S(1)} %collective-permute-done.4.refs_1_, bf16[8192,256]{1,0:T(8,128)(2,1)S(1)} %copy-done.1, bf16[8192,256]{1,0:T(8,128)(2,1)S(1)} %copy-done.3, f32[1,128]{1,0:T(1,128)S(1)} %bitcast.8), custom_call_target="tpu_custom_call" | custom-call | flops 1073741824 | bytes 8388608 | tf_op jit(solution)/shard_map/project_sides/pallas_call | solution.py:72
  31.9 3.2 %collective-permute-start.10 = (bf16[128,512]{1,0:T(8,128)(2,1)S(1)}, bf16[128,512]{1,0:T(8,128)(2,1)S(1)}, u32[]{:S(2)}, u32[]{:S(2)}) collective-permute-start(bf16[128,512]{1,0:T(8,128)(2,1)S(1)} %project_sides.1.refs_1_), channel_id=1, source_target_pairs={{0,8},{4,12},{8,16},{12,20},{16,24},{20,28},{24,32},{28,36},{32,40... | collective-permute-start | bytes 393224 | tf_op jit(solution)/shard_map/ppermute | solution.py:30
  35.1 7.7 %collective-permute-start.9 = (bf16[128,512]{1,0:T(8,128)(2,1)S(1)}, bf16[128,512]{1,0:T(8,128)(2,1)S(1)}, u32[]{:S(2)}, u32[]{:S(2)}) collective-permute-start(bf16[128,512]{1,0:T(8,128)(2,1)S(1)} %project_sides.1.refs_1_), channel_id=1, source_target_pairs={{0,4},{4,16},{8,12},{12,24},{16,20},{20,32},{24,28},{28,40},{32,36... | collective-permute-start | bytes 393224 | tf_op jit(solution)/shard_map/ppermute | solution.py:30
  42.9 1.6 %project_across.1.refs_1_ = bf16[64,512]{1,0:T(8,128)(2,1)S(1)} custom-call(bf16[32,8192]{1,0:T(8,128)(2,1)S(1)} %collective-permute-done.5.refs_0_, bf16[32,8192]{1,0:T(8,128)(2,1)S(1)} %collective-permute-done.6.refs_1_, bf16[8192,256]{1,0:T(8,128)(2,1)S(1)} %copy-done.1, bf16[8192,256]{1,0:T(8,128)(2,1)S(1)} %copy-done.3, f32[1,128]{1,0:T(1,128)S(1)} %bitcast.9), custom_call_target="tpu_custom_call" | custom-call | flops 536870912 | bytes 8388608 | tf_op jit(solution)/shard_map/project_across/pallas_call | solution.py:72
  44.6 2.6 %collective-permute-start.8 = (bf16[64,512]{1,0:T(8,128)(2,1)S(1)}, bf16[64,512]{1,0:T(8,128)(2,1)S(1)}, u32[]{:S(2)}, u32[]{:S(2)}) collective-permute-start(bf16[64,512]{1,0:T(8,128)(2,1)S(1)} %project_across.1.refs_1_), channel_id=1, source_target_pairs={{0,8},{4,12},{8,16},{12,20},{16,24},{20,28},{24,32},{28,36},{32,40... | collective-permute-start | bytes 196616 | tf_op jit(solution)/shard_map/ppermute | solution.py:30
  47.2 7.6 %collective-permute-start.7 = (bf16[64,512]{1,0:T(8,128)(2,1)S(1)}, bf16[64,512]{1,0:T(8,128)(2,1)S(1)}, u32[]{:S(2)}, u32[]{:S(2)}) collective-permute-start(bf16[64,512]{1,0:T(8,128)(2,1)S(1)} %project_across.1.refs_1_), channel_id=1, source_target_pairs={{0,4},{4,16},{8,12},{12,24},{16,20},{20,32},{24,28},{28,40},{32,36... | collective-permute-start | bytes 196616 | tf_op jit(solution)/shard_map/ppermute | solution.py:30
  54.9 2.6 %attend_sides.1 = (f32[256,2048]{1,0:T(8,128)S(1)}, f32[256,128]{1,0:T(8,128)S(1)}) custom-call(bf16[256,2048]{1,0:T(8,128)(2,1)S(1)} %get-tuple-element.19.refs_0_, bf16[128,512]{1,0:T(8,128)(2,1)S(1)} %project_sides.1.refs_1_, bf16[128,512]{1,0:T(8,128)(2,1)S(1)} %collective-permute-done.9.refs_2_, bf16[128,512]{1,0:T(8,128)(2,1)S(1)} %collective-permute-done.10.refs_3_, ...), custom_call_target="tpu_custom_call" | custom-call | flops 1073741824 | bytes 1048576 | tf_op jit(solution)/shard_map/attend_sides/pallas_call | solution.py:170
  57.6 1.2 %collective-permute-done.12.refs_4_ = bf16[64,512]{1,0:T(8,128)(2,1)S(1)} collective-permute-done((bf16[64,512]{1,0:T(8,128)(2,1)S(1)}, bf16[64,512]{1,0:T(8,128)(2,1)S(1)}, u32[]{:S(2)}, u32[]{:S(2)}) %collective-permute-start.12) | collective-permute-done | bytes 65568 | tf_op jit(solution)/shard_map/ppermute | solution.py:30
  58.9 2.5 %attend_across.1 = bf16[256,2048]{1,0:T(8,128)(2,1)} custom-call(bf16[256,2048]{1,0:T(8,128)(2,1)S(1)} %get-tuple-element.19.refs_0_, bf16[64,512]{1,0:T(8,128)(2,1)S(1)} %project_across.1.refs_1_, bf16[64,512]{1,0:T(8,128)(2,1)S(1)} %collective-permute-done.7.refs_2_, bf16[64,512]{1,0:T(8,128)(2,1)S(1)} %collective-permute-done.8.refs_3_, ...), custom_call_target="tpu_custom_call" | custom-call | flops 536870912 | bytes 1048576 | tf_op jit(solution)/shard_map/attend_across/pallas_call | solution.py:170
  (36 shorter events, 0.6 us)
Async XLA Ops:
  0.0 24.6 %collective-permute-start.4 = (bf16[64,8192]{1,0:T(8,128)(2,1)}, bf16[64,8192]{1,0:T(8,128)(2,1)S(1)}, u32[]{:S(2)}, u32[]{:S(2)}) collective-permute-start(bf16[64,8192]{1,0:T(8,128)(2,1)} %refs_0_.2), channel_id=1, source_target_pairs={{0,3},{1,0},{2,1},{3,2},{4,7},{5,4},{6,5},{7,6},{8,11},{9,8},{10,9... | collective-permute-start | bytes 3145736 | tf_op jit(solution)/shard_map/ppermute | solution.py:24
  2.5 25.1 %collective-permute-start.3 = (bf16[64,8192]{1,0:T(8,128)(2,1)}, bf16[64,8192]{1,0:T(8,128)(2,1)S(1)}, u32[]{:S(2)}, u32[]{:S(2)}) collective-permute-start(bf16[64,8192]{1,0:T(8,128)(2,1)} %refs_0_.2), channel_id=1, source_target_pairs={{0,1},{1,2},{2,3},{3,0},{4,5},{5,6},{6,7},{7,4},{8,9},{9,10},{10,1... | collective-permute-start | bytes 3145736 | tf_op jit(solution)/shard_map/ppermute | solution.py:24
  2.5 2.2 %copy-start = (bf16[8192,256]{1,0:T(8,128)(2,1)S(1)}, bf16[8192,256]{1,0:T(8,128)(2,1)}, u32[]{:S(2)}) copy-start(bf16[8192,256]{1,0:T(8,128)(2,1)} %refs_2_.5) | copy-start | bytes 12582916
  4.7 2.2 %copy-start.2 = (bf16[8192,256]{1,0:T(8,128)(2,1)S(1)}, bf16[8192,256]{1,0:T(8,128)(2,1)}, u32[]{:S(2)}) copy-start(bf16[8192,256]{1,0:T(8,128)(2,1)} %refs_3_.3) | copy-start | bytes 12582916
  6.9 1.2 %copy-start.4 = (bf16[64,8192]{1,0:T(8,128)(2,1)S(1)}, bf16[64,8192]{1,0:T(8,128)(2,1)}, u32[]{:S(2)}) copy-start(bf16[64,8192]{1,0:T(8,128)(2,1)} %refs_0_.2) | copy-start | bytes 3145732
  8.1 0.7 %copy-start.5 = (f32[128]{0:T(128)S(1)}, f32[128]{0:T(128)}, u32[]{:S(2)}) copy-start(f32[128]{0:T(128)} %param.12) | copy-start | bytes 1540
  8.7 11.2 %copy-start.9 = (f32[128]{0:T(128)S(1)}, f32[128]{0:T(128)}, u32[]{:S(2)}) copy-start(f32[128]{0:T(128)} %param.11) | copy-start | bytes 1540
  8.7 11.4 %copy-start.8 = (s32[4,64]{1,0:T(4,128)S(1)}, s32[4,64]{1,0:T(4,128)}, u32[]{:S(2)}) copy-start(s32[4,64]{1,0:T(4,128)} %param.13) | copy-start | bytes 3076
  8.7 12.6 %copy-start.7 = (bf16[256,2048]{1,0:T(8,128)(2,1)S(1)}, bf16[256,2048]{1,0:T(8,128)(2,1)}, u32[]{:S(2)}) copy-start(bf16[256,2048]{1,0:T(8,128)(2,1)} %refs_0_.3) | copy-start | bytes 3145732
  10.4 9.6 %collective-permute-start.1 = (bf16[64,512]{1,0:T(8,128)(2,1)S(1)}, bf16[64,512]{1,0:T(8,128)(2,1)S(1)}, u32[]{:S(2)}, u32[]{:S(2)}) collective-permute-start(bf16[64,512]{1,0:T(8,128)(2,1)S(1)} %project_own.1.refs_1_), channel_id=1, source_target_pairs={{0,8},{4,12},{8,16},{12,20},{16,24},{20,28},{24,32},{28,36},{32,40... | collective-permute-start | bytes 196616 | tf_op jit(solution)/shard_map/ppermute | solution.py:30
  13.6 7.6 %collective-permute-start = (bf16[64,512]{1,0:T(8,128)(2,1)S(1)}, bf16[64,512]{1,0:T(8,128)(2,1)S(1)}, u32[]{:S(2)}, u32[]{:S(2)}) collective-permute-start(bf16[64,512]{1,0:T(8,128)(2,1)S(1)} %project_own.1.refs_1_), channel_id=1, source_target_pairs={{0,4},{4,16},{8,12},{12,24},{16,20},{20,32},{24,28},{28,40},{32,36... | collective-permute-start | bytes 196616 | tf_op jit(solution)/shard_map/ppermute | solution.py:30
  20.0 1.3 %collective-permute-start.2 = (bf16[64,512]{1,0:T(8,128)(2,1)S(1)}, bf16[64,512]{1,0:T(8,128)(2,1)S(1)}, u32[]{:S(2)}, u32[]{:S(2)}) collective-permute-start(bf16[64,512]{1,0:T(8,128)(2,1)S(1)} %collective-permute-done.1.refs_3_), channel_id=1, source_target_pairs={{0,4},{4,0},{8,12},{12,8},{16,20},{20,16},{24,28},{28,24},{32,36},... | collective-permute-start | bytes 196616 | tf_op jit(solution)/shard_map/ppermute | solution.py:30
  21.4 9.1 %copy-start.1 = (bf16[8192,256]{1,0:T(8,128)(2,1)S(1)}, bf16[8192,256]{1,0:T(8,128)(2,1)}, u32[]{:S(2)}) copy-start(bf16[8192,256]{1,0:T(8,128)(2,1)} %refs_2_.5) | copy-start | bytes 12582916
  21.4 9.1 %copy-start.3 = (bf16[8192,256]{1,0:T(8,128)(2,1)S(1)}, bf16[8192,256]{1,0:T(8,128)(2,1)}, u32[]{:S(2)}) copy-start(bf16[8192,256]{1,0:T(8,128)(2,1)} %refs_3_.3) | copy-start | bytes 12582916
  21.4 9.1 %copy-start.6 = (f32[128]{0:T(128)S(1)}, f32[128]{0:T(128)}, u32[]{:S(2)}) copy-start(f32[128]{0:T(128)} %param.12) | copy-start | bytes 1540
  27.7 15.2 %collective-permute-start.5 = (bf16[32,8192]{1,0:T(8,128)(2,1)S(1)}, bf16[32,8192]{1,0:T(8,128)(2,1)S(1)}, u32[]{:S(2)}, u32[]{:S(2)}) collective-permute-start(bf16[32,8192]{1,0:T(8,128)(2,1)S(1)} %slice.6), channel_id=1, source_target_pairs={{0,1},{1,2},{2,3},{3,0},{4,5},{5,6},{6,7},{7,4},{8,9},{9,10},{10,1... | collective-permute-start | bytes 1572872 | tf_op jit(solution)/shard_map/ppermute | solution.py:24
  27.8 15.1 %collective-permute-start.6 = (bf16[32,8192]{1,0:T(8,128)(2,1)S(1)}, bf16[32,8192]{1,0:T(8,128)(2,1)S(1)}, u32[]{:S(2)}, u32[]{:S(2)}) collective-permute-start(bf16[32,8192]{1,0:T(8,128)(2,1)S(1)} %slice.7), channel_id=1, source_target_pairs={{0,3},{1,0},{2,1},{3,2},{4,7},{5,4},{6,5},{7,6},{8,11},{9,8},{10,9... | collective-permute-start | bytes 1572872 | tf_op jit(solution)/shard_map/ppermute | solution.py:24
  31.9 10.9 %collective-permute-start.10 = (bf16[128,512]{1,0:T(8,128)(2,1)S(1)}, bf16[128,512]{1,0:T(8,128)(2,1)S(1)}, u32[]{:S(2)}, u32[]{:S(2)}) collective-permute-start(bf16[128,512]{1,0:T(8,128)(2,1)S(1)} %project_sides.1.refs_1_), channel_id=1, source_target_pairs={{0,8},{4,12},{8,16},{12,20},{16,24},{20,28},{24,32},{28,36},{32,40... | collective-permute-start | bytes 393224 | tf_op jit(solution)/shard_map/ppermute | solution.py:30
  35.1 19.8 %collective-permute-start.9 = (bf16[128,512]{1,0:T(8,128)(2,1)S(1)}, bf16[128,512]{1,0:T(8,128)(2,1)S(1)}, u32[]{:S(2)}, u32[]{:S(2)}) collective-permute-start(bf16[128,512]{1,0:T(8,128)(2,1)S(1)} %project_sides.1.refs_1_), channel_id=1, source_target_pairs={{0,4},{4,16},{8,12},{12,24},{16,20},{20,32},{24,28},{28,40},{32,36... | collective-permute-start | bytes 393224 | tf_op jit(solution)/shard_map/ppermute | solution.py:30
  42.8 12.0 %collective-permute-start.11 = (bf16[128,512]{1,0:T(8,128)(2,1)S(1)}, bf16[128,512]{1,0:T(8,128)(2,1)S(1)}, u32[]{:S(2)}, u32[]{:S(2)}) collective-permute-start(bf16[128,512]{1,0:T(8,128)(2,1)S(1)} %collective-permute-done.10.refs_3_), channel_id=1, source_target_pairs={{0,4},{4,0},{8,12},{12,8},{16,20},{20,16},{24,28},{28,24},{32,36},... | collective-permute-start | bytes 393224 | tf_op jit(solution)/shard_map/ppermute | solution.py:30
  44.6 12.9 %collective-permute-start.8 = (bf16[64,512]{1,0:T(8,128)(2,1)S(1)}, bf16[64,512]{1,0:T(8,128)(2,1)S(1)}, u32[]{:S(2)}, u32[]{:S(2)}) collective-permute-start(bf16[64,512]{1,0:T(8,128)(2,1)S(1)} %project_across.1.refs_1_), channel_id=1, source_target_pairs={{0,8},{4,12},{8,16},{12,20},{16,24},{20,28},{24,32},{28,36},{32,40... | collective-permute-start | bytes 196616 | tf_op jit(solution)/shard_map/ppermute | solution.py:30
  47.2 10.4 %collective-permute-start.7 = (bf16[64,512]{1,0:T(8,128)(2,1)S(1)}, bf16[64,512]{1,0:T(8,128)(2,1)S(1)}, u32[]{:S(2)}, u32[]{:S(2)}) collective-permute-start(bf16[64,512]{1,0:T(8,128)(2,1)S(1)} %project_across.1.refs_1_), channel_id=1, source_target_pairs={{0,4},{4,16},{8,12},{12,24},{16,20},{20,32},{24,28},{28,40},{32,36... | collective-permute-start | bytes 196616 | tf_op jit(solution)/shard_map/ppermute | solution.py:30
  57.5 1.3 %collective-permute-start.12 = (bf16[64,512]{1,0:T(8,128)(2,1)S(1)}, bf16[64,512]{1,0:T(8,128)(2,1)S(1)}, u32[]{:S(2)}, u32[]{:S(2)}) collective-permute-start(bf16[64,512]{1,0:T(8,128)(2,1)S(1)} %collective-permute-done.8.refs_3_), channel_id=1, source_target_pairs={{0,4},{4,0},{8,12},{12,8},{16,20},{20,16},{24,28},{28,24},{32,36},... | collective-permute-start | bytes 196616 | tf_op jit(solution)/shard_map/ppermute | solution.py:30

commit v7 on v3

--- a/solution.py
+++ b/solution.py
@@ -16,6 +16,8 @@
 PROJECT_VMEM = 8 * 1024 * 1024
 ATTEND_VMEM = 20 * 1024 * 1024
 WHOLE = pl.BlockSpec(memory_space=pltpu.VMEM)
+IN_PLACE = pl.BlockSpec(memory_space=pl.ANY)
+HEADS_OUT = 4
 
 
 def turned(value, axis, by):
@@ -63,6 +65,9 @@
 
 def attend_kernel(first, last, kv_heads, *refs):
     refs = list(refs)
+    copies = []
+    if last:
+        sems, held = refs.pop(), refs.pop()
     query_ref = refs.pop(0)
     block_refs = [refs.pop(0) for _ in range(REACH)]
     open_ref = refs.pop(0)
@@ -118,12 +123,22 @@
                 safe = jnp.where(total > 0, total, jnp.ones_like(total))
                 inverse = pl.reciprocal(safe, approx=True)
                 inverse = inverse * (2.0 - safe * inverse)
-                refs[0][:, columns(head)] = (sums * inverse).astype(jnp.bfloat16)
+                held[:, columns(head)] = (sums * inverse).astype(jnp.bfloat16)
+                if head % HEADS_OUT == HEADS_OUT - 1:
+                    part = pl.ds((head + 1 - HEADS_OUT) * HEAD_SIZE, HEADS_OUT * HEAD_SIZE)
+                    copies.append(
+                        pltpu.make_async_copy(
+                            held.at[:, part], refs[0].at[:, part], sems.at[head // HEADS_OUT]
+                        )
+                    )
+                    copies[-1].start()
             else:
                 refs[0][:, columns(head)] = sums
                 totals = jnp.where(lane == head, total, totals)
     if not last:
         refs[1][...] = totals
+    for copy in copies:
+        copy.wait()
 
 
 def attend_cost(rows, width, keys):
@@ -139,8 +154,11 @@
     rows, width = query.shape
     kv_heads = blocks[0].shape[1] // (2 * HEAD_SIZE)
     operands = [query, *blocks, is_open] + ([gain] if first else list(carried))
+    scratch_shapes = []
     if last:
         out_shape = [jax.ShapeDtypeStruct((rows, width), jnp.bfloat16)]
+        scratch_shapes.append(pltpu.VMEM((rows, width), jnp.bfloat16))
+        scratch_shapes.append(pltpu.SemaphoreType.DMA((width // (HEADS_OUT * HEAD_SIZE),)))
     else:
         out_shape = [
             jax.ShapeDtypeStruct((rows, width), jnp.float32),
@@ -152,7 +170,8 @@
         functools.partial(attend_kernel, first, last, kv_heads),
         out_shape=out_shape,
         in_specs=[WHOLE] * len(operands),
-        out_specs=[WHOLE] * len(out_shape),
+        out_specs=[IN_PLACE if last else WHOLE] * len(out_shape),
+        scratch_shapes=scratch_shapes,
         cost_estimate=attend_cost(rows, width, REACH * blocks[0].shape[0]),
         compiler_params=pltpu.CompilerParams(vmem_limit_bytes=ATTEND_VMEM),
         name=name,

time: 59.3 us -> 59.3 us (level)
  no operation moved by 1% of the time
where the time goes in v7:
time: 59.3 us; the launch traced here: 59.1 us
  starting transfers between devices  22.1 us (37%)
  waiting for transfers between devices  18.8 us (32%)
  Pallas kernels  11.3 us (19%)
  local copies, waits for them, and re-layouts  6.36 us (11%)
    ppermute x13, starting transfers between devices, turned(): lax.ppermute(value, axis, [(i, (i + by) % length) for i in range(length)])  22.1 us
    ppermute x13, waiting for transfers between devices, turned(): lax.ppermute(value, axis, [(i, (i + by) % length) for i in range(length)])  18.8 us
    pallas_call x3, Pallas kernels, attend(): pl.pallas_call(functools.partial(attend_kernel, first, last, kv_heads), o...  6.59 us
    unnamed x20, local copies, waits for them, and re-layouts  6.28 us
    pallas_call x3, Pallas kernels, project(): pl.pallas_call(project_kernel, out_shape=jax.ShapeDtypeStruct((rows, 2 *...  4.69 us
  transfers between devices with their start and end apart: 13, of which 5 were waited for; matrix products, arithmetic and copies ran while one was open for 0% of the time, Pallas kernels for 15%

profile of v7, /device:TPU:1, one launch (start us, length us, event | category | flops | bytes accessed | tf_op | source)
XLA Modules:
  0.0 59.1 jit_solution(173078813035873339)
XLA Ops:
  0.0 3.3 %collective-permute-start.4 = (bf16[64,8192]{1,0:T(8,128)(2,1)}, bf16[64,8192]{1,0:T(8,128)(2,1)S(1)}, u32[]{:S(2)}, u32[]{:S(2)}) collective-permute-start(bf16[64,8192]{1,0:T(8,128)(2,1)} %refs_0_.2), channel_id=1, source_target_pairs={{0,3},{1,0},{2,1},{3,2},{4,7},{5,4},{6,5},{7,6},{8,11},{9,8},{10,9... | collective-permute-start | bytes 3145736 | tf_op jit(solution)/shard_map/ppermute | solution.py:25
  3.3 2.2 %copy-done = bf16[8192,256]{1,0:T(8,128)(2,1)S(1)} copy-done((bf16[8192,256]{1,0:T(8,128)(2,1)S(1)}, bf16[8192,256]{1,0:T(8,128)(2,1)}, u32[]{:S(2)}) %copy-start) | copy-done | bytes 4194328
  5.5 2.2 %copy-done.2 = bf16[8192,256]{1,0:T(8,128)(2,1)S(1)} copy-done((bf16[8192,256]{1,0:T(8,128)(2,1)S(1)}, bf16[8192,256]{1,0:T(8,128)(2,1)}, u32[]{:S(2)}) %copy-start.2) | copy-done | bytes 4194328
  7.7 1.2 %copy-done.4 = bf16[64,8192]{1,0:T(8,128)(2,1)S(1)} copy-done((bf16[64,8192]{1,0:T(8,128)(2,1)S(1)}, bf16[64,8192]{1,0:T(8,128)(2,1)}, u32[]{:S(2)}) %copy-start.4) | copy-done | bytes 1048600
  8.9 0.7 %copy-done.5 = f32[128]{0:T(128)S(1)} copy-done((f32[128]{0:T(128)S(1)}, f32[128]{0:T(128)}, u32[]{:S(2)}) %copy-start.5) | copy-done | bytes 536
  9.6 1.6 %project_own.1.refs_1_ = bf16[64,512]{1,0:T(8,128)(2,1)S(1)} custom-call(bf16[64,8192]{1,0:T(8,128)(2,1)S(1)} %copy-done.4, bf16[8192,256]{1,0:T(8,128)(2,1)S(1)} %copy-done, bf16[8192,256]{1,0:T(8,128)(2,1)S(1)} %copy-done.2, f32[1,128]{1,0:T(1,128)S(1)} %bitcast.7), custom_call_target="tpu_custom_call" | custom-call | flops 536870912 | bytes 8388608 | tf_op jit(solution)/shard_map/project_own/pallas_call | solution.py:55
  11.2 3.8 %collective-permute-start.2 = (bf16[64,512]{1,0:T(8,128)(2,1)S(1)}, bf16[64,512]{1,0:T(8,128)(2,1)S(1)}, u32[]{:S(2)}, u32[]{:S(2)}) collective-permute-start(bf16[64,512]{1,0:T(8,128)(2,1)S(1)} %project_own.1.refs_1_), channel_id=1, source_target_pairs={{0,12},{4,16},{8,20},{12,24},{16,28},{20,32},{24,36},{28,40},{32,4... | collective-permute-start | bytes 196616 | tf_op jit(solution)/shard_map/ppermute | solution.py:25
  15.1 0.4 collective-permute-start.1
  15.6 0.1 select_reduce_fusion
  15.7 7.4 %collective-permute-done.2.refs_4_ = bf16[64,512]{1,0:T(8,128)(2,1)S(1)} collective-permute-done((bf16[64,512]{1,0:T(8,128)(2,1)S(1)}, bf16[64,512]{1,0:T(8,128)(2,1)S(1)}, u32[]{:S(2)}, u32[]{:S(2)}) %collective-permute-start.2) | collective-permute-done | bytes 65568 | tf_op jit(solution)/shard_map/ppermute | solution.py:25
  23.2 1.7 %attend_own.1 = (bf16[256,2048]{1,0:T(8,128)(2,1)S(1)}, f32[256,2048]{1,0:T(8,128)S(1)}, f32[256,128]{1,0:T(8,128)S(1)}) custom-call(bf16[256,2048]{1,0:T(8,128)(2,1)S(1)} %copy-done.7, bf16[64,512]{1,0:T(8,128)(2,1)S(1)} %project_own.1.refs_1_, bf16[64,512]{1,0:T(8,128)(2,1)S(1)} %collective-permute-done.refs_2_, ...), custom_call_target="tpu_custom_call" | custom-call | flops 2147483648 | bytes 1048576 | tf_op jit(solution)/shard_map/attend_own/pallas_call | solution.py:169
  24.9 0.5 collective-permute-done.4.refs_1_
  25.5 3.0 %collective-permute-done.3.refs_0_ = bf16[64,8192]{1,0:T(8,128)(2,1)S(1)} collective-permute-done((bf16[64,8192]{1,0:T(8,128)(2,1)}, bf16[64,8192]{1,0:T(8,128)(2,1)S(1)}, u32[]{:S(2)}, u32[]{:S(2)}) %collective-permute-start.3) | collective-permute-done | bytes 1048608 | tf_op jit(solution)/shard_map/ppermute | solution.py:25
  28.6 2.7 %collective-permute-start.6 = (bf16[32,8192]{1,0:T(8,128)(2,1)S(1)}, bf16[32,8192]{1,0:T(8,128)(2,1)S(1)}, u32[]{:S(2)}, u32[]{:S(2)}) collective-permute-start(bf16[32,8192]{1,0:T(8,128)(2,1)S(1)} %slice.7), channel_id=1, source_target_pairs={{0,3},{1,0},{2,1},{3,2},{4,7},{5,4},{6,5},{7,6},{8,11},{9,8},{10,9... | collective-permute-start | bytes 1572872 | tf_op jit(solution)/shard_map/ppermute | solution.py:25
  31.3 1.4 %project_sides.1.refs_1_ = bf16[128,512]{1,0:T(8,128)(2,1)S(1)} custom-call(bf16[64,8192]{1,0:T(8,128)(2,1)S(1)} %collective-permute-done.3.refs_0_, bf16[64,8192]{1,0:T(8,128)(2,1)S(1)} %collective-permute-done.4.refs_1_, bf16[8192,256]{1,0:T(8,128)(2,1)S(1)} %copy-done.1, bf16[8192,256]{1,0:T(8,128)(2,1)S(1)} %copy-done.3, f32[1,128]{1,0:T(1,128)S(1)} %bitcast.8), custom_call_target="tpu_custom_call" | custom-call | flops 1073741824 | bytes 8388608 | tf_op jit(solution)/shard_map/project_sides/pallas_call | solution.py:55
  32.7 5.3 %collective-permute-start.12 = (bf16[128,512]{1,0:T(8,128)(2,1)S(1)}, bf16[128,512]{1,0:T(8,128)(2,1)S(1)}, u32[]{:S(2)}, u32[]{:S(2)}) collective-permute-start(bf16[128,512]{1,0:T(8,128)(2,1)S(1)} %project_sides.1.refs_1_), channel_id=1, source_target_pairs={{0,12},{4,16},{8,20},{12,24},{16,28},{20,32},{24,36},{28,40},{32,4... | collective-permute-start | bytes 393224 | tf_op jit(solution)/shard_map/ppermute | solution.py:25
  38.0 0.4 collective-permute-start.11
  38.4 3.0 %collective-permute-done.5.refs_0_ = bf16[32,8192]{1,0:T(8,128)(2,1)S(1)} collective-permute-done((bf16[32,8192]{1,0:T(8,128)(2,1)S(1)}, bf16[32,8192]{1,0:T(8,128)(2,1)S(1)}, u32[]{:S(2)}, u32[]{:S(2)}) %collective-permute-start.5) | collective-permute-done | bytes 524320 | tf_op jit(solution)/shard_map/ppermute | solution.py:25
  41.4 1.6 %project_across.1.refs_1_ = bf16[64,512]{1,0:T(8,128)(2,1)S(1)} custom-call(bf16[32,8192]{1,0:T(8,128)(2,1)S(1)} %collective-permute-done.5.refs_0_, bf16[32,8192]{1,0:T(8,128)(2,1)S(1)} %collective-permute-done.6.refs_1_, bf16[8192,256]{1,0:T(8,128)(2,1)S(1)} %copy-done.1, bf16[8192,256]{1,0:T(8,128)(2,1)S(1)} %copy-done.3, f32[1,128]{1,0:T(1,128)S(1)} %bitcast.9), custom_call_target="tpu_custom_call" | custom-call | flops 536870912 | bytes 8388608 | tf_op jit(solution)/shard_map/project_across/pallas_call | solution.py:55
  43.0 5.7 %collective-permute-start.9 = (bf16[64,512]{1,0:T(8,128)(2,1)S(1)}, bf16[64,512]{1,0:T(8,128)(2,1)S(1)}, u32[]{:S(2)}, u32[]{:S(2)}) collective-permute-start(bf16[64,512]{1,0:T(8,128)(2,1)S(1)} %project_across.1.refs_1_), channel_id=1, source_target_pairs={{0,12},{4,16},{8,20},{12,24},{16,28},{20,32},{24,36},{28,40},{32,4... | collective-permute-start | bytes 196616 | tf_op jit(solution)/shard_map/ppermute | solution.py:25
  48.7 0.4 collective-permute-start.8
  49.1 2.6 %attend_sides.1 = (f32[256,2048]{1,0:T(8,128)S(1)}, f32[256,128]{1,0:T(8,128)S(1)}) custom-call(bf16[256,2048]{1,0:T(8,128)(2,1)S(1)} %get-tuple-element.22.refs_0_, bf16[128,512]{1,0:T(8,128)(2,1)S(1)} %project_sides.1.refs_1_, bf16[128,512]{1,0:T(8,128)(2,1)S(1)} %collective-permute-done.10.refs_2_, bf16[128,512]{1,0:T(8,128)(2,1)S(1)} %collective-permute-done.11.refs_3_, ...), custom_call_target="tpu_custom_call" | custom-call | flops 4294967296 | bytes 1048576 | tf_op jit(solution)/shard_map/attend_sides/pallas_call | solution.py:169
  51.8 4.9 %collective-permute-done.9.refs_4_ = bf16[64,512]{1,0:T(8,128)(2,1)S(1)} collective-permute-done((bf16[64,512]{1,0:T(8,128)(2,1)S(1)}, bf16[64,512]{1,0:T(8,128)(2,1)S(1)}, u32[]{:S(2)}, u32[]{:S(2)}) %collective-permute-start.9) | collective-permute-done | bytes 65568 | tf_op jit(solution)/shard_map/ppermute | solution.py:25
  56.7 2.2 %attend_across.1 = bf16[256,2048]{1,0:T(8,128)(2,1)} custom-call(bf16[256,2048]{1,0:T(8,128)(2,1)S(1)} %get-tuple-element.22.refs_0_, bf16[64,512]{1,0:T(8,128)(2,1)S(1)} %project_across.1.refs_1_, bf16[64,512]{1,0:T(8,128)(2,1)S(1)} %collective-permute-done.7.refs_2_, bf16[64,512]{1,0:T(8,128)(2,1)S(1)} %collective-permute-done.8.refs_3_, ...), custom_call_target="tpu_custom_call" | custom-call | flops 2147483648 | bytes 1048576 | tf_op jit(solution)/shard_map/attend_across/pallas_call | solution.py:169
  (36 shorter events, 0.3 us)
Async XLA Ops:
  0.0 25.5 %collective-permute-start.4 = (bf16[64,8192]{1,0:T(8,128)(2,1)}, bf16[64,8192]{1,0:T(8,128)(2,1)S(1)}, u32[]{:S(2)}, u32[]{:S(2)}) collective-permute-start(bf16[64,8192]{1,0:T(8,128)(2,1)} %refs_0_.2), channel_id=1, source_target_pairs={{0,3},{1,0},{2,1},{3,2},{4,7},{5,4},{6,5},{7,6},{8,11},{9,8},{10,9... | collective-permute-start | bytes 3145736 | tf_op jit(solution)/shard_map/ppermute | solution.py:25
  3.3 25.1 %collective-permute-start.3 = (bf16[64,8192]{1,0:T(8,128)(2,1)}, bf16[64,8192]{1,0:T(8,128)(2,1)S(1)}, u32[]{:S(2)}, u32[]{:S(2)}) collective-permute-start(bf16[64,8192]{1,0:T(8,128)(2,1)} %refs_0_.2), channel_id=1, source_target_pairs={{0,1},{1,2},{2,3},{3,0},{4,5},{5,6},{6,7},{7,4},{8,9},{9,10},{10,1... | collective-permute-start | bytes 3145736 | tf_op jit(solution)/shard_map/ppermute | solution.py:25
  3.3 2.2 %copy-start = (bf16[8192,256]{1,0:T(8,128)(2,1)S(1)}, bf16[8192,256]{1,0:T(8,128)(2,1)}, u32[]{:S(2)}) copy-start(bf16[8192,256]{1,0:T(8,128)(2,1)} %refs_2_.5) | copy-start | bytes 12582916
  5.5 2.2 %copy-start.2 = (bf16[8192,256]{1,0:T(8,128)(2,1)S(1)}, bf16[8192,256]{1,0:T(8,128)(2,1)}, u32[]{:S(2)}) copy-start(bf16[8192,256]{1,0:T(8,128)(2,1)} %refs_3_.3) | copy-start | bytes 12582916
  7.7 1.2 %copy-start.4 = (bf16[64,8192]{1,0:T(8,128)(2,1)S(1)}, bf16[64,8192]{1,0:T(8,128)(2,1)}, u32[]{:S(2)}) copy-start(bf16[64,8192]{1,0:T(8,128)(2,1)} %refs_0_.2) | copy-start | bytes 3145732
  8.9 0.7 %copy-start.5 = (f32[128]{0:T(128)S(1)}, f32[128]{0:T(128)}, u32[]{:S(2)}) copy-start(f32[128]{0:T(128)} %param.12) | copy-start | bytes 1540
  9.6 6.0 %copy-start.9 = (f32[128]{0:T(128)S(1)}, f32[128]{0:T(128)}, u32[]{:S(2)}) copy-start(f32[128]{0:T(128)} %param.11) | copy-start | bytes 1540
  9.6 6.0 %copy-start.8 = (s32[4,64]{1,0:T(4,128)S(1)}, s32[4,64]{1,0:T(4,128)}, u32[]{:S(2)}) copy-start(s32[4,64]{1,0:T(4,128)} %param.13) | copy-start | bytes 3076
  9.6 13.6 %copy-start.7 = (bf16[256,2048]{1,0:T(8,128)(2,1)S(1)}, bf16[256,2048]{1,0:T(8,128)(2,1)}, u32[]{:S(2)}) copy-start(bf16[256,2048]{1,0:T(8,128)(2,1)} %refs_0_.3) | copy-start | bytes 3145732
  11.2 11.9 %collective-permute-start.2 = (bf16[64,512]{1,0:T(8,128)(2,1)S(1)}, bf16[64,512]{1,0:T(8,128)(2,1)S(1)}, u32[]{:S(2)}, u32[]{:S(2)}) collective-permute-start(bf16[64,512]{1,0:T(8,128)(2,1)S(1)} %project_own.1.refs_1_), channel_id=1, source_target_pairs={{0,12},{4,16},{8,20},{12,24},{16,28},{20,32},{24,36},{28,40},{32,4... | collective-permute-start | bytes 196616 | tf_op jit(solution)/shard_map/ppermute | solution.py:25
  15.1 8.1 %collective-permute-start.1 = (bf16[64,512]{1,0:T(8,128)(2,1)S(1)}, bf16[64,512]{1,0:T(8,128)(2,1)S(1)}, u32[]{:S(2)}, u32[]{:S(2)}) collective-permute-start(bf16[64,512]{1,0:T(8,128)(2,1)S(1)} %project_own.1.refs_1_), channel_id=1, source_target_pairs={{0,8},{4,12},{8,16},{12,20},{16,24},{20,28},{24,32},{28,36},{32,40... | collective-permute-start | bytes 196616 | tf_op jit(solution)/shard_map/ppermute | solution.py:25
  15.5 7.7 %collective-permute-start = (bf16[64,512]{1,0:T(8,128)(2,1)S(1)}, bf16[64,512]{1,0:T(8,128)(2,1)S(1)}, u32[]{:S(2)}, u32[]{:S(2)}) collective-permute-start(bf16[64,512]{1,0:T(8,128)(2,1)S(1)} %project_own.1.refs_1_), channel_id=1, source_target_pairs={{0,4},{4,8},{8,12},{12,16},{16,20},{20,24},{24,28},{28,32},{32,36}... | collective-permute-start | bytes 196616 | tf_op jit(solution)/shard_map/ppermute | solution.py:25
  23.2 8.1 %copy-start.1 = (bf16[8192,256]{1,0:T(8,128)(2,1)S(1)}, bf16[8192,256]{1,0:T(8,128)(2,1)}, u32[]{:S(2)}) copy-start(bf16[8192,256]{1,0:T(8,128)(2,1)} %refs_2_.5) | copy-start | bytes 12582916
  23.2 8.1 %copy-start.3 = (bf16[8192,256]{1,0:T(8,128)(2,1)S(1)}, bf16[8192,256]{1,0:T(8,128)(2,1)}, u32[]{:S(2)}) copy-start(bf16[8192,256]{1,0:T(8,128)(2,1)} %refs_3_.3) | copy-start | bytes 12582916
  23.2 8.1 %copy-start.6 = (f32[128]{0:T(128)S(1)}, f32[128]{0:T(128)}, u32[]{:S(2)}) copy-start(f32[128]{0:T(128)} %param.12) | copy-start | bytes 1540
  28.5 12.8 %collective-permute-start.5 = (bf16[32,8192]{1,0:T(8,128)(2,1)S(1)}, bf16[32,8192]{1,0:T(8,128)(2,1)S(1)}, u32[]{:S(2)}, u32[]{:S(2)}) collective-permute-start(bf16[32,8192]{1,0:T(8,128)(2,1)S(1)} %slice.6), channel_id=1, source_target_pairs={{0,1},{1,2},{2,3},{3,0},{4,5},{5,6},{6,7},{7,4},{8,9},{9,10},{10,1... | collective-permute-start | bytes 1572872 | tf_op jit(solution)/shard_map/ppermute | solution.py:25
  28.6 12.8 %collective-permute-start.6 = (bf16[32,8192]{1,0:T(8,128)(2,1)S(1)}, bf16[32,8192]{1,0:T(8,128)(2,1)S(1)}, u32[]{:S(2)}, u32[]{:S(2)}) collective-permute-start(bf16[32,8192]{1,0:T(8,128)(2,1)S(1)} %slice.7), channel_id=1, source_target_pairs={{0,3},{1,0},{2,1},{3,2},{4,7},{5,4},{6,5},{7,6},{8,11},{9,8},{10,9... | collective-permute-start | bytes 1572872 | tf_op jit(solution)/shard_map/ppermute | solution.py:25
  32.7 16.4 %collective-permute-start.12 = (bf16[128,512]{1,0:T(8,128)(2,1)S(1)}, bf16[128,512]{1,0:T(8,128)(2,1)S(1)}, u32[]{:S(2)}, u32[]{:S(2)}) collective-permute-start(bf16[128,512]{1,0:T(8,128)(2,1)S(1)} %project_sides.1.refs_1_), channel_id=1, source_target_pairs={{0,12},{4,16},{8,20},{12,24},{16,28},{20,32},{24,36},{28,40},{32,4... | collective-permute-start | bytes 393224 | tf_op jit(solution)/shard_map/ppermute | solution.py:25
  38.0 11.1 %collective-permute-start.11 = (bf16[128,512]{1,0:T(8,128)(2,1)S(1)}, bf16[128,512]{1,0:T(8,128)(2,1)S(1)}, u32[]{:S(2)}, u32[]{:S(2)}) collective-permute-start(bf16[128,512]{1,0:T(8,128)(2,1)S(1)} %project_sides.1.refs_1_), channel_id=1, source_target_pairs={{0,8},{4,12},{8,16},{12,20},{16,24},{20,28},{24,32},{28,36},{32,40... | collective-permute-start | bytes 393224 | tf_op jit(solution)/shard_map/ppermute | solution.py:25
  38.4 10.7 %collective-permute-start.10 = (bf16[128,512]{1,0:T(8,128)(2,1)S(1)}, bf16[128,512]{1,0:T(8,128)(2,1)S(1)}, u32[]{:S(2)}, u32[]{:S(2)}) collective-permute-start(bf16[128,512]{1,0:T(8,128)(2,1)S(1)} %project_sides.1.refs_1_), channel_id=1, source_target_pairs={{0,4},{4,8},{8,12},{12,16},{16,20},{20,24},{24,28},{28,32},{32,36}... | collective-permute-start | bytes 393224 | tf_op jit(solution)/shard_map/ppermute | solution.py:25
  43.0 13.7 %collective-permute-start.9 = (bf16[64,512]{1,0:T(8,128)(2,1)S(1)}, bf16[64,512]{1,0:T(8,128)(2,1)S(1)}, u32[]{:S(2)}, u32[]{:S(2)}) collective-permute-start(bf16[64,512]{1,0:T(8,128)(2,1)S(1)} %project_across.1.refs_1_), channel_id=1, source_target_pairs={{0,12},{4,16},{8,20},{12,24},{16,28},{20,32},{24,36},{28,40},{32,4... | collective-permute-start | bytes 196616 | tf_op jit(solution)/shard_map/ppermute | solution.py:25
  48.7 8.0 %collective-permute-start.8 = (bf16[64,512]{1,0:T(8,128)(2,1)S(1)}, bf16[64,512]{1,0:T(8,128)(2,1)S(1)}, u32[]{:S(2)}, u32[]{:S(2)}) collective-permute-start(bf16[64,512]{1,0:T(8,128)(2,1)S(1)} %project_across.1.refs_1_), channel_id=1, source_target_pairs={{0,8},{4,12},{8,16},{12,20},{16,24},{20,28},{24,32},{28,36},{32,40... | collective-permute-start | bytes 196616 | tf_op jit(solution)/shard_map/ppermute | solution.py:25
  49.1 7.6 %collective-permute-start.7 = (bf16[64,512]{1,0:T(8,128)(2,1)S(1)}, bf16[64,512]{1,0:T(8,128)(2,1)S(1)}, u32[]{:S(2)}, u32[]{:S(2)}) collective-permute-start(bf16[64,512]{1,0:T(8,128)(2,1)S(1)} %project_across.1.refs_1_), channel_id=1, source_target_pairs={{0,4},{4,8},{8,12},{12,16},{16,20},{20,24},{24,28},{28,32},{32,36}... | collective-permute-start | bytes 196616 | tf_op jit(solution)/shard_map/ppermute | solution.py:25

commit v8 on v7

--- a/solution.py
+++ b/solution.py
@@ -20,17 +20,14 @@
 HEADS_OUT = 4
 
 
-def turned(value, axis, by):
+def turned(value, axis, by, wraps=True):
     length = lax.axis_size(axis)
-    return lax.ppermute(value, axis, [(i, (i + by) % length) for i in range(length)])
-
-
-def project_rows(row_refs, key_ref, value_ref, gain_ref, out_ref):
-    width = key_ref.shape[1]
-    rows = [ref[...] for ref in row_refs]
-    rows = rows[0] if len(rows) == 1 else jnp.concatenate(rows, axis=0)
-    keys = jnp.dot(rows, key_ref[...], preferred_element_type=jnp.float32)
-    values = jnp.dot(rows, value_ref[...], preferred_element_type=jnp.float32)
+    pairs = [(i, (i + by) % length) for i in range(length) if wraps or i + by < length]
+    return lax.ppermute(value, axis, pairs)
+
+
+def write_keys_values(keys, values, gain_ref, out_ref):
+    width = keys.shape[1]
     for head in range(width // HEAD_SIZE):
         at = slice(head * HEAD_SIZE, (head + 1) * HEAD_SIZE)
         own = keys[:, at]
@@ -46,7 +43,11 @@
 
 def project_kernel(*refs):
     *row_refs, key_ref, value_ref, gain_ref, out_ref = refs
-    project_rows(row_refs, key_ref, value_ref, gain_ref, out_ref)
+    rows = [ref[...] for ref in row_refs]
+    rows = rows[0] if len(rows) == 1 else jnp.concatenate(rows, axis=0)
+    keys = jnp.dot(rows, key_ref[...], preferred_element_type=jnp.float32)
+    values = jnp.dot(rows, value_ref[...], preferred_element_type=jnp.float32)
+    write_keys_values(keys, values, gain_ref, out_ref)
 
 
 def project(row_parts, key_matrix, value_matrix, key_gain, name):
@@ -61,6 +62,48 @@
         compiler_params=pltpu.CompilerParams(vmem_limit_bytes=PROJECT_VMEM),
         name=name,
     )(*row_parts, key_matrix, value_matrix, key_gain)
+
+
+def first_columns_kernel(rows_ref, key_ref, value_ref, out_ref):
+    depth, width = rows_ref.shape[1], key_ref.shape[1]
+    rows = rows_ref[...]
+    out_ref[:, :width] = jnp.dot(rows, key_ref[:depth], preferred_element_type=jnp.float32)
+    out_ref[:, width:] = jnp.dot(rows, value_ref[:depth], preferred_element_type=jnp.float32)
+
+
+def last_columns_kernel(rows_ref, sums_ref, key_ref, value_ref, gain_ref, out_ref):
+    width = key_ref.shape[1]
+    before = key_ref.shape[0] - rows_ref.shape[1]
+    rows = rows_ref[...]
+    keys = jnp.dot(rows, key_ref[before:], preferred_element_type=jnp.float32)
+    values = jnp.dot(rows, value_ref[before:], preferred_element_type=jnp.float32)
+    write_keys_values(
+        sums_ref[:, :width] + keys, sums_ref[:, width:] + values, gain_ref, out_ref
+    )
+
+
+def project_by_columns(first_part, last_part, key_matrix, value_matrix, key_gain, name):
+    rows, width = first_part.shape[0], key_matrix.shape[1]
+    params = dict(
+        out_specs=WHOLE,
+        cost_estimate=project_cost(rows // 2, key_matrix),
+        compiler_params=pltpu.CompilerParams(vmem_limit_bytes=PROJECT_VMEM),
+    )
+    sums = pl.pallas_call(
+        first_columns_kernel,
+        out_shape=jax.ShapeDtypeStruct((rows, 2 * width), jnp.float32),
+        in_specs=[WHOLE] * 3,
+        name=name + "_first",
+        **params,
+    )(first_part, key_matrix, value_matrix)
+    last_part = after(last_part, sums)
+    return pl.pallas_call(
+        last_columns_kernel,
+        out_shape=jax.ShapeDtypeStruct((rows, 2 * width), jnp.bfloat16),
+        in_specs=[WHOLE] * 5,
+        name=name + "_last",
+        **params,
+    )(last_part, sums, key_matrix, value_matrix, key_gain)
 
 
 def attend_kernel(first, last, kv_heads, *refs):
@@ -196,25 +239,27 @@
     def projected(row_parts, name):
         return project(row_parts, key_matrix, value_matrix, key_gain, "project_" + name)
 
-    def reached(block):
-        return [block] + [turned(block, "seq", by) for by in range(1, REACH)]
+    def reached(block, wraps=True):
+        return [block] + [turned(block, "seq", by, wraps) for by in range(1, REACH)]
 
     left = turned(vision, "tp", 1)
     right = turned(vision, "tp", -1)
     own = projected([vision], "own")
-    own_blocks = reached(own)
+    own_blocks = reached(own, wraps=False)
     normed, *carried = attend(
         text_query_matrix, own_blocks, is_open, query_gain, None, False, "attend_own"
     )
 
-    half = vision.shape[0] // 2
+    half = vision.shape[1] // 2
     left, right = after((left, right), carried)
-    upper_across = turned(left[:half], "tp", 1)
-    lower_across = turned(right[half:], "tp", -1)
+    first_across = turned(left[:, :half], "tp", 1)
+    last_across = turned(right[:, half:], "tp", -1)
     sides = projected([left, right], "sides")
     side_blocks = reached(sides)
-    upper_across, lower_across = after((upper_across, lower_across), sides)
-    across = projected([upper_across, lower_across], "across")
+    first_across = after(first_across, sides)
+    across = project_by_columns(
+        first_across, last_across, key_matrix, value_matrix, key_gain, "project_across"
+    )
     across_blocks = reached(across)
     side_blocks = after(side_blocks, across)
     carried = attend(normed, side_blocks, is_open, None, carried, False, "attend_sides")

time: 59.3 us -> 59.4 us (level)
  waiting for transfers between devices: 18.8 us -> 13 us
  starting transfers between devices: 22.1 us -> 27.8 us
    ppermute x13, waiting for transfers between devices: 18.8 us -> 13 us  [turned(): return lax.ppermute(value, axis, pairs)]
    ppermute x13, starting transfers between devices: 22.1 us -> 27.8 us  [turned(): return lax.ppermute(value, axis, pairs)]
    pallas_call x0 -> x2, Pallas kernels: none -> 1.76 us  [the longest x1 0.93 us: project_by_columns(): pl.pallas_call(last_columns_kernel, out_shape=jax.ShapeDtypeStruct((rows,...]
    pallas_call x3 -> x2, Pallas kernels: 4.69 us -> 3.05 us  [project(): pl.pallas_call(project_kernel, out_shape=jax.ShapeDtypeStruct((rows, 2 *...]
  transfers between devices with their start and end apart: 13 -> 13, of which waited for: 5 -> 5; matrix products, arithmetic and copies ran while one was open for 0% -> 0% of each run, Pallas kernels for 15% -> 16%
where the time goes in v8:
time: 59.4 us; the launch traced here: 59.1 us
  starting transfers between devices  27.8 us (47%)
  waiting for transfers between devices  13 us (22%)
  Pallas kernels  11.4 us (19%)
  local copies, waits for them, and re-layouts  6.36 us (11%)
    ppermute x13, starting transfers between devices, turned(): return lax.ppermute(value, axis, pairs)  27.8 us
    ppermute x13, waiting for transfers between devices, turned(): return lax.ppermute(value, axis, pairs)  13 us
    pallas_call x3, Pallas kernels, attend(): pl.pallas_call(functools.partial(attend_kernel, first, last, kv_heads), o...  6.59 us
    unnamed x20, local copies, waits for them, and re-layouts  6.28 us
    pallas_call x2, Pallas kernels, project(): pl.pallas_call(project_kernel, out_shape=jax.ShapeDtypeStruct((rows, 2 *...  3.05 us
  transfers between devices with their start and end apart: 13, of which 5 were waited for; matrix products, arithmetic and copies ran while one was open for 0% of the time, Pallas kernels for 16%

profile of v8, /device:TPU:1, one launch (start us, length us, event | category | flops | bytes accessed | tf_op | source)
XLA Modules:
  0.0 59.1 jit_solution(8108735618332129557)
XLA Ops:
  0.0 3.3 %collective-permute-start.4 = (bf16[64,8192]{1,0:T(8,128)(2,1)}, bf16[64,8192]{1,0:T(8,128)(2,1)S(1)}, u32[]{:S(2)}, u32[]{:S(2)}) collective-permute-start(bf16[64,8192]{1,0:T(8,128)(2,1)} %refs_0_.2), channel_id=1, source_target_pairs={{0,3},{1,0},{2,1},{3,2},{4,7},{5,4},{6,5},{7,6},{8,11},{9,8},{10,9... | collective-permute-start | bytes 3145736 | tf_op jit(solution)/shard_map/ppermute | solution.py:26
  3.3 2.2 %copy-done = bf16[8192,256]{1,0:T(8,128)(2,1)S(1)} copy-done((bf16[8192,256]{1,0:T(8,128)(2,1)S(1)}, bf16[8192,256]{1,0:T(8,128)(2,1)}, u32[]{:S(2)}) %copy-start) | copy-done | bytes 4194328
  5.5 2.2 %copy-done.2 = bf16[8192,256]{1,0:T(8,128)(2,1)S(1)} copy-done((bf16[8192,256]{1,0:T(8,128)(2,1)S(1)}, bf16[8192,256]{1,0:T(8,128)(2,1)}, u32[]{:S(2)}) %copy-start.2) | copy-done | bytes 4194328
  7.7 1.2 %copy-done.4 = bf16[64,8192]{1,0:T(8,128)(2,1)S(1)} copy-done((bf16[64,8192]{1,0:T(8,128)(2,1)S(1)}, bf16[64,8192]{1,0:T(8,128)(2,1)}, u32[]{:S(2)}) %copy-start.4) | copy-done | bytes 1048600
  8.9 0.7 %copy-done.5 = f32[128]{0:T(128)S(1)} copy-done((f32[128]{0:T(128)S(1)}, f32[128]{0:T(128)}, u32[]{:S(2)}) %copy-start.5) | copy-done | bytes 536
  9.6 1.6 %project_own.1.refs_1_ = bf16[64,512]{1,0:T(8,128)(2,1)S(1)} custom-call(bf16[64,8192]{1,0:T(8,128)(2,1)S(1)} %copy-done.4, bf16[8192,256]{1,0:T(8,128)(2,1)S(1)} %copy-done, bf16[8192,256]{1,0:T(8,128)(2,1)S(1)} %copy-done.2, f32[1,128]{1,0:T(1,128)S(1)} %bitcast.7), custom_call_target="tpu_custom_call" | custom-call | flops 536870912 | bytes 8388608 | tf_op jit(solution)/shard_map/project_own/pallas_call | solution.py:56
  11.2 5.7 %collective-permute-start.2 = (bf16[64,512]{1,0:T(8,128)(2,1)S(1)}, bf16[64,512]{1,0:T(8,128)(2,1)S(1)}, u32[]{:S(2)}, u32[]{:S(2)}) collective-permute-start(bf16[64,512]{1,0:T(8,128)(2,1)S(1)} %project_own.1.refs_1_), channel_id=1, source_target_pairs={{0,12},{4,16},{8,20},{12,24},{16,28},{20,32},{24,36},{28,40},{32,4... | collective-permute-start | bytes 196616 | tf_op jit(solution)/shard_map/ppermute | solution.py:26
  16.9 2.3 %collective-permute-start.1 = (bf16[64,512]{1,0:T(8,128)(2,1)S(1)}, bf16[64,512]{1,0:T(8,128)(2,1)S(1)}, u32[]{:S(2)}, u32[]{:S(2)}) collective-permute-start(bf16[64,512]{1,0:T(8,128)(2,1)S(1)} %project_own.1.refs_1_), channel_id=1, source_target_pairs={{0,8},{4,12},{8,16},{12,20},{16,24},{20,28},{24,32},{28,36},{32,40... | collective-permute-start | bytes 196616 | tf_op jit(solution)/shard_map/ppermute | solution.py:26
  19.2 1.9 %collective-permute-start = (bf16[64,512]{1,0:T(8,128)(2,1)S(1)}, bf16[64,512]{1,0:T(8,128)(2,1)S(1)}, u32[]{:S(2)}, u32[]{:S(2)}) collective-permute-start(bf16[64,512]{1,0:T(8,128)(2,1)S(1)} %project_own.1.refs_1_), channel_id=1, source_target_pairs={{0,4},{4,8},{8,12},{12,16},{16,20},{20,24},{24,28},{28,32},{32,36}... | collective-permute-start | bytes 196616 | tf_op jit(solution)/shard_map/ppermute | solution.py:26
  21.4 1.0 %collective-permute-done.refs_2_ = bf16[64,512]{1,0:T(8,128)(2,1)S(1)} collective-permute-done((bf16[64,512]{1,0:T(8,128)(2,1)S(1)}, bf16[64,512]{1,0:T(8,128)(2,1)S(1)}, u32[]{:S(2)}, u32[]{:S(2)}) %collective-permute-start) | collective-permute-done | bytes 65568 | tf_op jit(solution)/shard_map/ppermute | solution.py:26
  22.5 1.7 %attend_own.1 = (bf16[256,2048]{1,0:T(8,128)(2,1)S(1)}, f32[256,2048]{1,0:T(8,128)S(1)}, f32[256,128]{1,0:T(8,128)S(1)}) custom-call(bf16[256,2048]{1,0:T(8,128)(2,1)S(1)} %copy-done.7, bf16[64,512]{1,0:T(8,128)(2,1)S(1)} %project_own.1.refs_1_, bf16[64,512]{1,0:T(8,128)(2,1)S(1)} %collective-permute-done.refs_2_, ...), custom_call_target="tpu_custom_call" | custom-call | flops 2147483648 | bytes 1048576 | tf_op jit(solution)/shard_map/attend_own/pallas_call | solution.py:212
  24.2 1.2 %collective-permute-done.4.refs_1_ = bf16[64,8192]{1,0:T(8,128)(2,1)S(1)} collective-permute-done((bf16[64,8192]{1,0:T(8,128)(2,1)}, bf16[64,8192]{1,0:T(8,128)(2,1)S(1)}, u32[]{:S(2)}, u32[]{:S(2)}) %collective-permute-start.4) | collective-permute-done | bytes 1048608 | tf_op jit(solution)/shard_map/ppermute | solution.py:26
  25.5 3.0 %collective-permute-done.3.refs_0_ = bf16[64,8192]{1,0:T(8,128)(2,1)S(1)} collective-permute-done((bf16[64,8192]{1,0:T(8,128)(2,1)}, bf16[64,8192]{1,0:T(8,128)(2,1)S(1)}, u32[]{:S(2)}, u32[]{:S(2)}) %collective-permute-start.3) | collective-permute-done | bytes 1048608 | tf_op jit(solution)/shard_map/ppermute | solution.py:26
  28.6 2.7 %collective-permute-start.5 = (bf16[64,4096]{1,0:T(8,128)(2,1)S(1)}, bf16[64,4096]{1,0:T(8,128)(2,1)S(1)}, u32[]{:S(2)}, u32[]{:S(2)}) collective-permute-start(bf16[64,4096]{1,0:T(8,128)(2,1)S(1)} %slice.6), channel_id=1, source_target_pairs={{0,3},{1,0},{2,1},{3,2},{4,7},{5,4},{6,5},{7,6},{8,11},{9,8},{10,9... | collective-permute-start | bytes 1572872 | tf_op jit(solution)/shard_map/ppermute | solution.py:26
  31.4 1.4 %project_sides.1.refs_1_ = bf16[128,512]{1,0:T(8,128)(2,1)S(1)} custom-call(bf16[64,8192]{1,0:T(8,128)(2,1)S(1)} %collective-permute-done.3.refs_0_, bf16[64,8192]{1,0:T(8,128)(2,1)S(1)} %collective-permute-done.4.refs_1_, bf16[8192,256]{1,0:T(8,128)(2,1)S(1)} %copy-done.1, bf16[8192,256]{1,0:T(8,128)(2,1)S(1)} %copy-done.3, f32[1,128]{1,0:T(1,128)S(1)} %bitcast.8), custom_call_target="tpu_custom_call" | custom-call | flops 1073741824 | bytes 8388608 | tf_op jit(solution)/shard_map/project_sides/pallas_call | solution.py:56
  32.8 5.3 %collective-permute-start.12 = (bf16[128,512]{1,0:T(8,128)(2,1)S(1)}, bf16[128,512]{1,0:T(8,128)(2,1)S(1)}, u32[]{:S(2)}, u32[]{:S(2)}) collective-permute-start(bf16[128,512]{1,0:T(8,128)(2,1)S(1)} %project_sides.1.refs_1_), channel_id=1, source_target_pairs={{0,12},{4,16},{8,20},{12,24},{16,28},{20,32},{24,36},{28,40},{32,4... | collective-permute-start | bytes 393224 | tf_op jit(solution)/shard_map/ppermute | solution.py:26
  38.5 2.9 %collective-permute-done.6.rows_ref = bf16[64,4096]{1,0:T(8,128)(2,1)S(1)} collective-permute-done((bf16[64,4096]{1,0:T(8,128)(2,1)S(1)}, bf16[64,4096]{1,0:T(8,128)(2,1)S(1)}, u32[]{:S(2)}, u32[]{:S(2)}) %collective-permute-start.6) | collective-permute-done | bytes 524320 | tf_op jit(solution)/shard_map/ppermute | solution.py:26
  41.3 0.8 %project_across_first.1.sums_ref = f32[64,512]{1,0:T(8,128)S(1)} custom-call(bf16[64,4096]{1,0:T(8,128)(2,1)S(1)} %collective-permute-done.6.rows_ref, bf16[8192,256]{1,0:T(8,128)(2,1)S(1)} %copy-done.1, bf16[8192,256]{1,0:T(8,128)(2,1)S(1)} %copy-done.3), custom_call_target="tpu_custom_call" | custom-call | flops 268435456 | bytes 8388608 | tf_op jit(solution)/shard_map/project_across_first/pallas_call | solution.py:92
  42.2 0.9 %project_across_last.1.refs_1_ = bf16[64,512]{1,0:T(8,128)(2,1)S(1)} custom-call(bf16[64,4096]{1,0:T(8,128)(2,1)S(1)} %collective-permute-done.5.rows_ref, f32[64,512]{1,0:T(8,128)S(1)} %project_across_first.1.sums_ref, bf16[8192,256]{1,0:T(8,128)(2,1)S(1)} %copy-done.1, bf16[8192,256]{1,0:T(8,128)(2,1)S(1)} %copy-done.3, f32[1,128]{1,0:T(1,128)S(1)} %bitcast.9), custom_call_target="tpu_custom_call" | custom-call | flops 268435456 | bytes 8388608 | tf_op jit(solution)/shard_map/project_across_last/pallas_call | solution.py:100
  43.1 5.7 %collective-permute-start.9 = (bf16[64,512]{1,0:T(8,128)(2,1)S(1)}, bf16[64,512]{1,0:T(8,128)(2,1)S(1)}, u32[]{:S(2)}, u32[]{:S(2)}) collective-permute-start(bf16[64,512]{1,0:T(8,128)(2,1)S(1)} %project_across_last.1.refs_1_), channel_id=1, source_target_pairs={{0,12},{4,16},{8,20},{12,24},{16,28},{20,32},{24,36},{28,40},{32,4... | collective-permute-start | bytes 196616 | tf_op jit(solution)/shard_map/ppermute | solution.py:26
  48.8 0.4 collective-permute-start.8
  49.2 2.6 %attend_sides.1 = (f32[256,2048]{1,0:T(8,128)S(1)}, f32[256,128]{1,0:T(8,128)S(1)}) custom-call(bf16[256,2048]{1,0:T(8,128)(2,1)S(1)} %get-tuple-element.22.refs_0_, bf16[128,512]{1,0:T(8,128)(2,1)S(1)} %project_sides.1.refs_1_, bf16[128,512]{1,0:T(8,128)(2,1)S(1)} %collective-permute-done.10.refs_2_, bf16[128,512]{1,0:T(8,128)(2,1)S(1)} %collective-permute-done.11.refs_3_, ...), custom_call_target="tpu_custom_call" | custom-call | flops 4294967296 | bytes 1048576 | tf_op jit(solution)/shard_map/attend_sides/pallas_call | solution.py:212
  51.8 4.9 %collective-permute-done.9.refs_4_ = bf16[64,512]{1,0:T(8,128)(2,1)S(1)} collective-permute-done((bf16[64,512]{1,0:T(8,128)(2,1)S(1)}, bf16[64,512]{1,0:T(8,128)(2,1)S(1)}, u32[]{:S(2)}, u32[]{:S(2)}) %collective-permute-start.9) | collective-permute-done | bytes 65568 | tf_op jit(solution)/shard_map/ppermute | solution.py:26
  56.8 2.2 %attend_across.1 = bf16[256,2048]{1,0:T(8,128)(2,1)} custom-call(bf16[256,2048]{1,0:T(8,128)(2,1)S(1)} %get-tuple-element.22.refs_0_, bf16[64,512]{1,0:T(8,128)(2,1)S(1)} %project_across_last.1.refs_1_, bf16[64,512]{1,0:T(8,128)(2,1)S(1)} %collective-permute-done.7.refs_2_, bf16[64,512]{1,0:T(8,128)(2,1)S(1)} %collective-permute-done.8.refs_3_, ...), custom_call_target="tpu_custom_call" | custom-call | flops 2147483648 | bytes 1048576 | tf_op jit(solution)/shard_map/attend_across/pallas_call | solution.py:212
  (37 shorter events, 0.9 us)
Async XLA Ops:
  0.0 25.5 %collective-permute-start.4 = (bf16[64,8192]{1,0:T(8,128)(2,1)}, bf16[64,8192]{1,0:T(8,128)(2,1)S(1)}, u32[]{:S(2)}, u32[]{:S(2)}) collective-permute-start(bf16[64,8192]{1,0:T(8,128)(2,1)} %refs_0_.2), channel_id=1, source_target_pairs={{0,3},{1,0},{2,1},{3,2},{4,7},{5,4},{6,5},{7,6},{8,11},{9,8},{10,9... | collective-permute-start | bytes 3145736 | tf_op jit(solution)/shard_map/ppermute | solution.py:26
  3.3 25.1 %collective-permute-start.3 = (bf16[64,8192]{1,0:T(8,128)(2,1)}, bf16[64,8192]{1,0:T(8,128)(2,1)S(1)}, u32[]{:S(2)}, u32[]{:S(2)}) collective-permute-start(bf16[64,8192]{1,0:T(8,128)(2,1)} %refs_0_.2), channel_id=1, source_target_pairs={{0,1},{1,2},{2,3},{3,0},{4,5},{5,6},{6,7},{7,4},{8,9},{9,10},{10,1... | collective-permute-start | bytes 3145736 | tf_op jit(solution)/shard_map/ppermute | solution.py:26
  3.3 2.2 %copy-start = (bf16[8192,256]{1,0:T(8,128)(2,1)S(1)}, bf16[8192,256]{1,0:T(8,128)(2,1)}, u32[]{:S(2)}) copy-start(bf16[8192,256]{1,0:T(8,128)(2,1)} %key_ref.3) | copy-start | bytes 12582916
  5.5 2.2 %copy-start.2 = (bf16[8192,256]{1,0:T(8,128)(2,1)S(1)}, bf16[8192,256]{1,0:T(8,128)(2,1)}, u32[]{:S(2)}) copy-start(bf16[8192,256]{1,0:T(8,128)(2,1)} %value_ref.3) | copy-start | bytes 12582916
  7.7 1.2 %copy-start.4 = (bf16[64,8192]{1,0:T(8,128)(2,1)S(1)}, bf16[64,8192]{1,0:T(8,128)(2,1)}, u32[]{:S(2)}) copy-start(bf16[64,8192]{1,0:T(8,128)(2,1)} %refs_0_.2) | copy-start | bytes 3145732
  8.9 0.7 %copy-start.5 = (f32[128]{0:T(128)S(1)}, f32[128]{0:T(128)}, u32[]{:S(2)}) copy-start(f32[128]{0:T(128)} %param.12) | copy-start | bytes 1540
  9.6 11.7 %copy-start.9 = (f32[128]{0:T(128)S(1)}, f32[128]{0:T(128)}, u32[]{:S(2)}) copy-start(f32[128]{0:T(128)} %param.11) | copy-start | bytes 1540
  9.6 11.7 %copy-start.8 = (s32[4,64]{1,0:T(4,128)S(1)}, s32[4,64]{1,0:T(4,128)}, u32[]{:S(2)}) copy-start(s32[4,64]{1,0:T(4,128)} %param.13) | copy-start | bytes 3076
  9.6 12.9 %copy-start.7 = (bf16[256,2048]{1,0:T(8,128)(2,1)S(1)}, bf16[256,2048]{1,0:T(8,128)(2,1)}, u32[]{:S(2)}) copy-start(bf16[256,2048]{1,0:T(8,128)(2,1)} %refs_0_.3) | copy-start | bytes 3145732
  11.2 10.2 %collective-permute-start.2 = (bf16[64,512]{1,0:T(8,128)(2,1)S(1)}, bf16[64,512]{1,0:T(8,128)(2,1)S(1)}, u32[]{:S(2)}, u32[]{:S(2)}) collective-permute-start(bf16[64,512]{1,0:T(8,128)(2,1)S(1)} %project_own.1.refs_1_), channel_id=1, source_target_pairs={{0,12},{4,16},{8,20},{12,24},{16,28},{20,32},{24,36},{28,40},{32,4... | collective-permute-start | bytes 196616 | tf_op jit(solution)/shard_map/ppermute | solution.py:26
  16.9 4.5 %collective-permute-start.1 = (bf16[64,512]{1,0:T(8,128)(2,1)S(1)}, bf16[64,512]{1,0:T(8,128)(2,1)S(1)}, u32[]{:S(2)}, u32[]{:S(2)}) collective-permute-start(bf16[64,512]{1,0:T(8,128)(2,1)S(1)} %project_own.1.refs_1_), channel_id=1, source_target_pairs={{0,8},{4,12},{8,16},{12,20},{16,24},{20,28},{24,32},{28,36},{32,40... | collective-permute-start | bytes 196616 | tf_op jit(solution)/shard_map/ppermute | solution.py:26
  19.2 3.2 %collective-permute-start = (bf16[64,512]{1,0:T(8,128)(2,1)S(1)}, bf16[64,512]{1,0:T(8,128)(2,1)S(1)}, u32[]{:S(2)}, u32[]{:S(2)}) collective-permute-start(bf16[64,512]{1,0:T(8,128)(2,1)S(1)} %project_own.1.refs_1_), channel_id=1, source_target_pairs={{0,4},{4,8},{8,12},{12,16},{16,20},{20,24},{24,28},{28,32},{32,36}... | collective-permute-start | bytes 196616 | tf_op jit(solution)/shard_map/ppermute | solution.py:26
  22.5 8.9 %copy-start.1 = (bf16[8192,256]{1,0:T(8,128)(2,1)S(1)}, bf16[8192,256]{1,0:T(8,128)(2,1)}, u32[]{:S(2)}) copy-start(bf16[8192,256]{1,0:T(8,128)(2,1)} %key_ref.3) | copy-start | bytes 12582916
  22.5 8.9 %copy-start.3 = (bf16[8192,256]{1,0:T(8,128)(2,1)S(1)}, bf16[8192,256]{1,0:T(8,128)(2,1)}, u32[]{:S(2)}) copy-start(bf16[8192,256]{1,0:T(8,128)(2,1)} %value_ref.3) | copy-start | bytes 12582916
  22.5 8.9 %copy-start.6 = (f32[128]{0:T(128)S(1)}, f32[128]{0:T(128)}, u32[]{:S(2)}) copy-start(f32[128]{0:T(128)} %param.12) | copy-start | bytes 1540
  28.5 12.8 %collective-permute-start.6 = (bf16[64,4096]{1,0:T(8,128)(2,1)S(1)}, bf16[64,4096]{1,0:T(8,128)(2,1)S(1)}, u32[]{:S(2)}, u32[]{:S(2)}) collective-permute-start(bf16[64,4096]{1,0:T(8,128)(2,1)S(1)} %slice.7), channel_id=1, source_target_pairs={{0,1},{1,2},{2,3},{3,0},{4,5},{5,6},{6,7},{7,4},{8,9},{9,10},{10,1... | collective-permute-start | bytes 1572872 | tf_op jit(solution)/shard_map/ppermute | solution.py:26
  28.6 13.5 %collective-permute-start.5 = (bf16[64,4096]{1,0:T(8,128)(2,1)S(1)}, bf16[64,4096]{1,0:T(8,128)(2,1)S(1)}, u32[]{:S(2)}, u32[]{:S(2)}) collective-permute-start(bf16[64,4096]{1,0:T(8,128)(2,1)S(1)} %slice.6), channel_id=1, source_target_pairs={{0,3},{1,0},{2,1},{3,2},{4,7},{5,4},{6,5},{7,6},{8,11},{9,8},{10,9... | collective-permute-start | bytes 1572872 | tf_op jit(solution)/shard_map/ppermute | solution.py:26
  32.8 16.4 %collective-permute-start.12 = (bf16[128,512]{1,0:T(8,128)(2,1)S(1)}, bf16[128,512]{1,0:T(8,128)(2,1)S(1)}, u32[]{:S(2)}, u32[]{:S(2)}) collective-permute-start(bf16[128,512]{1,0:T(8,128)(2,1)S(1)} %project_sides.1.refs_1_), channel_id=1, source_target_pairs={{0,12},{4,16},{8,20},{12,24},{16,28},{20,32},{24,36},{28,40},{32,4... | collective-permute-start | bytes 393224 | tf_op jit(solution)/shard_map/ppermute | solution.py:26
  38.1 11.1 %collective-permute-start.11 = (bf16[128,512]{1,0:T(8,128)(2,1)S(1)}, bf16[128,512]{1,0:T(8,128)(2,1)S(1)}, u32[]{:S(2)}, u32[]{:S(2)}) collective-permute-start(bf16[128,512]{1,0:T(8,128)(2,1)S(1)} %project_sides.1.refs_1_), channel_id=1, source_target_pairs={{0,8},{4,12},{8,16},{12,20},{16,24},{20,28},{24,32},{28,36},{32,40... | collective-permute-start | bytes 393224 | tf_op jit(solution)/shard_map/ppermute | solution.py:26
  38.5 10.7 %collective-permute-start.10 = (bf16[128,512]{1,0:T(8,128)(2,1)S(1)}, bf16[128,512]{1,0:T(8,128)(2,1)S(1)}, u32[]{:S(2)}, u32[]{:S(2)}) collective-permute-start(bf16[128,512]{1,0:T(8,128)(2,1)S(1)} %project_sides.1.refs_1_), channel_id=1, source_target_pairs={{0,4},{4,8},{8,12},{12,16},{16,20},{20,24},{24,28},{28,32},{32,36}... | collective-permute-start | bytes 393224 | tf_op jit(solution)/shard_map/ppermute | solution.py:26
  43.1 13.7 %collective-permute-start.9 = (bf16[64,512]{1,0:T(8,128)(2,1)S(1)}, bf16[64,512]{1,0:T(8,128)(2,1)S(1)}, u32[]{:S(2)}, u32[]{:S(2)}) collective-permute-start(bf16[64,512]{1,0:T(8,128)(2,1)S(1)} %project_across_last.1.refs_1_), channel_id=1, source_target_pairs={{0,12},{4,16},{8,20},{12,24},{16,28},{20,32},{24,36},{28,40},{32,4... | collective-permute-start | bytes 196616 | tf_op jit(solution)/shard_map/ppermute | solution.py:26
  48.8 8.0 %collective-permute-start.8 = (bf16[64,512]{1,0:T(8,128)(2,1)S(1)}, bf16[64,512]{1,0:T(8,128)(2,1)S(1)}, u32[]{:S(2)}, u32[]{:S(2)}) collective-permute-start(bf16[64,512]{1,0:T(8,128)(2,1)S(1)} %project_across_last.1.refs_1_), channel_id=1, source_target_pairs={{0,8},{4,12},{8,16},{12,20},{16,24},{20,28},{24,32},{28,36},{32,40... | collective-permute-start | bytes 196616 | tf_op jit(solution)/shard_map/ppermute | solution.py:26
  49.2 7.6 %collective-permute-start.7 = (bf16[64,512]{1,0:T(8,128)(2,1)S(1)}, bf16[64,512]{1,0:T(8,128)(2,1)S(1)}, u32[]{:S(2)}, u32[]{:S(2)}) collective-permute-start(bf16[64,512]{1,0:T(8,128)(2,1)S(1)} %project_across_last.1.refs_1_), channel_id=1, source_target_pairs={{0,4},{4,8},{8,12},{12,16},{16,20},{20,24},{24,28},{28,32},{32,36}... | collective-permute-start | bytes 196616 | tf_op jit(solution)/shard_map/ppermute | solution.py:26

commit v9 on v8

--- a/solution.py
+++ b/solution.py
@@ -64,46 +64,45 @@
     )(*row_parts, key_matrix, value_matrix, key_gain)
 
 
-def first_columns_kernel(rows_ref, key_ref, value_ref, out_ref):
+def last_half_kernel(rows_ref, key_ref, value_ref, out_ref):
     depth, width = rows_ref.shape[1], key_ref.shape[1]
     rows = rows_ref[...]
-    out_ref[:, :width] = jnp.dot(rows, key_ref[:depth], preferred_element_type=jnp.float32)
-    out_ref[:, width:] = jnp.dot(rows, value_ref[:depth], preferred_element_type=jnp.float32)
-
-
-def last_columns_kernel(rows_ref, sums_ref, key_ref, value_ref, gain_ref, out_ref):
-    width = key_ref.shape[1]
-    before = key_ref.shape[0] - rows_ref.shape[1]
+    out_ref[:, :width] = jnp.dot(rows, key_ref[depth:], preferred_element_type=jnp.float32)
+    out_ref[:, width:] = jnp.dot(rows, value_ref[depth:], preferred_element_type=jnp.float32)
+
+
+def first_half_kernel(rows_ref, sums_ref, key_ref, value_ref, gain_ref, out_ref):
+    depth, width = rows_ref.shape[1], key_ref.shape[1]
     rows = rows_ref[...]
-    keys = jnp.dot(rows, key_ref[before:], preferred_element_type=jnp.float32)
-    values = jnp.dot(rows, value_ref[before:], preferred_element_type=jnp.float32)
+    keys = jnp.dot(rows, key_ref[:depth], preferred_element_type=jnp.float32)
+    values = jnp.dot(rows, value_ref[:depth], preferred_element_type=jnp.float32)
     write_keys_values(
         sums_ref[:, :width] + keys, sums_ref[:, width:] + values, gain_ref, out_ref
     )
 
 
-def project_by_columns(first_part, last_part, key_matrix, value_matrix, key_gain, name):
-    rows, width = first_part.shape[0], key_matrix.shape[1]
+def project_by_halves(first_half, last_half, key_matrix, value_matrix, key_gain, name):
+    rows, width = first_half.shape[0], key_matrix.shape[1]
     params = dict(
         out_specs=WHOLE,
         cost_estimate=project_cost(rows // 2, key_matrix),
         compiler_params=pltpu.CompilerParams(vmem_limit_bytes=PROJECT_VMEM),
     )
     sums = pl.pallas_call(
-        first_columns_kernel,
+        last_half_kernel,
         out_shape=jax.ShapeDtypeStruct((rows, 2 * width), jnp.float32),
         in_specs=[WHOLE] * 3,
-        name=name + "_first",
+        name=name + "_last_half",
         **params,
-    )(first_part, key_matrix, value_matrix)
-    last_part = after(last_part, sums)
+    )(last_half, key_matrix, value_matrix)
+    first_half = after(first_half, sums)
     return pl.pallas_call(
-        last_columns_kernel,
+        first_half_kernel,
         out_shape=jax.ShapeDtypeStruct((rows, 2 * width), jnp.bfloat16),
         in_specs=[WHOLE] * 5,
-        name=name + "_last",
+        name=name + "_first_half",
         **params,
-    )(last_part, sums, key_matrix, value_matrix, key_gain)
+    )(first_half, sums, key_matrix, value_matrix, key_gain)
 
 
 def attend_kernel(first, last, kv_heads, *refs):
@@ -251,14 +250,15 @@
     )
 
     half = vision.shape[1] // 2
-    left, right = after((left, right), carried)
-    first_across = turned(left[:, :half], "tp", 1)
-    last_across = turned(right[:, half:], "tp", -1)
+    right = after(right, carried)
+    last_half = turned(right[:, half:], "tp", -1)
+    left = after(left, carried)
+    first_half = turned(left[:, :half], "tp", 1)
     sides = projected([left, right], "sides")
     side_blocks = reached(sides)
-    first_across = after(first_across, sides)
-    across = project_by_columns(
-        first_across, last_across, key_matrix, value_matrix, key_gain, "project_across"
+    last_half = after(last_half, sides)
+    across = project_by_halves(
+        first_half, last_half, key_matrix, value_matrix, key_gain, "project_across"
     )
     across_blocks = reached(across)
     side_blocks = after(side_blocks, across)

time: 59.4 us -> 59 us (level)
  transfers between devices with their start and end apart: 13 -> 13, of which waited for: 5 -> 5; matrix products, arithmetic and copies ran while one was open for 0% -> 1% of each run, Pallas kernels for 16% -> 16%
where the time goes in v9:
time: 59 us; the launch traced here: 58.7 us
  starting transfers between devices  27.8 us (47%)
  waiting for transfers between devices  12.6 us (21%)
  Pallas kernels  11.4 us (19%)
  local copies, waits for them, and re-layouts  6.36 us (11%)
    ppermute x13, starting transfers between devices, turned(): return lax.ppermute(value, axis, pairs)  27.8 us
    ppermute x13, waiting for transfers between devices, turned(): return lax.ppermute(value, axis, pairs)  12.6 us
    pallas_call x3, Pallas kernels, attend(): pl.pallas_call(functools.partial(attend_kernel, first, last, kv_heads), o...  6.59 us
    unnamed x20, local copies, waits for them, and re-layouts  6.28 us
    pallas_call x2, Pallas kernels, project(): pl.pallas_call(project_kernel, out_shape=jax.ShapeDtypeStruct((rows, 2 *...  3.05 us
  transfers between devices with their start and end apart: 13, of which 5 were waited for; matrix products, arithmetic and copies ran while one was open for 1% of the time, Pallas kernels for 16%

profile of v9, /device:TPU:1, one launch (start us, length us, event | category | flops | bytes accessed | tf_op | source)
XLA Modules:
  0.0 58.7 jit_solution(10408065673299598745)
XLA Ops:
  0.0 3.3 %collective-permute-start.5 = (bf16[64,8192]{1,0:T(8,128)(2,1)}, bf16[64,8192]{1,0:T(8,128)(2,1)S(1)}, u32[]{:S(2)}, u32[]{:S(2)}) collective-permute-start(bf16[64,8192]{1,0:T(8,128)(2,1)} %refs_0_.2), channel_id=1, source_target_pairs={{0,3},{1,0},{2,1},{3,2},{4,7},{5,4},{6,5},{7,6},{8,11},{9,8},{10,9... | collective-permute-start | bytes 3145736 | tf_op jit(solution)/shard_map/ppermute | solution.py:26
  3.3 2.2 %copy-done = bf16[8192,256]{1,0:T(8,128)(2,1)S(1)} copy-done((bf16[8192,256]{1,0:T(8,128)(2,1)S(1)}, bf16[8192,256]{1,0:T(8,128)(2,1)}, u32[]{:S(2)}) %copy-start) | copy-done | bytes 4194328
  5.5 2.2 %copy-done.2 = bf16[8192,256]{1,0:T(8,128)(2,1)S(1)} copy-done((bf16[8192,256]{1,0:T(8,128)(2,1)S(1)}, bf16[8192,256]{1,0:T(8,128)(2,1)}, u32[]{:S(2)}) %copy-start.2) | copy-done | bytes 4194328
  7.7 1.2 %copy-done.4 = bf16[64,8192]{1,0:T(8,128)(2,1)S(1)} copy-done((bf16[64,8192]{1,0:T(8,128)(2,1)S(1)}, bf16[64,8192]{1,0:T(8,128)(2,1)}, u32[]{:S(2)}) %copy-start.4) | copy-done | bytes 1048600
  8.9 0.7 %copy-done.5 = f32[128]{0:T(128)S(1)} copy-done((f32[128]{0:T(128)S(1)}, f32[128]{0:T(128)}, u32[]{:S(2)}) %copy-start.5) | copy-done | bytes 536
  9.6 1.6 %project_own.1.refs_1_ = bf16[64,512]{1,0:T(8,128)(2,1)S(1)} custom-call(bf16[64,8192]{1,0:T(8,128)(2,1)S(1)} %copy-done.4, bf16[8192,256]{1,0:T(8,128)(2,1)S(1)} %copy-done, bf16[8192,256]{1,0:T(8,128)(2,1)S(1)} %copy-done.2, f32[1,128]{1,0:T(1,128)S(1)} %bitcast.7), custom_call_target="tpu_custom_call" | custom-call | flops 536870912 | bytes 8388608 | tf_op jit(solution)/shard_map/project_own/pallas_call | solution.py:56
  11.2 5.7 %collective-permute-start.2 = (bf16[64,512]{1,0:T(8,128)(2,1)S(1)}, bf16[64,512]{1,0:T(8,128)(2,1)S(1)}, u32[]{:S(2)}, u32[]{:S(2)}) collective-permute-start(bf16[64,512]{1,0:T(8,128)(2,1)S(1)} %project_own.1.refs_1_), channel_id=1, source_target_pairs={{0,12},{4,16},{8,20},{12,24},{16,28},{20,32},{24,36},{28,40},{32,4... | collective-permute-start | bytes 196616 | tf_op jit(solution)/shard_map/ppermute | solution.py:26
  16.9 2.3 %collective-permute-start.1 = (bf16[64,512]{1,0:T(8,128)(2,1)S(1)}, bf16[64,512]{1,0:T(8,128)(2,1)S(1)}, u32[]{:S(2)}, u32[]{:S(2)}) collective-permute-start(bf16[64,512]{1,0:T(8,128)(2,1)S(1)} %project_own.1.refs_1_), channel_id=1, source_target_pairs={{0,8},{4,12},{8,16},{12,20},{16,24},{20,28},{24,32},{28,36},{32,40... | collective-permute-start | bytes 196616 | tf_op jit(solution)/shard_map/ppermute | solution.py:26
  19.2 1.9 %collective-permute-start = (bf16[64,512]{1,0:T(8,128)(2,1)S(1)}, bf16[64,512]{1,0:T(8,128)(2,1)S(1)}, u32[]{:S(2)}, u32[]{:S(2)}) collective-permute-start(bf16[64,512]{1,0:T(8,128)(2,1)S(1)} %project_own.1.refs_1_), channel_id=1, source_target_pairs={{0,4},{4,8},{8,12},{12,16},{16,20},{20,24},{24,28},{28,32},{32,36}... | collective-permute-start | bytes 196616 | tf_op jit(solution)/shard_map/ppermute | solution.py:26
  21.4 1.0 %collective-permute-done.refs_2_ = bf16[64,512]{1,0:T(8,128)(2,1)S(1)} collective-permute-done((bf16[64,512]{1,0:T(8,128)(2,1)S(1)}, bf16[64,512]{1,0:T(8,128)(2,1)S(1)}, u32[]{:S(2)}, u32[]{:S(2)}) %collective-permute-start) | collective-permute-done | bytes 65568 | tf_op jit(solution)/shard_map/ppermute | solution.py:26
  22.5 1.7 %attend_own.1 = (bf16[256,2048]{1,0:T(8,128)(2,1)S(1)}, f32[256,2048]{1,0:T(8,128)S(1)}, f32[256,128]{1,0:T(8,128)S(1)}) custom-call(bf16[256,2048]{1,0:T(8,128)(2,1)S(1)} %copy-done.7, bf16[64,512]{1,0:T(8,128)(2,1)S(1)} %project_own.1.refs_1_, bf16[64,512]{1,0:T(8,128)(2,1)S(1)} %collective-permute-done.refs_2_, ...), custom_call_target="tpu_custom_call" | custom-call | flops 2147483648 | bytes 1048576 | tf_op jit(solution)/shard_map/attend_own/pallas_call | solution.py:211
  24.2 1.2 %collective-permute-done.5.refs_1_ = bf16[64,8192]{1,0:T(8,128)(2,1)S(1)} collective-permute-done((bf16[64,8192]{1,0:T(8,128)(2,1)}, bf16[64,8192]{1,0:T(8,128)(2,1)S(1)}, u32[]{:S(2)}, u32[]{:S(2)}) %collective-permute-start.5) | collective-permute-done | bytes 1048608 | tf_op jit(solution)/shard_map/ppermute | solution.py:26
  25.5 3.4 %collective-permute-start.6 = (bf16[64,4096]{1,0:T(8,128)(2,1)S(1)}, bf16[64,4096]{1,0:T(8,128)(2,1)S(1)}, u32[]{:S(2)}, u32[]{:S(2)}) collective-permute-start(bf16[64,4096]{1,0:T(8,128)(2,1)S(1)} %slice.7), channel_id=1, source_target_pairs={{0,3},{1,0},{2,1},{3,2},{4,7},{5,4},{6,5},{7,6},{8,11},{9,8},{10,9... | collective-permute-start | bytes 1572872 | tf_op jit(solution)/shard_map/ppermute | solution.py:26
  29.0 1.4 %project_sides.1.refs_1_ = bf16[128,512]{1,0:T(8,128)(2,1)S(1)} custom-call(bf16[64,8192]{1,0:T(8,128)(2,1)S(1)} %collective-permute-done.3.refs_0_, bf16[64,8192]{1,0:T(8,128)(2,1)S(1)} %collective-permute-done.5.refs_1_, bf16[8192,256]{1,0:T(8,128)(2,1)S(1)} %copy-done.1, bf16[8192,256]{1,0:T(8,128)(2,1)S(1)} %copy-done.3, f32[1,128]{1,0:T(1,128)S(1)} %bitcast.8), custom_call_target="tpu_custom_call" | custom-call | flops 1073741824 | bytes 8388608 | tf_op jit(solution)/shard_map/project_sides/pallas_call | solution.py:56
  30.4 4.7 %collective-permute-start.12 = (bf16[128,512]{1,0:T(8,128)(2,1)S(1)}, bf16[128,512]{1,0:T(8,128)(2,1)S(1)}, u32[]{:S(2)}, u32[]{:S(2)}) collective-permute-start(bf16[128,512]{1,0:T(8,128)(2,1)S(1)} %project_sides.1.refs_1_), channel_id=1, source_target_pairs={{0,12},{4,16},{8,20},{12,24},{16,28},{20,32},{24,36},{28,40},{32,4... | collective-permute-start | bytes 393224 | tf_op jit(solution)/shard_map/ppermute | solution.py:26
  35.6 3.0 %collective-permute-done.6.rows_ref = bf16[64,4096]{1,0:T(8,128)(2,1)S(1)} collective-permute-done((bf16[64,4096]{1,0:T(8,128)(2,1)S(1)}, bf16[64,4096]{1,0:T(8,128)(2,1)S(1)}, u32[]{:S(2)}, u32[]{:S(2)}) %collective-permute-start.6) | collective-permute-done | bytes 524320 | tf_op jit(solution)/shard_map/ppermute | solution.py:26
  38.5 0.8 %project_across_last_half.1.sums_ref = f32[64,512]{1,0:T(8,128)S(1)} custom-call(bf16[64,4096]{1,0:T(8,128)(2,1)S(1)} %collective-permute-done.6.rows_ref, bf16[8192,256]{1,0:T(8,128)(2,1)S(1)} %copy-done.1, bf16[8192,256]{1,0:T(8,128)(2,1)S(1)} %copy-done.3), custom_call_target="tpu_custom_call" | custom-call | flops 268435456 | bytes 8388608 | tf_op jit(solution)/shard_map/project_across_last_half/pallas_call | solution.py:91
  39.4 2.4 %collective-permute-done.4.rows_ref = bf16[64,4096]{1,0:T(8,128)(2,1)S(1)} collective-permute-done((bf16[64,4096]{1,0:T(8,128)(2,1)S(1)}, bf16[64,4096]{1,0:T(8,128)(2,1)S(1)}, u32[]{:S(2)}, u32[]{:S(2)}) %collective-permute-start.4) | collective-permute-done | bytes 524320 | tf_op jit(solution)/shard_map/ppermute | solution.py:26
  41.8 0.9 %project_across_first_half.1.refs_1_ = bf16[64,512]{1,0:T(8,128)(2,1)S(1)} custom-call(bf16[64,4096]{1,0:T(8,128)(2,1)S(1)} %collective-permute-done.4.rows_ref, f32[64,512]{1,0:T(8,128)S(1)} %project_across_last_half.1.sums_ref, bf16[8192,256]{1,0:T(8,128)(2,1)S(1)} %copy-done.1, bf16[8192,256]{1,0:T(8,128)(2,1)S(1)} %copy-done.3, f32[1,128]{1,0:T(1,128)S(1)} %bitcast.9), custom_call_target="tpu_custom_call" | custom-call | flops 268435456 | bytes 8388608 | tf_op jit(solution)/shard_map/project_across_first_half/pallas_call | solution.py:99
  42.7 5.6 %collective-permute-start.9 = (bf16[64,512]{1,0:T(8,128)(2,1)S(1)}, bf16[64,512]{1,0:T(8,128)(2,1)S(1)}, u32[]{:S(2)}, u32[]{:S(2)}) collective-permute-start(bf16[64,512]{1,0:T(8,128)(2,1)S(1)} %project_across_first_half.1.refs_1_), channel_id=1, source_target_pairs={{0,12},{4,16},{8,20},{12,24},{16,28},{20,32},{24,36},{28,40},{32,4... | collective-permute-start | bytes 196616 | tf_op jit(solution)/shard_map/ppermute | solution.py:26
  48.4 0.4 collective-permute-start.8
  48.8 2.6 %attend_sides.1 = (f32[256,2048]{1,0:T(8,128)S(1)}, f32[256,128]{1,0:T(8,128)S(1)}) custom-call(bf16[256,2048]{1,0:T(8,128)(2,1)S(1)} %get-tuple-element.22.refs_0_, bf16[128,512]{1,0:T(8,128)(2,1)S(1)} %project_sides.1.refs_1_, bf16[128,512]{1,0:T(8,128)(2,1)S(1)} %collective-permute-done.10.refs_2_, bf16[128,512]{1,0:T(8,128)(2,1)S(1)} %collective-permute-done.11.refs_3_, ...), custom_call_target="tpu_custom_call" | custom-call | flops 4294967296 | bytes 1048576 | tf_op jit(solution)/shard_map/attend_sides/pallas_call | solution.py:211
  51.4 4.9 %collective-permute-done.9.refs_4_ = bf16[64,512]{1,0:T(8,128)(2,1)S(1)} collective-permute-done((bf16[64,512]{1,0:T(8,128)(2,1)S(1)}, bf16[64,512]{1,0:T(8,128)(2,1)S(1)}, u32[]{:S(2)}, u32[]{:S(2)}) %collective-permute-start.9) | collective-permute-done | bytes 65568 | tf_op jit(solution)/shard_map/ppermute | solution.py:26
  56.4 2.2 %attend_across.1 = bf16[256,2048]{1,0:T(8,128)(2,1)} custom-call(bf16[256,2048]{1,0:T(8,128)(2,1)S(1)} %get-tuple-element.22.refs_0_, bf16[64,512]{1,0:T(8,128)(2,1)S(1)} %project_across_first_half.1.refs_1_, bf16[64,512]{1,0:T(8,128)(2,1)S(1)} %collective-permute-done.7.refs_2_, bf16[64,512]{1,0:T(8,128)(2,1)S(1)} %collective-permute-done.8.refs_3_, ...), custom_call_target="tpu_custom_call" | custom-call | flops 2147483648 | bytes 1048576 | tf_op jit(solution)/shard_map/attend_across/pallas_call | solution.py:211
  (37 shorter events, 0.9 us)
Async XLA Ops:
  0.0 25.5 %collective-permute-start.5 = (bf16[64,8192]{1,0:T(8,128)(2,1)}, bf16[64,8192]{1,0:T(8,128)(2,1)S(1)}, u32[]{:S(2)}, u32[]{:S(2)}) collective-permute-start(bf16[64,8192]{1,0:T(8,128)(2,1)} %refs_0_.2), channel_id=1, source_target_pairs={{0,3},{1,0},{2,1},{3,2},{4,7},{5,4},{6,5},{7,6},{8,11},{9,8},{10,9... | collective-permute-start | bytes 3145736 | tf_op jit(solution)/shard_map/ppermute | solution.py:26
  3.3 25.6 %collective-permute-start.3 = (bf16[64,8192]{1,0:T(8,128)(2,1)}, bf16[64,8192]{1,0:T(8,128)(2,1)S(1)}, u32[]{:S(2)}, u32[]{:S(2)}) collective-permute-start(bf16[64,8192]{1,0:T(8,128)(2,1)} %refs_0_.2), channel_id=1, source_target_pairs={{0,1},{1,2},{2,3},{3,0},{4,5},{5,6},{6,7},{7,4},{8,9},{9,10},{10,1... | collective-permute-start | bytes 3145736 | tf_op jit(solution)/shard_map/ppermute | solution.py:26
  3.3 2.2 %copy-start = (bf16[8192,256]{1,0:T(8,128)(2,1)S(1)}, bf16[8192,256]{1,0:T(8,128)(2,1)}, u32[]{:S(2)}) copy-start(bf16[8192,256]{1,0:T(8,128)(2,1)} %key_ref.3) | copy-start | bytes 12582916
  5.5 2.2 %copy-start.2 = (bf16[8192,256]{1,0:T(8,128)(2,1)S(1)}, bf16[8192,256]{1,0:T(8,128)(2,1)}, u32[]{:S(2)}) copy-start(bf16[8192,256]{1,0:T(8,128)(2,1)} %value_ref.3) | copy-start | bytes 12582916
  7.7 1.2 %copy-start.4 = (bf16[64,8192]{1,0:T(8,128)(2,1)S(1)}, bf16[64,8192]{1,0:T(8,128)(2,1)}, u32[]{:S(2)}) copy-start(bf16[64,8192]{1,0:T(8,128)(2,1)} %refs_0_.2) | copy-start | bytes 3145732
  8.9 0.7 %copy-start.5 = (f32[128]{0:T(128)S(1)}, f32[128]{0:T(128)}, u32[]{:S(2)}) copy-start(f32[128]{0:T(128)} %param.12) | copy-start | bytes 1540
  9.6 11.7 %copy-start.9 = (f32[128]{0:T(128)S(1)}, f32[128]{0:T(128)}, u32[]{:S(2)}) copy-start(f32[128]{0:T(128)} %param.11) | copy-start | bytes 1540
  9.6 11.7 %copy-start.8 = (s32[4,64]{1,0:T(4,128)S(1)}, s32[4,64]{1,0:T(4,128)}, u32[]{:S(2)}) copy-start(s32[4,64]{1,0:T(4,128)} %param.13) | copy-start | bytes 3076
  9.6 12.9 %copy-start.7 = (bf16[256,2048]{1,0:T(8,128)(2,1)S(1)}, bf16[256,2048]{1,0:T(8,128)(2,1)}, u32[]{:S(2)}) copy-start(bf16[256,2048]{1,0:T(8,128)(2,1)} %refs_0_.3) | copy-start | bytes 3145732
  11.2 10.2 %collective-permute-start.2 = (bf16[64,512]{1,0:T(8,128)(2,1)S(1)}, bf16[64,512]{1,0:T(8,128)(2,1)S(1)}, u32[]{:S(2)}, u32[]{:S(2)}) collective-permute-start(bf16[64,512]{1,0:T(8,128)(2,1)S(1)} %project_own.1.refs_1_), channel_id=1, source_target_pairs={{0,12},{4,16},{8,20},{12,24},{16,28},{20,32},{24,36},{28,40},{32,4... | collective-permute-start | bytes 196616 | tf_op jit(solution)/shard_map/ppermute | solution.py:26
  16.9 4.5 %collective-permute-start.1 = (bf16[64,512]{1,0:T(8,128)(2,1)S(1)}, bf16[64,512]{1,0:T(8,128)(2,1)S(1)}, u32[]{:S(2)}, u32[]{:S(2)}) collective-permute-start(bf16[64,512]{1,0:T(8,128)(2,1)S(1)} %project_own.1.refs_1_), channel_id=1, source_target_pairs={{0,8},{4,12},{8,16},{12,20},{16,24},{20,28},{24,32},{28,36},{32,40... | collective-permute-start | bytes 196616 | tf_op jit(solution)/shard_map/ppermute | solution.py:26
  19.2 3.2 %collective-permute-start = (bf16[64,512]{1,0:T(8,128)(2,1)S(1)}, bf16[64,512]{1,0:T(8,128)(2,1)S(1)}, u32[]{:S(2)}, u32[]{:S(2)}) collective-permute-start(bf16[64,512]{1,0:T(8,128)(2,1)S(1)} %project_own.1.refs_1_), channel_id=1, source_target_pairs={{0,4},{4,8},{8,12},{12,16},{16,20},{20,24},{24,28},{28,32},{32,36}... | collective-permute-start | bytes 196616 | tf_op jit(solution)/shard_map/ppermute | solution.py:26
  22.5 6.5 %copy-start.1 = (bf16[8192,256]{1,0:T(8,128)(2,1)S(1)}, bf16[8192,256]{1,0:T(8,128)(2,1)}, u32[]{:S(2)}) copy-start(bf16[8192,256]{1,0:T(8,128)(2,1)} %key_ref.3) | copy-start | bytes 12582916
  22.5 6.5 %copy-start.3 = (bf16[8192,256]{1,0:T(8,128)(2,1)S(1)}, bf16[8192,256]{1,0:T(8,128)(2,1)}, u32[]{:S(2)}) copy-start(bf16[8192,256]{1,0:T(8,128)(2,1)} %value_ref.3) | copy-start | bytes 12582916
  22.5 6.5 %copy-start.6 = (f32[128]{0:T(128)S(1)}, f32[128]{0:T(128)}, u32[]{:S(2)}) copy-start(f32[128]{0:T(128)} %param.12) | copy-start | bytes 1540
  25.5 13.1 %collective-permute-start.6 = (bf16[64,4096]{1,0:T(8,128)(2,1)S(1)}, bf16[64,4096]{1,0:T(8,128)(2,1)S(1)}, u32[]{:S(2)}, u32[]{:S(2)}) collective-permute-start(bf16[64,4096]{1,0:T(8,128)(2,1)S(1)} %slice.7), channel_id=1, source_target_pairs={{0,3},{1,0},{2,1},{3,2},{4,7},{5,4},{6,5},{7,6},{8,11},{9,8},{10,9... | collective-permute-start | bytes 1572872 | tf_op jit(solution)/shard_map/ppermute | solution.py:26
  28.9 12.9 %collective-permute-start.4 = (bf16[64,4096]{1,0:T(8,128)(2,1)S(1)}, bf16[64,4096]{1,0:T(8,128)(2,1)S(1)}, u32[]{:S(2)}, u32[]{:S(2)}) collective-permute-start(bf16[64,4096]{1,0:T(8,128)(2,1)S(1)} %slice.6), channel_id=1, source_target_pairs={{0,1},{1,2},{2,3},{3,0},{4,5},{5,6},{6,7},{7,4},{8,9},{9,10},{10,1... | collective-permute-start | bytes 1572872 | tf_op jit(solution)/shard_map/ppermute | solution.py:26
  30.4 18.3 %collective-permute-start.12 = (bf16[128,512]{1,0:T(8,128)(2,1)S(1)}, bf16[128,512]{1,0:T(8,128)(2,1)S(1)}, u32[]{:S(2)}, u32[]{:S(2)}) collective-permute-start(bf16[128,512]{1,0:T(8,128)(2,1)S(1)} %project_sides.1.refs_1_), channel_id=1, source_target_pairs={{0,12},{4,16},{8,20},{12,24},{16,28},{20,32},{24,36},{28,40},{32,4... | collective-permute-start | bytes 393224 | tf_op jit(solution)/shard_map/ppermute | solution.py:26
  35.2 13.6 %collective-permute-start.11 = (bf16[128,512]{1,0:T(8,128)(2,1)S(1)}, bf16[128,512]{1,0:T(8,128)(2,1)S(1)}, u32[]{:S(2)}, u32[]{:S(2)}) collective-permute-start(bf16[128,512]{1,0:T(8,128)(2,1)S(1)} %project_sides.1.refs_1_), channel_id=1, source_target_pairs={{0,8},{4,12},{8,16},{12,20},{16,24},{20,28},{24,32},{28,36},{32,40... | collective-permute-start | bytes 393224 | tf_op jit(solution)/shard_map/ppermute | solution.py:26
  35.6 13.2 %collective-permute-start.10 = (bf16[128,512]{1,0:T(8,128)(2,1)S(1)}, bf16[128,512]{1,0:T(8,128)(2,1)S(1)}, u32[]{:S(2)}, u32[]{:S(2)}) collective-permute-start(bf16[128,512]{1,0:T(8,128)(2,1)S(1)} %project_sides.1.refs_1_), channel_id=1, source_target_pairs={{0,4},{4,8},{8,12},{12,16},{16,20},{20,24},{24,28},{28,32},{32,36}... | collective-permute-start | bytes 393224 | tf_op jit(solution)/shard_map/ppermute | solution.py:26
  42.7 13.6 %collective-permute-start.9 = (bf16[64,512]{1,0:T(8,128)(2,1)S(1)}, bf16[64,512]{1,0:T(8,128)(2,1)S(1)}, u32[]{:S(2)}, u32[]{:S(2)}) collective-permute-start(bf16[64,512]{1,0:T(8,128)(2,1)S(1)} %project_across_first_half.1.refs_1_), channel_id=1, source_target_pairs={{0,12},{4,16},{8,20},{12,24},{16,28},{20,32},{24,36},{28,40},{32,4... | collective-permute-start | bytes 196616 | tf_op jit(solution)/shard_map/ppermute | solution.py:26
  48.4 8.0 %collective-permute-start.8 = (bf16[64,512]{1,0:T(8,128)(2,1)S(1)}, bf16[64,512]{1,0:T(8,128)(2,1)S(1)}, u32[]{:S(2)}, u32[]{:S(2)}) collective-permute-start(bf16[64,512]{1,0:T(8,128)(2,1)S(1)} %project_across_first_half.1.refs_1_), channel_id=1, source_target_pairs={{0,8},{4,12},{8,16},{12,20},{16,24},{20,28},{24,32},{28,36},{32,40... | collective-permute-start | bytes 196616 | tf_op jit(solution)/shard_map/ppermute | solution.py:26
  48.8 7.6 %collective-permute-start.7 = (bf16[64,512]{1,0:T(8,128)(2,1)S(1)}, bf16[64,512]{1,0:T(8,128)(2,1)S(1)}, u32[]{:S(2)}, u32[]{:S(2)}) collective-permute-start(bf16[64,512]{1,0:T(8,128)(2,1)S(1)} %project_across_first_half.1.refs_1_), channel_id=1, source_target_pairs={{0,4},{4,8},{8,12},{12,16},{16,20},{20,24},{24,28},{28,32},{32,36}... | collective-permute-start | bytes 196616 | tf_op jit(solution)/shard_map/ppermute | solution.py:26

commit v10 on v9

--- a/solution.py
+++ b/solution.py
@@ -155,17 +155,21 @@
         )
         weights = (jnp.exp2(scores) * is_open).astype(jnp.bfloat16)
         both = jnp.dot(weights, values, preferred_element_type=jnp.float32)
+        both = [both[at * rows : (at + 1) * rows] for at in range(group)]
         for at, head in enumerate(heads):
-            sums = both[at * rows : (at + 1) * rows, :HEAD_SIZE]
-            total = both[at * rows : (at + 1) * rows, HEAD_SIZE:]
+            totals = jnp.where(lane == head, both[at][:, HEAD_SIZE:], totals)
+        if last:
+            whole = totals + totals_in[...]
+            safe = jnp.where(whole > 0, whole, jnp.ones_like(whole))
+            inverse = pl.reciprocal(safe, approx=True)
+            inverse = inverse * (2.0 - safe * inverse)
+        for at, head in enumerate(heads):
+            sums = both[at][:, :HEAD_SIZE]
             if not first:
                 sums = sums + sums_in[:, columns(head)]
-                total = total + totals_in[:, head : head + 1]
             if last:
-                safe = jnp.where(total > 0, total, jnp.ones_like(total))
-                inverse = pl.reciprocal(safe, approx=True)
-                inverse = inverse * (2.0 - safe * inverse)
-                held[:, columns(head)] = (sums * inverse).astype(jnp.bfloat16)
+                result = sums * inverse[:, head : head + 1]
+                held[:, columns(head)] = result.astype(jnp.bfloat16)
                 if head % HEADS_OUT == HEADS_OUT - 1:
                     part = pl.ds((head + 1 - HEADS_OUT) * HEAD_SIZE, HEADS_OUT * HEAD_SIZE)
                     copies.append(
@@ -176,7 +180,8 @@
                     copies[-1].start()
             else:
                 refs[0][:, columns(head)] = sums
-                totals = jnp.where(lane == head, total, totals)
+    if not first:
+        totals = totals + totals_in[...]
     if not last:
         refs[1][...] = totals
     for copy in copies:

time: 59 us -> 59.6 us (1.010)
  Pallas kernels: 11.4 us -> 12 us
  transfers between devices with their start and end apart: 13 -> 13, of which waited for: 5 -> 5; matrix products, arithmetic and copies ran while one was open for 1% -> 1% of each run, Pallas kernels for 16% -> 15%
where the time goes in v10:
time: 59.6 us; the launch traced here: 59.3 us
  starting transfers between devices  27.8 us (47%)
  waiting for transfers between devices  12.6 us (21%)
  Pallas kernels  12 us (20%)
  local copies, waits for them, and re-layouts  6.36 us (11%)
    ppermute x13, starting transfers between devices, turned(): return lax.ppermute(value, axis, pairs)  27.8 us
    ppermute x13, waiting for transfers between devices, turned(): return lax.ppermute(value, axis, pairs)  12.6 us
    pallas_call x3, Pallas kernels, attend(): pl.pallas_call(functools.partial(attend_kernel, first, last, kv_heads), o...  7.16 us
    unnamed x20, local copies, waits for them, and re-layouts  6.28 us
    pallas_call x2, Pallas kernels, project(): pl.pallas_call(project_kernel, out_shape=jax.ShapeDtypeStruct((rows, 2 *...  3.05 us
  transfers between devices with their start and end apart: 13, of which 5 were waited for; matrix products, arithmetic and copies ran while one was open for 1% of the time, Pallas kernels for 15%

profile of v10, /device:TPU:1, one launch (start us, length us, event | category | flops | bytes accessed | tf_op | source)
XLA Modules:
  0.0 59.3 jit_solution(2859445528164051915)
XLA Ops:
  0.0 3.3 %collective-permute-start.5 = (bf16[64,8192]{1,0:T(8,128)(2,1)}, bf16[64,8192]{1,0:T(8,128)(2,1)S(1)}, u32[]{:S(2)}, u32[]{:S(2)}) collective-permute-start(bf16[64,8192]{1,0:T(8,128)(2,1)} %refs_0_.2), channel_id=1, source_target_pairs={{0,3},{1,0},{2,1},{3,2},{4,7},{5,4},{6,5},{7,6},{8,11},{9,8},{10,9... | collective-permute-start | bytes 3145736 | tf_op jit(solution)/shard_map/ppermute | solution.py:26
  3.3 2.2 %copy-done = bf16[8192,256]{1,0:T(8,128)(2,1)S(1)} copy-done((bf16[8192,256]{1,0:T(8,128)(2,1)S(1)}, bf16[8192,256]{1,0:T(8,128)(2,1)}, u32[]{:S(2)}) %copy-start) | copy-done | bytes 4194328
  5.5 2.2 %copy-done.2 = bf16[8192,256]{1,0:T(8,128)(2,1)S(1)} copy-done((bf16[8192,256]{1,0:T(8,128)(2,1)S(1)}, bf16[8192,256]{1,0:T(8,128)(2,1)}, u32[]{:S(2)}) %copy-start.2) | copy-done | bytes 4194328
  7.7 1.2 %copy-done.4 = bf16[64,8192]{1,0:T(8,128)(2,1)S(1)} copy-done((bf16[64,8192]{1,0:T(8,128)(2,1)S(1)}, bf16[64,8192]{1,0:T(8,128)(2,1)}, u32[]{:S(2)}) %copy-start.4) | copy-done | bytes 1048600
  8.9 0.7 %copy-done.5 = f32[128]{0:T(128)S(1)} copy-done((f32[128]{0:T(128)S(1)}, f32[128]{0:T(128)}, u32[]{:S(2)}) %copy-start.5) | copy-done | bytes 536
  9.6 1.6 %project_own.1.refs_1_ = bf16[64,512]{1,0:T(8,128)(2,1)S(1)} custom-call(bf16[64,8192]{1,0:T(8,128)(2,1)S(1)} %copy-done.4, bf16[8192,256]{1,0:T(8,128)(2,1)S(1)} %copy-done, bf16[8192,256]{1,0:T(8,128)(2,1)S(1)} %copy-done.2, f32[1,128]{1,0:T(1,128)S(1)} %bitcast.7), custom_call_target="tpu_custom_call" | custom-call | flops 536870912 | bytes 8388608 | tf_op jit(solution)/shard_map/project_own/pallas_call | solution.py:56
  11.2 5.7 %collective-permute-start.2 = (bf16[64,512]{1,0:T(8,128)(2,1)S(1)}, bf16[64,512]{1,0:T(8,128)(2,1)S(1)}, u32[]{:S(2)}, u32[]{:S(2)}) collective-permute-start(bf16[64,512]{1,0:T(8,128)(2,1)S(1)} %project_own.1.refs_1_), channel_id=1, source_target_pairs={{0,12},{4,16},{8,20},{12,24},{16,28},{20,32},{24,36},{28,40},{32,4... | collective-permute-start | bytes 196616 | tf_op jit(solution)/shard_map/ppermute | solution.py:26
  16.9 2.3 %collective-permute-start.1 = (bf16[64,512]{1,0:T(8,128)(2,1)S(1)}, bf16[64,512]{1,0:T(8,128)(2,1)S(1)}, u32[]{:S(2)}, u32[]{:S(2)}) collective-permute-start(bf16[64,512]{1,0:T(8,128)(2,1)S(1)} %project_own.1.refs_1_), channel_id=1, source_target_pairs={{0,8},{4,12},{8,16},{12,20},{16,24},{20,28},{24,32},{28,36},{32,40... | collective-permute-start | bytes 196616 | tf_op jit(solution)/shard_map/ppermute | solution.py:26
  19.2 1.9 %collective-permute-start = (bf16[64,512]{1,0:T(8,128)(2,1)S(1)}, bf16[64,512]{1,0:T(8,128)(2,1)S(1)}, u32[]{:S(2)}, u32[]{:S(2)}) collective-permute-start(bf16[64,512]{1,0:T(8,128)(2,1)S(1)} %project_own.1.refs_1_), channel_id=1, source_target_pairs={{0,4},{4,8},{8,12},{12,16},{16,20},{20,24},{24,28},{28,32},{32,36}... | collective-permute-start | bytes 196616 | tf_op jit(solution)/shard_map/ppermute | solution.py:26
  21.4 1.0 %collective-permute-done.refs_2_ = bf16[64,512]{1,0:T(8,128)(2,1)S(1)} collective-permute-done((bf16[64,512]{1,0:T(8,128)(2,1)S(1)}, bf16[64,512]{1,0:T(8,128)(2,1)S(1)}, u32[]{:S(2)}, u32[]{:S(2)}) %collective-permute-start) | collective-permute-done | bytes 65568 | tf_op jit(solution)/shard_map/ppermute | solution.py:26
  22.5 1.7 %attend_own.1 = (bf16[256,2048]{1,0:T(8,128)(2,1)S(1)}, f32[256,2048]{1,0:T(8,128)S(1)}, f32[256,128]{1,0:T(8,128)S(1)}) custom-call(bf16[256,2048]{1,0:T(8,128)(2,1)S(1)} %copy-done.7, bf16[64,512]{1,0:T(8,128)(2,1)S(1)} %project_own.1.refs_1_, bf16[64,512]{1,0:T(8,128)(2,1)S(1)} %collective-permute-done.refs_2_, ...), custom_call_target="tpu_custom_call" | custom-call | flops 2147483648 | bytes 1048576 | tf_op jit(solution)/shard_map/attend_own/pallas_call | solution.py:216
  24.2 1.2 %collective-permute-done.5.refs_1_ = bf16[64,8192]{1,0:T(8,128)(2,1)S(1)} collective-permute-done((bf16[64,8192]{1,0:T(8,128)(2,1)}, bf16[64,8192]{1,0:T(8,128)(2,1)S(1)}, u32[]{:S(2)}, u32[]{:S(2)}) %collective-permute-start.5) | collective-permute-done | bytes 1048608 | tf_op jit(solution)/shard_map/ppermute | solution.py:26
  25.5 3.4 %collective-permute-start.6 = (bf16[64,4096]{1,0:T(8,128)(2,1)S(1)}, bf16[64,4096]{1,0:T(8,128)(2,1)S(1)}, u32[]{:S(2)}, u32[]{:S(2)}) collective-permute-start(bf16[64,4096]{1,0:T(8,128)(2,1)S(1)} %slice.7), channel_id=1, source_target_pairs={{0,3},{1,0},{2,1},{3,2},{4,7},{5,4},{6,5},{7,6},{8,11},{9,8},{10,9... | collective-permute-start | bytes 1572872 | tf_op jit(solution)/shard_map/ppermute | solution.py:26
  29.0 1.4 %project_sides.1.refs_1_ = bf16[128,512]{1,0:T(8,128)(2,1)S(1)} custom-call(bf16[64,8192]{1,0:T(8,128)(2,1)S(1)} %collective-permute-done.3.refs_0_, bf16[64,8192]{1,0:T(8,128)(2,1)S(1)} %collective-permute-done.5.refs_1_, bf16[8192,256]{1,0:T(8,128)(2,1)S(1)} %copy-done.1, bf16[8192,256]{1,0:T(8,128)(2,1)S(1)} %copy-done.3, f32[1,128]{1,0:T(1,128)S(1)} %bitcast.8), custom_call_target="tpu_custom_call" | custom-call | flops 1073741824 | bytes 8388608 | tf_op jit(solution)/shard_map/project_sides/pallas_call | solution.py:56
  30.4 4.7 %collective-permute-start.12 = (bf16[128,512]{1,0:T(8,128)(2,1)S(1)}, bf16[128,512]{1,0:T(8,128)(2,1)S(1)}, u32[]{:S(2)}, u32[]{:S(2)}) collective-permute-start(bf16[128,512]{1,0:T(8,128)(2,1)S(1)} %project_sides.1.refs_1_), channel_id=1, source_target_pairs={{0,12},{4,16},{8,20},{12,24},{16,28},{20,32},{24,36},{28,40},{32,4... | collective-permute-start | bytes 393224 | tf_op jit(solution)/shard_map/ppermute | solution.py:26
  35.6 3.0 %collective-permute-done.6.rows_ref = bf16[64,4096]{1,0:T(8,128)(2,1)S(1)} collective-permute-done((bf16[64,4096]{1,0:T(8,128)(2,1)S(1)}, bf16[64,4096]{1,0:T(8,128)(2,1)S(1)}, u32[]{:S(2)}, u32[]{:S(2)}) %collective-permute-start.6) | collective-permute-done | bytes 524320 | tf_op jit(solution)/shard_map/ppermute | solution.py:26
  38.5 0.8 %project_across_last_half.1.sums_ref = f32[64,512]{1,0:T(8,128)S(1)} custom-call(bf16[64,4096]{1,0:T(8,128)(2,1)S(1)} %collective-permute-done.6.rows_ref, bf16[8192,256]{1,0:T(8,128)(2,1)S(1)} %copy-done.1, bf16[8192,256]{1,0:T(8,128)(2,1)S(1)} %copy-done.3), custom_call_target="tpu_custom_call" | custom-call | flops 268435456 | bytes 8388608 | tf_op jit(solution)/shard_map/project_across_last_half/pallas_call | solution.py:91
  39.4 2.4 %collective-permute-done.4.rows_ref = bf16[64,4096]{1,0:T(8,128)(2,1)S(1)} collective-permute-done((bf16[64,4096]{1,0:T(8,128)(2,1)S(1)}, bf16[64,4096]{1,0:T(8,128)(2,1)S(1)}, u32[]{:S(2)}, u32[]{:S(2)}) %collective-permute-start.4) | collective-permute-done | bytes 524320 | tf_op jit(solution)/shard_map/ppermute | solution.py:26
  41.8 0.9 %project_across_first_half.1.refs_1_ = bf16[64,512]{1,0:T(8,128)(2,1)S(1)} custom-call(bf16[64,4096]{1,0:T(8,128)(2,1)S(1)} %collective-permute-done.4.rows_ref, f32[64,512]{1,0:T(8,128)S(1)} %project_across_last_half.1.sums_ref, bf16[8192,256]{1,0:T(8,128)(2,1)S(1)} %copy-done.1, bf16[8192,256]{1,0:T(8,128)(2,1)S(1)} %copy-done.3, f32[1,128]{1,0:T(1,128)S(1)} %bitcast.9), custom_call_target="tpu_custom_call" | custom-call | flops 268435456 | bytes 8388608 | tf_op jit(solution)/shard_map/project_across_first_half/pallas_call | solution.py:99
  42.7 5.6 %collective-permute-start.9 = (bf16[64,512]{1,0:T(8,128)(2,1)S(1)}, bf16[64,512]{1,0:T(8,128)(2,1)S(1)}, u32[]{:S(2)}, u32[]{:S(2)}) collective-permute-start(bf16[64,512]{1,0:T(8,128)(2,1)S(1)} %project_across_first_half.1.refs_1_), channel_id=1, source_target_pairs={{0,12},{4,16},{8,20},{12,24},{16,28},{20,32},{24,36},{28,40},{32,4... | collective-permute-start | bytes 196616 | tf_op jit(solution)/shard_map/ppermute | solution.py:26
  48.4 0.4 collective-permute-start.8
  48.8 2.6 %attend_sides.1 = (f32[256,2048]{1,0:T(8,128)S(1)}, f32[256,128]{1,0:T(8,128)S(1)}) custom-call(bf16[256,2048]{1,0:T(8,128)(2,1)S(1)} %get-tuple-element.22.refs_0_, bf16[128,512]{1,0:T(8,128)(2,1)S(1)} %project_sides.1.refs_1_, bf16[128,512]{1,0:T(8,128)(2,1)S(1)} %collective-permute-done.10.refs_2_, bf16[128,512]{1,0:T(8,128)(2,1)S(1)} %collective-permute-done.11.refs_3_, ...), custom_call_target="tpu_custom_call" | custom-call | flops 4294967296 | bytes 1048576 | tf_op jit(solution)/shard_map/attend_sides/pallas_call | solution.py:216
  51.4 4.9 %collective-permute-done.9.refs_4_ = bf16[64,512]{1,0:T(8,128)(2,1)S(1)} collective-permute-done((bf16[64,512]{1,0:T(8,128)(2,1)S(1)}, bf16[64,512]{1,0:T(8,128)(2,1)S(1)}, u32[]{:S(2)}, u32[]{:S(2)}) %collective-permute-start.9) | collective-permute-done | bytes 65568 | tf_op jit(solution)/shard_map/ppermute | solution.py:26
  56.4 2.8 %attend_across.1 = bf16[256,2048]{1,0:T(8,128)(2,1)} custom-call(bf16[256,2048]{1,0:T(8,128)(2,1)S(1)} %get-tuple-element.22.refs_0_, bf16[64,512]{1,0:T(8,128)(2,1)S(1)} %project_across_first_half.1.refs_1_, bf16[64,512]{1,0:T(8,128)(2,1)S(1)} %collective-permute-done.7.refs_2_, bf16[64,512]{1,0:T(8,128)(2,1)S(1)} %collective-permute-done.8.refs_3_, ...), custom_call_target="tpu_custom_call" | custom-call | flops 2147483648 | bytes 1048576 | tf_op jit(solution)/shard_map/attend_across/pallas_call | solution.py:216
  (37 shorter events, 0.9 us)
Async XLA Ops:
  0.0 25.5 %collective-permute-start.5 = (bf16[64,8192]{1,0:T(8,128)(2,1)}, bf16[64,8192]{1,0:T(8,128)(2,1)S(1)}, u32[]{:S(2)}, u32[]{:S(2)}) collective-permute-start(bf16[64,8192]{1,0:T(8,128)(2,1)} %refs_0_.2), channel_id=1, source_target_pairs={{0,3},{1,0},{2,1},{3,2},{4,7},{5,4},{6,5},{7,6},{8,11},{9,8},{10,9... | collective-permute-start | bytes 3145736 | tf_op jit(solution)/shard_map/ppermute | solution.py:26
  3.3 25.6 %collective-permute-start.3 = (bf16[64,8192]{1,0:T(8,128)(2,1)}, bf16[64,8192]{1,0:T(8,128)(2,1)S(1)}, u32[]{:S(2)}, u32[]{:S(2)}) collective-permute-start(bf16[64,8192]{1,0:T(8,128)(2,1)} %refs_0_.2), channel_id=1, source_target_pairs={{0,1},{1,2},{2,3},{3,0},{4,5},{5,6},{6,7},{7,4},{8,9},{9,10},{10,1... | collective-permute-start | bytes 3145736 | tf_op jit(solution)/shard_map/ppermute | solution.py:26
  3.3 2.2 %copy-start = (bf16[8192,256]{1,0:T(8,128)(2,1)S(1)}, bf16[8192,256]{1,0:T(8,128)(2,1)}, u32[]{:S(2)}) copy-start(bf16[8192,256]{1,0:T(8,128)(2,1)} %key_ref.3) | copy-start | bytes 12582916
  5.5 2.2 %copy-start.2 = (bf16[8192,256]{1,0:T(8,128)(2,1)S(1)}, bf16[8192,256]{1,0:T(8,128)(2,1)}, u32[]{:S(2)}) copy-start(bf16[8192,256]{1,0:T(8,128)(2,1)} %value_ref.3) | copy-start | bytes 12582916
  7.7 1.2 %copy-start.4 = (bf16[64,8192]{1,0:T(8,128)(2,1)S(1)}, bf16[64,8192]{1,0:T(8,128)(2,1)}, u32[]{:S(2)}) copy-start(bf16[64,8192]{1,0:T(8,128)(2,1)} %refs_0_.2) | copy-start | bytes 3145732
  8.9 0.7 %copy-start.5 = (f32[128]{0:T(128)S(1)}, f32[128]{0:T(128)}, u32[]{:S(2)}) copy-start(f32[128]{0:T(128)} %param.12) | copy-start | bytes 1540
  9.6 11.7 %copy-start.9 = (f32[128]{0:T(128)S(1)}, f32[128]{0:T(128)}, u32[]{:S(2)}) copy-start(f32[128]{0:T(128)} %param.11) | copy-start | bytes 1540
  9.6 11.7 %copy-start.8 = (s32[4,64]{1,0:T(4,128)S(1)}, s32[4,64]{1,0:T(4,128)}, u32[]{:S(2)}) copy-start(s32[4,64]{1,0:T(4,128)} %param.13) | copy-start | bytes 3076
  9.6 12.9 %copy-start.7 = (bf16[256,2048]{1,0:T(8,128)(2,1)S(1)}, bf16[256,2048]{1,0:T(8,128)(2,1)}, u32[]{:S(2)}) copy-start(bf16[256,2048]{1,0:T(8,128)(2,1)} %refs_0_.3) | copy-start | bytes 3145732
  11.2 10.2 %collective-permute-start.2 = (bf16[64,512]{1,0:T(8,128)(2,1)S(1)}, bf16[64,512]{1,0:T(8,128)(2,1)S(1)}, u32[]{:S(2)}, u32[]{:S(2)}) collective-permute-start(bf16[64,512]{1,0:T(8,128)(2,1)S(1)} %project_own.1.refs_1_), channel_id=1, source_target_pairs={{0,12},{4,16},{8,20},{12,24},{16,28},{20,32},{24,36},{28,40},{32,4... | collective-permute-start | bytes 196616 | tf_op jit(solution)/shard_map/ppermute | solution.py:26
  16.9 4.5 %collective-permute-start.1 = (bf16[64,512]{1,0:T(8,128)(2,1)S(1)}, bf16[64,512]{1,0:T(8,128)(2,1)S(1)}, u32[]{:S(2)}, u32[]{:S(2)}) collective-permute-start(bf16[64,512]{1,0:T(8,128)(2,1)S(1)} %project_own.1.refs_1_), channel_id=1, source_target_pairs={{0,8},{4,12},{8,16},{12,20},{16,24},{20,28},{24,32},{28,36},{32,40... | collective-permute-start | bytes 196616 | tf_op jit(solution)/shard_map/ppermute | solution.py:26
  19.2 3.2 %collective-permute-start = (bf16[64,512]{1,0:T(8,128)(2,1)S(1)}, bf16[64,512]{1,0:T(8,128)(2,1)S(1)}, u32[]{:S(2)}, u32[]{:S(2)}) collective-permute-start(bf16[64,512]{1,0:T(8,128)(2,1)S(1)} %project_own.1.refs_1_), channel_id=1, source_target_pairs={{0,4},{4,8},{8,12},{12,16},{16,20},{20,24},{24,28},{28,32},{32,36}... | collective-permute-start | bytes 196616 | tf_op jit(solution)/shard_map/ppermute | solution.py:26
  22.5 6.5 %copy-start.1 = (bf16[8192,256]{1,0:T(8,128)(2,1)S(1)}, bf16[8192,256]{1,0:T(8,128)(2,1)}, u32[]{:S(2)}) copy-start(bf16[8192,256]{1,0:T(8,128)(2,1)} %key_ref.3) | copy-start | bytes 12582916
  22.5 6.5 %copy-start.3 = (bf16[8192,256]{1,0:T(8,128)(2,1)S(1)}, bf16[8192,256]{1,0:T(8,128)(2,1)}, u32[]{:S(2)}) copy-start(bf16[8192,256]{1,0:T(8,128)(2,1)} %value_ref.3) | copy-start | bytes 12582916
  22.5 6.5 %copy-start.6 = (f32[128]{0:T(128)S(1)}, f32[128]{0:T(128)}, u32[]{:S(2)}) copy-start(f32[128]{0:T(128)} %param.12) | copy-start | bytes 1540
  25.5 13.1 %collective-permute-start.6 = (bf16[64,4096]{1,0:T(8,128)(2,1)S(1)}, bf16[64,4096]{1,0:T(8,128)(2,1)S(1)}, u32[]{:S(2)}, u32[]{:S(2)}) collective-permute-start(bf16[64,4096]{1,0:T(8,128)(2,1)S(1)} %slice.7), channel_id=1, source_target_pairs={{0,3},{1,0},{2,1},{3,2},{4,7},{5,4},{6,5},{7,6},{8,11},{9,8},{10,9... | collective-permute-start | bytes 1572872 | tf_op jit(solution)/shard_map/ppermute | solution.py:26
  28.9 12.9 %collective-permute-start.4 = (bf16[64,4096]{1,0:T(8,128)(2,1)S(1)}, bf16[64,4096]{1,0:T(8,128)(2,1)S(1)}, u32[]{:S(2)}, u32[]{:S(2)}) collective-permute-start(bf16[64,4096]{1,0:T(8,128)(2,1)S(1)} %slice.6), channel_id=1, source_target_pairs={{0,1},{1,2},{2,3},{3,0},{4,5},{5,6},{6,7},{7,4},{8,9},{9,10},{10,1... | collective-permute-start | bytes 1572872 | tf_op jit(solution)/shard_map/ppermute | solution.py:26
  30.4 18.3 %collective-permute-start.12 = (bf16[128,512]{1,0:T(8,128)(2,1)S(1)}, bf16[128,512]{1,0:T(8,128)(2,1)S(1)}, u32[]{:S(2)}, u32[]{:S(2)}) collective-permute-start(bf16[128,512]{1,0:T(8,128)(2,1)S(1)} %project_sides.1.refs_1_), channel_id=1, source_target_pairs={{0,12},{4,16},{8,20},{12,24},{16,28},{20,32},{24,36},{28,40},{32,4... | collective-permute-start | bytes 393224 | tf_op jit(solution)/shard_map/ppermute | solution.py:26
  35.2 13.6 %collective-permute-start.11 = (bf16[128,512]{1,0:T(8,128)(2,1)S(1)}, bf16[128,512]{1,0:T(8,128)(2,1)S(1)}, u32[]{:S(2)}, u32[]{:S(2)}) collective-permute-start(bf16[128,512]{1,0:T(8,128)(2,1)S(1)} %project_sides.1.refs_1_), channel_id=1, source_target_pairs={{0,8},{4,12},{8,16},{12,20},{16,24},{20,28},{24,32},{28,36},{32,40... | collective-permute-start | bytes 393224 | tf_op jit(solution)/shard_map/ppermute | solution.py:26
  35.6 13.2 %collective-permute-start.10 = (bf16[128,512]{1,0:T(8,128)(2,1)S(1)}, bf16[128,512]{1,0:T(8,128)(2,1)S(1)}, u32[]{:S(2)}, u32[]{:S(2)}) collective-permute-start(bf16[128,512]{1,0:T(8,128)(2,1)S(1)} %project_sides.1.refs_1_), channel_id=1, source_target_pairs={{0,4},{4,8},{8,12},{12,16},{16,20},{20,24},{24,28},{28,32},{32,36}... | collective-permute-start | bytes 393224 | tf_op jit(solution)/shard_map/ppermute | solution.py:26
  42.7 13.6 %collective-permute-start.9 = (bf16[64,512]{1,0:T(8,128)(2,1)S(1)}, bf16[64,512]{1,0:T(8,128)(2,1)S(1)}, u32[]{:S(2)}, u32[]{:S(2)}) collective-permute-start(bf16[64,512]{1,0:T(8,128)(2,1)S(1)} %project_across_first_half.1.refs_1_), channel_id=1, source_target_pairs={{0,12},{4,16},{8,20},{12,24},{16,28},{20,32},{24,36},{28,40},{32,4... | collective-permute-start | bytes 196616 | tf_op jit(solution)/shard_map/ppermute | solution.py:26
  48.4 8.0 %collective-permute-start.8 = (bf16[64,512]{1,0:T(8,128)(2,1)S(1)}, bf16[64,512]{1,0:T(8,128)(2,1)S(1)}, u32[]{:S(2)}, u32[]{:S(2)}) collective-permute-start(bf16[64,512]{1,0:T(8,128)(2,1)S(1)} %project_across_first_half.1.refs_1_), channel_id=1, source_target_pairs={{0,8},{4,12},{8,16},{12,20},{16,24},{20,28},{24,32},{28,36},{32,40... | collective-permute-start | bytes 196616 | tf_op jit(solution)/shard_map/ppermute | solution.py:26
  48.8 7.6 %collective-permute-start.7 = (bf16[64,512]{1,0:T(8,128)(2,1)S(1)}, bf16[64,512]{1,0:T(8,128)(2,1)S(1)}, u32[]{:S(2)}, u32[]{:S(2)}) collective-permute-start(bf16[64,512]{1,0:T(8,128)(2,1)S(1)} %project_across_first_half.1.refs_1_), channel_id=1, source_target_pairs={{0,4},{4,8},{8,12},{12,16},{16,20},{20,24},{24,28},{28,32},{32,36}... | collective-permute-start | bytes 196616 | tf_op jit(solution)/shard_map/ppermute | solution.py:26

commit v11 on v9

--- a/solution.py
+++ b/solution.py
@@ -24,6 +24,31 @@
     length = lax.axis_size(axis)
     pairs = [(i, (i + by) % length) for i in range(length) if wraps or i + by < length]
     return lax.ppermute(value, axis, pairs)
+
+
+def sent(value, axis, target):
+    length = lax.axis_size(axis)
+    return lax.ppermute(value, axis, [(i, target(i) % length) for i in range(length)])
+
+
+def paired_by_core(block):
+    two_chips = sent(block, "seq", lambda s: s + 1 + 2 * (s % 2))
+    other_core = sent(block, "seq", lambda s: s + 3 - 2 * (s % 2))
+    same_core = turned(block, "seq", 2)
+    return [block, same_core, other_core, two_chips]
+
+
+def paired_distances(position, at):
+    two_chips = jnp.where(position % 2 == 0, 3, 1)
+    return jnp.where(at == 3, two_chips, jnp.where(at == 2, 4 - two_chips, jnp.where(at == 1, 2, 0)))
+
+
+def open_columns(block_mask, position, distances):
+    images = lax.broadcasted_iota(jnp.int32, (1, block_mask.shape[1], REACH), 1)
+    at = lax.broadcasted_iota(jnp.int32, (1, block_mask.shape[1], REACH), 2)
+    wanted = position - distances(position, at)
+    is_open = jnp.sum(jnp.where(images == wanted, block_mask[:, :, None], 0), axis=1)
+    return jnp.repeat(is_open.astype(jnp.float32), BLOCK, axis=0)
 
 
 def write_keys_values(keys, values, gain_ref, out_ref):
@@ -228,10 +253,7 @@
     text_query_matrix, vision, key_matrix, value_matrix, query_norm_gain, key_gain, block_mask
 ):
     position = lax.axis_index("seq")
-    images = lax.broadcasted_iota(jnp.int32, (1, block_mask.shape[1], REACH), 1)
-    wanted = position - lax.broadcasted_iota(jnp.int32, (1, block_mask.shape[1], REACH), 2)
-    is_open = jnp.sum(jnp.where(images == wanted, block_mask[:, :, None], 0), axis=1)
-    is_open = jnp.repeat(is_open.astype(jnp.float32), BLOCK, axis=0)
+    is_open = open_columns(block_mask, position, lambda position, at: at)
     query_gain = (query_norm_gain * SCORE_SCALE).reshape(1, HEAD_SIZE)
     key_gain = key_gain.reshape(1, HEAD_SIZE)
 
@@ -260,11 +282,12 @@
     across = project_by_halves(
         first_half, last_half, key_matrix, value_matrix, key_gain, "project_across"
     )
-    across_blocks = reached(across)
+    across_blocks = paired_by_core(across)
+    is_open_paired = open_columns(after(block_mask, sides), position, paired_distances)
     side_blocks = after(side_blocks, across)
     carried = attend(normed, side_blocks, is_open, None, carried, False, "attend_sides")
     across_blocks = after(across_blocks, carried)
-    (result,) = attend(normed, across_blocks, is_open, None, carried, True, "attend_across")
+    (result,) = attend(normed, across_blocks, is_open_paired, None, carried, True, "attend_across")
     return result
 
 

time: 59 us -> 60 us (1.017)
  starting transfers between devices: 27.8 us -> 32.6 us
  waiting for transfers between devices: 12.6 us -> 8.38 us
    ppermute x0 -> x2, starting transfers between devices: none -> 7.37 us  [sent(): lax.ppermute(value, axis, [(i, target(i) % length) for i in range(length)])]
    ppermute x13 -> x11, waiting for transfers between devices: 12.6 us -> 6.78 us  [turned(): return lax.ppermute(value, axis, pairs)]
    ppermute x13 -> x11, starting transfers between devices: 27.8 us -> 25.3 us  [turned(): return lax.ppermute(value, axis, pairs)]
    ppermute x0 -> x2, waiting for transfers between devices: none -> 1.61 us  [sent(): lax.ppermute(value, axis, [(i, target(i) % length) for i in range(length)])]
  transfers between devices with their start and end apart: 13 -> 13, of which waited for: 5 -> 5; matrix products, arithmetic and copies ran while one was open for 1% -> 1% of each run, Pallas kernels for 16% -> 15%
where the time goes in v11:
time: 60 us; the launch traced here: 59.7 us
  starting transfers between devices  32.6 us (54%)
  Pallas kernels  11.4 us (19%)
  waiting for transfers between devices  8.38 us (14%)
  local copies, waits for them, and re-layouts  6.37 us (11%)
    ppermute x11, starting transfers between devices, turned(): return lax.ppermute(value, axis, pairs)  25.3 us
    ppermute x2, starting transfers between devices, sent(): lax.ppermute(value, axis, [(i, target(i) % length) for i in range(length)])  7.37 us
    ppermute x11, waiting for transfers between devices, turned(): return lax.ppermute(value, axis, pairs)  6.78 us
    pallas_call x3, Pallas kernels, attend(): pl.pallas_call(functools.partial(attend_kernel, first, last, kv_heads), o...  6.64 us
    unnamed x20, local copies, waits for them, and re-layouts  6.28 us
    pallas_call x2, Pallas kernels, project(): pl.pallas_call(project_kernel, out_shape=jax.ShapeDtypeStruct((rows, 2 *...  3.05 us
    ppermute x2, waiting for transfers between devices, sent(): lax.ppermute(value, axis, [(i, target(i) % length) for i in range(length)])  1.61 us
  transfers between devices with their start and end apart: 13, of which 5 were waited for; matrix products, arithmetic and copies ran while one was open for 1% of the time, Pallas kernels for 15%

profile of v11, /device:TPU:1, one launch (start us, length us, event | category | flops | bytes accessed | tf_op | source)
XLA Modules:
  0.0 59.7 jit_solution(16909929006224797317)
XLA Ops:
  0.0 3.3 %collective-permute-start.5 = (bf16[64,8192]{1,0:T(8,128)(2,1)}, bf16[64,8192]{1,0:T(8,128)(2,1)S(1)}, u32[]{:S(2)}, u32[]{:S(2)}) collective-permute-start(bf16[64,8192]{1,0:T(8,128)(2,1)} %refs_0_.2), channel_id=1, source_target_pairs={{0,3},{1,0},{2,1},{3,2},{4,7},{5,4},{6,5},{7,6},{8,11},{9,8},{10,9... | collective-permute-start | bytes 3145736 | tf_op jit(solution)/shard_map/ppermute | solution.py:26
  3.3 2.2 %copy-done = bf16[8192,256]{1,0:T(8,128)(2,1)S(1)} copy-done((bf16[8192,256]{1,0:T(8,128)(2,1)S(1)}, bf16[8192,256]{1,0:T(8,128)(2,1)}, u32[]{:S(2)}) %copy-start) | copy-done | bytes 4194328
  5.5 2.2 %copy-done.2 = bf16[8192,256]{1,0:T(8,128)(2,1)S(1)} copy-done((bf16[8192,256]{1,0:T(8,128)(2,1)S(1)}, bf16[8192,256]{1,0:T(8,128)(2,1)}, u32[]{:S(2)}) %copy-start.2) | copy-done | bytes 4194328
  7.7 1.2 %copy-done.4 = bf16[64,8192]{1,0:T(8,128)(2,1)S(1)} copy-done((bf16[64,8192]{1,0:T(8,128)(2,1)S(1)}, bf16[64,8192]{1,0:T(8,128)(2,1)}, u32[]{:S(2)}) %copy-start.4) | copy-done | bytes 1048600
  9.6 1.6 %project_own.1.refs_1_ = bf16[64,512]{1,0:T(8,128)(2,1)S(1)} custom-call(bf16[64,8192]{1,0:T(8,128)(2,1)S(1)} %copy-done.4, bf16[8192,256]{1,0:T(8,128)(2,1)S(1)} %copy-done, bf16[8192,256]{1,0:T(8,128)(2,1)S(1)} %copy-done.2, f32[1,128]{1,0:T(1,128)S(1)} %bitcast.8), custom_call_target="tpu_custom_call" | custom-call | flops 536870912 | bytes 8388608 | tf_op jit(solution)/shard_map/project_own/pallas_call | solution.py:81
  11.2 4.0 %collective-permute-start = (bf16[64,512]{1,0:T(8,128)(2,1)S(1)}, bf16[64,512]{1,0:T(8,128)(2,1)S(1)}, u32[]{:S(2)}, u32[]{:S(2)}) collective-permute-start(bf16[64,512]{1,0:T(8,128)(2,1)S(1)} %project_own.1.refs_1_), channel_id=1, source_target_pairs={{0,4},{4,8},{8,12},{12,16},{16,20},{20,24},{24,28},{28,32},{32,36}... | collective-permute-start | bytes 196616 | tf_op jit(solution)/shard_map/ppermute | solution.py:26
  15.3 3.2 %collective-permute-start.1 = (bf16[64,512]{1,0:T(8,128)(2,1)S(1)}, bf16[64,512]{1,0:T(8,128)(2,1)S(1)}, u32[]{:S(2)}, u32[]{:S(2)}) collective-permute-start(bf16[64,512]{1,0:T(8,128)(2,1)S(1)} %project_own.1.refs_1_), channel_id=1, source_target_pairs={{0,8},{4,12},{8,16},{12,20},{16,24},{20,28},{24,32},{28,36},{32,40... | collective-permute-start | bytes 196616 | tf_op jit(solution)/shard_map/ppermute | solution.py:26
  18.5 3.5 %collective-permute-start.2 = (bf16[64,512]{1,0:T(8,128)(2,1)S(1)}, bf16[64,512]{1,0:T(8,128)(2,1)S(1)}, u32[]{:S(2)}, u32[]{:S(2)}) collective-permute-start(bf16[64,512]{1,0:T(8,128)(2,1)S(1)} %project_own.1.refs_1_), channel_id=1, source_target_pairs={{0,12},{4,16},{8,20},{12,24},{16,28},{20,32},{24,36},{28,40},{32,4... | collective-permute-start | bytes 196616 | tf_op jit(solution)/shard_map/ppermute | solution.py:26
  22.3 1.6 %collective-permute-done.2.refs_4_ = bf16[64,512]{1,0:T(8,128)(2,1)S(1)} collective-permute-done((bf16[64,512]{1,0:T(8,128)(2,1)S(1)}, bf16[64,512]{1,0:T(8,128)(2,1)S(1)}, u32[]{:S(2)}, u32[]{:S(2)}) %collective-permute-start.2) | collective-permute-done | bytes 65568 | tf_op jit(solution)/shard_map/ppermute | solution.py:26
  24.0 1.7 %attend_own.1 = (bf16[256,2048]{1,0:T(8,128)(2,1)S(1)}, f32[256,2048]{1,0:T(8,128)S(1)}, f32[256,128]{1,0:T(8,128)S(1)}) custom-call(bf16[256,2048]{1,0:T(8,128)(2,1)S(1)} %copy-done.7, bf16[64,512]{1,0:T(8,128)(2,1)S(1)} %project_own.1.refs_1_, bf16[64,512]{1,0:T(8,128)(2,1)S(1)} %collective-permute-done.refs_2_, ...), custom_call_target="tpu_custom_call" | custom-call | flops 2147483648 | bytes 1048576 | tf_op jit(solution)/shard_map/attend_own/pallas_call | solution.py:236
  25.7 2.7 %collective-permute-done.3.refs_0_ = bf16[64,8192]{1,0:T(8,128)(2,1)S(1)} collective-permute-done((bf16[64,8192]{1,0:T(8,128)(2,1)}, bf16[64,8192]{1,0:T(8,128)(2,1)S(1)}, u32[]{:S(2)}, u32[]{:S(2)}) %collective-permute-start.3) | collective-permute-done | bytes 1048608 | tf_op jit(solution)/shard_map/ppermute | solution.py:26
  28.9 1.2 %collective-permute-start.4 = (bf16[64,4096]{1,0:T(8,128)(2,1)S(1)}, bf16[64,4096]{1,0:T(8,128)(2,1)S(1)}, u32[]{:S(2)}, u32[]{:S(2)}) collective-permute-start(bf16[64,4096]{1,0:T(8,128)(2,1)S(1)} %slice.6), channel_id=1, source_target_pairs={{0,1},{1,2},{2,3},{3,0},{4,5},{5,6},{6,7},{7,4},{8,9},{9,10},{10,1... | collective-permute-start | bytes 1572872 | tf_op jit(solution)/shard_map/ppermute | solution.py:26
  30.2 1.4 %project_sides.1.refs_1_ = bf16[128,512]{1,0:T(8,128)(2,1)S(1)} custom-call(bf16[64,8192]{1,0:T(8,128)(2,1)S(1)} %collective-permute-done.3.refs_0_, bf16[64,8192]{1,0:T(8,128)(2,1)S(1)} %collective-permute-done.5.refs_1_, bf16[8192,256]{1,0:T(8,128)(2,1)S(1)} %copy-done.1, bf16[8192,256]{1,0:T(8,128)(2,1)S(1)} %copy-done.3, f32[1,128]{1,0:T(1,128)S(1)} %bitcast.9), custom_call_target="tpu_custom_call" | custom-call | flops 1073741824 | bytes 8388608 | tf_op jit(solution)/shard_map/project_sides/pallas_call | solution.py:81
  31.7 3.7 %collective-permute-start.10 = (bf16[128,512]{1,0:T(8,128)(2,1)S(1)}, bf16[128,512]{1,0:T(8,128)(2,1)S(1)}, u32[]{:S(2)}, u32[]{:S(2)}) collective-permute-start(bf16[128,512]{1,0:T(8,128)(2,1)S(1)} %project_sides.1.refs_1_), channel_id=1, source_target_pairs={{0,4},{4,8},{8,12},{12,16},{16,20},{20,24},{24,28},{28,32},{32,36}... | collective-permute-start | bytes 393224 | tf_op jit(solution)/shard_map/ppermute | solution.py:26
  35.3 1.3 %collective-permute-start.11 = (bf16[128,512]{1,0:T(8,128)(2,1)S(1)}, bf16[128,512]{1,0:T(8,128)(2,1)S(1)}, u32[]{:S(2)}, u32[]{:S(2)}) collective-permute-start(bf16[128,512]{1,0:T(8,128)(2,1)S(1)} %project_sides.1.refs_1_), channel_id=1, source_target_pairs={{0,8},{4,12},{8,16},{12,20},{16,24},{20,28},{24,32},{28,36},{32,40... | collective-permute-start | bytes 393224 | tf_op jit(solution)/shard_map/ppermute | solution.py:26
  36.6 1.7 %collective-permute-start.12 = (bf16[128,512]{1,0:T(8,128)(2,1)S(1)}, bf16[128,512]{1,0:T(8,128)(2,1)S(1)}, u32[]{:S(2)}, u32[]{:S(2)}) collective-permute-start(bf16[128,512]{1,0:T(8,128)(2,1)S(1)} %project_sides.1.refs_1_), channel_id=1, source_target_pairs={{0,12},{4,16},{8,20},{12,24},{16,28},{20,32},{24,36},{28,40},{32,4... | collective-permute-start | bytes 393224 | tf_op jit(solution)/shard_map/ppermute | solution.py:26
  38.5 1.6 %collective-permute-done.6.rows_ref = bf16[64,4096]{1,0:T(8,128)(2,1)S(1)} collective-permute-done((bf16[64,4096]{1,0:T(8,128)(2,1)S(1)}, bf16[64,4096]{1,0:T(8,128)(2,1)S(1)}, u32[]{:S(2)}, u32[]{:S(2)}) %collective-permute-start.6) | collective-permute-done | bytes 524320 | tf_op jit(solution)/shard_map/ppermute | solution.py:26
  41.8 0.9 %project_across_first_half.1.refs_1_ = bf16[64,512]{1,0:T(8,128)(2,1)S(1)} custom-call(bf16[64,4096]{1,0:T(8,128)(2,1)S(1)} %collective-permute-done.4.rows_ref, f32[64,512]{1,0:T(8,128)S(1)} %project_across_last_half.1.sums_ref, bf16[8192,256]{1,0:T(8,128)(2,1)S(1)} %copy-done.1, bf16[8192,256]{1,0:T(8,128)(2,1)S(1)} %copy-done.3, f32[1,128]{1,0:T(1,128)S(1)} %bitcast.10), custom_call_target="tpu_custom_call" | custom-call | flops 268435456 | bytes 8388608 | tf_op jit(solution)/shard_map/project_across_first_half/pallas_call | solution.py:124
  42.7 2.9 %collective-permute-start.7 = (bf16[64,512]{1,0:T(8,128)(2,1)S(1)}, bf16[64,512]{1,0:T(8,128)(2,1)S(1)}, u32[]{:S(2)}, u32[]{:S(2)}) collective-permute-start(bf16[64,512]{1,0:T(8,128)(2,1)S(1)} %project_across_first_half.1.refs_1_), channel_id=1, source_target_pairs={{0,8},{4,12},{8,16},{12,20},{16,24},{20,28},{24,32},{28,36},{32,40... | collective-permute-start | bytes 196616 | tf_op jit(solution)/shard_map/ppermute | solution.py:26
  45.6 3.4 %collective-permute-start.8 = (bf16[64,512]{1,0:T(8,128)(2,1)S(1)}, bf16[64,512]{1,0:T(8,128)(2,1)S(1)}, u32[]{:S(2)}, u32[]{:S(2)}) collective-permute-start(bf16[64,512]{1,0:T(8,128)(2,1)S(1)} %project_across_first_half.1.refs_1_), channel_id=1, source_target_pairs={{0,12},{4,8},{8,20},{12,16},{16,28},{20,24},{24,36},{28,32},{32,44... | collective-permute-start | bytes 196616 | tf_op jit(solution)/shard_map/ppermute | solution.py:31
  49.0 3.9 %collective-permute-start.9 = (bf16[64,512]{1,0:T(8,128)(2,1)S(1)}, bf16[64,512]{1,0:T(8,128)(2,1)S(1)}, u32[]{:S(2)}, u32[]{:S(2)}) collective-permute-start(bf16[64,512]{1,0:T(8,128)(2,1)S(1)} %project_across_first_half.1.refs_1_), channel_id=1, source_target_pairs={{0,4},{4,16},{8,12},{12,24},{16,20},{20,32},{24,28},{28,40},{32,36... | collective-permute-start | bytes 196616 | tf_op jit(solution)/shard_map/ppermute | solution.py:31
  53.0 2.7 %attend_sides.1 = (f32[256,2048]{1,0:T(8,128)S(1)}, f32[256,128]{1,0:T(8,128)S(1)}) custom-call(bf16[256,2048]{1,0:T(8,128)(2,1)S(1)} %get-tuple-element.23.refs_0_, bf16[128,512]{1,0:T(8,128)(2,1)S(1)} %project_sides.1.refs_1_, bf16[128,512]{1,0:T(8,128)(2,1)S(1)} %collective-permute-done.10.refs_2_, bf16[128,512]{1,0:T(8,128)(2,1)S(1)} %collective-permute-done.11.refs_3_, ...), custom_call_target="tpu_custom_call" | custom-call | flops 4294967296 | bytes 1048576 | tf_op jit(solution)/shard_map/attend_sides/pallas_call | solution.py:236
  55.7 1.6 %collective-permute-done.8.refs_3_ = bf16[64,512]{1,0:T(8,128)(2,1)S(1)} collective-permute-done((bf16[64,512]{1,0:T(8,128)(2,1)S(1)}, bf16[64,512]{1,0:T(8,128)(2,1)S(1)}, u32[]{:S(2)}, u32[]{:S(2)}) %collective-permute-start.8) | collective-permute-done | bytes 65568 | tf_op jit(solution)/shard_map/ppermute | solution.py:31
  57.3 2.2 %attend_across.1 = bf16[256,2048]{1,0:T(8,128)(2,1)} custom-call(bf16[256,2048]{1,0:T(8,128)(2,1)S(1)} %get-tuple-element.23.refs_0_, bf16[64,512]{1,0:T(8,128)(2,1)S(1)} %project_across_first_half.1.refs_1_, bf16[64,512]{1,0:T(8,128)(2,1)S(1)} %collective-permute-done.7.refs_2_, bf16[64,512]{1,0:T(8,128)(2,1)S(1)} %collective-permute-done.8.refs_3_, ...), custom_call_target="tpu_custom_call" | custom-call | flops 2147483648 | bytes 1048576 | tf_op jit(solution)/shard_map/attend_across/pallas_call | solution.py:236
  (43 shorter events, 3.3 us)
Async XLA Ops:
  0.0 25.7 %collective-permute-start.5 = (bf16[64,8192]{1,0:T(8,128)(2,1)}, bf16[64,8192]{1,0:T(8,128)(2,1)S(1)}, u32[]{:S(2)}, u32[]{:S(2)}) collective-permute-start(bf16[64,8192]{1,0:T(8,128)(2,1)} %refs_0_.2), channel_id=1, source_target_pairs={{0,3},{1,0},{2,1},{3,2},{4,7},{5,4},{6,5},{7,6},{8,11},{9,8},{10,9... | collective-permute-start | bytes 3145736 | tf_op jit(solution)/shard_map/ppermute | solution.py:26
  3.3 25.1 %collective-permute-start.3 = (bf16[64,8192]{1,0:T(8,128)(2,1)}, bf16[64,8192]{1,0:T(8,128)(2,1)S(1)}, u32[]{:S(2)}, u32[]{:S(2)}) collective-permute-start(bf16[64,8192]{1,0:T(8,128)(2,1)} %refs_0_.2), channel_id=1, source_target_pairs={{0,1},{1,2},{2,3},{3,0},{4,5},{5,6},{6,7},{7,4},{8,9},{9,10},{10,1... | collective-permute-start | bytes 3145736 | tf_op jit(solution)/shard_map/ppermute | solution.py:26
  3.3 2.2 %copy-start = (bf16[8192,256]{1,0:T(8,128)(2,1)S(1)}, bf16[8192,256]{1,0:T(8,128)(2,1)}, u32[]{:S(2)}) copy-start(bf16[8192,256]{1,0:T(8,128)(2,1)} %key_ref.3) | copy-start | bytes 12582916
  5.5 2.2 %copy-start.2 = (bf16[8192,256]{1,0:T(8,128)(2,1)S(1)}, bf16[8192,256]{1,0:T(8,128)(2,1)}, u32[]{:S(2)}) copy-start(bf16[8192,256]{1,0:T(8,128)(2,1)} %value_ref.3) | copy-start | bytes 12582916
  7.7 1.2 %copy-start.4 = (bf16[64,8192]{1,0:T(8,128)(2,1)S(1)}, bf16[64,8192]{1,0:T(8,128)(2,1)}, u32[]{:S(2)}) copy-start(bf16[64,8192]{1,0:T(8,128)(2,1)} %refs_0_.2) | copy-start | bytes 3145732
  8.9 0.7 %copy-start.5 = (f32[128]{0:T(128)S(1)}, f32[128]{0:T(128)}, u32[]{:S(2)}) copy-start(f32[128]{0:T(128)} %param.12) | copy-start | bytes 1540
  9.6 12.6 %copy-start.8 = (s32[4,64]{1,0:T(4,128)S(1)}, s32[4,64]{1,0:T(4,128)}, u32[]{:S(2)}) copy-start(s32[4,64]{1,0:T(4,128)} %param.13) | copy-start | bytes 3076
  9.6 12.7 %copy-start.9 = (f32[128]{0:T(128)S(1)}, f32[128]{0:T(128)}, u32[]{:S(2)}) copy-start(f32[128]{0:T(128)} %param.11) | copy-start | bytes 1540
  9.6 14.4 %copy-start.7 = (bf16[256,2048]{1,0:T(8,128)(2,1)S(1)}, bf16[256,2048]{1,0:T(8,128)(2,1)}, u32[]{:S(2)}) copy-start(bf16[256,2048]{1,0:T(8,128)(2,1)} %refs_0_.3) | copy-start | bytes 3145732
  11.2 11.1 %collective-permute-start = (bf16[64,512]{1,0:T(8,128)(2,1)S(1)}, bf16[64,512]{1,0:T(8,128)(2,1)S(1)}, u32[]{:S(2)}, u32[]{:S(2)}) collective-permute-start(bf16[64,512]{1,0:T(8,128)(2,1)S(1)} %project_own.1.refs_1_), channel_id=1, source_target_pairs={{0,4},{4,8},{8,12},{12,16},{16,20},{20,24},{24,28},{28,32},{32,36}... | collective-permute-start | bytes 196616 | tf_op jit(solution)/shard_map/ppermute | solution.py:26
  15.3 7.1 %collective-permute-start.1 = (bf16[64,512]{1,0:T(8,128)(2,1)S(1)}, bf16[64,512]{1,0:T(8,128)(2,1)S(1)}, u32[]{:S(2)}, u32[]{:S(2)}) collective-permute-start(bf16[64,512]{1,0:T(8,128)(2,1)S(1)} %project_own.1.refs_1_), channel_id=1, source_target_pairs={{0,8},{4,12},{8,16},{12,20},{16,24},{20,28},{24,32},{28,36},{32,40... | collective-permute-start | bytes 196616 | tf_op jit(solution)/shard_map/ppermute | solution.py:26
  18.5 5.4 %collective-permute-start.2 = (bf16[64,512]{1,0:T(8,128)(2,1)S(1)}, bf16[64,512]{1,0:T(8,128)(2,1)S(1)}, u32[]{:S(2)}, u32[]{:S(2)}) collective-permute-start(bf16[64,512]{1,0:T(8,128)(2,1)S(1)} %project_own.1.refs_1_), channel_id=1, source_target_pairs={{0,12},{4,16},{8,20},{12,24},{16,28},{20,32},{24,36},{28,40},{32,4... | collective-permute-start | bytes 196616 | tf_op jit(solution)/shard_map/ppermute | solution.py:26
  23.9 6.3 %copy-start.1 = (bf16[8192,256]{1,0:T(8,128)(2,1)S(1)}, bf16[8192,256]{1,0:T(8,128)(2,1)}, u32[]{:S(2)}) copy-start(bf16[8192,256]{1,0:T(8,128)(2,1)} %key_ref.3) | copy-start | bytes 12582916
  24.0 6.3 %copy-start.3 = (bf16[8192,256]{1,0:T(8,128)(2,1)S(1)}, bf16[8192,256]{1,0:T(8,128)(2,1)}, u32[]{:S(2)}) copy-start(bf16[8192,256]{1,0:T(8,128)(2,1)} %value_ref.3) | copy-start | bytes 12582916
  24.0 6.3 %copy-start.6 = (f32[128]{0:T(128)S(1)}, f32[128]{0:T(128)}, u32[]{:S(2)}) copy-start(f32[128]{0:T(128)} %param.12) | copy-start | bytes 1540
  28.5 11.6 %collective-permute-start.6 = (bf16[64,4096]{1,0:T(8,128)(2,1)S(1)}, bf16[64,4096]{1,0:T(8,128)(2,1)S(1)}, u32[]{:S(2)}, u32[]{:S(2)}) collective-permute-start(bf16[64,4096]{1,0:T(8,128)(2,1)S(1)} %slice.7), channel_id=1, source_target_pairs={{0,3},{1,0},{2,1},{3,2},{4,7},{5,4},{6,5},{7,6},{8,11},{9,8},{10,9... | collective-permute-start | bytes 1572872 | tf_op jit(solution)/shard_map/ppermute | solution.py:26
  28.9 12.9 %collective-permute-start.4 = (bf16[64,4096]{1,0:T(8,128)(2,1)S(1)}, bf16[64,4096]{1,0:T(8,128)(2,1)S(1)}, u32[]{:S(2)}, u32[]{:S(2)}) collective-permute-start(bf16[64,4096]{1,0:T(8,128)(2,1)S(1)} %slice.6), channel_id=1, source_target_pairs={{0,1},{1,2},{2,3},{3,0},{4,5},{5,6},{6,7},{7,4},{8,9},{9,10},{10,1... | collective-permute-start | bytes 1572872 | tf_op jit(solution)/shard_map/ppermute | solution.py:26
  31.7 17.4 %collective-permute-start.10 = (bf16[128,512]{1,0:T(8,128)(2,1)S(1)}, bf16[128,512]{1,0:T(8,128)(2,1)S(1)}, u32[]{:S(2)}, u32[]{:S(2)}) collective-permute-start(bf16[128,512]{1,0:T(8,128)(2,1)S(1)} %project_sides.1.refs_1_), channel_id=1, source_target_pairs={{0,4},{4,8},{8,12},{12,16},{16,20},{20,24},{24,28},{28,32},{32,36}... | collective-permute-start | bytes 393224 | tf_op jit(solution)/shard_map/ppermute | solution.py:26
  35.3 17.7 %collective-permute-start.11 = (bf16[128,512]{1,0:T(8,128)(2,1)S(1)}, bf16[128,512]{1,0:T(8,128)(2,1)S(1)}, u32[]{:S(2)}, u32[]{:S(2)}) collective-permute-start(bf16[128,512]{1,0:T(8,128)(2,1)S(1)} %project_sides.1.refs_1_), channel_id=1, source_target_pairs={{0,8},{4,12},{8,16},{12,20},{16,24},{20,28},{24,32},{28,36},{32,40... | collective-permute-start | bytes 393224 | tf_op jit(solution)/shard_map/ppermute | solution.py:26
  36.6 16.4 %collective-permute-start.12 = (bf16[128,512]{1,0:T(8,128)(2,1)S(1)}, bf16[128,512]{1,0:T(8,128)(2,1)S(1)}, u32[]{:S(2)}, u32[]{:S(2)}) collective-permute-start(bf16[128,512]{1,0:T(8,128)(2,1)S(1)} %project_sides.1.refs_1_), channel_id=1, source_target_pairs={{0,12},{4,16},{8,20},{12,24},{16,28},{20,32},{24,36},{28,40},{32,4... | collective-permute-start | bytes 393224 | tf_op jit(solution)/shard_map/ppermute | solution.py:26
  42.7 13.0 %collective-permute-start.7 = (bf16[64,512]{1,0:T(8,128)(2,1)S(1)}, bf16[64,512]{1,0:T(8,128)(2,1)S(1)}, u32[]{:S(2)}, u32[]{:S(2)}) collective-permute-start(bf16[64,512]{1,0:T(8,128)(2,1)S(1)} %project_across_first_half.1.refs_1_), channel_id=1, source_target_pairs={{0,8},{4,12},{8,16},{12,20},{16,24},{20,28},{24,32},{28,36},{32,40... | collective-permute-start | bytes 196616 | tf_op jit(solution)/shard_map/ppermute | solution.py:26
  45.6 11.7 %collective-permute-start.8 = (bf16[64,512]{1,0:T(8,128)(2,1)S(1)}, bf16[64,512]{1,0:T(8,128)(2,1)S(1)}, u32[]{:S(2)}, u32[]{:S(2)}) collective-permute-start(bf16[64,512]{1,0:T(8,128)(2,1)S(1)} %project_across_first_half.1.refs_1_), channel_id=1, source_target_pairs={{0,12},{4,8},{8,20},{12,16},{16,28},{20,24},{24,36},{28,32},{32,44... | collective-permute-start | bytes 196616 | tf_op jit(solution)/shard_map/ppermute | solution.py:31
  49.0 8.3 %collective-permute-start.9 = (bf16[64,512]{1,0:T(8,128)(2,1)S(1)}, bf16[64,512]{1,0:T(8,128)(2,1)S(1)}, u32[]{:S(2)}, u32[]{:S(2)}) collective-permute-start(bf16[64,512]{1,0:T(8,128)(2,1)S(1)} %project_across_first_half.1.refs_1_), channel_id=1, source_target_pairs={{0,4},{4,16},{8,12},{12,24},{16,20},{20,32},{24,28},{28,40},{32,36... | collective-permute-start | bytes 196616 | tf_op jit(solution)/shard_map/ppermute | solution.py:31

commit v12 on v9

--- a/solution.py
+++ b/solution.py
@@ -65,10 +65,10 @@
 
 
 def last_half_kernel(rows_ref, key_ref, value_ref, out_ref):
-    depth, width = rows_ref.shape[1], key_ref.shape[1]
+    before, width = key_ref.shape[0] - rows_ref.shape[1], key_ref.shape[1]
     rows = rows_ref[...]
-    out_ref[:, :width] = jnp.dot(rows, key_ref[depth:], preferred_element_type=jnp.float32)
-    out_ref[:, width:] = jnp.dot(rows, value_ref[depth:], preferred_element_type=jnp.float32)
+    out_ref[:, :width] = jnp.dot(rows, key_ref[before:], preferred_element_type=jnp.float32)
+    out_ref[:, width:] = jnp.dot(rows, value_ref[before:], preferred_element_type=jnp.float32)
 
 
 def first_half_kernel(rows_ref, sums_ref, key_ref, value_ref, gain_ref, out_ref):
@@ -249,7 +249,7 @@
         text_query_matrix, own_blocks, is_open, query_gain, None, False, "attend_own"
     )
 
-    half = vision.shape[1] // 2
+    half = vision.shape[1] * 13 // 32
     right = after(right, carried)
     last_half = turned(right[:, half:], "tp", -1)
     left = after(left, carried)

time: 59 us -> 73.3 us (1.24)
  waiting for transfers between devices: 12.6 us -> 25.8 us
  Pallas kernels: 11.4 us -> 12.7 us
  local copies, waits for them, and re-layouts: 6.36 us -> 5.14 us
  starting transfers between devices: 27.8 us -> 28.7 us
    ppermute x13, waiting for transfers between devices: 12.6 us -> 25.8 us  [turned(): return lax.ppermute(value, axis, pairs)]
    pallas_call x2, Pallas kernels: 3.05 us -> 4.36 us  [project(): pl.pallas_call(project_kernel, out_shape=jax.ShapeDtypeStruct((rows, 2 *...]
    unnamed x20 -> x18, local copies, waits for them, and re-layouts: 6.28 us -> 5.06 us
    ppermute x13, starting transfers between devices: 27.8 us -> 28.7 us  [turned(): return lax.ppermute(value, axis, pairs)]
  transfers between devices with their start and end apart: 13 -> 13, of which waited for: 5 -> 5; matrix products, arithmetic and copies ran while one was open for 1% -> 0% of each run, Pallas kernels for 16% -> 14%
where the time goes in v12:
time: 73.3 us; the launch traced here: 73 us
  starting transfers between devices  28.7 us (39%)
  waiting for transfers between devices  25.8 us (35%)
  Pallas kernels  12.7 us (17%)
  local copies, waits for them, and re-layouts  5.14 us (7%)
    ppermute x13, starting transfers between devices, turned(): return lax.ppermute(value, axis, pairs)  28.7 us
    ppermute x13, waiting for transfers between devices, turned(): return lax.ppermute(value, axis, pairs)  25.8 us
    pallas_call x3, Pallas kernels, attend(): pl.pallas_call(functools.partial(attend_kernel, first, last, kv_heads), o...  6.59 us
    unnamed x18, local copies, waits for them, and re-layouts  5.06 us
    pallas_call x2, Pallas kernels, project(): pl.pallas_call(project_kernel, out_shape=jax.ShapeDtypeStruct((rows, 2 *...  4.36 us
  transfers between devices with their start and end apart: 13, of which 5 were waited for; matrix products, arithmetic and copies ran while one was open for 0% of the time, Pallas kernels for 14%

profile of v12, /device:TPU:1, one launch (start us, length us, event | category | flops | bytes accessed | tf_op | source)
XLA Modules:
  0.0 73.0 jit_solution(12575531905714550617)
XLA Ops:
  0.0 3.3 %collective-permute-start.5 = (bf16[64,8192]{1,0:T(8,128)(2,1)}, bf16[64,8192]{1,0:T(8,128)(2,1)S(1)}, u32[]{:S(2)}, u32[]{:S(2)}) collective-permute-start(bf16[64,8192]{1,0:T(8,128)(2,1)} %refs_0_.2), channel_id=1, source_target_pairs={{0,3},{1,0},{2,1},{3,2},{4,7},{5,4},{6,5},{7,6},{8,11},{9,8},{10,9... | collective-permute-start | bytes 3145736 | tf_op jit(solution)/shard_map/ppermute | solution.py:26
  3.3 2.2 %copy-done = bf16[8192,256]{1,0:T(8,128)(2,1)S(1)} copy-done((bf16[8192,256]{1,0:T(8,128)(2,1)S(1)}, bf16[8192,256]{1,0:T(8,128)(2,1)}, u32[]{:S(2)}) %copy-start) | copy-done | bytes 4194328
  5.5 2.2 %copy-done.2 = bf16[8192,256]{1,0:T(8,128)(2,1)S(1)} copy-done((bf16[8192,256]{1,0:T(8,128)(2,1)S(1)}, bf16[8192,256]{1,0:T(8,128)(2,1)}, u32[]{:S(2)}) %copy-start.2) | copy-done | bytes 4194328
  7.7 0.7 copy-done.4
  8.3 3.0 %project_own.1.refs_1_ = bf16[64,512]{1,0:T(8,128)(2,1)S(1)} custom-call(bf16[64,8192]{1,0:T(8,128)(2,1)} %refs_0_.2, bf16[8192,256]{1,0:T(8,128)(2,1)S(1)} %copy-done, bf16[8192,256]{1,0:T(8,128)(2,1)S(1)} %copy-done.2, f32[1,128]{1,0:T(1,128)S(1)} %bitcast.7), custom_call_target="tpu_custom_call" | custom-call | flops 536870912 | bytes 8388608 | tf_op jit(solution)/shard_map/project_own/pallas_call | solution.py:56
  11.3 5.7 %collective-permute-start.2 = (bf16[64,512]{1,0:T(8,128)(2,1)S(1)}, bf16[64,512]{1,0:T(8,128)(2,1)S(1)}, u32[]{:S(2)}, u32[]{:S(2)}) collective-permute-start(bf16[64,512]{1,0:T(8,128)(2,1)S(1)} %project_own.1.refs_1_), channel_id=1, source_target_pairs={{0,12},{4,16},{8,20},{12,24},{16,28},{20,32},{24,36},{28,40},{32,4... | collective-permute-start | bytes 196616 | tf_op jit(solution)/shard_map/ppermute | solution.py:26
  17.0 2.3 %collective-permute-start.1 = (bf16[64,512]{1,0:T(8,128)(2,1)S(1)}, bf16[64,512]{1,0:T(8,128)(2,1)S(1)}, u32[]{:S(2)}, u32[]{:S(2)}) collective-permute-start(bf16[64,512]{1,0:T(8,128)(2,1)S(1)} %project_own.1.refs_1_), channel_id=1, source_target_pairs={{0,8},{4,12},{8,16},{12,20},{16,24},{20,28},{24,32},{28,36},{32,40... | collective-permute-start | bytes 196616 | tf_op jit(solution)/shard_map/ppermute | solution.py:26
  19.3 1.9 %collective-permute-start = (bf16[64,512]{1,0:T(8,128)(2,1)S(1)}, bf16[64,512]{1,0:T(8,128)(2,1)S(1)}, u32[]{:S(2)}, u32[]{:S(2)}) collective-permute-start(bf16[64,512]{1,0:T(8,128)(2,1)S(1)} %project_own.1.refs_1_), channel_id=1, source_target_pairs={{0,4},{4,8},{8,12},{12,16},{16,20},{20,24},{24,28},{28,32},{32,36}... | collective-permute-start | bytes 196616 | tf_op jit(solution)/shard_map/ppermute | solution.py:26
  21.6 0.9 %collective-permute-done.refs_2_ = bf16[64,512]{1,0:T(8,128)(2,1)S(1)} collective-permute-done((bf16[64,512]{1,0:T(8,128)(2,1)S(1)}, bf16[64,512]{1,0:T(8,128)(2,1)S(1)}, u32[]{:S(2)}, u32[]{:S(2)}) %collective-permute-start) | collective-permute-done | bytes 65568 | tf_op jit(solution)/shard_map/ppermute | solution.py:26
  22.6 1.7 %attend_own.1 = (bf16[256,2048]{1,0:T(8,128)(2,1)S(1)}, f32[256,2048]{1,0:T(8,128)S(1)}, f32[256,128]{1,0:T(8,128)S(1)}) custom-call(bf16[256,2048]{1,0:T(8,128)(2,1)S(1)} %copy-done.6, bf16[64,512]{1,0:T(8,128)(2,1)S(1)} %project_own.1.refs_1_, bf16[64,512]{1,0:T(8,128)(2,1)S(1)} %collective-permute-done.refs_2_, ...), custom_call_target="tpu_custom_call" | custom-call | flops 2147483648 | bytes 1048576 | tf_op jit(solution)/shard_map/attend_own/pallas_call | solution.py:211
  24.3 1.1 %collective-permute-done.5.refs_1_ = bf16[64,8192]{1,0:T(8,128)(2,1)S(1)} collective-permute-done((bf16[64,8192]{1,0:T(8,128)(2,1)}, bf16[64,8192]{1,0:T(8,128)(2,1)S(1)}, u32[]{:S(2)}, u32[]{:S(2)}) %collective-permute-start.5) | collective-permute-done | bytes 1048608 | tf_op jit(solution)/shard_map/ppermute | solution.py:26
  25.5 3.4 %collective-permute-start.6 = (bf16[64,4864]{1,0:T(8,128)(2,1)S(1)}, bf16[64,4864]{1,0:T(8,128)(2,1)S(1)}, u32[]{:S(2)}, u32[]{:S(2)}) collective-permute-start(bf16[64,4864]{1,0:T(8,128)(2,1)S(1)} %slice.7), channel_id=1, source_target_pairs={{0,3},{1,0},{2,1},{3,2},{4,7},{5,4},{6,5},{7,6},{8,11},{9,8},{10,9... | collective-permute-start | bytes 1867784 | tf_op jit(solution)/shard_map/ppermute | solution.py:26
  28.9 18.1 %collective-permute-done.3.refs_0_ = bf16[64,8192]{1,0:T(8,128)(2,1)S(1)} collective-permute-done((bf16[64,8192]{1,0:T(8,128)(2,1)}, bf16[64,8192]{1,0:T(8,128)(2,1)S(1)}, u32[]{:S(2)}, u32[]{:S(2)}) %collective-permute-start.3) | collective-permute-done | bytes 1048608 | tf_op jit(solution)/shard_map/ppermute | solution.py:26
  47.1 1.4 %project_sides.1.refs_1_ = bf16[128,512]{1,0:T(8,128)(2,1)S(1)} custom-call(bf16[64,8192]{1,0:T(8,128)(2,1)S(1)} %collective-permute-done.3.refs_0_, bf16[64,8192]{1,0:T(8,128)(2,1)S(1)} %collective-permute-done.5.refs_1_, bf16[8192,256]{1,0:T(8,128)(2,1)S(1)} %copy-done.1, bf16[8192,256]{1,0:T(8,128)(2,1)S(1)} %copy-done.3, f32[1,128]{1,0:T(1,128)S(1)} %bitcast.8), custom_call_target="tpu_custom_call" | custom-call | flops 1073741824 | bytes 8388608 | tf_op jit(solution)/shard_map/project_sides/pallas_call | solution.py:56
  48.5 4.2 %collective-permute-start.12 = (bf16[128,512]{1,0:T(8,128)(2,1)S(1)}, bf16[128,512]{1,0:T(8,128)(2,1)S(1)}, u32[]{:S(2)}, u32[]{:S(2)}) collective-permute-start(bf16[128,512]{1,0:T(8,128)(2,1)S(1)} %project_sides.1.refs_1_), channel_id=1, source_target_pairs={{0,12},{4,16},{8,20},{12,24},{16,28},{20,32},{24,36},{28,40},{32,4... | collective-permute-start | bytes 393224 | tf_op jit(solution)/shard_map/ppermute | solution.py:26
  52.7 1.3 %collective-permute-start.11 = (bf16[128,512]{1,0:T(8,128)(2,1)S(1)}, bf16[128,512]{1,0:T(8,128)(2,1)S(1)}, u32[]{:S(2)}, u32[]{:S(2)}) collective-permute-start(bf16[128,512]{1,0:T(8,128)(2,1)S(1)} %project_sides.1.refs_1_), channel_id=1, source_target_pairs={{0,8},{4,12},{8,16},{12,20},{16,24},{20,28},{24,32},{28,36},{32,40... | collective-permute-start | bytes 393224 | tf_op jit(solution)/shard_map/ppermute | solution.py:26
  54.0 1.0 %project_across_last_half.1.sums_ref = f32[64,512]{1,0:T(8,128)S(1)} custom-call(bf16[64,4864]{1,0:T(8,128)(2,1)S(1)} %collective-permute-done.6.rows_ref, bf16[8192,256]{1,0:T(8,128)(2,1)S(1)} %copy-done.1, bf16[8192,256]{1,0:T(8,128)(2,1)S(1)} %copy-done.3), custom_call_target="tpu_custom_call" | custom-call | flops 268435456 | bytes 8388608 | tf_op jit(solution)/shard_map/project_across_last_half/pallas_call | solution.py:91
  55.0 3.2 %collective-permute-done.4.rows_ref = bf16[64,3328]{1,0:T(8,128)(2,1)S(1)} collective-permute-done((bf16[64,3328]{1,0:T(8,128)(2,1)S(1)}, bf16[64,3328]{1,0:T(8,128)(2,1)S(1)}, u32[]{:S(2)}, u32[]{:S(2)}) %collective-permute-start.4) | collective-permute-done | bytes 426016 | tf_op jit(solution)/shard_map/ppermute | solution.py:26
  58.2 0.8 %project_across_first_half.1.refs_1_ = bf16[64,512]{1,0:T(8,128)(2,1)S(1)} custom-call(bf16[64,3328]{1,0:T(8,128)(2,1)S(1)} %collective-permute-done.4.rows_ref, f32[64,512]{1,0:T(8,128)S(1)} %project_across_last_half.1.sums_ref, bf16[8192,256]{1,0:T(8,128)(2,1)S(1)} %copy-done.1, bf16[8192,256]{1,0:T(8,128)(2,1)S(1)} %copy-done.3, f32[1,128]{1,0:T(1,128)S(1)} %bitcast.9), custom_call_target="tpu_custom_call" | custom-call | flops 268435456 | bytes 8388608 | tf_op jit(solution)/shard_map/project_across_first_half/pallas_call | solution.py:99
  59.1 5.1 %collective-permute-start.9 = (bf16[64,512]{1,0:T(8,128)(2,1)S(1)}, bf16[64,512]{1,0:T(8,128)(2,1)S(1)}, u32[]{:S(2)}, u32[]{:S(2)}) collective-permute-start(bf16[64,512]{1,0:T(8,128)(2,1)S(1)} %project_across_first_half.1.refs_1_), channel_id=1, source_target_pairs={{0,12},{4,16},{8,20},{12,24},{16,28},{20,32},{24,36},{28,40},{32,4... | collective-permute-start | bytes 196616 | tf_op jit(solution)/shard_map/ppermute | solution.py:26
  64.2 1.3 %collective-permute-start.8 = (bf16[64,512]{1,0:T(8,128)(2,1)S(1)}, bf16[64,512]{1,0:T(8,128)(2,1)S(1)}, u32[]{:S(2)}, u32[]{:S(2)}) collective-permute-start(bf16[64,512]{1,0:T(8,128)(2,1)S(1)} %project_across_first_half.1.refs_1_), channel_id=1, source_target_pairs={{0,8},{4,12},{8,16},{12,20},{16,24},{20,28},{24,32},{28,36},{32,40... | collective-permute-start | bytes 196616 | tf_op jit(solution)/shard_map/ppermute | solution.py:26
  65.5 2.6 %attend_sides.1 = (f32[256,2048]{1,0:T(8,128)S(1)}, f32[256,128]{1,0:T(8,128)S(1)}) custom-call(bf16[256,2048]{1,0:T(8,128)(2,1)S(1)} %get-tuple-element.22.refs_0_, bf16[128,512]{1,0:T(8,128)(2,1)S(1)} %project_sides.1.refs_1_, bf16[128,512]{1,0:T(8,128)(2,1)S(1)} %collective-permute-done.10.refs_2_, bf16[128,512]{1,0:T(8,128)(2,1)S(1)} %collective-permute-done.11.refs_3_, ...), custom_call_target="tpu_custom_call" | custom-call | flops 4294967296 | bytes 1048576 | tf_op jit(solution)/shard_map/attend_sides/pallas_call | solution.py:211
  68.2 2.5 %collective-permute-done.8.refs_3_ = bf16[64,512]{1,0:T(8,128)(2,1)S(1)} collective-permute-done((bf16[64,512]{1,0:T(8,128)(2,1)S(1)}, bf16[64,512]{1,0:T(8,128)(2,1)S(1)}, u32[]{:S(2)}, u32[]{:S(2)}) %collective-permute-start.8) | collective-permute-done | bytes 65568 | tf_op jit(solution)/shard_map/ppermute | solution.py:26
  70.6 2.2 %attend_across.1 = bf16[256,2048]{1,0:T(8,128)(2,1)} custom-call(bf16[256,2048]{1,0:T(8,128)(2,1)S(1)} %get-tuple-element.22.refs_0_, bf16[64,512]{1,0:T(8,128)(2,1)S(1)} %project_across_first_half.1.refs_1_, bf16[64,512]{1,0:T(8,128)(2,1)S(1)} %collective-permute-done.7.refs_2_, bf16[64,512]{1,0:T(8,128)(2,1)S(1)} %collective-permute-done.8.refs_3_, ...), custom_call_target="tpu_custom_call" | custom-call | flops 2147483648 | bytes 1048576 | tf_op jit(solution)/shard_map/attend_across/pallas_call | solution.py:211
  (35 shorter events, 0.5 us)
Async XLA Ops:
  0.0 25.5 %collective-permute-start.5 = (bf16[64,8192]{1,0:T(8,128)(2,1)}, bf16[64,8192]{1,0:T(8,128)(2,1)S(1)}, u32[]{:S(2)}, u32[]{:S(2)}) collective-permute-start(bf16[64,8192]{1,0:T(8,128)(2,1)} %refs_0_.2), channel_id=1, source_target_pairs={{0,3},{1,0},{2,1},{3,2},{4,7},{5,4},{6,5},{7,6},{8,11},{9,8},{10,9... | collective-permute-start | bytes 3145736 | tf_op jit(solution)/shard_map/ppermute | solution.py:26
  3.3 2.2 %copy-start = (bf16[8192,256]{1,0:T(8,128)(2,1)S(1)}, bf16[8192,256]{1,0:T(8,128)(2,1)}, u32[]{:S(2)}) copy-start(bf16[8192,256]{1,0:T(8,128)(2,1)} %key_ref.3) | copy-start | bytes 12582916
  5.5 2.2 %copy-start.2 = (bf16[8192,256]{1,0:T(8,128)(2,1)S(1)}, bf16[8192,256]{1,0:T(8,128)(2,1)}, u32[]{:S(2)}) copy-start(bf16[8192,256]{1,0:T(8,128)(2,1)} %value_ref.3) | copy-start | bytes 12582916
  7.7 0.7 copy-start.4
  8.3 13.1 %copy-start.8 = (f32[128]{0:T(128)S(1)}, f32[128]{0:T(128)}, u32[]{:S(2)}) copy-start(f32[128]{0:T(128)} %param.11) | copy-start | bytes 1540
  8.3 13.1 %copy-start.7 = (s32[4,64]{1,0:T(4,128)S(1)}, s32[4,64]{1,0:T(4,128)}, u32[]{:S(2)}) copy-start(s32[4,64]{1,0:T(4,128)} %param.13) | copy-start | bytes 3076
  8.3 14.2 %copy-start.6 = (bf16[256,2048]{1,0:T(8,128)(2,1)S(1)}, bf16[256,2048]{1,0:T(8,128)(2,1)}, u32[]{:S(2)}) copy-start(bf16[256,2048]{1,0:T(8,128)(2,1)} %refs_0_.3) | copy-start | bytes 3145732
  11.3 10.3 %collective-permute-start.2 = (bf16[64,512]{1,0:T(8,128)(2,1)S(1)}, bf16[64,512]{1,0:T(8,128)(2,1)S(1)}, u32[]{:S(2)}, u32[]{:S(2)}) collective-permute-start(bf16[64,512]{1,0:T(8,128)(2,1)S(1)} %project_own.1.refs_1_), channel_id=1, source_target_pairs={{0,12},{4,16},{8,20},{12,24},{16,28},{20,32},{24,36},{28,40},{32,4... | collective-permute-start | bytes 196616 | tf_op jit(solution)/shard_map/ppermute | solution.py:26
  17.0 4.6 %collective-permute-start.1 = (bf16[64,512]{1,0:T(8,128)(2,1)S(1)}, bf16[64,512]{1,0:T(8,128)(2,1)S(1)}, u32[]{:S(2)}, u32[]{:S(2)}) collective-permute-start(bf16[64,512]{1,0:T(8,128)(2,1)S(1)} %project_own.1.refs_1_), channel_id=1, source_target_pairs={{0,8},{4,12},{8,16},{12,20},{16,24},{20,28},{24,32},{28,36},{32,40... | collective-permute-start | bytes 196616 | tf_op jit(solution)/shard_map/ppermute | solution.py:26
  19.3 3.2 %collective-permute-start = (bf16[64,512]{1,0:T(8,128)(2,1)S(1)}, bf16[64,512]{1,0:T(8,128)(2,1)S(1)}, u32[]{:S(2)}, u32[]{:S(2)}) collective-permute-start(bf16[64,512]{1,0:T(8,128)(2,1)S(1)} %project_own.1.refs_1_), channel_id=1, source_target_pairs={{0,4},{4,8},{8,12},{12,16},{16,20},{20,24},{24,28},{28,32},{32,36}... | collective-permute-start | bytes 196616 | tf_op jit(solution)/shard_map/ppermute | solution.py:26
  21.2 25.7 %collective-permute-start.3 = (bf16[64,8192]{1,0:T(8,128)(2,1)}, bf16[64,8192]{1,0:T(8,128)(2,1)S(1)}, u32[]{:S(2)}, u32[]{:S(2)}) collective-permute-start(bf16[64,8192]{1,0:T(8,128)(2,1)} %refs_0_.2), channel_id=1, source_target_pairs={{0,1},{1,2},{2,3},{3,0},{4,5},{5,6},{6,7},{7,4},{8,9},{9,10},{10,1... | collective-permute-start | bytes 3145736 | tf_op jit(solution)/shard_map/ppermute | solution.py:26
  22.6 24.5 %copy-start.1 = (bf16[8192,256]{1,0:T(8,128)(2,1)S(1)}, bf16[8192,256]{1,0:T(8,128)(2,1)}, u32[]{:S(2)}) copy-start(bf16[8192,256]{1,0:T(8,128)(2,1)} %key_ref.3) | copy-start | bytes 12582916
  22.6 24.5 %copy-start.3 = (bf16[8192,256]{1,0:T(8,128)(2,1)S(1)}, bf16[8192,256]{1,0:T(8,128)(2,1)}, u32[]{:S(2)}) copy-start(bf16[8192,256]{1,0:T(8,128)(2,1)} %value_ref.3) | copy-start | bytes 12582916
  22.6 24.5 %copy-start.5 = (f32[128]{0:T(128)S(1)}, f32[128]{0:T(128)}, u32[]{:S(2)}) copy-start(f32[128]{0:T(128)} %param.12) | copy-start | bytes 1540
  25.5 28.5 %collective-permute-start.6 = (bf16[64,4864]{1,0:T(8,128)(2,1)S(1)}, bf16[64,4864]{1,0:T(8,128)(2,1)S(1)}, u32[]{:S(2)}, u32[]{:S(2)}) collective-permute-start(bf16[64,4864]{1,0:T(8,128)(2,1)S(1)} %slice.7), channel_id=1, source_target_pairs={{0,3},{1,0},{2,1},{3,2},{4,7},{5,4},{6,5},{7,6},{8,11},{9,8},{10,9... | collective-permute-start | bytes 1867784 | tf_op jit(solution)/shard_map/ppermute | solution.py:26
  47.0 11.3 %collective-permute-start.4 = (bf16[64,3328]{1,0:T(8,128)(2,1)S(1)}, bf16[64,3328]{1,0:T(8,128)(2,1)S(1)}, u32[]{:S(2)}, u32[]{:S(2)}) collective-permute-start(bf16[64,3328]{1,0:T(8,128)(2,1)S(1)} %slice.6), channel_id=1, source_target_pairs={{0,1},{1,2},{2,3},{3,0},{4,5},{5,6},{6,7},{7,4},{8,9},{9,10},{10,1... | collective-permute-start | bytes 1277960 | tf_op jit(solution)/shard_map/ppermute | solution.py:26
  48.5 17.0 %collective-permute-start.12 = (bf16[128,512]{1,0:T(8,128)(2,1)S(1)}, bf16[128,512]{1,0:T(8,128)(2,1)S(1)}, u32[]{:S(2)}, u32[]{:S(2)}) collective-permute-start(bf16[128,512]{1,0:T(8,128)(2,1)S(1)} %project_sides.1.refs_1_), channel_id=1, source_target_pairs={{0,12},{4,16},{8,20},{12,24},{16,28},{20,32},{24,36},{28,40},{32,4... | collective-permute-start | bytes 393224 | tf_op jit(solution)/shard_map/ppermute | solution.py:26
  52.7 12.8 %collective-permute-start.11 = (bf16[128,512]{1,0:T(8,128)(2,1)S(1)}, bf16[128,512]{1,0:T(8,128)(2,1)S(1)}, u32[]{:S(2)}, u32[]{:S(2)}) collective-permute-start(bf16[128,512]{1,0:T(8,128)(2,1)S(1)} %project_sides.1.refs_1_), channel_id=1, source_target_pairs={{0,8},{4,12},{8,16},{12,20},{16,24},{20,28},{24,32},{28,36},{32,40... | collective-permute-start | bytes 393224 | tf_op jit(solution)/shard_map/ppermute | solution.py:26
  54.0 11.5 %collective-permute-start.10 = (bf16[128,512]{1,0:T(8,128)(2,1)S(1)}, bf16[128,512]{1,0:T(8,128)(2,1)S(1)}, u32[]{:S(2)}, u32[]{:S(2)}) collective-permute-start(bf16[128,512]{1,0:T(8,128)(2,1)S(1)} %project_sides.1.refs_1_), channel_id=1, source_target_pairs={{0,4},{4,8},{8,12},{12,16},{16,20},{20,24},{24,28},{28,32},{32,36}... | collective-permute-start | bytes 393224 | tf_op jit(solution)/shard_map/ppermute | solution.py:26
  59.1 9.1 %collective-permute-start.9 = (bf16[64,512]{1,0:T(8,128)(2,1)S(1)}, bf16[64,512]{1,0:T(8,128)(2,1)S(1)}, u32[]{:S(2)}, u32[]{:S(2)}) collective-permute-start(bf16[64,512]{1,0:T(8,128)(2,1)S(1)} %project_across_first_half.1.refs_1_), channel_id=1, source_target_pairs={{0,12},{4,16},{8,20},{12,24},{16,28},{20,32},{24,36},{28,40},{32,4... | collective-permute-start | bytes 196616 | tf_op jit(solution)/shard_map/ppermute | solution.py:26
  64.2 6.4 %collective-permute-start.8 = (bf16[64,512]{1,0:T(8,128)(2,1)S(1)}, bf16[64,512]{1,0:T(8,128)(2,1)S(1)}, u32[]{:S(2)}, u32[]{:S(2)}) collective-permute-start(bf16[64,512]{1,0:T(8,128)(2,1)S(1)} %project_across_first_half.1.refs_1_), channel_id=1, source_target_pairs={{0,8},{4,12},{8,16},{12,20},{16,24},{20,28},{24,32},{28,36},{32,40... | collective-permute-start | bytes 196616 | tf_op jit(solution)/shard_map/ppermute | solution.py:26
  65.5 5.1 %collective-permute-start.7 = (bf16[64,512]{1,0:T(8,128)(2,1)S(1)}, bf16[64,512]{1,0:T(8,128)(2,1)S(1)}, u32[]{:S(2)}, u32[]{:S(2)}) collective-permute-start(bf16[64,512]{1,0:T(8,128)(2,1)S(1)} %project_across_first_half.1.refs_1_), channel_id=1, source_target_pairs={{0,4},{4,8},{8,12},{12,16},{16,20},{20,24},{24,28},{28,32},{32,36}... | collective-permute-start | bytes 196616 | tf_op jit(solution)/shard_map/ppermute | solution.py:26

commit v13 on v12

--- a/solution.py
+++ b/solution.py
@@ -185,7 +185,7 @@
 
 def attend_cost(rows, width, keys):
     return pl.CostEstimate(
-        flops=16 * rows * width * keys,
+        flops=10 * rows * width * keys,
         transcendentals=rows * width // HEAD_SIZE * keys,
         bytes_accessed=2 * rows * width,
     )

time: 73.3 us -> 59.1 us (0.81)
  waiting for transfers between devices: 25.8 us -> 10 us
  local copies, waits for them, and re-layouts: 5.14 us -> 8.54 us
  Pallas kernels: 12.7 us -> 11.5 us
  starting transfers between devices: 28.7 us -> 27.5 us
    ppermute x13, waiting for transfers between devices: 25.8 us -> 10 us  [turned(): return lax.ppermute(value, axis, pairs)]
    unnamed x18 -> x20, local copies, waits for them, and re-layouts: 5.06 us -> 8.46 us
    pallas_call x2, Pallas kernels: 4.36 us -> 3.04 us  [project(): pl.pallas_call(project_kernel, out_shape=jax.ShapeDtypeStruct((rows, 2 *...]
    ppermute x13, starting transfers between devices: 28.7 us -> 27.5 us  [turned(): return lax.ppermute(value, axis, pairs)]
  transfers between devices with their start and end apart: 13 -> 13, of which waited for: 5 -> 4; matrix products, arithmetic and copies ran while one was open for 0% -> 1% of each run, Pallas kernels for 14% -> 16%
where the time goes in v13:
time: 59.1 us; the launch traced here: 58.2 us
  starting transfers between devices  27.5 us (47%)
  Pallas kernels  11.5 us (19%)
  waiting for transfers between devices  10 us (17%)
  local copies, waits for them, and re-layouts  8.54 us (14%)
    ppermute x13, starting transfers between devices, turned(): return lax.ppermute(value, axis, pairs)  27.5 us
    ppermute x13, waiting for transfers between devices, turned(): return lax.ppermute(value, axis, pairs)  10 us
    unnamed x20, local copies, waits for them, and re-layouts  8.46 us
    pallas_call x3, Pallas kernels, attend(): pl.pallas_call(functools.partial(attend_kernel, first, last, kv_heads), o...  6.68 us
    pallas_call x2, Pallas kernels, project(): pl.pallas_call(project_kernel, out_shape=jax.ShapeDtypeStruct((rows, 2 *...  3.04 us
  transfers between devices with their start and end apart: 13, of which 4 were waited for; matrix products, arithmetic and copies ran while one was open for 1% of the time, Pallas kernels for 16%

profile of v13, /device:TPU:1, one launch (start us, length us, event | category | flops | bytes accessed | tf_op | source)
XLA Modules:
  0.0 58.2 jit_solution(2935356131718492404)
XLA Ops:
  0.0 3.3 %collective-permute-start.5 = (bf16[64,8192]{1,0:T(8,128)(2,1)}, bf16[64,8192]{1,0:T(8,128)(2,1)S(1)}, u32[]{:S(2)}, u32[]{:S(2)}) collective-permute-start(bf16[64,8192]{1,0:T(8,128)(2,1)} %refs_0_.2), channel_id=1, source_target_pairs={{0,3},{1,0},{2,1},{3,2},{4,7},{5,4},{6,5},{7,6},{8,11},{9,8},{10,9... | collective-permute-start | bytes 3145736 | tf_op jit(solution)/shard_map/ppermute | solution.py:26
  3.3 2.2 %copy-done = bf16[8192,256]{1,0:T(8,128)(2,1)S(1)} copy-done((bf16[8192,256]{1,0:T(8,128)(2,1)S(1)}, bf16[8192,256]{1,0:T(8,128)(2,1)}, u32[]{:S(2)}) %copy-start) | copy-done | bytes 4194328
  5.5 2.2 %copy-done.2 = bf16[8192,256]{1,0:T(8,128)(2,1)S(1)} copy-done((bf16[8192,256]{1,0:T(8,128)(2,1)S(1)}, bf16[8192,256]{1,0:T(8,128)(2,1)}, u32[]{:S(2)}) %copy-start.2) | copy-done | bytes 4194328
  7.7 1.2 %copy-done.4 = bf16[64,8192]{1,0:T(8,128)(2,1)S(1)} copy-done((bf16[64,8192]{1,0:T(8,128)(2,1)S(1)}, bf16[64,8192]{1,0:T(8,128)(2,1)}, u32[]{:S(2)}) %copy-start.4) | copy-done | bytes 1048600
  8.9 0.7 %copy-done.5 = f32[128]{0:T(128)S(1)} copy-done((f32[128]{0:T(128)S(1)}, f32[128]{0:T(128)}, u32[]{:S(2)}) %copy-start.5) | copy-done | bytes 536
  9.6 1.6 %project_own.1.refs_1_ = bf16[64,512]{1,0:T(8,128)(2,1)S(1)} custom-call(bf16[64,8192]{1,0:T(8,128)(2,1)S(1)} %copy-done.4, bf16[8192,256]{1,0:T(8,128)(2,1)S(1)} %copy-done, bf16[8192,256]{1,0:T(8,128)(2,1)S(1)} %copy-done.2, f32[1,128]{1,0:T(1,128)S(1)} %bitcast.7), custom_call_target="tpu_custom_call" | custom-call | flops 536870912 | bytes 8388608 | tf_op jit(solution)/shard_map/project_own/pallas_call | solution.py:56
  11.2 5.7 %collective-permute-start.2 = (bf16[64,512]{1,0:T(8,128)(2,1)S(1)}, bf16[64,512]{1,0:T(8,128)(2,1)S(1)}, u32[]{:S(2)}, u32[]{:S(2)}) collective-permute-start(bf16[64,512]{1,0:T(8,128)(2,1)S(1)} %project_own.1.refs_1_), channel_id=1, source_target_pairs={{0,12},{4,16},{8,20},{12,24},{16,28},{20,32},{24,36},{28,40},{32,4... | collective-permute-start | bytes 196616 | tf_op jit(solution)/shard_map/ppermute | solution.py:26
  16.9 2.3 %collective-permute-start.1 = (bf16[64,512]{1,0:T(8,128)(2,1)S(1)}, bf16[64,512]{1,0:T(8,128)(2,1)S(1)}, u32[]{:S(2)}, u32[]{:S(2)}) collective-permute-start(bf16[64,512]{1,0:T(8,128)(2,1)S(1)} %project_own.1.refs_1_), channel_id=1, source_target_pairs={{0,8},{4,12},{8,16},{12,20},{16,24},{20,28},{24,32},{28,36},{32,40... | collective-permute-start | bytes 196616 | tf_op jit(solution)/shard_map/ppermute | solution.py:26
  19.2 1.9 %collective-permute-start = (bf16[64,512]{1,0:T(8,128)(2,1)S(1)}, bf16[64,512]{1,0:T(8,128)(2,1)S(1)}, u32[]{:S(2)}, u32[]{:S(2)}) collective-permute-start(bf16[64,512]{1,0:T(8,128)(2,1)S(1)} %project_own.1.refs_1_), channel_id=1, source_target_pairs={{0,4},{4,8},{8,12},{12,16},{16,20},{20,24},{24,28},{28,32},{32,36}... | collective-permute-start | bytes 196616 | tf_op jit(solution)/shard_map/ppermute | solution.py:26
  21.4 1.0 %collective-permute-done.refs_2_ = bf16[64,512]{1,0:T(8,128)(2,1)S(1)} collective-permute-done((bf16[64,512]{1,0:T(8,128)(2,1)S(1)}, bf16[64,512]{1,0:T(8,128)(2,1)S(1)}, u32[]{:S(2)}, u32[]{:S(2)}) %collective-permute-start) | collective-permute-done | bytes 65568 | tf_op jit(solution)/shard_map/ppermute | solution.py:26
  22.5 1.8 %attend_own.1 = (bf16[256,2048]{1,0:T(8,128)(2,1)S(1)}, f32[256,2048]{1,0:T(8,128)S(1)}, f32[256,128]{1,0:T(8,128)S(1)}) custom-call(bf16[256,2048]{1,0:T(8,128)(2,1)S(1)} %copy-done.7, bf16[64,512]{1,0:T(8,128)(2,1)S(1)} %project_own.1.refs_1_, bf16[64,512]{1,0:T(8,128)(2,1)S(1)} %collective-permute-done.refs_2_, ...), custom_call_target="tpu_custom_call" | custom-call | flops 1342177280 | bytes 1048576 | tf_op jit(solution)/shard_map/attend_own/pallas_call | solution.py:211
  24.3 1.2 %collective-permute-done.5.refs_1_ = bf16[64,8192]{1,0:T(8,128)(2,1)S(1)} collective-permute-done((bf16[64,8192]{1,0:T(8,128)(2,1)}, bf16[64,8192]{1,0:T(8,128)(2,1)S(1)}, u32[]{:S(2)}, u32[]{:S(2)}) %collective-permute-start.5) | collective-permute-done | bytes 1048608 | tf_op jit(solution)/shard_map/ppermute | solution.py:26
  25.5 3.4 %collective-permute-start.6 = (bf16[64,4864]{1,0:T(8,128)(2,1)S(1)}, bf16[64,4864]{1,0:T(8,128)(2,1)S(1)}, u32[]{:S(2)}, u32[]{:S(2)}) collective-permute-start(bf16[64,4864]{1,0:T(8,128)(2,1)S(1)} %slice.7), channel_id=1, source_target_pairs={{0,3},{1,0},{2,1},{3,2},{4,7},{5,4},{6,5},{7,6},{8,11},{9,8},{10,9... | collective-permute-start | bytes 1867784 | tf_op jit(solution)/shard_map/ppermute | solution.py:26
  29.0 2.2 %copy-done.3 = bf16[8192,256]{1,0:T(8,128)(2,1)S(1)} copy-done((bf16[8192,256]{1,0:T(8,128)(2,1)S(1)}, bf16[8192,256]{1,0:T(8,128)(2,1)}, u32[]{:S(2)}) %copy-start.3) | copy-done | bytes 4194328
  31.2 1.4 %project_sides.1.refs_1_ = bf16[128,512]{1,0:T(8,128)(2,1)S(1)} custom-call(bf16[64,8192]{1,0:T(8,128)(2,1)S(1)} %collective-permute-done.3.refs_0_, bf16[64,8192]{1,0:T(8,128)(2,1)S(1)} %collective-permute-done.5.refs_1_, bf16[8192,256]{1,0:T(8,128)(2,1)S(1)} %copy-done.1, bf16[8192,256]{1,0:T(8,128)(2,1)S(1)} %copy-done.3, f32[1,128]{1,0:T(1,128)S(1)} %bitcast.8), custom_call_target="tpu_custom_call" | custom-call | flops 1073741824 | bytes 8388608 | tf_op jit(solution)/shard_map/project_sides/pallas_call | solution.py:56
  32.6 4.7 %collective-permute-start.12 = (bf16[128,512]{1,0:T(8,128)(2,1)S(1)}, bf16[128,512]{1,0:T(8,128)(2,1)S(1)}, u32[]{:S(2)}, u32[]{:S(2)}) collective-permute-start(bf16[128,512]{1,0:T(8,128)(2,1)S(1)} %project_sides.1.refs_1_), channel_id=1, source_target_pairs={{0,12},{4,16},{8,20},{12,24},{16,28},{20,32},{24,36},{28,40},{32,4... | collective-permute-start | bytes 393224 | tf_op jit(solution)/shard_map/ppermute | solution.py:26
  37.7 2.9 %collective-permute-done.6.rows_ref = bf16[64,4864]{1,0:T(8,128)(2,1)S(1)} collective-permute-done((bf16[64,4864]{1,0:T(8,128)(2,1)S(1)}, bf16[64,4864]{1,0:T(8,128)(2,1)S(1)}, u32[]{:S(2)}, u32[]{:S(2)}) %collective-permute-start.6) | collective-permute-done | bytes 622624 | tf_op jit(solution)/shard_map/ppermute | solution.py:26
  40.7 1.0 %project_across_last_half.1.sums_ref = f32[64,512]{1,0:T(8,128)S(1)} custom-call(bf16[64,4864]{1,0:T(8,128)(2,1)S(1)} %collective-permute-done.6.rows_ref, bf16[8192,256]{1,0:T(8,128)(2,1)S(1)} %copy-done.1, bf16[8192,256]{1,0:T(8,128)(2,1)S(1)} %copy-done.3), custom_call_target="tpu_custom_call" | custom-call | flops 268435456 | bytes 8388608 | tf_op jit(solution)/shard_map/project_across_last_half/pallas_call | solution.py:91
  41.6 0.8 %project_across_first_half.1.refs_1_ = bf16[64,512]{1,0:T(8,128)(2,1)S(1)} custom-call(bf16[64,3328]{1,0:T(8,128)(2,1)S(1)} %collective-permute-done.4.rows_ref, f32[64,512]{1,0:T(8,128)S(1)} %project_across_last_half.1.sums_ref, bf16[8192,256]{1,0:T(8,128)(2,1)S(1)} %copy-done.1, bf16[8192,256]{1,0:T(8,128)(2,1)S(1)} %copy-done.3, f32[1,128]{1,0:T(1,128)S(1)} %bitcast.9), custom_call_target="tpu_custom_call" | custom-call | flops 268435456 | bytes 8388608 | tf_op jit(solution)/shard_map/project_across_first_half/pallas_call | solution.py:99
  42.5 5.3 %collective-permute-start.9 = (bf16[64,512]{1,0:T(8,128)(2,1)S(1)}, bf16[64,512]{1,0:T(8,128)(2,1)S(1)}, u32[]{:S(2)}, u32[]{:S(2)}) collective-permute-start(bf16[64,512]{1,0:T(8,128)(2,1)S(1)} %project_across_first_half.1.refs_1_), channel_id=1, source_target_pairs={{0,12},{4,16},{8,20},{12,24},{16,28},{20,32},{24,36},{28,40},{32,4... | collective-permute-start | bytes 196616 | tf_op jit(solution)/shard_map/ppermute | solution.py:26
  47.8 0.4 collective-permute-start.8
  48.2 2.7 %attend_sides.1 = (f32[256,2048]{1,0:T(8,128)S(1)}, f32[256,128]{1,0:T(8,128)S(1)}) custom-call(bf16[256,2048]{1,0:T(8,128)(2,1)S(1)} %get-tuple-element.22.refs_0_, bf16[128,512]{1,0:T(8,128)(2,1)S(1)} %project_sides.1.refs_1_, bf16[128,512]{1,0:T(8,128)(2,1)S(1)} %collective-permute-done.10.refs_2_, bf16[128,512]{1,0:T(8,128)(2,1)S(1)} %collective-permute-done.11.refs_3_, ...), custom_call_target="tpu_custom_call" | custom-call | flops 2684354560 | bytes 1048576 | tf_op jit(solution)/shard_map/attend_sides/pallas_call | solution.py:211
  50.9 4.9 %collective-permute-done.9.refs_4_ = bf16[64,512]{1,0:T(8,128)(2,1)S(1)} collective-permute-done((bf16[64,512]{1,0:T(8,128)(2,1)S(1)}, bf16[64,512]{1,0:T(8,128)(2,1)S(1)}, u32[]{:S(2)}, u32[]{:S(2)}) %collective-permute-start.9) | collective-permute-done | bytes 65568 | tf_op jit(solution)/shard_map/ppermute | solution.py:26
  55.8 2.2 %attend_across.1 = bf16[256,2048]{1,0:T(8,128)(2,1)} custom-call(bf16[256,2048]{1,0:T(8,128)(2,1)S(1)} %get-tuple-element.22.refs_0_, bf16[64,512]{1,0:T(8,128)(2,1)S(1)} %project_across_first_half.1.refs_1_, bf16[64,512]{1,0:T(8,128)(2,1)S(1)} %collective-permute-done.7.refs_2_, bf16[64,512]{1,0:T(8,128)(2,1)S(1)} %collective-permute-done.8.refs_3_, ...), custom_call_target="tpu_custom_call" | custom-call | flops 1342177280 | bytes 1048576 | tf_op jit(solution)/shard_map/attend_across/pallas_call | solution.py:211
  (37 shorter events, 0.9 us)
Async XLA Ops:
  0.0 25.5 %collective-permute-start.5 = (bf16[64,8192]{1,0:T(8,128)(2,1)}, bf16[64,8192]{1,0:T(8,128)(2,1)S(1)}, u32[]{:S(2)}, u32[]{:S(2)}) collective-permute-start(bf16[64,8192]{1,0:T(8,128)(2,1)} %refs_0_.2), channel_id=1, source_target_pairs={{0,3},{1,0},{2,1},{3,2},{4,7},{5,4},{6,5},{7,6},{8,11},{9,8},{10,9... | collective-permute-start | bytes 3145736 | tf_op jit(solution)/shard_map/ppermute | solution.py:26
  3.3 25.6 %collective-permute-start.3 = (bf16[64,8192]{1,0:T(8,128)(2,1)}, bf16[64,8192]{1,0:T(8,128)(2,1)S(1)}, u32[]{:S(2)}, u32[]{:S(2)}) collective-permute-start(bf16[64,8192]{1,0:T(8,128)(2,1)} %refs_0_.2), channel_id=1, source_target_pairs={{0,1},{1,2},{2,3},{3,0},{4,5},{5,6},{6,7},{7,4},{8,9},{9,10},{10,1... | collective-permute-start | bytes 3145736 | tf_op jit(solution)/shard_map/ppermute | solution.py:26
  3.3 2.2 %copy-start = (bf16[8192,256]{1,0:T(8,128)(2,1)S(1)}, bf16[8192,256]{1,0:T(8,128)(2,1)}, u32[]{:S(2)}) copy-start(bf16[8192,256]{1,0:T(8,128)(2,1)} %key_ref.3) | copy-start | bytes 12582916
  5.5 2.2 %copy-start.2 = (bf16[8192,256]{1,0:T(8,128)(2,1)S(1)}, bf16[8192,256]{1,0:T(8,128)(2,1)}, u32[]{:S(2)}) copy-start(bf16[8192,256]{1,0:T(8,128)(2,1)} %value_ref.3) | copy-start | bytes 12582916
  7.7 1.2 %copy-start.4 = (bf16[64,8192]{1,0:T(8,128)(2,1)S(1)}, bf16[64,8192]{1,0:T(8,128)(2,1)}, u32[]{:S(2)}) copy-start(bf16[64,8192]{1,0:T(8,128)(2,1)} %refs_0_.2) | copy-start | bytes 3145732
  8.9 0.7 %copy-start.5 = (f32[128]{0:T(128)S(1)}, f32[128]{0:T(128)}, u32[]{:S(2)}) copy-start(f32[128]{0:T(128)} %param.12) | copy-start | bytes 1540
  9.6 11.7 %copy-start.9 = (f32[128]{0:T(128)S(1)}, f32[128]{0:T(128)}, u32[]{:S(2)}) copy-start(f32[128]{0:T(128)} %param.11) | copy-start | bytes 1540
  9.6 11.7 %copy-start.8 = (s32[4,64]{1,0:T(4,128)S(1)}, s32[4,64]{1,0:T(4,128)}, u32[]{:S(2)}) copy-start(s32[4,64]{1,0:T(4,128)} %param.13) | copy-start | bytes 3076
  9.6 12.9 %copy-start.7 = (bf16[256,2048]{1,0:T(8,128)(2,1)S(1)}, bf16[256,2048]{1,0:T(8,128)(2,1)}, u32[]{:S(2)}) copy-start(bf16[256,2048]{1,0:T(8,128)(2,1)} %refs_0_.3) | copy-start | bytes 3145732
  11.2 17.8 %copy-start.6 = (f32[128]{0:T(128)S(1)}, f32[128]{0:T(128)}, u32[]{:S(2)}) copy-start(f32[128]{0:T(128)} %param.12) | copy-start | bytes 1540
  11.2 10.2 %collective-permute-start.2 = (bf16[64,512]{1,0:T(8,128)(2,1)S(1)}, bf16[64,512]{1,0:T(8,128)(2,1)S(1)}, u32[]{:S(2)}, u32[]{:S(2)}) collective-permute-start(bf16[64,512]{1,0:T(8,128)(2,1)S(1)} %project_own.1.refs_1_), channel_id=1, source_target_pairs={{0,12},{4,16},{8,20},{12,24},{16,28},{20,32},{24,36},{28,40},{32,4... | collective-permute-start | bytes 196616 | tf_op jit(solution)/shard_map/ppermute | solution.py:26
  16.9 4.5 %collective-permute-start.1 = (bf16[64,512]{1,0:T(8,128)(2,1)S(1)}, bf16[64,512]{1,0:T(8,128)(2,1)S(1)}, u32[]{:S(2)}, u32[]{:S(2)}) collective-permute-start(bf16[64,512]{1,0:T(8,128)(2,1)S(1)} %project_own.1.refs_1_), channel_id=1, source_target_pairs={{0,8},{4,12},{8,16},{12,20},{16,24},{20,28},{24,32},{28,36},{32,40... | collective-permute-start | bytes 196616 | tf_op jit(solution)/shard_map/ppermute | solution.py:26
  19.2 3.2 %collective-permute-start = (bf16[64,512]{1,0:T(8,128)(2,1)S(1)}, bf16[64,512]{1,0:T(8,128)(2,1)S(1)}, u32[]{:S(2)}, u32[]{:S(2)}) collective-permute-start(bf16[64,512]{1,0:T(8,128)(2,1)S(1)} %project_own.1.refs_1_), channel_id=1, source_target_pairs={{0,4},{4,8},{8,12},{12,16},{16,20},{20,24},{24,28},{28,32},{32,36}... | collective-permute-start | bytes 196616 | tf_op jit(solution)/shard_map/ppermute | solution.py:26
  21.2 7.9 %copy-start.1 = (bf16[8192,256]{1,0:T(8,128)(2,1)S(1)}, bf16[8192,256]{1,0:T(8,128)(2,1)}, u32[]{:S(2)}) copy-start(bf16[8192,256]{1,0:T(8,128)(2,1)} %key_ref.3) | copy-start | bytes 12582916
  25.5 15.2 %collective-permute-start.6 = (bf16[64,4864]{1,0:T(8,128)(2,1)S(1)}, bf16[64,4864]{1,0:T(8,128)(2,1)S(1)}, u32[]{:S(2)}, u32[]{:S(2)}) collective-permute-start(bf16[64,4864]{1,0:T(8,128)(2,1)S(1)} %slice.7), channel_id=1, source_target_pairs={{0,3},{1,0},{2,1},{3,2},{4,7},{5,4},{6,5},{7,6},{8,11},{9,8},{10,9... | collective-permute-start | bytes 1867784 | tf_op jit(solution)/shard_map/ppermute | solution.py:26
  28.9 12.7 %collective-permute-start.4 = (bf16[64,3328]{1,0:T(8,128)(2,1)S(1)}, bf16[64,3328]{1,0:T(8,128)(2,1)S(1)}, u32[]{:S(2)}, u32[]{:S(2)}) collective-permute-start(bf16[64,3328]{1,0:T(8,128)(2,1)S(1)} %slice.6), channel_id=1, source_target_pairs={{0,1},{1,2},{2,3},{3,0},{4,5},{5,6},{6,7},{7,4},{8,9},{9,10},{10,1... | collective-permute-start | bytes 1277960 | tf_op jit(solution)/shard_map/ppermute | solution.py:26
  29.0 2.2 %copy-start.3 = (bf16[8192,256]{1,0:T(8,128)(2,1)S(1)}, bf16[8192,256]{1,0:T(8,128)(2,1)}, u32[]{:S(2)}) copy-start(bf16[8192,256]{1,0:T(8,128)(2,1)} %value_ref.3) | copy-start | bytes 12582916
  32.6 15.6 %collective-permute-start.12 = (bf16[128,512]{1,0:T(8,128)(2,1)S(1)}, bf16[128,512]{1,0:T(8,128)(2,1)S(1)}, u32[]{:S(2)}, u32[]{:S(2)}) collective-permute-start(bf16[128,512]{1,0:T(8,128)(2,1)S(1)} %project_sides.1.refs_1_), channel_id=1, source_target_pairs={{0,12},{4,16},{8,20},{12,24},{16,28},{20,32},{24,36},{28,40},{32,4... | collective-permute-start | bytes 393224 | tf_op jit(solution)/shard_map/ppermute | solution.py:26
  37.3 10.9 %collective-permute-start.11 = (bf16[128,512]{1,0:T(8,128)(2,1)S(1)}, bf16[128,512]{1,0:T(8,128)(2,1)S(1)}, u32[]{:S(2)}, u32[]{:S(2)}) collective-permute-start(bf16[128,512]{1,0:T(8,128)(2,1)S(1)} %project_sides.1.refs_1_), channel_id=1, source_target_pairs={{0,8},{4,12},{8,16},{12,20},{16,24},{20,28},{24,32},{28,36},{32,40... | collective-permute-start | bytes 393224 | tf_op jit(solution)/shard_map/ppermute | solution.py:26
  37.7 10.5 %collective-permute-start.10 = (bf16[128,512]{1,0:T(8,128)(2,1)S(1)}, bf16[128,512]{1,0:T(8,128)(2,1)S(1)}, u32[]{:S(2)}, u32[]{:S(2)}) collective-permute-start(bf16[128,512]{1,0:T(8,128)(2,1)S(1)} %project_sides.1.refs_1_), channel_id=1, source_target_pairs={{0,4},{4,8},{8,12},{12,16},{16,20},{20,24},{24,28},{28,32},{32,36}... | collective-permute-start | bytes 393224 | tf_op jit(solution)/shard_map/ppermute | solution.py:26
  42.5 13.3 %collective-permute-start.9 = (bf16[64,512]{1,0:T(8,128)(2,1)S(1)}, bf16[64,512]{1,0:T(8,128)(2,1)S(1)}, u32[]{:S(2)}, u32[]{:S(2)}) collective-permute-start(bf16[64,512]{1,0:T(8,128)(2,1)S(1)} %project_across_first_half.1.refs_1_), channel_id=1, source_target_pairs={{0,12},{4,16},{8,20},{12,24},{16,28},{20,32},{24,36},{28,40},{32,4... | collective-permute-start | bytes 196616 | tf_op jit(solution)/shard_map/ppermute | solution.py:26
  47.8 8.0 %collective-permute-start.8 = (bf16[64,512]{1,0:T(8,128)(2,1)S(1)}, bf16[64,512]{1,0:T(8,128)(2,1)S(1)}, u32[]{:S(2)}, u32[]{:S(2)}) collective-permute-start(bf16[64,512]{1,0:T(8,128)(2,1)S(1)} %project_across_first_half.1.refs_1_), channel_id=1, source_target_pairs={{0,8},{4,12},{8,16},{12,20},{16,24},{20,28},{24,32},{28,36},{32,40... | collective-permute-start | bytes 196616 | tf_op jit(solution)/shard_map/ppermute | solution.py:26
  48.2 7.6 %collective-permute-start.7 = (bf16[64,512]{1,0:T(8,128)(2,1)S(1)}, bf16[64,512]{1,0:T(8,128)(2,1)S(1)}, u32[]{:S(2)}, u32[]{:S(2)}) collective-permute-start(bf16[64,512]{1,0:T(8,128)(2,1)S(1)} %project_across_first_half.1.refs_1_), channel_id=1, source_target_pairs={{0,4},{4,8},{8,12},{12,16},{16,20},{20,24},{24,28},{28,32},{32,36}... | collective-permute-start | bytes 196616 | tf_op jit(solution)/shard_map/ppermute | solution.py:26
